TPU v7x, 128 devices: a whole 4x4x4 slice. The times are simulated.
128 devices in a mesh: row: 8 (over y_lo, z), col: 16 (over x, y_hi, core).
Axes of the slice: x: 4, y: 4 (y_hi: 2, y_lo: 2; y = y_hi * 2 + y_lo), z: 4, core: 2. Of those that a mesh axis runs over, the one named last changes fastest.
Arguments:
- inputs: bfloat16 [12288, 8192], P('row', 'col'), may hold values from -6 to 6
- cotangent: bfloat16 [12288, 8192], P('row', 'col'), may hold values from -6 to 6
- conv_out: bfloat16 [12288, 8192], P('row', 'col'), may hold values from -6 to 6
- pre_act: bfloat16 [12288, 2048], P('row', 'col'), may hold values from -6 to 6
- weight_in: bfloat16 [8192, 2048], P('col', 'row'), may hold values from -0.0625 to 0.0625
- weight_out: bfloat16 [2048, 8192], P('row', 'col'), may hold values from -0.125 to 0.125
- scale_mid: float32 [2048], P('col'), may hold values from 0.3 to 3
- scale_wide: float32 [8192], P('col'), may hold values from 0.3 to 3
- keep_mid: int32 [2048], P('col'), may hold values 0 or 1
- keep_wide: int32 [8192], P('col'), may hold values 0 or 1
Outputs:
- grad_x: bfloat16 [12288, 8192], P('row', 'col')
- grad_win: float32 [8192, 2048], P('col', 'row')
- grad_wout: float32 [2048, 8192], P('row', 'col')
- grad_smid: float32 [2048], P('col')
- grad_swide: float32 [8192], P('col')
All inputs are finite; a program needn't handle non-finite values. No bound on the sum of `keep_mid` or of `keep_wide` on one device may be relied on, other than what follows from the above.
Results may differ from a plain program's by a relative error of at most 0.03.
Values may be sent and summed in bfloat16 or wider, within the bound.
No kernel may reach another device: no remote copies, remote signals or barrier semaphores. Data moves between devices by JAX's collectives and lax.ppermute only.
A program may use at most 128 MiB of HBM per device.

v0:
```python
import functools
import math

import jax
import jax.numpy as jnp
from jax import lax
from jax.experimental import pallas as pl
from jax.experimental.pallas import tpu as pltpu
from jax.sharding import PartitionSpec as P

F32 = jnp.float32
BF16 = jnp.bfloat16
AXES = ("row", "col")
STEPS = (0, 1, 3, 2)


def permute(v, target):
    pairs = []
    for row in range(8):
        for col in range(16):
            y_lo, z, x, y_hi, core = target(
                row // 4, row % 4, col // 4, (col // 2) % 2, col % 2
            )
            pairs.append(
                (row * 16 + col, (y_lo * 4 + z % 4) * 16 + (x % 4) * 4 + y_hi * 2 + core)
            )
    return lax.ppermute(v, AXES, pairs)


def core_swap(v):
    return permute(v, lambda yl, z, x, yh, c: (yl, z, x, yh, 1 - c))


def y_hi_swap(v):
    return permute(v, lambda yl, z, x, yh, c: (yl, z, x, 1 - yh, c))


def y_lo_swap(v):
    return permute(v, lambda yl, z, x, yh, c: (1 - yl, z, x, yh, c))


def z_flip(v, mask):
    return permute(v, lambda yl, z, x, yh, c: (yl, z ^ mask, x, yh, c))


def x_shift(v, step):
    return permute(v, lambda yl, z, x, yh, c: (yl, z, x + step, yh, c))


def z_shift(v, step):
    return permute(v, lambda yl, z, x, yh, c: (yl, z + step, x, yh, c))


def x_split(v, way):
    return permute(v, lambda yl, z, x, yh, c: (yl, z, x + way * (1 - 2 * c), yh, c))


def z_split(v, way):
    return permute(v, lambda yl, z, x, yh, c: (yl, z + way * (1 - 2 * c), x, yh, c))


def dot(a, b, ca, cb):
    return lax.dot_general(a, b, (((ca,), (cb,)), ((), ())), preferred_element_type=F32)


def gather(block, core, swap, shift, split):
    above, below = shift(block, -1), shift(block, 1)
    beside = swap(block)
    beside_above, beside_below = shift(beside, -1), shift(beside, 1)
    across = onward(above, below, core, split)
    beside_across = onward(beside_above, beside_below, core, split)
    return [block, beside, above, beside_above, below, beside_below, across, beside_across]


def onward(above, below, core, split):
    return split(jnp.where(core == 0, below, above), 1)


def place_of(v):
    row, col = v[0], v[1]
    return row, row >> 2, row & 3, col >> 2, (col >> 1) & 1, col & 1


def slot_of(step):
    step = step & 3
    return jnp.where(step >= 2, 5 - step, step)


def load(copies):
    for copy in copies:
        copy.start()
    for copy in copies:
        copy.wait()


def call(body, outs, scratch, loads, flops, here, vmem_args, any_args):
    vmem = pl.BlockSpec(memory_space=pltpu.VMEM)
    return pl.pallas_call(
        body,
        out_shape=outs,
        in_specs=[pl.BlockSpec(memory_space=pltpu.SMEM)]
        + [vmem] * len(vmem_args)
        + [pl.BlockSpec(memory_space=pl.ANY)] * len(any_args),
        out_specs=[vmem] * len(outs),
        scratch_shapes=[
            pltpu.VMEM(scratch, BF16),
            pltpu.SemaphoreType.DMA((len(any_args),)),
        ],
        compiler_params=pltpu.CompilerParams(vmem_limit_bytes=60 * 1024 * 1024),
        cost_estimate=pl.CostEstimate(flops=flops, bytes_accessed=loads, transcendentals=0),
    )(here, *vmem_args, *any_args)


def hid_kernel(ways, here, conv_mine, conv_beside, *refs):
    blocks, outs, (held, sems) = refs[:8], refs[8:10], refs[10:]
    load(
        [
            pltpu.make_async_copy(
                ref,
                held.at[pl.ds((k % 4) * 2, 2), :, pl.ds((k // 4) * 512, 512)],
                sems.at[k],
            )
            for k, ref in enumerate(blocks)
        ]
    )
    row, y_lo, z, x, y_hi, core = place_of(here)
    ahead = 1 - 2 * core
    for out, (fixed, way) in zip(outs, ways):
        step = fixed + way * ahead
        for i in range(2):
            block = ((x + step) & 3) * 2 + (y_hi ^ i)
            slot = slot_of((block & 3) - z) * 2 + ((block >> 2) ^ y_lo)
            total = lax.dot_general(
                conv_mine[...], held[slot, :, :512], (((1,), (1,)), ((), ())),
                preferred_element_type=F32,
            ) + lax.dot_general(
                conv_beside[...], held[slot, :, 512:], (((1,), (1,)), ((), ())),
                preferred_element_type=F32,
            )
            out[i] = total.astype(BF16)


def hid_partial(here, conv_mine, conv_beside, blocks, beside, ways):
    return call(
        functools.partial(hid_kernel, ways), [jax.ShapeDtypeStruct((2, 768, 256), BF16)] * 2,
        (8, 256, 1024), 7 << 20, 1536 * 512 * 2048, here, [conv_mine, conv_beside],
        [*blocks, *beside],
    )


def hidden_slot(block, x, y_hi):
    return slot_of((block >> 1) - x) * 2 + ((block & 1) ^ y_hi)


def load_hid(blocks, held, sems, core):
    copies = []
    for k, ref in enumerate(blocks):
        at = core if k < 8 else 1 - core
        columns = pl.ds(pl.multiple_of(at * 128, 128), 128)
        copies.append(pltpu.make_async_copy(ref, held.at[k % 8, :, columns], sems.at[k]))
    load(copies)


def load_act(blocks, held, sems, core):
    copies = []
    for k, ref in enumerate(blocks):
        at = core if k < 8 else 1 - core
        rows = pl.ds(pl.multiple_of(at * 768, 768), 768)
        copies.append(pltpu.make_async_copy(ref, held.at[k % 8, rows, :], sems.at[k]))
    load(copies)


def weight_kernel(load_blocks, here, left, *refs):
    blocks, outs, (held, sems) = refs[:16], refs[16:20], refs[20:]
    row, y_lo, z, x, y_hi, core = place_of(here)
    load_blocks(blocks, held, sems, core)
    ahead = 1 - 2 * core
    for out, step in zip(outs, (2, -ahead, ahead, 0)):
        for i in range(2):
            block = (y_lo ^ i) * 4 + ((z + step) & 3)
            out[i] = jnp.dot(
                left[...], held[hidden_slot(block, x, y_hi)], preferred_element_type=F32
            ).astype(BF16)


def weight_partial(load_blocks, here, left, blocks, beside):
    return call(
        functools.partial(weight_kernel, load_blocks), [jax.ShapeDtypeStruct((2, 512, 256), BF16)] * 4, (8, 1536, 256),
        10 << 20, 2 * 1536 * 512 * 2048, here, [left], [*blocks, *beside],
    )


def out_kernel(here, weights, cot, *refs):
    blocks, out, (held, sems) = refs[:16], refs[16], refs[17:]
    row, y_lo, z, x, y_hi, core = place_of(here)
    load_act(blocks, held, sems, core)
    for at in range(0, 1536, 256):
        total = cot[at : at + 256, :].astype(F32)
        for block in range(8):
            total = total + lax.dot_general(
                held[hidden_slot(block, x, y_hi), at : at + 256, :],
                weights[:, block * 256 : block * 256 + 256],
                (((1,), (1,)), ((), ())),
                preferred_element_type=F32,
            )
        out[at : at + 256, :] = total.astype(BF16)


def out_gradient(here, weights, cot, blocks, beside):
    return call(
        out_kernel, [jax.ShapeDtypeStruct((1536, 512), BF16)], (8, 1536, 256),
        12 << 20, 2 * 1536 * 512 * 2048, here, [weights, cot], [*blocks, *beside],
    )[0]


def tie(*values):
    return lax.optimization_barrier(values)


def add(terms):
    return sum(term.astype(F32) for term in terms)


def local(
    inputs,
    cotangent,
    conv_out,
    pre_act,
    weight_in,
    weight_out,
    scale_mid,
    scale_wide,
    keep_mid,
    keep_wide,
):
    rows = inputs.shape[0]
    half = rows // 2
    scaling = 1.0 / math.sqrt(rows * lax.axis_size("row"))
    row, col = lax.axis_index("row"), lax.axis_index("col")
    y_lo, z = row // 4, row % 4
    x, y_hi, core = col // 4, (col // 2) % 2, col % 2
    place = jnp.stack([row, col]).astype(jnp.int32)

    def mine(v):
        return lax.dynamic_slice_in_dim(v, core * half, half, 0)

    def theirs(v):
        return lax.dynamic_slice_in_dim(v, (1 - core) * half, half, 0)

    mid_gain = scale_mid * keep_mid.astype(F32)
    hidden = jnp.maximum(pre_act.astype(F32) * mid_gain, 0.0).astype(BF16)
    out_beside = y_lo_swap(weight_out)
    hid_above, hid_below = x_shift(hidden, -1), x_shift(hidden, 1)
    out_beside, hidden, cotangent, pre_act, inputs, conv_out = tie(
        out_beside, hidden, cotangent, pre_act, inputs, conv_out
    )
    hid_near = y_hi_swap(hidden)
    out_here = jnp.stack([weight_out, out_beside])
    out_above, out_below = z_shift(out_here, -1), z_shift(out_here, 1)
    out_above, hid_above, hid_below = tie(out_above, hid_above, hid_below)
    out_across = onward(out_above, out_below, core, z_split)
    out_blocks = [out_here, out_above, out_below, out_across]
    hid_across = onward(hid_above, hid_below, core, x_split)
    hid = [hidden, hid_near, hid_above, y_hi_swap(hid_above)]
    hid += [hid_below, y_hi_swap(hid_below), hid_across, y_hi_swap(hid_across)]

    wide_gain = scale_wide * keep_wide.astype(F32)
    cot_float = cotangent.astype(F32)
    grad_conv = (cot_float * wide_gain).astype(BF16)
    wide_part = jnp.sum(cot_float * conv_out.astype(F32), axis=0)
    conv_mine = mine(grad_conv)
    conv_beside = core_swap(theirs(grad_conv))

    gain_pair = jnp.stack([scale_mid, keep_mid.astype(F32)])
    gain_beside = core_swap(gain_pair)
    pre_mine = mine(pre_act)
    pre_beside = core_swap(theirs(pre_act))

    def chip_order(a, b):
        return jnp.concatenate(
            [jnp.where(core == 0, a, b), jnp.where(core == 0, b, a)], axis=1
        )

    pre_chip = chip_order(pre_mine, pre_beside).astype(F32)
    gain_chip = chip_order(gain_pair, gain_beside)
    mid_gain = gain_chip[0] * gain_chip[1]

    out_beside = [core_swap(block) for block in out_blocks]
    input_turned, conv_turned = inputs.T, grad_conv.T
    out_beside[3], weight_in, hid[1], hid[6], input_turned, conv_turned = tie(
        out_beside[3], weight_in, hid[1], hid[6], input_turned, conv_turned
    )
    in_full = lax.all_gather(weight_in, "row", axis=1, tiled=True)
    hid_beside = [core_swap(block) for block in hid]
    away, there = hid_partial(
        place, conv_mine, conv_beside, out_blocks, out_beside, ((2, 0), (0, -1))
    )
    passed, back = x_split(away, 1), x_split(there, -1)
    further, own = hid_partial(
        place, conv_mine, conv_beside, out_blocks, out_beside, ((0, 1), (0, 0))
    )
    passed, own = tie(passed, own)
    further = x_split(add([further, passed]).astype(BF16), 1)
    wout = weight_partial(load_hid, place, conv_turned, hid, hid_beside)
    further, wout, in_full = tie(further, wout, in_full)
    terms = [own, back, further]
    wout_back, wout_passed = z_split(wout[1], -1), z_split(wout[0], 1)
    total = add(terms)
    grad_hid = total[0] + y_hi_swap(total[1].astype(BF16)).astype(F32)
    alive = (pre_chip > 0) & (gain_chip[1] > 0)[None, :]
    grad_pre = jnp.where(alive, grad_hid, 0.0)
    mid_part = jnp.sum(grad_pre * pre_chip, axis=0).reshape(2, 128)
    grad_act = (grad_pre * mid_gain).astype(BF16)
    act = gather(grad_act, core, y_hi_swap, x_shift, x_split)

    mid_own = lax.dynamic_index_in_dim(mid_part, core, 0, keepdims=False)
    mid_away = lax.dynamic_index_in_dim(mid_part, 1 - core, 0, keepdims=False)
    mid_own = mid_own + core_swap(mid_away)
    sums = jnp.concatenate([mid_own, wide_part]).reshape(5, 128)
    sums = sums + z_flip(sums, 1)
    sums = sums + z_flip(sums, 2)
    sums = sums + y_lo_swap(sums)
    act_beside = [core_swap(block) for block in act]
    wout_onward = z_split(add([wout[2], wout_passed]).astype(BF16), 1)
    wout_total = add([wout[3], wout_back, wout_onward])
    wout_away = y_lo_swap(wout_total[1].astype(BF16))
    act[7], wout_total, sums = tie(act[7], wout_total, sums)
    win = weight_partial(load_act, place, input_turned, act, act_beside)
    passed, back = z_split(win[0], 1), z_split(win[1], -1)
    grad_x = out_gradient(place, in_full, cotangent, act, act_beside)
    passed, grad_x = tie(passed, grad_x)
    total = add([win[3], back, z_split(add([win[2], passed]).astype(BF16), 1)])
    grad_win = add([total[0], y_lo_swap(total[1].astype(BF16))]) * scaling
    grad_wout = add([wout_total[0], wout_away]).T * scaling
    grad_smid = keep_mid.astype(F32) * scaling * sums[0]
    grad_swide = keep_wide.astype(F32) * scaling * sums[1:].reshape(512)
    return (grad_x, grad_win, grad_wout, grad_smid, grad_swide)


def solution(mesh):
    return jax.shard_map(
        local,
        mesh=mesh,
        in_specs=(
            P("row", "col"),
            P("row", "col"),
            P("row", "col"),
            P("row", "col"),
            P("col", "row"),
            P("row", "col"),
            P("col"),
            P("col"),
            P("col"),
            P("col"),
        ),
        out_specs=(P("row", "col"), P("col", "row"), P("row", "col"), P("col"), P("col")),
        check_vma=False,
    )
```

profile of v0, /device:TPU:0, one launch (start us, length us, event | category | flops | bytes accessed | tf_op | source)
XLA Modules:
  0.0 246.9 jit_solution(3214197392153949120)
XLA Ops:
  10.7 4.7 %collective-permute-done = bf16[256,512]{1,0:T(8,128)(2,1)S(1)} collective-permute-done((bf16[256,512]{1,0:T(8,128)(2,1)}, bf16[256,512]{1,0:T(8,128)(2,1)S(1)}, u32[]{:S(2)}, u32[]{:S(2)}) %collective-permute-start) | collective-permute-done | bytes 262176 | tf_op jit(solution)/shard_map/ppermute | solution.py:27
  17.3 4.2 %collective-permute-start.2 = (bf16[2,256,512]{2,1,0:T(8,128)(2,1)}, bf16[2,256,512]{2,1,0:T(8,128)(2,1)}, u32[]{:S(2)}, u32[]{:S(2)}) collective-permute-start(bf16[2,256,512]{2,1,0:T(8,128)(2,1)} %pad_maximum_fusion.refs_0_), channel_id=1, source_target_pairs={{0,48},{1,49},{2,50},{3,51},{4,52},{5,53},{6,54},{7,55},{8,56},{9,... | collective-permute-start | bytes 1572872 | tf_op jit(solution)/shard_map/ppermute | solution.py:27
  21.5 2.8 %collective-permute-start.3 = (bf16[1536,128]{1,0:T(8,128)(2,1)S(1)}, bf16[1536,128]{1,0:T(8,128)(2,1)S(1)}, u32[]{:S(2)}, u32[]{:S(2)}) collective-permute-start(bf16[1536,128]{1,0:T(8,128)(2,1)S(1)} %maximum_convert_fusion.refs_0_), channel_id=1, source_target_pairs={{0,12},{1,13},{2,14},{3,15},{4,0},{5,1},{6,2},{7,3},{8,4},{9,5},{1... | collective-permute-start | bytes 1179656 | tf_op jit(solution)/shard_map/ppermute | solution.py:27
  24.2 7.2 %collective-permute-done.3.refs_2_ = bf16[1536,128]{1,0:T(8,128)(2,1)S(1)} collective-permute-done((bf16[1536,128]{1,0:T(8,128)(2,1)S(1)}, bf16[1536,128]{1,0:T(8,128)(2,1)S(1)}, u32[]{:S(2)}, u32[]{:S(2)}) %collective-permute-start.3) | collective-permute-done | bytes 393248 | tf_op jit(solution)/shard_map/ppermute | solution.py:27
  31.5 3.4 %collective-permute-done.4.refs_4_ = bf16[1536,128]{1,0:T(8,128)(2,1)S(1)} collective-permute-done((bf16[1536,128]{1,0:T(8,128)(2,1)S(1)}, bf16[1536,128]{1,0:T(8,128)(2,1)S(1)}, u32[]{:S(2)}, u32[]{:S(2)}) %collective-permute-start.4) | collective-permute-done | bytes 393248 | tf_op jit(solution)/shard_map/ppermute | solution.py:27
  36.7 3.3 %collective-permute-start.7 = (bf16[1536,128]{1,0:T(8,128)(2,1)S(1)}, bf16[1536,128]{1,0:T(8,128)(2,1)}, u32[]{:S(2)}, u32[]{:S(2)}) collective-permute-start(bf16[1536,128]{1,0:T(8,128)(2,1)S(1)} %maximum_convert_fusion.refs_0_), channel_id=1, source_target_pairs={{0,2},{1,3},{2,0},{3,1},{4,6},{5,7},{6,4},{7,5},{8,10},{9,11},{10,... | collective-permute-start | bytes 1179656 | tf_op jit(solution)/shard_map/ppermute | solution.py:27
  42.2 4.9 %collective-permute-done.5.refs_3_ = bf16[2,256,512]{2,1,0:T(8,128)(2,1)} collective-permute-done((bf16[2,256,512]{2,1,0:T(8,128)(2,1)S(1)}, bf16[2,256,512]{2,1,0:T(8,128)(2,1)}, u32[]{:S(2)}, u32[]{:S(2)}) %collective-permute-start.5) | collective-permute-done | bytes 524320 | tf_op jit(solution)/shard_map/ppermute | solution.py:27
  60.9 6.4 %shard_map.137 = (bf16[2,768,256]{2,1,0:T(8,128)(2,1)}, bf16[2,768,256]{2,1,0:T(8,128)(2,1)}) custom-call(s32[2]{0:T(128)} %pad_add_fusion.here, bf16[768,512]{1,0:T(8,128)(2,1)} %copy.17.conv_mine, bf16[768,512]{1,0:T(8,128)(2,1)} %copy.18.conv_beside, bf16[2,256,512]{2,1,0:T(8,128)(2,1)} %pad_maximum_fusion.refs_0_, ...), custom_call_target="tpu_custom_call" | custom-call | flops 1610612736 | bytes 7340032 | tf_op jit(solution)/shard_map/pallas_call | solution.py:98
  70.2 3.2 %collective-permute-start.18 = (bf16[1536,128]{1,0:T(8,128)(2,1)S(1)}, bf16[1536,128]{1,0:T(8,128)(2,1)}, u32[]{:S(2)}, u32[]{:S(2)}) collective-permute-start(bf16[1536,128]{1,0:T(8,128)(2,1)S(1)} %copy-done.12), channel_id=1, source_target_pairs={{0,2},{1,3},{2,0},{3,1},{4,6},{5,7},{6,4},{7,5},{8,10},{9,11},{10,... | collective-permute-start | bytes 1179656 | tf_op jit(solution)/shard_map/ppermute | solution.py:27
  75.5 14.4 %collective-permute-done.18.refs_3_ = bf16[1536,128]{1,0:T(8,128)(2,1)} collective-permute-done((bf16[1536,128]{1,0:T(8,128)(2,1)S(1)}, bf16[1536,128]{1,0:T(8,128)(2,1)}, u32[]{:S(2)}, u32[]{:S(2)}) %collective-permute-start.18) | collective-permute-done | bytes 393248 | tf_op jit(solution)/shard_map/ppermute | solution.py:27
  89.9 2.8 %collective-permute-start.20 = (bf16[1536,128]{1,0:T(8,128)(2,1)}, bf16[1536,128]{1,0:T(8,128)(2,1)}, u32[]{:S(2)}, u32[]{:S(2)}) collective-permute-start(bf16[1536,128]{1,0:T(8,128)(2,1)} %collective-permute-done.8.refs_6_), channel_id=1, source_target_pairs={{0,2},{1,3},{2,0},{3,1},{4,6},{5,7},{6,4},{7,5},{8,10},{9,11},{10,... | collective-permute-start | bytes 1179656 | tf_op jit(solution)/shard_map/ppermute | solution.py:27
  92.7 12.9 %collective-permute-done.19.refs_5_ = bf16[1536,128]{1,0:T(8,128)(2,1)} collective-permute-done((bf16[1536,128]{1,0:T(8,128)(2,1)S(1)}, bf16[1536,128]{1,0:T(8,128)(2,1)}, u32[]{:S(2)}, u32[]{:S(2)}) %collective-permute-start.19) | collective-permute-done | bytes 393248 | tf_op jit(solution)/shard_map/ppermute | solution.py:27
  106.1 6.3 %shard_map.138 = (bf16[2,768,256]{2,1,0:T(8,128)(2,1)}, bf16[2,768,256]{2,1,0:T(8,128)(2,1)}) custom-call(s32[2]{0:T(128)} %pad_add_fusion.here, bf16[768,512]{1,0:T(8,128)(2,1)} %copy.17.conv_mine, bf16[768,512]{1,0:T(8,128)(2,1)} %copy.18.conv_beside, bf16[2,256,512]{2,1,0:T(8,128)(2,1)} %pad_maximum_fusion.refs_0_, ...), custom_call_target="tpu_custom_call" | custom-call | flops 1610612736 | bytes 7340032 | tf_op jit(solution)/shard_map/pallas_call | solution.py:98
  121.8 8.5 %shard_map.139 = (bf16[2,512,256]{2,1,0:T(8,128)(2,1)}, bf16[2,512,256]{2,1,0:T(8,128)(2,1)}, bf16[2,512,256]{2,1,0:T(8,128)(2,1)}, bf16[2,512,256]{2,1,0:T(8,128)(2,1)}) custom-call(s32[2]{0:T(128)} %pad_add_fusion.here, bf16[512,1536]{1,0:T(8,128)(2,1)} %bitcast.57, bf16[1536,128]{1,0:T(8,128)(2,1)} %copy-done.10, ...), custom_call_target="tpu_custom_call" | custom-call | flops 3221225472 | bytes 10485760 | tf_op jit(solution)/shard_map/pallas_call | solution.py:98
  130.4 3.8 %collective-permute-done.17 = bf16[2,768,256]{2,1,0:T(8,128)(2,1)S(1)} collective-permute-done((bf16[2,768,256]{2,1,0:T(8,128)(2,1)S(1)}, bf16[2,768,256]{2,1,0:T(8,128)(2,1)S(1)}, u32[]{:S(2)}, u32[]{:S(2)}) %collective-permute-start.17) | collective-permute-done | bytes 786464 | tf_op jit(solution)/shard_map/ppermute | solution.py:27
  134.5 3.5 %collective-permute-start.29 = (bf16[768,256]{1,0:T(8,128)(2,1)S(1)}, bf16[768,256]{1,0:T(8,128)(2,1)S(1)}, u32[]{:S(2)}, u32[]{:S(2)}) collective-permute-start(bf16[768,256]{1,0:T(8,128)(2,1)S(1)} %fusion.10), channel_id=1, source_target_pairs={{0,2},{1,3},{2,0},{3,1},{4,6},{5,7},{6,4},{7,5},{8,10},{9,11},{10,... | collective-permute-start | bytes 1179656 | tf_op jit(solution)/shard_map/ppermute | solution.py:27
  139.0 8.9 %collective-permute-done.29 = bf16[768,256]{1,0:T(8,128)(2,1)S(1)} collective-permute-done((bf16[768,256]{1,0:T(8,128)(2,1)S(1)}, bf16[768,256]{1,0:T(8,128)(2,1)S(1)}, u32[]{:S(2)}, u32[]{:S(2)}) %collective-permute-start.29) | collective-permute-done | bytes 393248 | tf_op jit(solution)/shard_map/ppermute | solution.py:27
  149.6 3.4 %collective-permute-start.30 = (bf16[768,256]{1,0:T(8,128)(2,1)S(1)}, bf16[768,256]{1,0:T(8,128)(2,1)S(1)}, u32[]{:S(2)}, u32[]{:S(2)}) collective-permute-start(bf16[768,256]{1,0:T(8,128)(2,1)S(1)} %get-tuple-element.93.refs_0_), channel_id=1, source_target_pairs={{0,2},{1,3},{2,0},{3,1},{4,6},{5,7},{6,4},{7,5},{8,10},{9,11},{10,... | collective-permute-start | bytes 1179656 | tf_op jit(solution)/shard_map/ppermute | solution.py:27
  157.0 3.4 %collective-permute-start.37 = (bf16[2,512,256]{2,1,0:T(8,128)(2,1)}, bf16[2,512,256]{2,1,0:T(8,128)(2,1)S(1)}, u32[]{:S(2)}, u32[]{:S(2)}) collective-permute-start(bf16[2,512,256]{2,1,0:T(8,128)(2,1)} %get-tuple-element.71), channel_id=1, source_target_pairs={{0,48},{1,17},{2,50},{3,19},{4,52},{5,21},{6,54},{7,23},{8,56},{9,... | collective-permute-start | bytes 1572872 | tf_op jit(solution)/shard_map/ppermute | solution.py:27
  165.2 6.1 %collective-permute-done.31.refs_2_ = bf16[768,256]{1,0:T(8,128)(2,1)S(1)} collective-permute-done((bf16[768,256]{1,0:T(8,128)(2,1)S(1)}, bf16[768,256]{1,0:T(8,128)(2,1)S(1)}, u32[]{:S(2)}, u32[]{:S(2)}) %collective-permute-start.31) | collective-permute-done | bytes 393248 | tf_op jit(solution)/shard_map/ppermute | solution.py:27
  171.2 3.4 %collective-permute-done.33.refs_4_ = bf16[768,256]{1,0:T(8,128)(2,1)S(1)} collective-permute-done((bf16[768,256]{1,0:T(8,128)(2,1)S(1)}, bf16[768,256]{1,0:T(8,128)(2,1)S(1)}, u32[]{:S(2)}, u32[]{:S(2)}) %collective-permute-start.33) | collective-permute-done | bytes 393248 | tf_op jit(solution)/shard_map/ppermute | solution.py:27
  179.2 3.0 %collective-permute-done.34.refs_5_ = bf16[768,256]{1,0:T(8,128)(2,1)S(1)} collective-permute-done((bf16[768,256]{1,0:T(8,128)(2,1)S(1)}, bf16[768,256]{1,0:T(8,128)(2,1)S(1)}, u32[]{:S(2)}, u32[]{:S(2)}) %collective-permute-start.34) | collective-permute-done | bytes 393248 | tf_op jit(solution)/shard_map/ppermute | solution.py:27
  183.4 3.9 %collective-permute-done.39 = bf16[2,512,256]{2,1,0:T(8,128)(2,1)S(1)} collective-permute-done((bf16[2,512,256]{2,1,0:T(8,128)(2,1)S(1)}, bf16[2,512,256]{2,1,0:T(8,128)(2,1)S(1)}, u32[]{:S(2)}, u32[]{:S(2)}) %collective-permute-start.39) | collective-permute-done | bytes 524320 | tf_op jit(solution)/shard_map/ppermute | solution.py:27
  187.3 3.9 %collective-permute-done.35.refs_6_ = bf16[768,256]{1,0:T(8,128)(2,1)S(1)} collective-permute-done((bf16[768,256]{1,0:T(8,128)(2,1)S(1)}, bf16[768,256]{1,0:T(8,128)(2,1)S(1)}, u32[]{:S(2)}, u32[]{:S(2)}) %collective-permute-start.35) | collective-permute-done | bytes 393248 | tf_op jit(solution)/shard_map/ppermute | solution.py:27
  191.8 3.6 %collective-permute-done.36.refs_7_ = bf16[768,256]{1,0:T(8,128)(2,1)S(1)} collective-permute-done((bf16[768,256]{1,0:T(8,128)(2,1)S(1)}, bf16[768,256]{1,0:T(8,128)(2,1)S(1)}, u32[]{:S(2)}, u32[]{:S(2)}) %collective-permute-start.36) | collective-permute-done | bytes 393248 | tf_op jit(solution)/shard_map/ppermute | solution.py:27
  197.4 8.5 %shard_map.140 = (bf16[2,512,256]{2,1,0:T(8,128)(2,1)}, bf16[2,512,256]{2,1,0:T(8,128)(2,1)}, bf16[2,512,256]{2,1,0:T(8,128)(2,1)}, bf16[2,512,256]{2,1,0:T(8,128)(2,1)}) custom-call(s32[2]{0:T(128)} %pad_add_fusion.here, bf16[512,1536]{1,0:T(8,128)(2,1)} %bitcast.58, bf16[768,256]{1,0:T(8,128)(2,1)} %copy-done.9, bf16[768,256]{1,0:T(8,128)(2,1)} %copy-done.28, ...), custom_call_target="tpu_custom_call" | custom-call | flops 3221225472 | bytes 10485760 | tf_op jit(solution)/shard_map/pallas_call | solution.py:98
  206.1 3.2 %collective-permute-start.53 = (bf16[2,512,256]{2,1,0:T(8,128)(2,1)}, bf16[2,512,256]{2,1,0:T(8,128)(2,1)S(1)}, u32[]{:S(2)}, u32[]{:S(2)}) collective-permute-start(bf16[2,512,256]{2,1,0:T(8,128)(2,1)} %get-tuple-element.80), channel_id=1, source_target_pairs={{0,48},{1,17},{2,50},{3,19},{4,52},{5,21},{6,54},{7,23},{8,56},{9,... | collective-permute-start | bytes 1572872 | tf_op jit(solution)/shard_map/ppermute | solution.py:27
  209.3 9.5 %shard_map.141 = bf16[1536,512]{1,0:T(8,128)(2,1)} custom-call(s32[2]{0:T(128)} %pad_add_fusion.here, bf16[512,2048]{1,0:T(8,128)(2,1)} %all-gather.2.cloned.1.call-done.weights, bf16[1536,512]{1,0:T(8,128)(2,1)} %cot, bf16[768,256]{1,0:T(8,128)(2,1)} %copy-done.9, bf16[768,256]{1,0:T(8,128)(2,1)} %copy-done.28, bf16[768,256]{1,0:T(8,128)(2,1)} %copy-done.15, ...), custom_call_target="tpu_custom_call" | custom-call | flops 3221225472 | bytes 12582912 | tf_op jit(solution)/shard_map/pallas_call | solution.py:98
  218.9 3.0 %collective-permute-done.52 = bf16[2,512,256]{2,1,0:T(8,128)(2,1)S(1)} collective-permute-done((bf16[2,512,256]{2,1,0:T(8,128)(2,1)}, bf16[2,512,256]{2,1,0:T(8,128)(2,1)S(1)}, u32[]{:S(2)}, u32[]{:S(2)}) %collective-permute-start.52) | collective-permute-done | bytes 524320 | tf_op jit(solution)/shard_map/ppermute | solution.py:27
  222.9 6.0 %collective-permute-done.56 = bf16[512,256]{1,0:T(8,128)(2,1)S(1)} collective-permute-done((bf16[512,256]{1,0:T(8,128)(2,1)S(1)}, bf16[512,256]{1,0:T(8,128)(2,1)S(1)}, u32[]{:S(2)}, u32[]{:S(2)}) %collective-permute-start.56) | collective-permute-done | bytes 262176 | tf_op jit(solution)/shard_map/ppermute | solution.py:27
  228.9 3.6 %collective-permute-done.54 = bf16[2,512,256]{2,1,0:T(8,128)(2,1)S(1)} collective-permute-done((bf16[2,512,256]{2,1,0:T(8,128)(2,1)S(1)}, bf16[2,512,256]{2,1,0:T(8,128)(2,1)S(1)}, u32[]{:S(2)}, u32[]{:S(2)}) %collective-permute-start.54) | collective-permute-done | bytes 524320 | tf_op jit(solution)/shard_map/ppermute | solution.py:27
  235.5 3.7 %collective-permute-done.55 = bf16[512,256]{1,0:T(8,128)(2,1)S(1)} collective-permute-done((bf16[512,256]{1,0:T(8,128)(2,1)S(1)}, bf16[512,256]{1,0:T(8,128)(2,1)S(1)}, u32[]{:S(2)}, u32[]{:S(2)}) %collective-permute-start.55) | collective-permute-done | bytes 262176 | tf_op jit(solution)/shard_map/ppermute | solution.py:27
  (220 shorter events, 62.9 us)
Async XLA Ops:
  7.2 127.0 %all-gather.2.cloned.1.call-start = ((), (), s32[]{:S(2)}) async-start(), calls=%async_computation | async-start | bytes 2359296 | tf_op jit(solution)/shard_map/all_gather | solution.py:293
  17.3 17.6 %collective-permute-start.2 = (bf16[2,256,512]{2,1,0:T(8,128)(2,1)}, bf16[2,256,512]{2,1,0:T(8,128)(2,1)}, u32[]{:S(2)}, u32[]{:S(2)}) collective-permute-start(bf16[2,256,512]{2,1,0:T(8,128)(2,1)} %pad_maximum_fusion.refs_0_), channel_id=1, source_target_pairs={{0,48},{1,49},{2,50},{3,51},{4,52},{5,53},{6,54},{7,55},{8,56},{9,... | collective-permute-start | bytes 1572872 | tf_op jit(solution)/shard_map/ppermute | solution.py:27
  21.5 14.0 %collective-permute-start.1 = (bf16[2,256,512]{2,1,0:T(8,128)(2,1)}, bf16[2,256,512]{2,1,0:T(8,128)(2,1)}, u32[]{:S(2)}, u32[]{:S(2)}) collective-permute-start(bf16[2,256,512]{2,1,0:T(8,128)(2,1)} %pad_maximum_fusion.refs_0_), channel_id=1, source_target_pairs={{0,16},{1,17},{2,18},{3,19},{4,20},{5,21},{6,22},{7,23},{8,24},{9,... | collective-permute-start | bytes 1572872 | tf_op jit(solution)/shard_map/ppermute | solution.py:27
  24.2 10.6 %collective-permute-start.4 = (bf16[1536,128]{1,0:T(8,128)(2,1)S(1)}, bf16[1536,128]{1,0:T(8,128)(2,1)S(1)}, u32[]{:S(2)}, u32[]{:S(2)}) collective-permute-start(bf16[1536,128]{1,0:T(8,128)(2,1)S(1)} %maximum_convert_fusion.refs_0_), channel_id=1, source_target_pairs={{0,4},{1,5},{2,6},{3,7},{4,8},{5,9},{6,10},{7,11},{8,12},{9,13},{1... | collective-permute-start | bytes 1179656 | tf_op jit(solution)/shard_map/ppermute | solution.py:27
  36.6 10.6 %collective-permute-start.5 = (bf16[2,256,512]{2,1,0:T(8,128)(2,1)S(1)}, bf16[2,256,512]{2,1,0:T(8,128)(2,1)}, u32[]{:S(2)}, u32[]{:S(2)}) collective-permute-start(bf16[2,256,512]{2,1,0:T(8,128)(2,1)S(1)} %broadcast_select_fusion), channel_id=1, source_target_pairs={{0,16},{1,49},{2,18},{3,51},{4,20},{5,53},{6,22},{7,55},{8,24},{9,... | collective-permute-start | bytes 1572872 | tf_op jit(solution)/shard_map/ppermute | solution.py:27
  36.7 17.6 %collective-permute-start.7 = (bf16[1536,128]{1,0:T(8,128)(2,1)S(1)}, bf16[1536,128]{1,0:T(8,128)(2,1)}, u32[]{:S(2)}, u32[]{:S(2)}) collective-permute-start(bf16[1536,128]{1,0:T(8,128)(2,1)S(1)} %maximum_convert_fusion.refs_0_), channel_id=1, source_target_pairs={{0,2},{1,3},{2,0},{3,1},{4,6},{5,7},{6,4},{7,5},{8,10},{9,11},{10,... | collective-permute-start | bytes 1179656 | tf_op jit(solution)/shard_map/ppermute | solution.py:27
  40.8 13.6 %collective-permute-start.8 = (bf16[1536,128]{1,0:T(8,128)(2,1)}, bf16[1536,128]{1,0:T(8,128)(2,1)}, u32[]{:S(2)}, u32[]{:S(2)}) collective-permute-start(bf16[1536,128]{1,0:T(8,128)(2,1)} %broadcast_select_fusion.3), channel_id=1, source_target_pairs={{0,4},{1,13},{2,6},{3,15},{4,8},{5,1},{6,10},{7,3},{8,12},{9,5},{1... | collective-permute-start | bytes 1179656 | tf_op jit(solution)/shard_map/ppermute | solution.py:27
  67.3 38.3 %collective-permute-start.15 = (bf16[2,768,256]{2,1,0:T(8,128)(2,1)}, bf16[2,768,256]{2,1,0:T(8,128)(2,1)S(1)}, u32[]{:S(2)}, u32[]{:S(2)}) collective-permute-start(bf16[2,768,256]{2,1,0:T(8,128)(2,1)} %get-tuple-element.55), channel_id=1, source_target_pairs={{0,4},{1,13},{2,6},{3,15},{4,8},{5,1},{6,10},{7,3},{8,12},{9,5},{1... | collective-permute-start | bytes 2359304 | tf_op jit(solution)/shard_map/ppermute | solution.py:27
  70.2 19.7 %collective-permute-start.18 = (bf16[1536,128]{1,0:T(8,128)(2,1)S(1)}, bf16[1536,128]{1,0:T(8,128)(2,1)}, u32[]{:S(2)}, u32[]{:S(2)}) collective-permute-start(bf16[1536,128]{1,0:T(8,128)(2,1)S(1)} %copy-done.12), channel_id=1, source_target_pairs={{0,2},{1,3},{2,0},{3,1},{4,6},{5,7},{6,4},{7,5},{8,10},{9,11},{10,... | collective-permute-start | bytes 1179656 | tf_op jit(solution)/shard_map/ppermute | solution.py:27
  73.4 32.2 %collective-permute-start.19 = (bf16[1536,128]{1,0:T(8,128)(2,1)S(1)}, bf16[1536,128]{1,0:T(8,128)(2,1)}, u32[]{:S(2)}, u32[]{:S(2)}) collective-permute-start(bf16[1536,128]{1,0:T(8,128)(2,1)S(1)} %copy-done.14), channel_id=1, source_target_pairs={{0,2},{1,3},{2,0},{3,1},{4,6},{5,7},{6,4},{7,5},{8,10},{9,11},{10,... | collective-permute-start | bytes 1179656 | tf_op jit(solution)/shard_map/ppermute | solution.py:27
  75.0 38.8 %collective-permute-start.23 = (bf16[1536,128]{1,0:T(8,128)(2,1)S(1)}, bf16[1536,128]{1,0:T(8,128)(2,1)}, u32[]{:S(2)}, u32[]{:S(2)}) collective-permute-start(bf16[1536,128]{1,0:T(8,128)(2,1)S(1)} %copy-done.12), channel_id=1, source_target_pairs={{0,1},{1,0},{2,3},{3,2},{4,5},{5,4},{6,7},{7,6},{8,9},{9,8},{10,11... | collective-permute-start | bytes 1179656 | tf_op jit(solution)/shard_map/ppermute | solution.py:27
  75.2 39.5 %collective-permute-start.25 = (bf16[1536,128]{1,0:T(8,128)(2,1)S(1)}, bf16[1536,128]{1,0:T(8,128)(2,1)S(1)}, u32[]{:S(2)}, u32[]{:S(2)}) collective-permute-start(bf16[1536,128]{1,0:T(8,128)(2,1)S(1)} %copy-done.14), channel_id=1, source_target_pairs={{0,1},{1,0},{2,3},{3,2},{4,5},{5,4},{6,7},{7,6},{8,9},{9,8},{10,11... | collective-permute-start | bytes 1179656 | tf_op jit(solution)/shard_map/ppermute | solution.py:27
  89.9 28.1 %collective-permute-start.20 = (bf16[1536,128]{1,0:T(8,128)(2,1)}, bf16[1536,128]{1,0:T(8,128)(2,1)}, u32[]{:S(2)}, u32[]{:S(2)}) collective-permute-start(bf16[1536,128]{1,0:T(8,128)(2,1)} %collective-permute-done.8.refs_6_), channel_id=1, source_target_pairs={{0,2},{1,3},{2,0},{3,1},{4,6},{5,7},{6,4},{7,5},{8,10},{9,11},{10,... | collective-permute-start | bytes 1179656 | tf_op jit(solution)/shard_map/ppermute | solution.py:27
  105.6 12.4 %collective-permute-start.24 = (bf16[1536,128]{1,0:T(8,128)(2,1)}, bf16[1536,128]{1,0:T(8,128)(2,1)}, u32[]{:S(2)}, u32[]{:S(2)}) collective-permute-start(bf16[1536,128]{1,0:T(8,128)(2,1)} %collective-permute-done.18.refs_3_), channel_id=1, source_target_pairs={{0,1},{1,0},{2,3},{3,2},{4,5},{5,4},{6,7},{7,6},{8,9},{9,8},{10,11... | collective-permute-start | bytes 1179656 | tf_op jit(solution)/shard_map/ppermute | solution.py:27
  105.6 12.9 %collective-permute-start.26 = (bf16[1536,128]{1,0:T(8,128)(2,1)}, bf16[1536,128]{1,0:T(8,128)(2,1)}, u32[]{:S(2)}, u32[]{:S(2)}) collective-permute-start(bf16[1536,128]{1,0:T(8,128)(2,1)} %collective-permute-done.19.refs_5_), channel_id=1, source_target_pairs={{0,1},{1,0},{2,3},{3,2},{4,5},{5,4},{6,7},{7,6},{8,9},{9,8},{10,11... | collective-permute-start | bytes 1179656 | tf_op jit(solution)/shard_map/ppermute | solution.py:27
  113.8 20.3 %collective-permute-start.17 = (bf16[2,768,256]{2,1,0:T(8,128)(2,1)S(1)}, bf16[2,768,256]{2,1,0:T(8,128)(2,1)S(1)}, u32[]{:S(2)}, u32[]{:S(2)}) collective-permute-start(bf16[2,768,256]{2,1,0:T(8,128)(2,1)S(1)} %add_convert_fusion), channel_id=1, source_target_pairs={{0,4},{1,13},{2,6},{3,15},{4,8},{5,1},{6,10},{7,3},{8,12},{9,5},{1... | collective-permute-start | bytes 2359304 | tf_op jit(solution)/shard_map/ppermute | solution.py:27
  115.5 18.7 %collective-permute-start.16 = (bf16[2,768,256]{2,1,0:T(8,128)(2,1)}, bf16[2,768,256]{2,1,0:T(8,128)(2,1)S(1)}, u32[]{:S(2)}, u32[]{:S(2)}) collective-permute-start(bf16[2,768,256]{2,1,0:T(8,128)(2,1)} %get-tuple-element.58), channel_id=1, source_target_pairs={{0,12},{1,5},{2,14},{3,7},{4,0},{5,9},{6,2},{7,11},{8,4},{9,13},{1... | collective-permute-start | bytes 2359304 | tf_op jit(solution)/shard_map/ppermute | solution.py:27
  121.0 17.0 %collective-permute-start.9 = (bf16[768,128]{1,0:T(8,128)(2,1)}, bf16[768,128]{1,0:T(8,128)(2,1)}, u32[]{:S(2)}, u32[]{:S(2)}) collective-permute-start(bf16[768,128]{1,0:T(8,128)(2,1)} %constant_dynamic-slice_fusion.4), channel_id=1, source_target_pairs={{0,1},{1,0},{2,3},{3,2},{4,5},{5,4},{6,7},{7,6},{8,9},{9,8},{10,11... | collective-permute-start | bytes 589832 | tf_op jit(solution)/shard_map/ppermute | solution.py:27
  134.5 13.4 %collective-permute-start.29 = (bf16[768,256]{1,0:T(8,128)(2,1)S(1)}, bf16[768,256]{1,0:T(8,128)(2,1)S(1)}, u32[]{:S(2)}, u32[]{:S(2)}) collective-permute-start(bf16[768,256]{1,0:T(8,128)(2,1)S(1)} %fusion.10), channel_id=1, source_target_pairs={{0,2},{1,3},{2,0},{3,1},{4,6},{5,7},{6,4},{7,5},{8,10},{9,11},{10,... | collective-permute-start | bytes 1179656 | tf_op jit(solution)/shard_map/ppermute | solution.py:27
  148.4 16.4 %collective-permute-start.38 = (bf16[2,512,256]{2,1,0:T(8,128)(2,1)S(1)}, bf16[2,512,256]{2,1,0:T(8,128)(2,1)S(1)}, u32[]{:S(2)}, u32[]{:S(2)}) collective-permute-start(bf16[2,512,256]{2,1,0:T(8,128)(2,1)S(1)} %copy-done.26), channel_id=1, source_target_pairs={{0,16},{1,49},{2,18},{3,51},{4,20},{5,53},{6,22},{7,55},{8,24},{9,... | collective-permute-start | bytes 1572872 | tf_op jit(solution)/shard_map/ppermute | solution.py:27
  149.6 13.4 %collective-permute-start.30 = (bf16[768,256]{1,0:T(8,128)(2,1)S(1)}, bf16[768,256]{1,0:T(8,128)(2,1)S(1)}, u32[]{:S(2)}, u32[]{:S(2)}) collective-permute-start(bf16[768,256]{1,0:T(8,128)(2,1)S(1)} %get-tuple-element.93.refs_0_), channel_id=1, source_target_pairs={{0,2},{1,3},{2,0},{3,1},{4,6},{5,7},{6,4},{7,5},{8,10},{9,11},{10,... | collective-permute-start | bytes 1179656 | tf_op jit(solution)/shard_map/ppermute | solution.py:27
  157.0 25.4 %collective-permute-start.37 = (bf16[2,512,256]{2,1,0:T(8,128)(2,1)}, bf16[2,512,256]{2,1,0:T(8,128)(2,1)S(1)}, u32[]{:S(2)}, u32[]{:S(2)}) collective-permute-start(bf16[2,512,256]{2,1,0:T(8,128)(2,1)} %get-tuple-element.71), channel_id=1, source_target_pairs={{0,48},{1,17},{2,50},{3,19},{4,52},{5,21},{6,54},{7,23},{8,56},{9,... | collective-permute-start | bytes 1572872 | tf_op jit(solution)/shard_map/ppermute | solution.py:27
  160.4 10.8 %collective-permute-start.31 = (bf16[768,256]{1,0:T(8,128)(2,1)S(1)}, bf16[768,256]{1,0:T(8,128)(2,1)S(1)}, u32[]{:S(2)}, u32[]{:S(2)}) collective-permute-start(bf16[768,256]{1,0:T(8,128)(2,1)S(1)} %get-tuple-element.93.refs_0_), channel_id=1, source_target_pairs={{0,12},{1,13},{2,14},{3,15},{4,0},{5,1},{6,2},{7,3},{8,4},{9,5},{1... | collective-permute-start | bytes 1179656 | tf_op jit(solution)/shard_map/ppermute | solution.py:27
  161.5 13.2 %collective-permute-start.33 = (bf16[768,256]{1,0:T(8,128)(2,1)S(1)}, bf16[768,256]{1,0:T(8,128)(2,1)S(1)}, u32[]{:S(2)}, u32[]{:S(2)}) collective-permute-start(bf16[768,256]{1,0:T(8,128)(2,1)S(1)} %get-tuple-element.93.refs_0_), channel_id=1, source_target_pairs={{0,4},{1,5},{2,6},{3,7},{4,8},{5,9},{6,10},{7,11},{8,12},{9,13},{1... | collective-permute-start | bytes 1179656 | tf_op jit(solution)/shard_map/ppermute | solution.py:27
  163.0 13.9 %collective-permute-start.32 = (bf16[768,256]{1,0:T(8,128)(2,1)S(1)}, bf16[768,256]{1,0:T(8,128)(2,1)S(1)}, u32[]{:S(2)}, u32[]{:S(2)}) collective-permute-start(bf16[768,256]{1,0:T(8,128)(2,1)S(1)} %collective-permute-done.30.refs_1_), channel_id=1, source_target_pairs={{0,12},{1,13},{2,14},{3,15},{4,0},{5,1},{6,2},{7,3},{8,4},{9,5},{1... | collective-permute-start | bytes 1179656 | tf_op jit(solution)/shard_map/ppermute | solution.py:27
  164.8 17.4 %collective-permute-start.34 = (bf16[768,256]{1,0:T(8,128)(2,1)S(1)}, bf16[768,256]{1,0:T(8,128)(2,1)S(1)}, u32[]{:S(2)}, u32[]{:S(2)}) collective-permute-start(bf16[768,256]{1,0:T(8,128)(2,1)S(1)} %collective-permute-done.30.refs_1_), channel_id=1, source_target_pairs={{0,4},{1,5},{2,6},{3,7},{4,8},{5,9},{6,10},{7,11},{8,12},{9,13},{1... | collective-permute-start | bytes 1179656 | tf_op jit(solution)/shard_map/ppermute | solution.py:27
  171.2 11.6 %collective-permute-start.44 = (bf16[768,256]{1,0:T(8,128)(2,1)S(1)}, bf16[768,256]{1,0:T(8,128)(2,1)S(1)}, u32[]{:S(2)}, u32[]{:S(2)}) collective-permute-start(bf16[768,256]{1,0:T(8,128)(2,1)S(1)} %get-tuple-element.93.refs_0_), channel_id=1, source_target_pairs={{0,1},{1,0},{2,3},{3,2},{4,5},{5,4},{6,7},{7,6},{8,9},{9,8},{10,11... | collective-permute-start | bytes 1179656 | tf_op jit(solution)/shard_map/ppermute | solution.py:27
  176.9 10.4 %collective-permute-start.39 = (bf16[2,512,256]{2,1,0:T(8,128)(2,1)S(1)}, bf16[2,512,256]{2,1,0:T(8,128)(2,1)S(1)}, u32[]{:S(2)}, u32[]{:S(2)}) collective-permute-start(bf16[2,512,256]{2,1,0:T(8,128)(2,1)S(1)} %add_convert_fusion.2), channel_id=1, source_target_pairs={{0,16},{1,49},{2,18},{3,51},{4,20},{5,53},{6,22},{7,55},{8,24},{9,... | collective-permute-start | bytes 1572872 | tf_op jit(solution)/shard_map/ppermute | solution.py:27
  182.9 12.5 %collective-permute-start.36 = (bf16[768,256]{1,0:T(8,128)(2,1)S(1)}, bf16[768,256]{1,0:T(8,128)(2,1)S(1)}, u32[]{:S(2)}, u32[]{:S(2)}) collective-permute-start(bf16[768,256]{1,0:T(8,128)(2,1)S(1)} %broadcast_select_fusion.1), channel_id=1, source_target_pairs={{0,4},{1,13},{2,6},{3,15},{4,8},{5,1},{6,10},{7,3},{8,12},{9,5},{1... | collective-permute-start | bytes 1179656 | tf_op jit(solution)/shard_map/ppermute | solution.py:27
  206.0 15.9 %collective-permute-start.52 = (bf16[2,512,256]{2,1,0:T(8,128)(2,1)}, bf16[2,512,256]{2,1,0:T(8,128)(2,1)S(1)}, u32[]{:S(2)}, u32[]{:S(2)}) collective-permute-start(bf16[2,512,256]{2,1,0:T(8,128)(2,1)} %get-tuple-element.76), channel_id=1, source_target_pairs={{0,16},{1,49},{2,18},{3,51},{4,20},{5,53},{6,22},{7,55},{8,24},{9,... | collective-permute-start | bytes 1572872 | tf_op jit(solution)/shard_map/ppermute | solution.py:27
  206.1 22.8 %collective-permute-start.53 = (bf16[2,512,256]{2,1,0:T(8,128)(2,1)}, bf16[2,512,256]{2,1,0:T(8,128)(2,1)S(1)}, u32[]{:S(2)}, u32[]{:S(2)}) collective-permute-start(bf16[2,512,256]{2,1,0:T(8,128)(2,1)} %get-tuple-element.80), channel_id=1, source_target_pairs={{0,48},{1,17},{2,50},{3,19},{4,52},{5,21},{6,54},{7,23},{8,56},{9,... | collective-permute-start | bytes 1572872 | tf_op jit(solution)/shard_map/ppermute | solution.py:27
  222.0 10.5 %collective-permute-start.54 = (bf16[2,512,256]{2,1,0:T(8,128)(2,1)S(1)}, bf16[2,512,256]{2,1,0:T(8,128)(2,1)S(1)}, u32[]{:S(2)}, u32[]{:S(2)}) collective-permute-start(bf16[2,512,256]{2,1,0:T(8,128)(2,1)S(1)} %add_convert_fusion.1), channel_id=1, source_target_pairs={{0,16},{1,49},{2,18},{3,51},{4,20},{5,53},{6,22},{7,55},{8,24},{9,... | collective-permute-start | bytes 1572872 | tf_op jit(solution)/shard_map/ppermute | solution.py:27
  (69 other events, 798.1 us)
Sparse Core Ops, SparseCore 0:
  54.5 51.7 all-gather.1
where the time goes:
time: 247 us
  waiting for transfers between devices  109 us (44%)
  starting transfers between devices  54.6 us (22%)
  Pallas kernels  39.3 us (16%)
  other arithmetic  15.7 us (6%)
  between operations  14.7 us (6%)
  local copies, waits for them, and re-layouts  13.7 us (6%)
    ppermute x57, waiting for transfers between devices, permute(): return lax.ppermute(v, AXES, pairs)  109 us
    ppermute x57, starting transfers between devices, permute(): return lax.ppermute(v, AXES, pairs)  54.6 us
    pallas_call x5, Pallas kernels, call(): pl.pallas_call(body, out_shape=outs, in_specs=[pl.BlockSpec(memory_space=...  39.3 us
    unnamed x87, local copies, waits for them, and re-layouts  5.42 us
    optimization_barrier x3, local copies, waits for them, and re-layouts, tie(): return lax.optimization_barrier(values)  4.96 us
  transfers between devices with their start and end apart: 58, of which 26 were waited for; matrix products, arithmetic and copies ran while one was open for 8% of the time, Pallas kernels for 12%

commit v1 on v0

--- a/solution.py
+++ b/solution.py
@@ -61,15 +61,6 @@
 
 def dot(a, b, ca, cb):
     return lax.dot_general(a, b, (((ca,), (cb,)), ((), ())), preferred_element_type=F32)
-
-
-def gather(block, core, swap, shift, split):
-    above, below = shift(block, -1), shift(block, 1)
-    beside = swap(block)
-    beside_above, beside_below = shift(beside, -1), shift(beside, 1)
-    across = onward(above, below, core, split)
-    beside_across = onward(beside_above, beside_below, core, split)
-    return [block, beside, above, beside_above, below, beside_below, across, beside_across]
 
 
 def onward(above, below, core, split):
@@ -102,10 +93,7 @@
         + [vmem] * len(vmem_args)
         + [pl.BlockSpec(memory_space=pl.ANY)] * len(any_args),
         out_specs=[vmem] * len(outs),
-        scratch_shapes=[
-            pltpu.VMEM(scratch, BF16),
-            pltpu.SemaphoreType.DMA((len(any_args),)),
-        ],
+        scratch_shapes=[*scratch, pltpu.SemaphoreType.DMA((len(any_args),))],
         compiler_params=pltpu.CompilerParams(vmem_limit_bytes=60 * 1024 * 1024),
         cost_estimate=pl.CostEstimate(flops=flops, bytes_accessed=loads, transcendentals=0),
     )(here, *vmem_args, *any_args)
@@ -129,7 +117,7 @@
         step = fixed + way * ahead
         for i in range(2):
             block = ((x + step) & 3) * 2 + (y_hi ^ i)
-            slot = slot_of((block & 3) - z) * 2 + ((block >> 2) ^ y_lo)
+            slot = row_slot(block, y_lo, z)
             total = lax.dot_general(
                 conv_mine[...], held[slot, :, :512], (((1,), (1,)), ((), ())),
                 preferred_element_type=F32,
@@ -143,22 +131,17 @@
 def hid_partial(here, conv_mine, conv_beside, blocks, beside, ways):
     return call(
         functools.partial(hid_kernel, ways), [jax.ShapeDtypeStruct((2, 768, 256), BF16)] * 2,
-        (8, 256, 1024), 7 << 20, 1536 * 512 * 2048, here, [conv_mine, conv_beside],
+        [pltpu.VMEM((8, 256, 1024), BF16)], 7 << 20, 1536 * 512 * 2048, here, [conv_mine, conv_beside],
         [*blocks, *beside],
     )
+
+
+def row_slot(block, y_lo, z):
+    return slot_of((block & 3) - z) * 2 + ((block >> 2) ^ y_lo)
 
 
 def hidden_slot(block, x, y_hi):
     return slot_of((block >> 1) - x) * 2 + ((block & 1) ^ y_hi)
-
-
-def load_hid(blocks, held, sems, core):
-    copies = []
-    for k, ref in enumerate(blocks):
-        at = core if k < 8 else 1 - core
-        columns = pl.ds(pl.multiple_of(at * 128, 128), 128)
-        copies.append(pltpu.make_async_copy(ref, held.at[k % 8, :, columns], sems.at[k]))
-    load(copies)
 
 
 def load_act(blocks, held, sems, core):
@@ -170,10 +153,10 @@
     load(copies)
 
 
-def weight_kernel(load_blocks, here, left, *refs):
+def win_kernel(here, left, *refs):
     blocks, outs, (held, sems) = refs[:16], refs[16:20], refs[20:]
     row, y_lo, z, x, y_hi, core = place_of(here)
-    load_blocks(blocks, held, sems, core)
+    load_act(blocks, held, sems, core)
     ahead = 1 - 2 * core
     for out, step in zip(outs, (2, -ahead, ahead, 0)):
         for i in range(2):
@@ -183,33 +166,42 @@
             ).astype(BF16)
 
 
-def weight_partial(load_blocks, here, left, blocks, beside):
+def win_partial(here, left, blocks, beside):
     return call(
-        functools.partial(weight_kernel, load_blocks), [jax.ShapeDtypeStruct((2, 512, 256), BF16)] * 4, (8, 1536, 256),
-        10 << 20, 2 * 1536 * 512 * 2048, here, [left], [*blocks, *beside],
-    )
-
-
-def out_kernel(here, weights, cot, *refs):
-    blocks, out, (held, sems) = refs[:16], refs[16], refs[17:]
+        win_kernel, [jax.ShapeDtypeStruct((2, 512, 256), BF16)] * 4,
+        [pltpu.VMEM((8, 1536, 256), BF16)], 10 << 20, 2 * 1536 * 512 * 2048, here, [left],
+        [*blocks, *beside],
+    )
+
+
+def out_kernel(here, cot, *refs):
+    blocks, parts, out = refs[:16], refs[16:20], refs[20]
+    held, weights, sems = refs[21:]
     row, y_lo, z, x, y_hi, core = place_of(here)
+    load(
+        [
+            pltpu.make_async_copy(ref, weights.at[pl.ds(k * 2, 2)], sems.at[16 + k])
+            for k, ref in enumerate(parts)
+        ]
+    )
     load_act(blocks, held, sems, core)
-    for at in range(0, 1536, 256):
-        total = cot[at : at + 256, :].astype(F32)
+    for at in range(0, 1536, 512):
+        total = cot[at : at + 512, :].astype(F32)
         for block in range(8):
             total = total + lax.dot_general(
-                held[hidden_slot(block, x, y_hi), at : at + 256, :],
-                weights[:, block * 256 : block * 256 + 256],
+                held[hidden_slot(block, x, y_hi), at : at + 512, :],
+                weights[row_slot(block, y_lo, z)],
                 (((1,), (1,)), ((), ())),
                 preferred_element_type=F32,
             )
-        out[at : at + 256, :] = total.astype(BF16)
-
-
-def out_gradient(here, weights, cot, blocks, beside):
+        out[at : at + 512, :] = total.astype(BF16)
+
+
+def out_gradient(here, cot, blocks, beside, weights):
     return call(
-        out_kernel, [jax.ShapeDtypeStruct((1536, 512), BF16)], (8, 1536, 256),
-        12 << 20, 2 * 1536 * 512 * 2048, here, [weights, cot], [*blocks, *beside],
+        out_kernel, [jax.ShapeDtypeStruct((1536, 512), BF16)],
+        [pltpu.VMEM((8, 1536, 256), BF16), pltpu.VMEM((8, 512, 256), BF16)], 12 << 20,
+        2 * 1536 * 512 * 2048, here, [cot], [*blocks, *beside, *weights],
     )[0]
 
 
@@ -249,20 +241,14 @@
 
     mid_gain = scale_mid * keep_mid.astype(F32)
     hidden = jnp.maximum(pre_act.astype(F32) * mid_gain, 0.0).astype(BF16)
-    out_beside = y_lo_swap(weight_out)
-    hid_above, hid_below = x_shift(hidden, -1), x_shift(hidden, 1)
-    out_beside, hidden, cotangent, pre_act, inputs, conv_out = tie(
-        out_beside, hidden, cotangent, pre_act, inputs, conv_out
-    )
-    hid_near = y_hi_swap(hidden)
-    out_here = jnp.stack([weight_out, out_beside])
+    hidden_full = lax.all_gather(hidden, "col", axis=1, tiled=True)
+    out_near = y_lo_swap(weight_out)
+    out_near, cotangent, pre_act, inputs, conv_out = tie(
+        out_near, cotangent, pre_act, inputs, conv_out
+    )
+    out_here = jnp.stack([weight_out, out_near])
     out_above, out_below = z_shift(out_here, -1), z_shift(out_here, 1)
-    out_above, hid_above, hid_below = tie(out_above, hid_above, hid_below)
-    out_across = onward(out_above, out_below, core, z_split)
-    out_blocks = [out_here, out_above, out_below, out_across]
-    hid_across = onward(hid_above, hid_below, core, x_split)
-    hid = [hidden, hid_near, hid_above, y_hi_swap(hid_above)]
-    hid += [hid_below, y_hi_swap(hid_below), hid_across, y_hi_swap(hid_across)]
+    out_blocks = [out_here, out_above, out_below, onward(out_above, out_below, core, z_split)]
 
     wide_gain = scale_wide * keep_wide.astype(F32)
     cot_float = cotangent.astype(F32)
@@ -286,12 +272,9 @@
     mid_gain = gain_chip[0] * gain_chip[1]
 
     out_beside = [core_swap(block) for block in out_blocks]
-    input_turned, conv_turned = inputs.T, grad_conv.T
-    out_beside[3], weight_in, hid[1], hid[6], input_turned, conv_turned = tie(
-        out_beside[3], weight_in, hid[1], hid[6], input_turned, conv_turned
-    )
-    in_full = lax.all_gather(weight_in, "row", axis=1, tiled=True)
-    hid_beside = [core_swap(block) for block in hid]
+    input_turned = inputs.T
+    out_beside[3], weight_in, input_turned = tie(out_beside[3], weight_in, input_turned)
+    in_near = y_lo_swap(weight_in)
     away, there = hid_partial(
         place, conv_mine, conv_beside, out_blocks, out_beside, ((2, 0), (0, -1))
     )
@@ -299,39 +282,46 @@
     further, own = hid_partial(
         place, conv_mine, conv_beside, out_blocks, out_beside, ((0, 1), (0, 0))
     )
-    passed, own = tie(passed, own)
+    passed, own, in_near = tie(passed, own, in_near)
+    in_here = jnp.stack([weight_in, in_near])
+    in_above, in_below = z_shift(in_here, -1), z_shift(in_here, 1)
     further = x_split(add([further, passed]).astype(BF16), 1)
-    wout = weight_partial(load_hid, place, conv_turned, hid, hid_beside)
-    further, wout, in_full = tie(further, wout, in_full)
     terms = [own, back, further]
-    wout_back, wout_passed = z_split(wout[1], -1), z_split(wout[0], 1)
     total = add(terms)
     grad_hid = total[0] + y_hi_swap(total[1].astype(BF16)).astype(F32)
     alive = (pre_chip > 0) & (gain_chip[1] > 0)[None, :]
     grad_pre = jnp.where(alive, grad_hid, 0.0)
     mid_part = jnp.sum(grad_pre * pre_chip, axis=0).reshape(2, 128)
     grad_act = (grad_pre * mid_gain).astype(BF16)
-    act = gather(grad_act, core, y_hi_swap, x_shift, x_split)
+    grad_act, in_above, in_below = tie(grad_act, in_above, in_below)
+    act_near = y_hi_swap(grad_act)
+    act_above, act_below = x_shift(grad_act, -1), x_shift(grad_act, 1)
+    in_blocks = [in_here, in_above, in_below, onward(in_above, in_below, core, z_split)]
+    wout = dot(hidden_full, grad_conv, 0, 0).astype(BF16)
+    act_above, wout = tie(act_above, wout)
+    wout = lax.psum_scatter(wout, "row", scatter_dimension=0, tiled=True)
+    near_above, near_below = x_shift(act_near, -1), x_shift(act_near, 1)
+    act_across = onward(act_above, act_below, core, x_split)
+    near_across = onward(near_above, near_below, core, x_split)
+    act = [
+        grad_act, act_near, act_above, near_above, act_below, near_below, act_across, near_across
+    ]
 
     mid_own = lax.dynamic_index_in_dim(mid_part, core, 0, keepdims=False)
     mid_away = lax.dynamic_index_in_dim(mid_part, 1 - core, 0, keepdims=False)
     mid_own = mid_own + core_swap(mid_away)
     sums = jnp.concatenate([mid_own, wide_part]).reshape(5, 128)
-    sums = sums + z_flip(sums, 1)
-    sums = sums + z_flip(sums, 2)
-    sums = sums + y_lo_swap(sums)
+    sums = jnp.sum(lax.all_gather(sums, "row", axis=0), axis=0)
+
     act_beside = [core_swap(block) for block in act]
-    wout_onward = z_split(add([wout[2], wout_passed]).astype(BF16), 1)
-    wout_total = add([wout[3], wout_back, wout_onward])
-    wout_away = y_lo_swap(wout_total[1].astype(BF16))
-    act[7], wout_total, sums = tie(act[7], wout_total, sums)
-    win = weight_partial(load_act, place, input_turned, act, act_beside)
+    act[7], sums = tie(act[7], sums)
+    win = win_partial(place, input_turned, act, act_beside)
     passed, back = z_split(win[0], 1), z_split(win[1], -1)
-    grad_x = out_gradient(place, in_full, cotangent, act, act_beside)
+    grad_x = out_gradient(place, cotangent, act, act_beside, in_blocks)
     passed, grad_x = tie(passed, grad_x)
     total = add([win[3], back, z_split(add([win[2], passed]).astype(BF16), 1)])
     grad_win = add([total[0], y_lo_swap(total[1].astype(BF16))]) * scaling
-    grad_wout = add([wout_total[0], wout_away]).T * scaling
+    grad_wout = wout.astype(F32) * scaling
     grad_smid = keep_mid.astype(F32) * scaling * sums[0]
     grad_swide = keep_wide.astype(F32) * scaling * sums[1:].reshape(512)
     return (grad_x, grad_win, grad_wout, grad_smid, grad_swide)

time: 247 us -> 312 us (1.26)
  waiting for transfers between devices: 109 us -> 162 us
  blocking collectives: 0 us -> 28.1 us
  starting transfers between devices: 54.6 us -> 45.3 us
  matrix products: 0 us -> 7.64 us
  Pallas kernels: 39.3 us -> 31.8 us
  local copies, waits for them, and re-layouts: 13.7 us -> 6.43 us
    all_gather x1, waiting for transfers between devices: 0.01 us -> 67.7 us  [local(): hidden_full = lax.all_gather(hidden, 'col', axis=1, tiled=True)]
    all_gather x0 -> x1, blocking collectives: none -> 28.1 us  [local(): sums = jnp.sum(lax.all_gather(sums, 'row', axis=0), axis=0)]
    ppermute x57 -> x39, waiting for transfers between devices: 109 us -> 94.4 us  [permute(): return lax.ppermute(v, AXES, pairs)]
    ppermute x57 -> x39, starting transfers between devices: 54.6 us -> 45.2 us  [permute(): return lax.ppermute(v, AXES, pairs)]
    dot_general x0 -> x1, matrix products: none -> 7.64 us  [dot(): lax.dot_general(a, b, (((ca,), (cb,)), ((), ())), preferred_element_type=...]
    pallas_call x5 -> x4, Pallas kernels: 39.3 us -> 31.8 us  [call(): pl.pallas_call(body, out_shape=outs, in_specs=[pl.BlockSpec(memory_space=...]
    optimization_barrier x3 -> x1, local copies, waits for them, and re-layouts: 4.96 us -> 1.56 us  [tie(): return lax.optimization_barrier(values)]
  transfers between devices with their start and end apart: 58 -> 41, of which waited for: 26 -> 19; matrix products, arithmetic and copies ran while one was open for 8% -> 6% of each run, Pallas kernels for 12% -> 8%
where the time goes in v1:
time: 312 us; the launch traced here: 310 us
  waiting for transfers between devices  162 us (52%)
  starting transfers between devices  45.3 us (15%)
  Pallas kernels  31.8 us (10%)
  blocking collectives  28.1 us (9%)
  other arithmetic  14.6 us (5%)
  between operations  14.4 us (5%)
  matrix products  7.64 us (2%)
  local copies, waits for them, and re-layouts  6.43 us (2%)
    ppermute x39, waiting for transfers between devices, permute(): return lax.ppermute(v, AXES, pairs)  94.4 us
    all_gather x1, waiting for transfers between devices, local(): hidden_full = lax.all_gather(hidden, 'col', axis=1, tiled=True)  67.7 us
    ppermute x39, starting transfers between devices, permute(): return lax.ppermute(v, AXES, pairs)  45.2 us
    pallas_call x4, Pallas kernels, call(): pl.pallas_call(body, out_shape=outs, in_specs=[pl.BlockSpec(memory_space=...  31.8 us
    all_gather x1, blocking collectives, local(): sums = jnp.sum(lax.all_gather(sums, 'row', axis=0), axis=0)  28.1 us
    dot_general x1, matrix products, dot(): lax.dot_general(a, b, (((ca,), (cb,)), ((), ())), preferred_element_type=...  7.64 us
  transfers between devices with their start and end apart: 41, of which 19 were waited for; matrix products, arithmetic and copies ran while one was open for 6% of the time, Pallas kernels for 8%

profile of v1, /device:TPU:0, one launch (start us, length us, event | category | flops | bytes accessed | tf_op | source)
XLA Modules:
  0.0 310.4 jit_solution(2043439408592456261)
XLA Ops:
  9.0 6.5 %collective-permute-done = bf16[256,512]{1,0:T(8,128)(2,1)S(1)} collective-permute-done((bf16[256,512]{1,0:T(8,128)(2,1)}, bf16[256,512]{1,0:T(8,128)(2,1)S(1)}, u32[]{:S(2)}, u32[]{:S(2)}) %collective-permute-start) | collective-permute-done | bytes 262176 | tf_op jit(solution)/shard_map/ppermute | solution.py:27
  17.3 2.1 collective-permute-start.1
  19.4 2.1 collective-permute-start.2
  22.2 10.7 %collective-permute-done.1.refs_2_ = bf16[2,256,512]{2,1,0:T(8,128)(2,1)} collective-permute-done((bf16[2,256,512]{2,1,0:T(8,128)(2,1)}, bf16[2,256,512]{2,1,0:T(8,128)(2,1)}, u32[]{:S(2)}, u32[]{:S(2)}) %collective-permute-start.1) | collective-permute-done | bytes 524320 | tf_op jit(solution)/shard_map/ppermute | solution.py:27
  35.3 2.1 fusion.1
  38.7 5.9 %collective-permute-done.3.refs_3_ = bf16[2,256,512]{2,1,0:T(8,128)(2,1)} collective-permute-done((bf16[2,256,512]{2,1,0:T(8,128)(2,1)S(1)}, bf16[2,256,512]{2,1,0:T(8,128)(2,1)}, u32[]{:S(2)}, u32[]{:S(2)}) %collective-permute-start.3) | collective-permute-done | bytes 524320 | tf_op jit(solution)/shard_map/ppermute | solution.py:27
  49.0 6.3 %shard_map.137 = (bf16[2,768,256]{2,1,0:T(8,128)(2,1)}, bf16[2,768,256]{2,1,0:T(8,128)(2,1)}) custom-call(s32[2]{0:T(128)} %pad_add_fusion.here, bf16[768,512]{1,0:T(8,128)(2,1)} %get-tuple-element.68.conv_mine, bf16[768,512]{1,0:T(8,128)(2,1)} %collective-permute-done.7.conv_beside, bf16[2,256,512]{2,1,0:T(8,128)(2,1)} %pad_maximum_fusion.refs_0_, ...), custom_call_target="tpu_custom_call" | custom-call | flops 1610612736 | bytes 7340032 | tf_op jit(solution)/shard_map/pallas_call | solution.py:89
  60.3 6.4 %shard_map.138 = (bf16[2,768,256]{2,1,0:T(8,128)(2,1)}, bf16[2,768,256]{2,1,0:T(8,128)(2,1)}) custom-call(s32[2]{0:T(128)} %pad_add_fusion.here, bf16[768,512]{1,0:T(8,128)(2,1)} %get-tuple-element.68.conv_mine, bf16[768,512]{1,0:T(8,128)(2,1)} %collective-permute-done.7.conv_beside, bf16[2,256,512]{2,1,0:T(8,128)(2,1)} %pad_maximum_fusion.refs_0_, ...), custom_call_target="tpu_custom_call" | custom-call | flops 1610612736 | bytes 7340032 | tf_op jit(solution)/shard_map/pallas_call | solution.py:89
  66.7 7.6 %collective-permute-done.11 = bf16[2,768,256]{2,1,0:T(8,128)(2,1)S(1)} collective-permute-done((bf16[2,768,256]{2,1,0:T(8,128)(2,1)}, bf16[2,768,256]{2,1,0:T(8,128)(2,1)S(1)}, u32[]{:S(2)}, u32[]{:S(2)}) %collective-permute-start.11) | collective-permute-done | bytes 786464 | tf_op jit(solution)/shard_map/ppermute | solution.py:27
  75.7 1.8 collective-permute-start.14
  80.1 1.8 collective-permute-start.16
  82.2 7.1 %collective-permute-done.14 = bf16[2,768,256]{2,1,0:T(8,128)(2,1)S(1)} collective-permute-done((bf16[2,768,256]{2,1,0:T(8,128)(2,1)S(1)}, bf16[2,768,256]{2,1,0:T(8,128)(2,1)S(1)}, u32[]{:S(2)}, u32[]{:S(2)}) %collective-permute-start.14) | collective-permute-done | bytes 786464 | tf_op jit(solution)/shard_map/ppermute | solution.py:27
  89.6 3.6 %collective-permute-start.15 = (bf16[768,256]{1,0:T(8,128)(2,1)S(1)}, bf16[768,256]{1,0:T(8,128)(2,1)S(1)}, u32[]{:S(2)}, u32[]{:S(2)}) collective-permute-start(bf16[768,256]{1,0:T(8,128)(2,1)S(1)} %fusion.8), channel_id=1, source_target_pairs={{0,2},{1,3},{2,0},{3,1},{4,6},{5,7},{6,4},{7,5},{8,10},{9,11},{10,... | collective-permute-start | bytes 1179656 | tf_op jit(solution)/shard_map/ppermute | solution.py:27
  93.3 6.4 %collective-permute-done.15 = bf16[768,256]{1,0:T(8,128)(2,1)S(1)} collective-permute-done((bf16[768,256]{1,0:T(8,128)(2,1)S(1)}, bf16[768,256]{1,0:T(8,128)(2,1)S(1)}, u32[]{:S(2)}, u32[]{:S(2)}) %collective-permute-start.15) | collective-permute-done | bytes 393248 | tf_op jit(solution)/shard_map/ppermute | solution.py:27
  101.6 3.2 %collective-permute-start.18 = (bf16[768,256]{1,0:T(8,128)(2,1)S(1)}, bf16[768,256]{1,0:T(8,128)(2,1)S(1)}, u32[]{:S(2)}, u32[]{:S(2)}) collective-permute-start(bf16[768,256]{1,0:T(8,128)(2,1)S(1)} %get-tuple-element.47.refs_0_), channel_id=1, source_target_pairs={{0,2},{1,3},{2,0},{3,1},{4,6},{5,7},{6,4},{7,5},{8,10},{9,11},{10,... | collective-permute-start | bytes 1179656 | tf_op jit(solution)/shard_map/ppermute | solution.py:27
  104.9 6.0 %collective-permute-done.18.refs_1_ = bf16[768,256]{1,0:T(8,128)(2,1)S(1)} collective-permute-done((bf16[768,256]{1,0:T(8,128)(2,1)S(1)}, bf16[768,256]{1,0:T(8,128)(2,1)S(1)}, u32[]{:S(2)}, u32[]{:S(2)}) %collective-permute-start.18) | collective-permute-done | bytes 393248 | tf_op jit(solution)/shard_map/ppermute | solution.py:27
  112.1 4.0 %collective-permute-start.20 = (bf16[768,256]{1,0:T(8,128)(2,1)S(1)}, bf16[768,256]{1,0:T(8,128)(2,1)}, u32[]{:S(2)}, u32[]{:S(2)}) collective-permute-start(bf16[768,256]{1,0:T(8,128)(2,1)S(1)} %collective-permute-done.18.refs_1_), channel_id=1, source_target_pairs={{0,12},{1,13},{2,14},{3,15},{4,0},{5,1},{6,2},{7,3},{8,4},{9,5},{1... | collective-permute-start | bytes 1179656 | tf_op jit(solution)/shard_map/ppermute | solution.py:27
  116.1 6.6 %collective-permute-done.22.refs_5_ = bf16[768,256]{1,0:T(8,128)(2,1)S(1)} collective-permute-done((bf16[768,256]{1,0:T(8,128)(2,1)S(1)}, bf16[768,256]{1,0:T(8,128)(2,1)S(1)}, u32[]{:S(2)}, u32[]{:S(2)}) %collective-permute-start.22) | collective-permute-done | bytes 393248 | tf_op jit(solution)/shard_map/ppermute | solution.py:27
  125.2 28.1 %all_gather.7 = f32[8,5,128]{2,1,0:T(8,128)S(1)} all-gather(f32[1,5,128]{2,1,0:T(8,128)S(1)} %maximum_bitcast_fusion), channel_id=1, replica_groups=mesh['row'=8,'col'=16] {'row'}, dimensions={0}, use_global_device_ids=true | all-gather | bytes 23040 | tf_op jit(solution)/shard_map/all_gather | solution.py:314
  154.7 2.1 collective-permute-start.19
  156.8 67.7 %all-gather.2.cloned.1.call-done = bf16[1536,2048]{1,0:T(8,128)(2,1)} async-done(((bf16[1536,128]{1,0:T(8,128)(2,1)}), bf16[1536,2048]{1,0:T(8,128)(2,1)}) %all-gather.2.cloned.1.call-update) | async-done | bytes 6291472 | tf_op jit(solution)/shard_map/all_gather | solution.py:244
  224.5 7.6 %convolution_convert_fusion = bf16[2048,512]{1,0:T(8,128)(2,1)} fusion(bf16[1536,2048]{1,0:T(8,128)(2,1)} %all-gather.2.cloned.1.call-done, bf16[1536,512]{1,0:T(8,128)(2,1)S(1)} %get-tuple-element.66), kind=kOutput, calls=%fused_computation.4 | convolution fusion | flops 3222274048 | bytes 9961472 | tf_op jit(solution)/shard_map/dot_general | solution.py:63
  233.9 10.8 %collective-permute-done.21.refs_4_ = bf16[768,256]{1,0:T(8,128)(2,1)S(1)} collective-permute-done((bf16[768,256]{1,0:T(8,128)(2,1)S(1)}, bf16[768,256]{1,0:T(8,128)(2,1)S(1)}, u32[]{:S(2)}, u32[]{:S(2)}) %collective-permute-start.21) | collective-permute-done | bytes 393248 | tf_op jit(solution)/shard_map/ppermute | solution.py:27
  244.8 2.2 collective-permute-start.29
  247.7 6.1 %collective-permute-done.23.refs_6_ = bf16[768,256]{1,0:T(8,128)(2,1)S(1)} collective-permute-done((bf16[768,256]{1,0:T(8,128)(2,1)S(1)}, bf16[768,256]{1,0:T(8,128)(2,1)S(1)}, u32[]{:S(2)}, u32[]{:S(2)}) %collective-permute-start.23) | collective-permute-done | bytes 393248 | tf_op jit(solution)/shard_map/ppermute | solution.py:27
  256.7 8.7 %shard_map.139 = (bf16[2,512,256]{2,1,0:T(8,128)(2,1)}, bf16[2,512,256]{2,1,0:T(8,128)(2,1)}, bf16[2,512,256]{2,1,0:T(8,128)(2,1)}, bf16[2,512,256]{2,1,0:T(8,128)(2,1)}) custom-call(s32[2]{0:T(128)} %pad_add_fusion.here, bf16[512,1536]{1,0:T(8,128)(2,1)} %bitcast.46, bf16[768,256]{1,0:T(8,128)(2,1)} %copy-done.11, bf16[768,256]{1,0:T(8,128)(2,1)} %copy-done.19, ...), custom_call_target="tpu_custom_call" | custom-call | flops 3221225472 | bytes 10485760 | tf_op jit(solution)/shard_map/pallas_call | solution.py:89
  268.6 2.8 collective-permute-done.35.refs_19_
  272.2 10.5 %shard_map.140 = bf16[1536,512]{1,0:T(8,128)(2,1)} custom-call(s32[2]{0:T(128)} %pad_add_fusion.here, bf16[1536,512]{1,0:T(8,128)(2,1)} %cot, bf16[768,256]{1,0:T(8,128)(2,1)} %copy-done.11, bf16[768,256]{1,0:T(8,128)(2,1)} %copy-done.19, bf16[768,256]{1,0:T(8,128)(2,1)} %collective-permute-done.19.refs_2_, ...), custom_call_target="tpu_custom_call" | custom-call | flops 3221225472 | bytes 12582912 | tf_op jit(solution)/shard_map/pallas_call | solution.py:89
  283.2 2.1 collective-permute-start.37
  285.3 8.3 %collective-permute-done.37 = bf16[2,512,256]{2,1,0:T(8,128)(2,1)S(1)} collective-permute-done((bf16[2,512,256]{2,1,0:T(8,128)(2,1)S(1)}, bf16[2,512,256]{2,1,0:T(8,128)(2,1)S(1)}, u32[]{:S(2)}, u32[]{:S(2)}) %collective-permute-start.37) | collective-permute-done | bytes 524320 | tf_op jit(solution)/shard_map/ppermute | solution.py:27
  295.0 5.9 %collective-permute-done.38 = bf16[512,256]{1,0:T(8,128)(2,1)S(1)} collective-permute-done((bf16[512,256]{1,0:T(8,128)(2,1)S(1)}, bf16[512,256]{1,0:T(8,128)(2,1)S(1)}, u32[]{:S(2)}, u32[]{:S(2)}) %collective-permute-start.38) | collective-permute-done | bytes 262176 | tf_op jit(solution)/shard_map/ppermute | solution.py:27
  301.7 1.8 convert_multiply_fusion.3
  (150 shorter events, 41.3 us)
Async XLA Ops:
  7.2 217.3 %all-gather.2.cloned.1.call-start = ((), (), s32[]{:S(2)}) async-start(), calls=%async_computation.1 | async-start | bytes 6684672 | tf_op jit(solution)/shard_map/all_gather | solution.py:244
  7.2 8.3 %collective-permute-start = (bf16[256,512]{1,0:T(8,128)(2,1)}, bf16[256,512]{1,0:T(8,128)(2,1)S(1)}, u32[]{:S(2)}, u32[]{:S(2)}) collective-permute-start(bf16[256,512]{1,0:T(8,128)(2,1)} %param.15), channel_id=1, source_target_pairs={{0,64},{1,65},{2,66},{3,67},{4,68},{5,69},{6,70},{7,71},{8,72},{9,... | collective-permute-start | bytes 786440 | tf_op jit(solution)/shard_map/ppermute | solution.py:27
  17.3 15.6 %collective-permute-start.1 = (bf16[2,256,512]{2,1,0:T(8,128)(2,1)}, bf16[2,256,512]{2,1,0:T(8,128)(2,1)}, u32[]{:S(2)}, u32[]{:S(2)}) collective-permute-start(bf16[2,256,512]{2,1,0:T(8,128)(2,1)} %pad_maximum_fusion.refs_0_), channel_id=1, source_target_pairs={{0,16},{1,17},{2,18},{3,19},{4,20},{5,21},{6,22},{7,23},{8,24},{9,... | collective-permute-start | bytes 1572872 | tf_op jit(solution)/shard_map/ppermute | solution.py:27
  19.4 13.5 %collective-permute-start.2 = (bf16[2,256,512]{2,1,0:T(8,128)(2,1)}, bf16[2,256,512]{2,1,0:T(8,128)(2,1)}, u32[]{:S(2)}, u32[]{:S(2)}) collective-permute-start(bf16[2,256,512]{2,1,0:T(8,128)(2,1)} %pad_maximum_fusion.refs_0_), channel_id=1, source_target_pairs={{0,48},{1,49},{2,50},{3,51},{4,52},{5,53},{6,54},{7,55},{8,56},{9,... | collective-permute-start | bytes 1572872 | tf_op jit(solution)/shard_map/ppermute | solution.py:27
  33.9 10.6 %collective-permute-start.3 = (bf16[2,256,512]{2,1,0:T(8,128)(2,1)S(1)}, bf16[2,256,512]{2,1,0:T(8,128)(2,1)}, u32[]{:S(2)}, u32[]{:S(2)}) collective-permute-start(bf16[2,256,512]{2,1,0:T(8,128)(2,1)S(1)} %broadcast_select_fusion.1), channel_id=1, source_target_pairs={{0,16},{1,49},{2,18},{3,51},{4,20},{5,53},{6,22},{7,55},{8,24},{9,... | collective-permute-start | bytes 1572872 | tf_op jit(solution)/shard_map/ppermute | solution.py:27
  38.6 9.1 %collective-permute-start.7 = (bf16[768,512]{1,0:T(8,128)(2,1)}, bf16[768,512]{1,0:T(8,128)(2,1)}, u32[]{:S(2)}, u32[]{:S(2)}) collective-permute-start(bf16[768,512]{1,0:T(8,128)(2,1)} %get-tuple-element.67), channel_id=1, source_target_pairs={{0,1},{1,0},{2,3},{3,2},{4,5},{5,4},{6,7},{7,6},{8,9},{9,8},{10,11... | collective-permute-start | bytes 2359304 | tf_op jit(solution)/shard_map/ppermute | solution.py:27
  55.4 18.9 %collective-permute-start.11 = (bf16[2,768,256]{2,1,0:T(8,128)(2,1)}, bf16[2,768,256]{2,1,0:T(8,128)(2,1)S(1)}, u32[]{:S(2)}, u32[]{:S(2)}) collective-permute-start(bf16[2,768,256]{2,1,0:T(8,128)(2,1)} %get-tuple-element.39), channel_id=1, source_target_pairs={{0,4},{1,13},{2,6},{3,15},{4,8},{5,1},{6,10},{7,3},{8,12},{9,5},{1... | collective-permute-start | bytes 2359304 | tf_op jit(solution)/shard_map/ppermute | solution.py:27
  56.9 9.7 %collective-permute-start.12 = (bf16[512,256]{1,0:T(8,128)(2,1)S(1)}, bf16[512,256]{1,0:T(8,128)(2,1)}, u32[]{:S(2)}, u32[]{:S(2)}) collective-permute-start(bf16[512,256]{1,0:T(8,128)(2,1)S(1)} %copy-done.14), channel_id=1, source_target_pairs={{0,64},{1,65},{2,66},{3,67},{4,68},{5,69},{6,70},{7,71},{8,72},{9,... | collective-permute-start | bytes 786440 | tf_op jit(solution)/shard_map/ppermute | solution.py:27
  58.5 23.6 %collective-permute-start.13 = (bf16[2,768,256]{2,1,0:T(8,128)(2,1)}, bf16[2,768,256]{2,1,0:T(8,128)(2,1)S(1)}, u32[]{:S(2)}, u32[]{:S(2)}) collective-permute-start(bf16[2,768,256]{2,1,0:T(8,128)(2,1)} %get-tuple-element.43), channel_id=1, source_target_pairs={{0,12},{1,5},{2,14},{3,7},{4,0},{5,9},{6,2},{7,11},{8,4},{9,13},{1... | collective-permute-start | bytes 2359304 | tf_op jit(solution)/shard_map/ppermute | solution.py:27
  75.7 13.6 %collective-permute-start.14 = (bf16[2,768,256]{2,1,0:T(8,128)(2,1)S(1)}, bf16[2,768,256]{2,1,0:T(8,128)(2,1)S(1)}, u32[]{:S(2)}, u32[]{:S(2)}) collective-permute-start(bf16[2,768,256]{2,1,0:T(8,128)(2,1)S(1)} %add_convert_fusion), channel_id=1, source_target_pairs={{0,4},{1,13},{2,6},{3,15},{4,8},{5,1},{6,10},{7,3},{8,12},{9,5},{1... | collective-permute-start | bytes 2359304 | tf_op jit(solution)/shard_map/ppermute | solution.py:27
  78.8 14.4 %collective-permute-start.5 = (bf16[768,128]{1,0:T(8,128)(2,1)S(1)}, bf16[768,128]{1,0:T(8,128)(2,1)S(1)}, u32[]{:S(2)}, u32[]{:S(2)}) collective-permute-start(bf16[768,128]{1,0:T(8,128)(2,1)S(1)} %constant_dynamic-slice_fusion.4), channel_id=1, source_target_pairs={{0,1},{1,0},{2,3},{3,2},{4,5},{5,4},{6,7},{7,6},{8,9},{9,8},{10,11... | collective-permute-start | bytes 589832 | tf_op jit(solution)/shard_map/ppermute | solution.py:27
  80.1 19.9 %collective-permute-start.16 = (bf16[2,512,256]{2,1,0:T(8,128)(2,1)S(1)}, bf16[2,512,256]{2,1,0:T(8,128)(2,1)S(1)}, u32[]{:S(2)}, u32[]{:S(2)}) collective-permute-start(bf16[2,512,256]{2,1,0:T(8,128)(2,1)S(1)} %pad_maximum_fusion.1.refs_16_), channel_id=1, source_target_pairs={{0,48},{1,49},{2,50},{3,51},{4,52},{5,53},{6,54},{7,55},{8,56},{9,... | collective-permute-start | bytes 1572872 | tf_op jit(solution)/shard_map/ppermute | solution.py:27
  81.9 18.2 %collective-permute-start.17 = (bf16[2,512,256]{2,1,0:T(8,128)(2,1)S(1)}, bf16[2,512,256]{2,1,0:T(8,128)(2,1)S(1)}, u32[]{:S(2)}, u32[]{:S(2)}) collective-permute-start(bf16[2,512,256]{2,1,0:T(8,128)(2,1)S(1)} %pad_maximum_fusion.1.refs_16_), channel_id=1, source_target_pairs={{0,16},{1,17},{2,18},{3,19},{4,20},{5,21},{6,22},{7,23},{8,24},{9,... | collective-permute-start | bytes 1572872 | tf_op jit(solution)/shard_map/ppermute | solution.py:27
  89.6 10.1 %collective-permute-start.15 = (bf16[768,256]{1,0:T(8,128)(2,1)S(1)}, bf16[768,256]{1,0:T(8,128)(2,1)S(1)}, u32[]{:S(2)}, u32[]{:S(2)}) collective-permute-start(bf16[768,256]{1,0:T(8,128)(2,1)S(1)} %fusion.8), channel_id=1, source_target_pairs={{0,2},{1,3},{2,0},{3,1},{4,6},{5,7},{6,4},{7,5},{8,10},{9,11},{10,... | collective-permute-start | bytes 1179656 | tf_op jit(solution)/shard_map/ppermute | solution.py:27
  101.6 9.3 %collective-permute-start.18 = (bf16[768,256]{1,0:T(8,128)(2,1)S(1)}, bf16[768,256]{1,0:T(8,128)(2,1)S(1)}, u32[]{:S(2)}, u32[]{:S(2)}) collective-permute-start(bf16[768,256]{1,0:T(8,128)(2,1)S(1)} %get-tuple-element.47.refs_0_), channel_id=1, source_target_pairs={{0,2},{1,3},{2,0},{3,1},{4,6},{5,7},{6,4},{7,5},{8,10},{9,11},{10,... | collective-permute-start | bytes 1179656 | tf_op jit(solution)/shard_map/ppermute | solution.py:27
  110.9 11.7 %collective-permute-start.22 = (bf16[768,256]{1,0:T(8,128)(2,1)S(1)}, bf16[768,256]{1,0:T(8,128)(2,1)S(1)}, u32[]{:S(2)}, u32[]{:S(2)}) collective-permute-start(bf16[768,256]{1,0:T(8,128)(2,1)S(1)} %collective-permute-done.18.refs_1_), channel_id=1, source_target_pairs={{0,4},{1,5},{2,6},{3,7},{4,8},{5,9},{6,10},{7,11},{8,12},{9,13},{1... | collective-permute-start | bytes 1179656 | tf_op jit(solution)/shard_map/ppermute | solution.py:27
  112.1 10.5 %collective-permute-start.20 = (bf16[768,256]{1,0:T(8,128)(2,1)S(1)}, bf16[768,256]{1,0:T(8,128)(2,1)}, u32[]{:S(2)}, u32[]{:S(2)}) collective-permute-start(bf16[768,256]{1,0:T(8,128)(2,1)S(1)} %collective-permute-done.18.refs_1_), channel_id=1, source_target_pairs={{0,12},{1,13},{2,14},{3,15},{4,0},{5,1},{6,2},{7,3},{8,4},{9,5},{1... | collective-permute-start | bytes 1179656 | tf_op jit(solution)/shard_map/ppermute | solution.py:27
  122.7 30.5 %collective-permute-start.24 = (bf16[768,256]{1,0:T(8,128)(2,1)S(1)}, bf16[768,256]{1,0:T(8,128)(2,1)}, u32[]{:S(2)}, u32[]{:S(2)}) collective-permute-start(bf16[768,256]{1,0:T(8,128)(2,1)S(1)} %broadcast_select_fusion.2), channel_id=1, source_target_pairs={{0,4},{1,13},{2,6},{3,15},{4,8},{5,1},{6,10},{7,3},{8,12},{9,5},{1... | collective-permute-start | bytes 1179656 | tf_op jit(solution)/shard_map/ppermute | solution.py:27
  154.6 147.1 %reduce-scatter.2.cloned.1.call-start = ((), (), s32[]{:S(2)}) async-start(), calls=%async_computation.2 | async-start | bytes 2359296 | tf_op jit(solution)/shard_map/reduce_scatter | solution.py:302
  154.7 77.4 %collective-permute-start.19 = (bf16[768,256]{1,0:T(8,128)(2,1)S(1)}, bf16[768,256]{1,0:T(8,128)(2,1)}, u32[]{:S(2)}, u32[]{:S(2)}) collective-permute-start(bf16[768,256]{1,0:T(8,128)(2,1)S(1)} %get-tuple-element.47.refs_0_), channel_id=1, source_target_pairs={{0,12},{1,13},{2,14},{3,15},{4,0},{5,1},{6,2},{7,3},{8,4},{9,5},{1... | collective-permute-start | bytes 1179656 | tf_op jit(solution)/shard_map/ppermute | solution.py:27
  232.1 12.6 %collective-permute-start.21 = (bf16[768,256]{1,0:T(8,128)(2,1)S(1)}, bf16[768,256]{1,0:T(8,128)(2,1)S(1)}, u32[]{:S(2)}, u32[]{:S(2)}) collective-permute-start(bf16[768,256]{1,0:T(8,128)(2,1)S(1)} %get-tuple-element.47.refs_0_), channel_id=1, source_target_pairs={{0,4},{1,5},{2,6},{3,7},{4,8},{5,9},{6,10},{7,11},{8,12},{9,13},{1... | collective-permute-start | bytes 1179656 | tf_op jit(solution)/shard_map/ppermute | solution.py:27
  233.4 13.6 %collective-permute-start.26 = (bf16[768,256]{1,0:T(8,128)(2,1)S(1)}, bf16[768,256]{1,0:T(8,128)(2,1)S(1)}, u32[]{:S(2)}, u32[]{:S(2)}) collective-permute-start(bf16[768,256]{1,0:T(8,128)(2,1)S(1)} %get-tuple-element.47.refs_0_), channel_id=1, source_target_pairs={{0,1},{1,0},{2,3},{3,2},{4,5},{5,4},{6,7},{7,6},{8,9},{9,8},{10,11... | collective-permute-start | bytes 1179656 | tf_op jit(solution)/shard_map/ppermute | solution.py:27
  233.4 13.7 %collective-permute-start.27 = (bf16[768,256]{1,0:T(8,128)(2,1)S(1)}, bf16[768,256]{1,0:T(8,128)(2,1)S(1)}, u32[]{:S(2)}, u32[]{:S(2)}) collective-permute-start(bf16[768,256]{1,0:T(8,128)(2,1)S(1)} %copy-done.20), channel_id=1, source_target_pairs={{0,1},{1,0},{2,3},{3,2},{4,5},{5,4},{6,7},{7,6},{8,9},{9,8},{10,11... | collective-permute-start | bytes 1179656 | tf_op jit(solution)/shard_map/ppermute | solution.py:27
  244.8 9.1 %collective-permute-start.23 = (bf16[768,256]{1,0:T(8,128)(2,1)S(1)}, bf16[768,256]{1,0:T(8,128)(2,1)S(1)}, u32[]{:S(2)}, u32[]{:S(2)}) collective-permute-start(bf16[768,256]{1,0:T(8,128)(2,1)S(1)} %broadcast_select_fusion.3), channel_id=1, source_target_pairs={{0,4},{1,13},{2,6},{3,15},{4,8},{5,1},{6,10},{7,3},{8,12},{9,5},{1... | collective-permute-start | bytes 1179656 | tf_op jit(solution)/shard_map/ppermute | solution.py:27
  244.8 9.2 %collective-permute-start.29 = (bf16[768,256]{1,0:T(8,128)(2,1)}, bf16[768,256]{1,0:T(8,128)(2,1)S(1)}, u32[]{:S(2)}, u32[]{:S(2)}) collective-permute-start(bf16[768,256]{1,0:T(8,128)(2,1)} %collective-permute-done.20.refs_3_), channel_id=1, source_target_pairs={{0,1},{1,0},{2,3},{3,2},{4,5},{5,4},{6,7},{7,6},{8,9},{9,8},{10,11... | collective-permute-start | bytes 1179656 | tf_op jit(solution)/shard_map/ppermute | solution.py:27
  247.0 8.6 %collective-permute-start.31 = (bf16[768,256]{1,0:T(8,128)(2,1)S(1)}, bf16[768,256]{1,0:T(8,128)(2,1)S(1)}, u32[]{:S(2)}, u32[]{:S(2)}) collective-permute-start(bf16[768,256]{1,0:T(8,128)(2,1)S(1)} %collective-permute-done.22.refs_5_), channel_id=1, source_target_pairs={{0,1},{1,0},{2,3},{3,2},{4,5},{5,4},{6,7},{7,6},{8,9},{9,8},{10,11... | collective-permute-start | bytes 1179656 | tf_op jit(solution)/shard_map/ppermute | solution.py:27
  247.1 8.5 %collective-permute-start.33 = (bf16[768,256]{1,0:T(8,128)(2,1)}, bf16[768,256]{1,0:T(8,128)(2,1)S(1)}, u32[]{:S(2)}, u32[]{:S(2)}) collective-permute-start(bf16[768,256]{1,0:T(8,128)(2,1)} %collective-permute-done.24.refs_7_), channel_id=1, source_target_pairs={{0,1},{1,0},{2,3},{3,2},{4,5},{5,4},{6,7},{7,6},{8,9},{9,8},{10,11... | collective-permute-start | bytes 1179656 | tf_op jit(solution)/shard_map/ppermute | solution.py:27
  247.6 8.1 %collective-permute-start.28 = (bf16[768,256]{1,0:T(8,128)(2,1)}, bf16[768,256]{1,0:T(8,128)(2,1)S(1)}, u32[]{:S(2)}, u32[]{:S(2)}) collective-permute-start(bf16[768,256]{1,0:T(8,128)(2,1)} %collective-permute-done.19.refs_2_), channel_id=1, source_target_pairs={{0,1},{1,0},{2,3},{3,2},{4,5},{5,4},{6,7},{7,6},{8,9},{9,8},{10,11... | collective-permute-start | bytes 1179656 | tf_op jit(solution)/shard_map/ppermute | solution.py:27
  254.0 17.4 %collective-permute-start.35 = (bf16[2,512,256]{2,1,0:T(8,128)(2,1)S(1)}, bf16[2,512,256]{2,1,0:T(8,128)(2,1)S(1)}, u32[]{:S(2)}, u32[]{:S(2)}) collective-permute-start(bf16[2,512,256]{2,1,0:T(8,128)(2,1)S(1)} %broadcast_select_fusion), channel_id=1, source_target_pairs={{0,16},{1,49},{2,18},{3,51},{4,20},{5,53},{6,22},{7,55},{8,24},{9,... | collective-permute-start | bytes 1572872 | tf_op jit(solution)/shard_map/ppermute | solution.py:27
  265.3 17.7 %collective-permute-start.34 = (bf16[2,512,256]{2,1,0:T(8,128)(2,1)}, bf16[2,512,256]{2,1,0:T(8,128)(2,1)S(1)}, u32[]{:S(2)}, u32[]{:S(2)}) collective-permute-start(bf16[2,512,256]{2,1,0:T(8,128)(2,1)} %get-tuple-element.51), channel_id=1, source_target_pairs={{0,16},{1,49},{2,18},{3,51},{4,20},{5,53},{6,22},{7,55},{8,24},{9,... | collective-permute-start | bytes 1572872 | tf_op jit(solution)/shard_map/ppermute | solution.py:27
  266.9 18.4 %collective-permute-start.36 = (bf16[2,512,256]{2,1,0:T(8,128)(2,1)}, bf16[2,512,256]{2,1,0:T(8,128)(2,1)S(1)}, u32[]{:S(2)}, u32[]{:S(2)}) collective-permute-start(bf16[2,512,256]{2,1,0:T(8,128)(2,1)} %get-tuple-element.56), channel_id=1, source_target_pairs={{0,48},{1,17},{2,50},{3,19},{4,52},{5,21},{6,54},{7,23},{8,56},{9,... | collective-permute-start | bytes 1572872 | tf_op jit(solution)/shard_map/ppermute | solution.py:27
  283.2 10.5 %collective-permute-start.37 = (bf16[2,512,256]{2,1,0:T(8,128)(2,1)S(1)}, bf16[2,512,256]{2,1,0:T(8,128)(2,1)S(1)}, u32[]{:S(2)}, u32[]{:S(2)}) collective-permute-start(bf16[2,512,256]{2,1,0:T(8,128)(2,1)S(1)} %add_convert_fusion.1), channel_id=1, source_target_pairs={{0,16},{1,49},{2,18},{3,51},{4,20},{5,53},{6,22},{7,55},{8,24},{9,... | collective-permute-start | bytes 1572872 | tf_op jit(solution)/shard_map/ppermute | solution.py:27
  (38 other events, 516.7 us)
Sparse Core Ops, SparseCore 0:
  154.8 69.6 all-gather.1
  232.3 41.5 reduce-scatter.1

commit v2 on v1

--- a/solution.py
+++ b/solution.py
@@ -286,6 +286,7 @@
     in_here = jnp.stack([weight_in, in_near])
     in_above, in_below = z_shift(in_here, -1), z_shift(in_here, 1)
     further = x_split(add([further, passed]).astype(BF16), 1)
+    further, hidden_full = tie(further, hidden_full)
     terms = [own, back, further]
     total = add(terms)
     grad_hid = total[0] + y_hi_swap(total[1].astype(BF16)).astype(F32)
@@ -311,7 +312,9 @@
     mid_away = lax.dynamic_index_in_dim(mid_part, 1 - core, 0, keepdims=False)
     mid_own = mid_own + core_swap(mid_away)
     sums = jnp.concatenate([mid_own, wide_part]).reshape(5, 128)
-    sums = jnp.sum(lax.all_gather(sums, "row", axis=0), axis=0)
+    sums = sums + z_flip(sums, 1)
+    sums = sums + z_flip(sums, 2)
+    sums = sums + y_lo_swap(sums)
 
     act_beside = [core_swap(block) for block in act]
     act[7], sums = tie(act[7], sums)

time: 312 us -> 215 us (0.69)
  waiting for transfers between devices: 162 us -> 82.8 us
  blocking collectives: 28.1 us -> 0 us
  other arithmetic: 14.6 us -> 22.7 us
    all_gather x1, waiting for transfers between devices: 67.7 us -> 0.01 us  [local(): hidden_full = lax.all_gather(hidden, 'col', axis=1, tiled=True)]
    all_gather x1 -> x0, blocking collectives: 28.1 us -> none  [local(): sums = jnp.sum(lax.all_gather(sums, 'row', axis=0), axis=0)]
    ppermute x39 -> x42, waiting for transfers between devices: 94.4 us -> 82.8 us  [permute(): return lax.ppermute(v, AXES, pairs)]
    ppermute x39 -> x42, starting transfers between devices: 45.2 us -> 47.8 us  [permute(): return lax.ppermute(v, AXES, pairs)]
  transfers between devices with their start and end apart: 41 -> 44, of which waited for: 19 -> 20; matrix products, arithmetic and copies ran while one was open for 6% -> 14% of each run, Pallas kernels for 8% -> 15%
where the time goes in v2:
time: 215 us; the launch traced here: 213 us
  waiting for transfers between devices  82.8 us (39%)
  starting transfers between devices  47.8 us (22%)
  Pallas kernels  31.8 us (15%)
  other arithmetic  22.7 us (11%)
  between operations  14.5 us (7%)
  matrix products  7.69 us (4%)
  local copies, waits for them, and re-layouts  6.1 us (3%)
    ppermute x42, waiting for transfers between devices, permute(): return lax.ppermute(v, AXES, pairs)  82.8 us
    ppermute x42, starting transfers between devices, permute(): return lax.ppermute(v, AXES, pairs)  47.8 us
    pallas_call x4, Pallas kernels, call(): pl.pallas_call(body, out_shape=outs, in_specs=[pl.BlockSpec(memory_space=...  31.8 us
    dot_general x1, matrix products, dot(): lax.dot_general(a, b, (((ca,), (cb,)), ((), ())), preferred_element_type=...  7.69 us
  transfers between devices with their start and end apart: 44, of which 20 were waited for; matrix products, arithmetic and copies ran while one was open for 14% of the time, Pallas kernels for 15%

profile of v2, /device:TPU:0, one launch (start us, length us, event | category | flops | bytes accessed | tf_op | source)
XLA Modules:
  0.0 213.4 jit_solution(3039693742891093576)
XLA Ops:
  7.9 1.8 maximum_convert_fusion
  11.6 6.5 %collective-permute-done = bf16[256,512]{1,0:T(8,128)(2,1)S(1)} collective-permute-done((bf16[256,512]{1,0:T(8,128)(2,1)}, bf16[256,512]{1,0:T(8,128)(2,1)S(1)}, u32[]{:S(2)}, u32[]{:S(2)}) %collective-permute-start) | collective-permute-done | bytes 262176 | tf_op jit(solution)/shard_map/ppermute | solution.py:27
  18.1 1.8 pad_maximum_fusion.refs_0_
  19.9 2.1 collective-permute-start.1
  22.0 2.1 collective-permute-start.2
  24.1 11.3 %collective-permute-done.1.refs_2_ = bf16[2,256,512]{2,1,0:T(8,128)(2,1)} collective-permute-done((bf16[2,256,512]{2,1,0:T(8,128)(2,1)}, bf16[2,256,512]{2,1,0:T(8,128)(2,1)}, u32[]{:S(2)}, u32[]{:S(2)}) %collective-permute-start.1) | collective-permute-done | bytes 524320 | tf_op jit(solution)/shard_map/ppermute | solution.py:27
  37.9 2.1 fusion.1
  41.2 5.9 %collective-permute-done.3.refs_3_ = bf16[2,256,512]{2,1,0:T(8,128)(2,1)} collective-permute-done((bf16[2,256,512]{2,1,0:T(8,128)(2,1)S(1)}, bf16[2,256,512]{2,1,0:T(8,128)(2,1)}, u32[]{:S(2)}, u32[]{:S(2)}) %collective-permute-start.3) | collective-permute-done | bytes 524320 | tf_op jit(solution)/shard_map/ppermute | solution.py:27
  51.8 6.4 %shard_map.137 = (bf16[2,768,256]{2,1,0:T(8,128)(2,1)}, bf16[2,768,256]{2,1,0:T(8,128)(2,1)}) custom-call(s32[2]{0:T(128)} %pad_add_fusion.here, bf16[768,512]{1,0:T(8,128)(2,1)} %get-tuple-element.72.conv_mine, bf16[768,512]{1,0:T(8,128)(2,1)} %collective-permute-done.7.conv_beside, bf16[2,256,512]{2,1,0:T(8,128)(2,1)} %pad_maximum_fusion.refs_0_, ...), custom_call_target="tpu_custom_call" | custom-call | flops 1610612736 | bytes 7340032 | tf_op jit(solution)/shard_map/pallas_call | solution.py:89
  63.1 6.3 %shard_map.138 = (bf16[2,768,256]{2,1,0:T(8,128)(2,1)}, bf16[2,768,256]{2,1,0:T(8,128)(2,1)}) custom-call(s32[2]{0:T(128)} %pad_add_fusion.here, bf16[768,512]{1,0:T(8,128)(2,1)} %get-tuple-element.72.conv_mine, bf16[768,512]{1,0:T(8,128)(2,1)} %collective-permute-done.7.conv_beside, bf16[2,256,512]{2,1,0:T(8,128)(2,1)} %pad_maximum_fusion.refs_0_, ...), custom_call_target="tpu_custom_call" | custom-call | flops 1610612736 | bytes 7340032 | tf_op jit(solution)/shard_map/pallas_call | solution.py:89
  71.0 9.5 %collective-permute-done.11 = bf16[2,768,256]{2,1,0:T(8,128)(2,1)S(1)} collective-permute-done((bf16[2,768,256]{2,1,0:T(8,128)(2,1)}, bf16[2,768,256]{2,1,0:T(8,128)(2,1)S(1)}, u32[]{:S(2)}, u32[]{:S(2)}) %collective-permute-start.11) | collective-permute-done | bytes 786464 | tf_op jit(solution)/shard_map/ppermute | solution.py:27
  81.8 4.7 %collective-permute-start.14 = (bf16[2,768,256]{2,1,0:T(8,128)(2,1)S(1)}, bf16[2,768,256]{2,1,0:T(8,128)(2,1)S(1)}, u32[]{:S(2)}, u32[]{:S(2)}) collective-permute-start(bf16[2,768,256]{2,1,0:T(8,128)(2,1)S(1)} %add_convert_fusion), channel_id=1, source_target_pairs={{0,4},{1,13},{2,6},{3,15},{4,8},{5,1},{6,10},{7,3},{8,12},{9,5},{1... | collective-permute-start | bytes 2359304 | tf_op jit(solution)/shard_map/ppermute | solution.py:27
  91.1 5.9 %collective-permute-done.14 = bf16[2,768,256]{2,1,0:T(8,128)(2,1)S(1)} collective-permute-done((bf16[2,768,256]{2,1,0:T(8,128)(2,1)S(1)}, bf16[2,768,256]{2,1,0:T(8,128)(2,1)S(1)}, u32[]{:S(2)}, u32[]{:S(2)}) %collective-permute-start.14) | collective-permute-done | bytes 786464 | tf_op jit(solution)/shard_map/ppermute | solution.py:27
  98.7 5.7 %collective-permute-start.15 = (bf16[768,256]{1,0:T(8,128)(2,1)S(1)}, bf16[768,256]{1,0:T(8,128)(2,1)S(1)}, u32[]{:S(2)}, u32[]{:S(2)}) collective-permute-start(bf16[768,256]{1,0:T(8,128)(2,1)S(1)} %fusion.8), channel_id=1, source_target_pairs={{0,2},{1,3},{2,0},{3,1},{4,6},{5,7},{6,4},{7,5},{8,10},{9,11},{10,... | collective-permute-start | bytes 1179656 | tf_op jit(solution)/shard_map/ppermute | solution.py:27
  106.2 3.0 %collective-permute-start.16 = (bf16[2,512,256]{2,1,0:T(8,128)(2,1)S(1)}, bf16[2,512,256]{2,1,0:T(8,128)(2,1)S(1)}, u32[]{:S(2)}, u32[]{:S(2)}) collective-permute-start(bf16[2,512,256]{2,1,0:T(8,128)(2,1)S(1)} %pad_maximum_fusion.1.refs_16_), channel_id=1, source_target_pairs={{0,48},{1,49},{2,50},{3,51},{4,52},{5,53},{6,54},{7,55},{8,56},{9,... | collective-permute-start | bytes 1572872 | tf_op jit(solution)/shard_map/ppermute | solution.py:27
  112.4 2.1 collective-permute-start.26
  116.2 3.4 %collective-permute-done.17.refs_18_ = bf16[2,512,256]{2,1,0:T(8,128)(2,1)S(1)} collective-permute-done((bf16[2,512,256]{2,1,0:T(8,128)(2,1)S(1)}, bf16[2,512,256]{2,1,0:T(8,128)(2,1)S(1)}, u32[]{:S(2)}, u32[]{:S(2)}) %collective-permute-start.17) | collective-permute-done | bytes 524320 | tf_op jit(solution)/shard_map/ppermute | solution.py:27
  120.1 3.4 %collective-permute-start.19 = (bf16[768,256]{1,0:T(8,128)(2,1)S(1)}, bf16[768,256]{1,0:T(8,128)(2,1)}, u32[]{:S(2)}, u32[]{:S(2)}) collective-permute-start(bf16[768,256]{1,0:T(8,128)(2,1)S(1)} %get-tuple-element.50.refs_0_), channel_id=1, source_target_pairs={{0,12},{1,13},{2,14},{3,15},{4,0},{5,1},{6,2},{7,3},{8,4},{9,5},{1... | collective-permute-start | bytes 1179656 | tf_op jit(solution)/shard_map/ppermute | solution.py:27
  124.1 7.7 %convolution_convert_fusion = bf16[2048,512]{1,0:T(8,128)(2,1)} fusion(bf16[1536,2048]{1,0:T(8,128)(2,1)} %all-gather.2.cloned.1.call-done, bf16[1536,512]{1,0:T(8,128)(2,1)S(1)} %get-tuple-element.70), kind=kOutput, calls=%fused_computation.4 | convolution fusion | flops 3222274048 | bytes 9961472 | tf_op jit(solution)/shard_map/dot_general | solution.py:63
  131.8 3.3 %collective-permute-start.20 = (bf16[768,256]{1,0:T(8,128)(2,1)}, bf16[768,256]{1,0:T(8,128)(2,1)S(1)}, u32[]{:S(2)}, u32[]{:S(2)}) collective-permute-start(bf16[768,256]{1,0:T(8,128)(2,1)} %collective-permute-done.18.refs_1_), channel_id=1, source_target_pairs={{0,12},{1,13},{2,14},{3,15},{4,0},{5,1},{6,2},{7,3},{8,4},{9,5},{1... | collective-permute-start | bytes 1179656 | tf_op jit(solution)/shard_map/ppermute | solution.py:27
  138.4 6.0 %collective-permute-done.20.refs_3_ = bf16[768,256]{1,0:T(8,128)(2,1)S(1)} collective-permute-done((bf16[768,256]{1,0:T(8,128)(2,1)}, bf16[768,256]{1,0:T(8,128)(2,1)S(1)}, u32[]{:S(2)}, u32[]{:S(2)}) %collective-permute-start.20) | collective-permute-done | bytes 393248 | tf_op jit(solution)/shard_map/ppermute | solution.py:27
  144.8 2.9 %collective-permute-done.22.refs_5_ = bf16[768,256]{1,0:T(8,128)(2,1)S(1)} collective-permute-done((bf16[768,256]{1,0:T(8,128)(2,1)}, bf16[768,256]{1,0:T(8,128)(2,1)S(1)}, u32[]{:S(2)}, u32[]{:S(2)}) %collective-permute-start.22) | collective-permute-done | bytes 393248 | tf_op jit(solution)/shard_map/ppermute | solution.py:27
  148.5 5.3 %collective-permute-done.23.refs_6_ = bf16[768,256]{1,0:T(8,128)(2,1)S(1)} collective-permute-done((bf16[768,256]{1,0:T(8,128)(2,1)S(1)}, bf16[768,256]{1,0:T(8,128)(2,1)S(1)}, u32[]{:S(2)}, u32[]{:S(2)}) %collective-permute-start.23) | collective-permute-done | bytes 393248 | tf_op jit(solution)/shard_map/ppermute | solution.py:27
  154.4 3.6 %collective-permute-done.24.refs_7_ = bf16[768,256]{1,0:T(8,128)(2,1)S(1)} collective-permute-done((bf16[768,256]{1,0:T(8,128)(2,1)S(1)}, bf16[768,256]{1,0:T(8,128)(2,1)S(1)}, u32[]{:S(2)}, u32[]{:S(2)}) %collective-permute-start.24) | collective-permute-done | bytes 393248 | tf_op jit(solution)/shard_map/ppermute | solution.py:27
  161.1 8.6 %shard_map.139 = (bf16[2,512,256]{2,1,0:T(8,128)(2,1)}, bf16[2,512,256]{2,1,0:T(8,128)(2,1)}, bf16[2,512,256]{2,1,0:T(8,128)(2,1)}, bf16[2,512,256]{2,1,0:T(8,128)(2,1)}) custom-call(s32[2]{0:T(128)} %pad_add_fusion.here, bf16[512,1536]{1,0:T(8,128)(2,1)} %bitcast.50, bf16[768,256]{1,0:T(8,128)(2,1)} %copy-done.8, ...), custom_call_target="tpu_custom_call" | custom-call | flops 3221225472 | bytes 10485760 | tf_op jit(solution)/shard_map/pallas_call | solution.py:89
  169.7 2.4 %collective-permute-start.37 = (bf16[2,512,256]{2,1,0:T(8,128)(2,1)}, bf16[2,512,256]{2,1,0:T(8,128)(2,1)S(1)}, u32[]{:S(2)}, u32[]{:S(2)}) collective-permute-start(bf16[2,512,256]{2,1,0:T(8,128)(2,1)} %get-tuple-element.55), channel_id=1, source_target_pairs={{0,16},{1,49},{2,18},{3,51},{4,20},{5,53},{6,22},{7,55},{8,24},{9,... | collective-permute-start | bytes 1572872 | tf_op jit(solution)/shard_map/ppermute | solution.py:27
  173.0 2.1 collective-permute-done.38.refs_19_
  176.0 10.5 %shard_map.140 = bf16[1536,512]{1,0:T(8,128)(2,1)} custom-call(s32[2]{0:T(128)} %pad_add_fusion.here, bf16[1536,512]{1,0:T(8,128)(2,1)} %cot, bf16[768,256]{1,0:T(8,128)(2,1)} %copy-done.8, bf16[768,256]{1,0:T(8,128)(2,1)} %collective-permute-done.18.refs_1_, bf16[768,256]{1,0:T(8,128)(2,1)} %collective-permute-done.19.refs_2_, bf16[768,256]{1,0:T(8,128)(2,1)} %copy-done.9, ...), custom_call_target="tpu_custom_call" | custom-call | flops 3221225472 | bytes 12582912 | tf_op jit(solution)/shard_map/pallas_call | solution.py:89
  188.2 8.9 %collective-permute-done.40 = bf16[2,512,256]{2,1,0:T(8,128)(2,1)S(1)} collective-permute-done((bf16[2,512,256]{2,1,0:T(8,128)(2,1)S(1)}, bf16[2,512,256]{2,1,0:T(8,128)(2,1)S(1)}, u32[]{:S(2)}, u32[]{:S(2)}) %collective-permute-start.40) | collective-permute-done | bytes 524320 | tf_op jit(solution)/shard_map/ppermute | solution.py:27
  197.3 2.3 %collective-permute-start.41 = (bf16[512,256]{1,0:T(8,128)(2,1)S(1)}, bf16[512,256]{1,0:T(8,128)(2,1)S(1)}, u32[]{:S(2)}, u32[]{:S(2)}) collective-permute-start(bf16[512,256]{1,0:T(8,128)(2,1)S(1)} %fusion.9), channel_id=1, source_target_pairs={{0,64},{1,65},{2,66},{3,67},{4,68},{5,69},{6,70},{7,71},{8,72},{9,... | collective-permute-start | bytes 786440 | tf_op jit(solution)/shard_map/ppermute | solution.py:27
  200.7 3.3 %collective-permute-done.41 = bf16[512,256]{1,0:T(8,128)(2,1)S(1)} collective-permute-done((bf16[512,256]{1,0:T(8,128)(2,1)S(1)}, bf16[512,256]{1,0:T(8,128)(2,1)S(1)}, u32[]{:S(2)}, u32[]{:S(2)}) %collective-permute-start.41) | collective-permute-done | bytes 262176 | tf_op jit(solution)/shard_map/ppermute | solution.py:27
  204.8 1.8 convert_multiply_fusion.3
  (164 shorter events, 46.3 us)
Async XLA Ops:
  7.2 89.8 %all-gather.2.cloned.1.call-start = ((), (), s32[]{:S(2)}) async-start(), calls=%async_computation.1 | async-start | bytes 6684672 | tf_op jit(solution)/shard_map/all_gather | solution.py:244
  9.8 195.0 %reduce-scatter.2.cloned.1.call-start = ((), (), s32[]{:S(2)}) async-start(), calls=%async_computation.2 | async-start | bytes 2359296 | tf_op jit(solution)/shard_map/reduce_scatter | solution.py:303
  9.8 8.3 %collective-permute-start = (bf16[256,512]{1,0:T(8,128)(2,1)}, bf16[256,512]{1,0:T(8,128)(2,1)S(1)}, u32[]{:S(2)}, u32[]{:S(2)}) collective-permute-start(bf16[256,512]{1,0:T(8,128)(2,1)} %param.15), channel_id=1, source_target_pairs={{0,64},{1,65},{2,66},{3,67},{4,68},{5,69},{6,70},{7,71},{8,72},{9,... | collective-permute-start | bytes 786440 | tf_op jit(solution)/shard_map/ppermute | solution.py:27
  19.9 15.6 %collective-permute-start.1 = (bf16[2,256,512]{2,1,0:T(8,128)(2,1)}, bf16[2,256,512]{2,1,0:T(8,128)(2,1)}, u32[]{:S(2)}, u32[]{:S(2)}) collective-permute-start(bf16[2,256,512]{2,1,0:T(8,128)(2,1)} %pad_maximum_fusion.refs_0_), channel_id=1, source_target_pairs={{0,16},{1,17},{2,18},{3,19},{4,20},{5,21},{6,22},{7,23},{8,24},{9,... | collective-permute-start | bytes 1572872 | tf_op jit(solution)/shard_map/ppermute | solution.py:27
  22.0 13.5 %collective-permute-start.2 = (bf16[2,256,512]{2,1,0:T(8,128)(2,1)}, bf16[2,256,512]{2,1,0:T(8,128)(2,1)}, u32[]{:S(2)}, u32[]{:S(2)}) collective-permute-start(bf16[2,256,512]{2,1,0:T(8,128)(2,1)} %pad_maximum_fusion.refs_0_), channel_id=1, source_target_pairs={{0,48},{1,49},{2,50},{3,51},{4,52},{5,53},{6,54},{7,55},{8,56},{9,... | collective-permute-start | bytes 1572872 | tf_op jit(solution)/shard_map/ppermute | solution.py:27
  36.6 10.6 %collective-permute-start.3 = (bf16[2,256,512]{2,1,0:T(8,128)(2,1)S(1)}, bf16[2,256,512]{2,1,0:T(8,128)(2,1)}, u32[]{:S(2)}, u32[]{:S(2)}) collective-permute-start(bf16[2,256,512]{2,1,0:T(8,128)(2,1)S(1)} %broadcast_select_fusion.1), channel_id=1, source_target_pairs={{0,16},{1,49},{2,18},{3,51},{4,20},{5,53},{6,22},{7,55},{8,24},{9,... | collective-permute-start | bytes 1572872 | tf_op jit(solution)/shard_map/ppermute | solution.py:27
  41.2 9.1 %collective-permute-start.7 = (bf16[768,512]{1,0:T(8,128)(2,1)}, bf16[768,512]{1,0:T(8,128)(2,1)}, u32[]{:S(2)}, u32[]{:S(2)}) collective-permute-start(bf16[768,512]{1,0:T(8,128)(2,1)} %get-tuple-element.71), channel_id=1, source_target_pairs={{0,1},{1,0},{2,3},{3,2},{4,5},{5,4},{6,7},{7,6},{8,9},{9,8},{10,11... | collective-permute-start | bytes 2359304 | tf_op jit(solution)/shard_map/ppermute | solution.py:27
  58.2 22.3 %collective-permute-start.11 = (bf16[2,768,256]{2,1,0:T(8,128)(2,1)}, bf16[2,768,256]{2,1,0:T(8,128)(2,1)S(1)}, u32[]{:S(2)}, u32[]{:S(2)}) collective-permute-start(bf16[2,768,256]{2,1,0:T(8,128)(2,1)} %get-tuple-element.41), channel_id=1, source_target_pairs={{0,4},{1,13},{2,6},{3,15},{4,8},{5,1},{6,10},{7,3},{8,12},{9,5},{1... | collective-permute-start | bytes 2359304 | tf_op jit(solution)/shard_map/ppermute | solution.py:27
  59.9 11.1 %collective-permute-start.12 = (bf16[512,256]{1,0:T(8,128)(2,1)S(1)}, bf16[512,256]{1,0:T(8,128)(2,1)S(1)}, u32[]{:S(2)}, u32[]{:S(2)}) collective-permute-start(bf16[512,256]{1,0:T(8,128)(2,1)S(1)} %copy-done.11), channel_id=1, source_target_pairs={{0,64},{1,65},{2,66},{3,67},{4,68},{5,69},{6,70},{7,71},{8,72},{9,... | collective-permute-start | bytes 786440 | tf_op jit(solution)/shard_map/ppermute | solution.py:27
  61.4 35.6 %collective-permute-start.13 = (bf16[2,768,256]{2,1,0:T(8,128)(2,1)}, bf16[2,768,256]{2,1,0:T(8,128)(2,1)}, u32[]{:S(2)}, u32[]{:S(2)}) collective-permute-start(bf16[2,768,256]{2,1,0:T(8,128)(2,1)} %get-tuple-element.45), channel_id=1, source_target_pairs={{0,12},{1,5},{2,14},{3,7},{4,0},{5,9},{6,2},{7,11},{8,4},{9,13},{1... | collective-permute-start | bytes 2359304 | tf_op jit(solution)/shard_map/ppermute | solution.py:27
  81.8 15.1 %collective-permute-start.14 = (bf16[2,768,256]{2,1,0:T(8,128)(2,1)S(1)}, bf16[2,768,256]{2,1,0:T(8,128)(2,1)S(1)}, u32[]{:S(2)}, u32[]{:S(2)}) collective-permute-start(bf16[2,768,256]{2,1,0:T(8,128)(2,1)S(1)} %add_convert_fusion), channel_id=1, source_target_pairs={{0,4},{1,13},{2,6},{3,15},{4,8},{5,1},{6,10},{7,3},{8,12},{9,5},{1... | collective-permute-start | bytes 2359304 | tf_op jit(solution)/shard_map/ppermute | solution.py:27
  90.9 14.2 %collective-permute-start.5 = (bf16[768,128]{1,0:T(8,128)(2,1)}, bf16[768,128]{1,0:T(8,128)(2,1)}, u32[]{:S(2)}, u32[]{:S(2)}) collective-permute-start(bf16[768,128]{1,0:T(8,128)(2,1)} %constant_dynamic-slice_fusion.4), channel_id=1, source_target_pairs={{0,1},{1,0},{2,3},{3,2},{4,5},{5,4},{6,7},{7,6},{8,9},{9,8},{10,11... | collective-permute-start | bytes 589832 | tf_op jit(solution)/shard_map/ppermute | solution.py:27
  98.7 11.5 %collective-permute-start.15 = (bf16[768,256]{1,0:T(8,128)(2,1)S(1)}, bf16[768,256]{1,0:T(8,128)(2,1)S(1)}, u32[]{:S(2)}, u32[]{:S(2)}) collective-permute-start(bf16[768,256]{1,0:T(8,128)(2,1)S(1)} %fusion.8), channel_id=1, source_target_pairs={{0,2},{1,3},{2,0},{3,1},{4,6},{5,7},{6,4},{7,5},{8,10},{9,11},{10,... | collective-permute-start | bytes 1179656 | tf_op jit(solution)/shard_map/ppermute | solution.py:27
  106.2 10.1 %collective-permute-start.16 = (bf16[2,512,256]{2,1,0:T(8,128)(2,1)S(1)}, bf16[2,512,256]{2,1,0:T(8,128)(2,1)S(1)}, u32[]{:S(2)}, u32[]{:S(2)}) collective-permute-start(bf16[2,512,256]{2,1,0:T(8,128)(2,1)S(1)} %pad_maximum_fusion.1.refs_16_), channel_id=1, source_target_pairs={{0,48},{1,49},{2,50},{3,51},{4,52},{5,53},{6,54},{7,55},{8,56},{9,... | collective-permute-start | bytes 1572872 | tf_op jit(solution)/shard_map/ppermute | solution.py:27
  109.2 10.4 %collective-permute-start.17 = (bf16[2,512,256]{2,1,0:T(8,128)(2,1)S(1)}, bf16[2,512,256]{2,1,0:T(8,128)(2,1)S(1)}, u32[]{:S(2)}, u32[]{:S(2)}) collective-permute-start(bf16[2,512,256]{2,1,0:T(8,128)(2,1)S(1)} %pad_maximum_fusion.1.refs_16_), channel_id=1, source_target_pairs={{0,16},{1,17},{2,18},{3,19},{4,20},{5,21},{6,22},{7,23},{8,24},{9,... | collective-permute-start | bytes 1572872 | tf_op jit(solution)/shard_map/ppermute | solution.py:27
  112.4 11.1 %collective-permute-start.26 = (f32[5,128]{1,0:T(8,128)S(1)}, f32[5,128]{1,0:T(8,128)S(1)}, u32[]{:S(2)}, u32[]{:S(2)}) collective-permute-start(f32[5,128]{1,0:T(8,128)S(1)} %maximum_bitcast_fusion), channel_id=1, source_target_pairs={{0,16},{1,17},{2,18},{3,19},{4,20},{5,21},{6,22},{7,23},{8,24},{9,... | collective-permute-start | bytes 7688 | tf_op jit(solution)/shard_map/ppermute | solution.py:27
  119.7 12.1 %collective-permute-start.18 = (bf16[768,256]{1,0:T(8,128)(2,1)S(1)}, bf16[768,256]{1,0:T(8,128)(2,1)}, u32[]{:S(2)}, u32[]{:S(2)}) collective-permute-start(bf16[768,256]{1,0:T(8,128)(2,1)S(1)} %get-tuple-element.50.refs_0_), channel_id=1, source_target_pairs={{0,2},{1,3},{2,0},{3,1},{4,6},{5,7},{6,4},{7,5},{8,10},{9,11},{10,... | collective-permute-start | bytes 1179656 | tf_op jit(solution)/shard_map/ppermute | solution.py:27
  120.1 11.7 %collective-permute-start.19 = (bf16[768,256]{1,0:T(8,128)(2,1)S(1)}, bf16[768,256]{1,0:T(8,128)(2,1)}, u32[]{:S(2)}, u32[]{:S(2)}) collective-permute-start(bf16[768,256]{1,0:T(8,128)(2,1)S(1)} %get-tuple-element.50.refs_0_), channel_id=1, source_target_pairs={{0,12},{1,13},{2,14},{3,15},{4,0},{5,1},{6,2},{7,3},{8,4},{9,5},{1... | collective-permute-start | bytes 1179656 | tf_op jit(solution)/shard_map/ppermute | solution.py:27
  123.5 13.9 %collective-permute-start.21 = (bf16[768,256]{1,0:T(8,128)(2,1)S(1)}, bf16[768,256]{1,0:T(8,128)(2,1)}, u32[]{:S(2)}, u32[]{:S(2)}) collective-permute-start(bf16[768,256]{1,0:T(8,128)(2,1)S(1)} %get-tuple-element.50.refs_0_), channel_id=1, source_target_pairs={{0,4},{1,5},{2,6},{3,7},{4,8},{5,9},{6,10},{7,11},{8,12},{9,13},{1... | collective-permute-start | bytes 1179656 | tf_op jit(solution)/shard_map/ppermute | solution.py:27
  124.1 11.1 %collective-permute-start.27 = (f32[5,128]{1,0:T(8,128)}, f32[5,128]{1,0:T(8,128)}, u32[]{:S(2)}, u32[]{:S(2)}) collective-permute-start(f32[5,128]{1,0:T(8,128)} %fusion.15), channel_id=1, source_target_pairs={{0,32},{1,33},{2,34},{3,35},{4,36},{5,37},{6,38},{7,39},{8,40},{9,... | collective-permute-start | bytes 7688 | tf_op jit(solution)/shard_map/ppermute | solution.py:27
  131.8 16.2 %collective-permute-start.29 = (bf16[768,256]{1,0:T(8,128)(2,1)S(1)}, bf16[768,256]{1,0:T(8,128)(2,1)S(1)}, u32[]{:S(2)}, u32[]{:S(2)}) collective-permute-start(bf16[768,256]{1,0:T(8,128)(2,1)S(1)} %get-tuple-element.50.refs_0_), channel_id=1, source_target_pairs={{0,1},{1,0},{2,3},{3,2},{4,5},{5,4},{6,7},{7,6},{8,9},{9,8},{10,11... | collective-permute-start | bytes 1179656 | tf_op jit(solution)/shard_map/ppermute | solution.py:27
  131.8 12.7 %collective-permute-start.20 = (bf16[768,256]{1,0:T(8,128)(2,1)}, bf16[768,256]{1,0:T(8,128)(2,1)S(1)}, u32[]{:S(2)}, u32[]{:S(2)}) collective-permute-start(bf16[768,256]{1,0:T(8,128)(2,1)} %collective-permute-done.18.refs_1_), channel_id=1, source_target_pairs={{0,12},{1,13},{2,14},{3,15},{4,0},{5,1},{6,2},{7,3},{8,4},{9,5},{1... | collective-permute-start | bytes 1179656 | tf_op jit(solution)/shard_map/ppermute | solution.py:27
  135.1 12.7 %collective-permute-start.22 = (bf16[768,256]{1,0:T(8,128)(2,1)}, bf16[768,256]{1,0:T(8,128)(2,1)S(1)}, u32[]{:S(2)}, u32[]{:S(2)}) collective-permute-start(bf16[768,256]{1,0:T(8,128)(2,1)} %collective-permute-done.18.refs_1_), channel_id=1, source_target_pairs={{0,4},{1,5},{2,6},{3,7},{4,8},{5,9},{6,10},{7,11},{8,12},{9,13},{1... | collective-permute-start | bytes 1179656 | tf_op jit(solution)/shard_map/ppermute | solution.py:27
  135.8 12.0 %collective-permute-start.28 = (f32[5,128]{1,0:T(8,128)S(1)}, f32[5,128]{1,0:T(8,128)S(1)}, u32[]{:S(2)}, u32[]{:S(2)}) collective-permute-start(f32[5,128]{1,0:T(8,128)S(1)} %fusion.19), channel_id=1, source_target_pairs={{0,64},{1,65},{2,66},{3,67},{4,68},{5,69},{6,70},{7,71},{8,72},{9,... | collective-permute-start | bytes 7688 | tf_op jit(solution)/shard_map/ppermute | solution.py:27
  137.4 16.9 %collective-permute-start.31 = (bf16[768,256]{1,0:T(8,128)(2,1)}, bf16[768,256]{1,0:T(8,128)(2,1)S(1)}, u32[]{:S(2)}, u32[]{:S(2)}) collective-permute-start(bf16[768,256]{1,0:T(8,128)(2,1)} %collective-permute-done.19.refs_2_), channel_id=1, source_target_pairs={{0,1},{1,0},{2,3},{3,2},{4,5},{5,4},{6,7},{7,6},{8,9},{9,8},{10,11... | collective-permute-start | bytes 1179656 | tf_op jit(solution)/shard_map/ppermute | solution.py:27
  144.5 9.3 %collective-permute-start.23 = (bf16[768,256]{1,0:T(8,128)(2,1)S(1)}, bf16[768,256]{1,0:T(8,128)(2,1)S(1)}, u32[]{:S(2)}, u32[]{:S(2)}) collective-permute-start(bf16[768,256]{1,0:T(8,128)(2,1)S(1)} %broadcast_select_fusion.3), channel_id=1, source_target_pairs={{0,4},{1,13},{2,6},{3,15},{4,8},{5,1},{6,10},{7,3},{8,12},{9,5},{1... | collective-permute-start | bytes 1179656 | tf_op jit(solution)/shard_map/ppermute | solution.py:27
  147.8 10.2 %collective-permute-start.24 = (bf16[768,256]{1,0:T(8,128)(2,1)S(1)}, bf16[768,256]{1,0:T(8,128)(2,1)S(1)}, u32[]{:S(2)}, u32[]{:S(2)}) collective-permute-start(bf16[768,256]{1,0:T(8,128)(2,1)S(1)} %broadcast_select_fusion.2), channel_id=1, source_target_pairs={{0,4},{1,13},{2,6},{3,15},{4,8},{5,1},{6,10},{7,3},{8,12},{9,5},{1... | collective-permute-start | bytes 1179656 | tf_op jit(solution)/shard_map/ppermute | solution.py:27
  147.9 10.2 %collective-permute-start.33 = (bf16[768,256]{1,0:T(8,128)(2,1)}, bf16[768,256]{1,0:T(8,128)(2,1)S(1)}, u32[]{:S(2)}, u32[]{:S(2)}) collective-permute-start(bf16[768,256]{1,0:T(8,128)(2,1)} %collective-permute-done.21.refs_4_), channel_id=1, source_target_pairs={{0,1},{1,0},{2,3},{3,2},{4,5},{5,4},{6,7},{7,6},{8,9},{9,8},{10,11... | collective-permute-start | bytes 1179656 | tf_op jit(solution)/shard_map/ppermute | solution.py:27
  158.1 17.0 %collective-permute-start.38 = (bf16[2,512,256]{2,1,0:T(8,128)(2,1)S(1)}, bf16[2,512,256]{2,1,0:T(8,128)(2,1)S(1)}, u32[]{:S(2)}, u32[]{:S(2)}) collective-permute-start(bf16[2,512,256]{2,1,0:T(8,128)(2,1)S(1)} %broadcast_select_fusion), channel_id=1, source_target_pairs={{0,16},{1,49},{2,18},{3,51},{4,20},{5,53},{6,22},{7,55},{8,24},{9,... | collective-permute-start | bytes 1572872 | tf_op jit(solution)/shard_map/ppermute | solution.py:27
  169.7 16.7 %collective-permute-start.37 = (bf16[2,512,256]{2,1,0:T(8,128)(2,1)}, bf16[2,512,256]{2,1,0:T(8,128)(2,1)S(1)}, u32[]{:S(2)}, u32[]{:S(2)}) collective-permute-start(bf16[2,512,256]{2,1,0:T(8,128)(2,1)} %get-tuple-element.55), channel_id=1, source_target_pairs={{0,16},{1,49},{2,18},{3,51},{4,20},{5,53},{6,22},{7,55},{8,24},{9,... | collective-permute-start | bytes 1572872 | tf_op jit(solution)/shard_map/ppermute | solution.py:27
  172.1 16.1 %collective-permute-start.39 = (bf16[2,512,256]{2,1,0:T(8,128)(2,1)}, bf16[2,512,256]{2,1,0:T(8,128)(2,1)S(1)}, u32[]{:S(2)}, u32[]{:S(2)}) collective-permute-start(bf16[2,512,256]{2,1,0:T(8,128)(2,1)} %get-tuple-element.60), channel_id=1, source_target_pairs={{0,48},{1,17},{2,50},{3,19},{4,52},{5,21},{6,54},{7,23},{8,56},{9,... | collective-permute-start | bytes 1572872 | tf_op jit(solution)/shard_map/ppermute | solution.py:27
  186.6 10.5 %collective-permute-start.40 = (bf16[2,512,256]{2,1,0:T(8,128)(2,1)S(1)}, bf16[2,512,256]{2,1,0:T(8,128)(2,1)S(1)}, u32[]{:S(2)}, u32[]{:S(2)}) collective-permute-start(bf16[2,512,256]{2,1,0:T(8,128)(2,1)S(1)} %add_convert_fusion.1), channel_id=1, source_target_pairs={{0,16},{1,49},{2,18},{3,51},{4,20},{5,53},{6,22},{7,55},{8,24},{9,... | collective-permute-start | bytes 1572872 | tf_op jit(solution)/shard_map/ppermute | solution.py:27
  (44 other events, 446.6 us)
Sparse Core Ops, SparseCore 0:
  10.8 80.1 all-gather.1
  131.9 45.1 reduce-scatter.1

commit v3 on v2

--- a/solution.py
+++ b/solution.py
@@ -75,13 +75,6 @@
 def slot_of(step):
     step = step & 3
     return jnp.where(step >= 2, 5 - step, step)
-
-
-def load(copies):
-    for copy in copies:
-        copy.start()
-    for copy in copies:
-        copy.wait()
 
 
 def call(body, outs, scratch, loads, flops, here, vmem_args, any_args):
@@ -99,78 +92,116 @@
     )(here, *vmem_args, *any_args)
 
 
+def row_slot(block, y_lo, z):
+    return slot_of((block & 3) - z) * 2 + ((block >> 2) ^ y_lo)
+
+
+def hidden_slot(block, x, y_hi):
+    return slot_of((block >> 1) - x) * 2 + ((block & 1) ^ y_hi)
+
+
+def fetch(copy_of, slots):
+    if len(slots) == 2:
+        for j, slot in enumerate(slots):
+            for k in range(8):
+
+                @pl.when(slot == k)
+                def _(j=j, k=k):
+                    copy_of(k, 0, j).start()
+                    copy_of(k, 1, j).start()
+
+        def ready(j):
+            copy_of(0, 0, j).wait()
+            copy_of(0, 1, j).wait()
+            return j
+    else:
+        for k in range(8):
+            copy_of(k, 0, k).start()
+            copy_of(k, 1, k).start()
+
+        def ready(j):
+            copy_of(0, 0, slots[j]).wait()
+            copy_of(0, 1, slots[j]).wait()
+            return slots[j]
+    return ready
+
+
 def hid_kernel(ways, here, conv_mine, conv_beside, *refs):
-    blocks, outs, (held, sems) = refs[:8], refs[8:10], refs[10:]
-    load(
-        [
-            pltpu.make_async_copy(
-                ref,
-                held.at[pl.ds((k % 4) * 2, 2), :, pl.ds((k // 4) * 512, 512)],
-                sems.at[k],
-            )
-            for k, ref in enumerate(blocks)
-        ]
-    )
+    count = len(ways)
+    blocks, outs, (held, sems) = refs[:16], refs[16 : 16 + count], refs[16 + count :]
     row, y_lo, z, x, y_hi, core = place_of(here)
     ahead = 1 - 2 * core
-    for out, (fixed, way) in zip(outs, ways):
-        step = fixed + way * ahead
-        for i in range(2):
-            block = ((x + step) & 3) * 2 + (y_hi ^ i)
-            slot = row_slot(block, y_lo, z)
+    steps = [fixed + way * ahead for fixed, way in ways] + [2] * (count - 1)
+    slots = [
+        row_slot(((x + step) & 3) * 2 + (y_hi ^ i), y_lo, z)
+        for step in steps[: 4 if count > 1 else 1]
+        for i in range(2)
+    ]
+
+    def copy_of(k, part, at):
+        return pltpu.make_async_copy(
+            blocks[part * 8 + k], held.at[at, :, pl.ds(part * 512, 512)], sems.at[at * 2 + part]
+        )
+
+    ready = fetch(copy_of, slots)
+    for j in range(len(slots)):
+        at = ready(j)
+        if j < 2 * count:
             total = lax.dot_general(
-                conv_mine[...], held[slot, :, :512], (((1,), (1,)), ((), ())),
+                conv_mine[...], held[at, :, :512], (((1,), (1,)), ((), ())),
                 preferred_element_type=F32,
             ) + lax.dot_general(
-                conv_beside[...], held[slot, :, 512:], (((1,), (1,)), ((), ())),
+                conv_beside[...], held[at, :, 512:], (((1,), (1,)), ((), ())),
                 preferred_element_type=F32,
             )
-            out[i] = total.astype(BF16)
+            outs[j // 2][j % 2] = total.astype(BF16)
 
 
 def hid_partial(here, conv_mine, conv_beside, blocks, beside, ways):
     return call(
-        functools.partial(hid_kernel, ways), [jax.ShapeDtypeStruct((2, 768, 256), BF16)] * 2,
-        [pltpu.VMEM((8, 256, 1024), BF16)], 7 << 20, 1536 * 512 * 2048, here, [conv_mine, conv_beside],
-        [*blocks, *beside],
-    )
-
-
-def row_slot(block, y_lo, z):
-    return slot_of((block & 3) - z) * 2 + ((block >> 2) ^ y_lo)
-
-
-def hidden_slot(block, x, y_hi):
-    return slot_of((block >> 1) - x) * 2 + ((block & 1) ^ y_hi)
-
-
-def load_act(blocks, held, sems, core):
-    copies = []
-    for k, ref in enumerate(blocks):
-        at = core if k < 8 else 1 - core
-        rows = pl.ds(pl.multiple_of(at * 768, 768), 768)
-        copies.append(pltpu.make_async_copy(ref, held.at[k % 8, rows, :], sems.at[k]))
-    load(copies)
-
-
-def win_kernel(here, left, *refs):
-    blocks, outs, (held, sems) = refs[:16], refs[16:20], refs[20:]
+        functools.partial(hid_kernel, ways),
+        [jax.ShapeDtypeStruct((2, 768, 256), BF16)] * len(ways),
+        [pltpu.VMEM((8, 256, 1024), BF16)], len(ways) * 2 << 20, len(ways) * 768 * 512 * 2048,
+        here, [conv_mine, conv_beside], [*blocks, *beside],
+    )
+
+
+def act_copy(blocks, held, sems, core):
+    def copy_of(k, part, at):
+        rows = pl.ds(pl.multiple_of((core ^ part) * 768, 768), 768)
+        return pltpu.make_async_copy(
+            blocks[part * 8 + k], held.at[at, rows, :], sems.at[at * 2 + part]
+        )
+
+    return copy_of
+
+
+def win_kernel(ways, here, left, *refs):
+    count = len(ways)
+    blocks, outs, (held, sems) = refs[:16], refs[16 : 16 + count], refs[16 + count :]
     row, y_lo, z, x, y_hi, core = place_of(here)
-    load_act(blocks, held, sems, core)
     ahead = 1 - 2 * core
-    for out, step in zip(outs, (2, -ahead, ahead, 0)):
-        for i in range(2):
-            block = (y_lo ^ i) * 4 + ((z + step) & 3)
-            out[i] = jnp.dot(
-                left[...], held[hidden_slot(block, x, y_hi)], preferred_element_type=F32
+    steps = [fixed + way * ahead for fixed, way in ways] + [2] * (count - 1)
+    slots = [
+        hidden_slot((y_lo ^ i) * 4 + ((z + step) & 3), x, y_hi)
+        for step in steps[: 4 if count > 1 else 1]
+        for i in range(2)
+    ]
+    ready = fetch(act_copy(blocks, held, sems, core), slots)
+    for j in range(len(slots)):
+        at = ready(j)
+        if j < 2 * count:
+            outs[j // 2][j % 2] = jnp.dot(
+                left[...], held[at], preferred_element_type=F32
             ).astype(BF16)
 
 
-def win_partial(here, left, blocks, beside):
+def win_partial(here, left, blocks, beside, ways):
     return call(
-        win_kernel, [jax.ShapeDtypeStruct((2, 512, 256), BF16)] * 4,
-        [pltpu.VMEM((8, 1536, 256), BF16)], 10 << 20, 2 * 1536 * 512 * 2048, here, [left],
-        [*blocks, *beside],
+        functools.partial(win_kernel, ways),
+        [jax.ShapeDtypeStruct((2, 512, 256), BF16)] * len(ways),
+        [pltpu.VMEM((8, 1536, 256), BF16)], len(ways) * 3 << 20, len(ways) * 768 * 512 * 2048,
+        here, [left], [*blocks, *beside],
     )
 
 
@@ -178,23 +209,26 @@
     blocks, parts, out = refs[:16], refs[16:20], refs[20]
     held, weights, sems = refs[21:]
     row, y_lo, z, x, y_hi, core = place_of(here)
-    load(
-        [
-            pltpu.make_async_copy(ref, weights.at[pl.ds(k * 2, 2)], sems.at[16 + k])
-            for k, ref in enumerate(parts)
-        ]
-    )
-    load_act(blocks, held, sems, core)
-    for at in range(0, 1536, 512):
-        total = cot[at : at + 512, :].astype(F32)
+    copy_of = act_copy(blocks, held, sems, core)
+    copies = [
+        pltpu.make_async_copy(ref, weights.at[pl.ds(k * 2, 2)], sems.at[16 + k])
+        for k, ref in enumerate(parts)
+    ]
+    copies += [copy_of(k, part, k) for k in range(8) for part in range(2)]
+    for copy in copies:
+        copy.start()
+    for copy in copies:
+        copy.wait()
+    for at in range(0, 1536, 256):
+        total = cot[at : at + 256, :].astype(F32)
         for block in range(8):
             total = total + lax.dot_general(
-                held[hidden_slot(block, x, y_hi), at : at + 512, :],
+                held[hidden_slot(block, x, y_hi), at : at + 256, :],
                 weights[row_slot(block, y_lo, z)],
                 (((1,), (1,)), ((), ())),
                 preferred_element_type=F32,
             )
-        out[at : at + 512, :] = total.astype(BF16)
+        out[at : at + 256, :] = total.astype(BF16)
 
 
 def out_gradient(here, cot, blocks, beside, weights):
@@ -242,13 +276,13 @@
     mid_gain = scale_mid * keep_mid.astype(F32)
     hidden = jnp.maximum(pre_act.astype(F32) * mid_gain, 0.0).astype(BF16)
     hidden_full = lax.all_gather(hidden, "col", axis=1, tiled=True)
+    out_above, out_below = z_shift(weight_out, -1), z_shift(weight_out, 1)
     out_near = y_lo_swap(weight_out)
     out_near, cotangent, pre_act, inputs, conv_out = tie(
         out_near, cotangent, pre_act, inputs, conv_out
     )
-    out_here = jnp.stack([weight_out, out_near])
-    out_above, out_below = z_shift(out_here, -1), z_shift(out_here, 1)
-    out_blocks = [out_here, out_above, out_below, onward(out_above, out_below, core, z_split)]
+    near_above, near_below = z_shift(out_near, -1), z_shift(out_near, 1)
+    out_across = onward(out_above, out_below, core, z_split)
 
     wide_gain = scale_wide * keep_wide.astype(F32)
     cot_float = cotangent.astype(F32)
@@ -257,6 +291,15 @@
     conv_mine = mine(grad_conv)
     conv_beside = core_swap(theirs(grad_conv))
 
+    input_turned = inputs.T
+    near_above, conv_beside, input_turned, wide_part = tie(
+        near_above, conv_beside, input_turned, wide_part
+    )
+    near_across = onward(near_above, near_below, core, z_split)
+    out_blocks = [
+        weight_out, out_near, out_above, near_above, out_below, near_below, out_across, near_across
+    ]
+
     gain_pair = jnp.stack([scale_mid, keep_mid.astype(F32)])
     gain_beside = core_swap(gain_pair)
     pre_mine = mine(pre_act)
@@ -272,16 +315,15 @@
     mid_gain = gain_chip[0] * gain_chip[1]
 
     out_beside = [core_swap(block) for block in out_blocks]
-    input_turned = inputs.T
-    out_beside[3], weight_in, input_turned = tie(out_beside[3], weight_in, input_turned)
+    near_across, weight_in = tie(near_across, weight_in)
+    out_blocks[7] = near_across
     in_near = y_lo_swap(weight_in)
-    away, there = hid_partial(
-        place, conv_mine, conv_beside, out_blocks, out_beside, ((2, 0), (0, -1))
-    )
-    passed, back = x_split(away, 1), x_split(there, -1)
-    further, own = hid_partial(
-        place, conv_mine, conv_beside, out_blocks, out_beside, ((0, 1), (0, 0))
-    )
+    (away,) = hid_partial(place, conv_mine, conv_beside, out_blocks, out_beside, ((2, 0),))
+    passed = x_split(away, 1)
+    there, further, own = hid_partial(
+        place, conv_mine, conv_beside, out_blocks, out_beside, ((0, -1), (0, 1), (0, 0))
+    )
+    back = x_split(there, -1)
     passed, own, in_near = tie(passed, own, in_near)
     in_here = jnp.stack([weight_in, in_near])
     in_above, in_below = z_shift(in_here, -1), z_shift(in_here, 1)
@@ -289,7 +331,10 @@
     further, hidden_full = tie(further, hidden_full)
     terms = [own, back, further]
     total = add(terms)
-    grad_hid = total[0] + y_hi_swap(total[1].astype(BF16)).astype(F32)
+    wout = dot(hidden_full, grad_conv, 0, 0).astype(BF16)
+    crossed, wout = tie(y_hi_swap(total[1].astype(BF16)), wout)
+    wout = lax.psum_scatter(wout, "row", scatter_dimension=0, tiled=True)
+    grad_hid = add([total[0], crossed])
     alive = (pre_chip > 0) & (gain_chip[1] > 0)[None, :]
     grad_pre = jnp.where(alive, grad_hid, 0.0)
     mid_part = jnp.sum(grad_pre * pre_chip, axis=0).reshape(2, 128)
@@ -298,9 +343,6 @@
     act_near = y_hi_swap(grad_act)
     act_above, act_below = x_shift(grad_act, -1), x_shift(grad_act, 1)
     in_blocks = [in_here, in_above, in_below, onward(in_above, in_below, core, z_split)]
-    wout = dot(hidden_full, grad_conv, 0, 0).astype(BF16)
-    act_above, wout = tie(act_above, wout)
-    wout = lax.psum_scatter(wout, "row", scatter_dimension=0, tiled=True)
     near_above, near_below = x_shift(act_near, -1), x_shift(act_near, 1)
     act_across = onward(act_above, act_below, core, x_split)
     near_across = onward(near_above, near_below, core, x_split)
@@ -318,11 +360,17 @@
 
     act_beside = [core_swap(block) for block in act]
     act[7], sums = tie(act[7], sums)
-    win = win_partial(place, input_turned, act, act_beside)
-    passed, back = z_split(win[0], 1), z_split(win[1], -1)
+    (away,) = win_partial(place, input_turned, act, act_beside, ((2, 0),))
+    passed = z_split(away, 1)
+    there, further, own = win_partial(
+        place, input_turned, act, act_beside, ((0, -1), (0, 1), (0, 0))
+    )
+    back = z_split(there, -1)
+    passed, own = tie(passed, own)
+    further = z_split(add([further, passed]).astype(BF16), 1)
     grad_x = out_gradient(place, cotangent, act, act_beside, in_blocks)
-    passed, grad_x = tie(passed, grad_x)
-    total = add([win[3], back, z_split(add([win[2], passed]).astype(BF16), 1)])
+    back, grad_x, wout = tie(back, grad_x, wout)
+    total = add([own, back, further])
     grad_win = add([total[0], y_lo_swap(total[1].astype(BF16))]) * scaling
     grad_wout = wout.astype(F32) * scaling
     grad_smid = keep_mid.astype(F32) * scaling * sums[0]

time: 215 us -> 234 us (1.088)
  Pallas kernels: 31.8 us -> 42 us
  starting transfers between devices: 47.8 us -> 53.2 us
  waiting for transfers between devices: 82.8 us -> 87.9 us
  other arithmetic: 22.7 us -> 20.2 us
    pallas_call x4 -> x5, Pallas kernels: 31.8 us -> 42 us  [call(): pl.pallas_call(body, out_shape=outs, in_specs=[pl.BlockSpec(memory_space=...]
    ppermute x42 -> x49, starting transfers between devices: 47.8 us -> 53.1 us  [permute(): return lax.ppermute(v, AXES, pairs)]
    ppermute x42 -> x49, waiting for transfers between devices: 82.8 us -> 87.8 us  [permute(): return lax.ppermute(v, AXES, pairs)]
  transfers between devices with their start and end apart: 44 -> 51, of which waited for: 20 -> 20; matrix products, arithmetic and copies ran while one was open for 14% -> 12% of each run, Pallas kernels for 15% -> 18%
where the time goes in v3:
time: 234 us
  waiting for transfers between devices  87.9 us (38%)
  starting transfers between devices  53.2 us (23%)
  Pallas kernels  42 us (18%)
  other arithmetic  20.2 us (9%)
  between operations  14.6 us (6%)
  local copies, waits for them, and re-layouts  8.03 us (3%)
  matrix products  7.68 us (3%)
    ppermute x49, waiting for transfers between devices, permute(): return lax.ppermute(v, AXES, pairs)  87.8 us
    ppermute x49, starting transfers between devices, permute(): return lax.ppermute(v, AXES, pairs)  53.1 us
    pallas_call x5, Pallas kernels, call(): pl.pallas_call(body, out_shape=outs, in_specs=[pl.BlockSpec(memory_space=...  42 us
    dot_general x1, matrix products, dot(): lax.dot_general(a, b, (((ca,), (cb,)), ((), ())), preferred_element_type=...  7.68 us
  transfers between devices with their start and end apart: 51, of which 20 were waited for; matrix products, arithmetic and copies ran while one was open for 12% of the time, Pallas kernels for 18%

profile of v3, /device:TPU:0, one launch (start us, length us, event | category | flops | bytes accessed | tf_op | source)
XLA Modules:
  0.0 233.5 jit_solution(5076023492922341533)
XLA Ops:
  12.2 5.9 %collective-permute-done.refs_1_ = bf16[256,512]{1,0:T(8,128)(2,1)} collective-permute-done((bf16[256,512]{1,0:T(8,128)(2,1)}, bf16[256,512]{1,0:T(8,128)(2,1)}, u32[]{:S(2)}, u32[]{:S(2)}) %collective-permute-start) | collective-permute-done | bytes 262176 | tf_op jit(solution)/shard_map/ppermute | solution.py:27
  18.2 2.6 %fusion.1 = (f32[512]{0:T(512)S(1)}, bf16[1536,512]{1,0:T(8,128)(2,1)S(1)}) fusion(bf16[1536,512]{1,0:T(8,128)(2,1)} %cot, bf16[1536,512]{1,0:T(8,128)(2,1)} %param.12, f32[512]{0:T(512)S(1)} %convert_multiply_fusion.4), kind=kLoop, calls=%fused_computation.3 | loop fusion | flops 4718080 | bytes 4722688 | tf_op jit(solution)/shard_map/reduce_sum | solution.py:290
  22.0 4.2 %collective-permute-start.5 = (bf16[256,512]{1,0:T(8,128)(2,1)}, bf16[256,512]{1,0:T(8,128)(2,1)S(1)}, u32[]{:S(2)}, u32[]{:S(2)}) collective-permute-start(bf16[256,512]{1,0:T(8,128)(2,1)} %refs_0_.3), channel_id=1, source_target_pairs={{0,48},{1,49},{2,50},{3,51},{4,52},{5,53},{6,54},{7,55},{8,56},{9,... | collective-permute-start | bytes 786440 | tf_op jit(solution)/shard_map/ppermute | solution.py:27
  26.2 3.2 %collective-permute-start.1 = (bf16[256,512]{1,0:T(8,128)(2,1)}, bf16[256,512]{1,0:T(8,128)(2,1)}, u32[]{:S(2)}, u32[]{:S(2)}) collective-permute-start(bf16[256,512]{1,0:T(8,128)(2,1)} %collective-permute-done.refs_1_), channel_id=1, source_target_pairs={{0,48},{1,49},{2,50},{3,51},{4,52},{5,53},{6,54},{7,55},{8,56},{9,... | collective-permute-start | bytes 786440 | tf_op jit(solution)/shard_map/ppermute | solution.py:27
  31.1 2.1 collective-permute-done.5.refs_2_
  33.2 3.7 %collective-permute-done.6.refs_4_ = bf16[256,512]{1,0:T(8,128)(2,1)} collective-permute-done((bf16[256,512]{1,0:T(8,128)(2,1)}, bf16[256,512]{1,0:T(8,128)(2,1)}, u32[]{:S(2)}, u32[]{:S(2)}) %collective-permute-start.6) | collective-permute-done | bytes 262176 | tf_op jit(solution)/shard_map/ppermute | solution.py:27
  39.0 2.6 %collective-permute-start.12 = (bf16[256,512]{1,0:T(8,128)(2,1)S(1)}, bf16[256,512]{1,0:T(8,128)(2,1)S(1)}, u32[]{:S(2)}, u32[]{:S(2)}) collective-permute-start(bf16[256,512]{1,0:T(8,128)(2,1)S(1)} %collective-permute-done.5.refs_2_), channel_id=1, source_target_pairs={{0,1},{1,0},{2,3},{3,2},{4,5},{5,4},{6,7},{7,6},{8,9},{9,8},{10,11... | collective-permute-start | bytes 786440 | tf_op jit(solution)/shard_map/ppermute | solution.py:27
  43.4 3.0 %collective-permute-done.8.refs_6_ = bf16[256,512]{1,0:T(8,128)(2,1)S(1)} collective-permute-done((bf16[256,512]{1,0:T(8,128)(2,1)S(1)}, bf16[256,512]{1,0:T(8,128)(2,1)S(1)}, u32[]{:S(2)}, u32[]{:S(2)}) %collective-permute-start.8) | collective-permute-done | bytes 262176 | tf_op jit(solution)/shard_map/ppermute | solution.py:27
  47.1 3.4 %collective-permute-done.9.refs_7_ = bf16[256,512]{1,0:T(8,128)(2,1)S(1)} collective-permute-done((bf16[256,512]{1,0:T(8,128)(2,1)S(1)}, bf16[256,512]{1,0:T(8,128)(2,1)S(1)}, u32[]{:S(2)}, u32[]{:S(2)}) %collective-permute-start.9) | collective-permute-done | bytes 262176 | tf_op jit(solution)/shard_map/ppermute | solution.py:27
  52.2 5.5 %shard_map.137 = bf16[2,768,256]{2,1,0:T(8,128)(2,1)} custom-call(s32[2]{0:T(128)} %pad_add_fusion.here, bf16[768,512]{1,0:T(8,128)(2,1)} %get-tuple-element.77.conv_mine, bf16[768,512]{1,0:T(8,128)(2,1)} %collective-permute-done.2.conv_beside, bf16[256,512]{1,0:T(8,128)(2,1)} %refs_0_.3, bf16[256,512]{1,0:T(8,128)(2,1)} %collective-permute-done.refs_1_, ...), custom_call_target="tpu_custom_call" | custom-call | flops 805306368 | bytes 2097152 | tf_op jit(solution)/shard_map/pallas_call | solution.py:82
  60.9 11.2 %shard_map.138 = (bf16[2,768,256]{2,1,0:T(8,128)(2,1)}, bf16[2,768,256]{2,1,0:T(8,128)(2,1)}, bf16[2,768,256]{2,1,0:T(8,128)(2,1)}) custom-call(s32[2]{0:T(128)} %pad_add_fusion.here, bf16[768,512]{1,0:T(8,128)(2,1)} %get-tuple-element.77.conv_mine, bf16[768,512]{1,0:T(8,128)(2,1)} %collective-permute-done.2.conv_beside, bf16[256,512]{1,0:T(8,128)(2,1)} %refs_0_.3, ...), custom_call_target="tpu_custom_call" | custom-call | flops 2415919104 | bytes 6291456 | tf_op jit(solution)/shard_map/pallas_call | solution.py:82
  80.0 19.0 %collective-permute-done.21 = bf16[2,768,256]{2,1,0:T(8,128)(2,1)S(1)} collective-permute-done((bf16[2,768,256]{2,1,0:T(8,128)(2,1)S(1)}, bf16[2,768,256]{2,1,0:T(8,128)(2,1)S(1)}, u32[]{:S(2)}, u32[]{:S(2)}) %collective-permute-start.21) | collective-permute-done | bytes 786464 | tf_op jit(solution)/shard_map/ppermute | solution.py:27
  104.0 7.7 %convolution_convert_fusion = bf16[2048,512]{1,0:T(8,128)(2,1)} fusion(bf16[1536,2048]{1,0:T(8,128)(2,1)} %all-gather.2.cloned.1.call-done, bf16[1536,512]{1,0:T(8,128)(2,1)S(1)} %get-tuple-element.80), kind=kOutput, calls=%fused_computation.4 | convolution fusion | flops 3222274048 | bytes 9961472 | tf_op jit(solution)/shard_map/dot_general | solution.py:63
  111.7 2.5 %collective-permute-done.22 = bf16[768,256]{1,0:T(8,128)(2,1)} collective-permute-done((bf16[768,256]{1,0:T(8,128)(2,1)}, bf16[768,256]{1,0:T(8,128)(2,1)}, u32[]{:S(2)}, u32[]{:S(2)}) %collective-permute-start.22) | collective-permute-done | bytes 393248 | tf_op jit(solution)/shard_map/ppermute | solution.py:27
  114.4 4.0 %collective-permute-start.23 = (bf16[2,512,256]{2,1,0:T(8,128)(2,1)S(1)}, bf16[2,512,256]{2,1,0:T(8,128)(2,1)}, u32[]{:S(2)}, u32[]{:S(2)}) collective-permute-start(bf16[2,512,256]{2,1,0:T(8,128)(2,1)S(1)} %pad_maximum_fusion.refs_16_), channel_id=1, source_target_pairs={{0,48},{1,49},{2,50},{3,51},{4,52},{5,53},{6,54},{7,55},{8,56},{9,... | collective-permute-start | bytes 1572872 | tf_op jit(solution)/shard_map/ppermute | solution.py:27
  120.9 14.5 %collective-permute-done.23.refs_17_ = bf16[2,512,256]{2,1,0:T(8,128)(2,1)} collective-permute-done((bf16[2,512,256]{2,1,0:T(8,128)(2,1)S(1)}, bf16[2,512,256]{2,1,0:T(8,128)(2,1)}, u32[]{:S(2)}, u32[]{:S(2)}) %collective-permute-start.23) | collective-permute-done | bytes 524320 | tf_op jit(solution)/shard_map/ppermute | solution.py:27
  135.4 4.7 %collective-permute-done.24.refs_18_ = bf16[2,512,256]{2,1,0:T(8,128)(2,1)} collective-permute-done((bf16[2,512,256]{2,1,0:T(8,128)(2,1)S(1)}, bf16[2,512,256]{2,1,0:T(8,128)(2,1)}, u32[]{:S(2)}, u32[]{:S(2)}) %collective-permute-start.24) | collective-permute-done | bytes 524320 | tf_op jit(solution)/shard_map/ppermute | solution.py:27
  140.1 3.2 %collective-permute-start.26 = (bf16[768,256]{1,0:T(8,128)(2,1)S(1)}, bf16[768,256]{1,0:T(8,128)(2,1)S(1)}, u32[]{:S(2)}, u32[]{:S(2)}) collective-permute-start(bf16[768,256]{1,0:T(8,128)(2,1)S(1)} %get-tuple-element.58.refs_0_), channel_id=1, source_target_pairs={{0,12},{1,13},{2,14},{3,15},{4,0},{5,1},{6,2},{7,3},{8,4},{9,5},{1... | collective-permute-start | bytes 1179656 | tf_op jit(solution)/shard_map/ppermute | solution.py:27
  143.4 2.1 collective-permute-start.28
  146.3 9.6 %collective-permute-done.25.refs_1_ = bf16[768,256]{1,0:T(8,128)(2,1)S(1)} collective-permute-done((bf16[768,256]{1,0:T(8,128)(2,1)S(1)}, bf16[768,256]{1,0:T(8,128)(2,1)S(1)}, u32[]{:S(2)}, u32[]{:S(2)}) %collective-permute-start.25) | collective-permute-done | bytes 393248 | tf_op jit(solution)/shard_map/ppermute | solution.py:27
  155.8 4.4 %collective-permute-start.27 = (bf16[768,256]{1,0:T(8,128)(2,1)S(1)}, bf16[768,256]{1,0:T(8,128)(2,1)S(1)}, u32[]{:S(2)}, u32[]{:S(2)}) collective-permute-start(bf16[768,256]{1,0:T(8,128)(2,1)S(1)} %collective-permute-done.25.refs_1_), channel_id=1, source_target_pairs={{0,12},{1,13},{2,14},{3,15},{4,0},{5,1},{6,2},{7,3},{8,4},{9,5},{1... | collective-permute-start | bytes 1179656 | tf_op jit(solution)/shard_map/ppermute | solution.py:27
  162.0 1.9 collective-permute-start.35
  164.0 2.0 collective-permute-start.30
  166.0 5.1 %collective-permute-done.27.refs_3_ = bf16[768,256]{1,0:T(8,128)(2,1)S(1)} collective-permute-done((bf16[768,256]{1,0:T(8,128)(2,1)S(1)}, bf16[768,256]{1,0:T(8,128)(2,1)S(1)}, u32[]{:S(2)}, u32[]{:S(2)}) %collective-permute-start.27) | collective-permute-done | bytes 393248 | tf_op jit(solution)/shard_map/ppermute | solution.py:27
  171.7 2.9 %collective-permute-start.31 = (bf16[768,256]{1,0:T(8,128)(2,1)S(1)}, bf16[768,256]{1,0:T(8,128)(2,1)S(1)}, u32[]{:S(2)}, u32[]{:S(2)}) collective-permute-start(bf16[768,256]{1,0:T(8,128)(2,1)S(1)} %broadcast_select_fusion.1), channel_id=1, source_target_pairs={{0,4},{1,13},{2,6},{3,15},{4,8},{5,1},{6,10},{7,3},{8,12},{9,5},{1... | collective-permute-start | bytes 1179656 | tf_op jit(solution)/shard_map/ppermute | solution.py:27
  176.1 4.7 %collective-permute-done.31.refs_7_ = bf16[768,256]{1,0:T(8,128)(2,1)S(1)} collective-permute-done((bf16[768,256]{1,0:T(8,128)(2,1)S(1)}, bf16[768,256]{1,0:T(8,128)(2,1)S(1)}, u32[]{:S(2)}, u32[]{:S(2)}) %collective-permute-start.31) | collective-permute-done | bytes 393248 | tf_op jit(solution)/shard_map/ppermute | solution.py:27
  182.7 5.4 %shard_map.141 = bf16[2,512,256]{2,1,0:T(8,128)(2,1)} custom-call(s32[2]{0:T(128)} %pad_add_fusion.here, bf16[512,1536]{1,0:T(8,128)(2,1)} %bitcast.48, bf16[768,256]{1,0:T(8,128)(2,1)} %copy-done, bf16[768,256]{1,0:T(8,128)(2,1)} %copy-done.11, bf16[768,256]{1,0:T(8,128)(2,1)} %copy-done.1, bf16[768,256]{1,0:T(8,128)(2,1)} %copy-done.3, ...), custom_call_target="tpu_custom_call" | custom-call | flops 805306368 | bytes 3145728 | tf_op jit(solution)/shard_map/pallas_call | solution.py:82
  189.6 10.3 %shard_map.139 = (bf16[2,512,256]{2,1,0:T(8,128)(2,1)}, bf16[2,512,256]{2,1,0:T(8,128)(2,1)}, bf16[2,512,256]{2,1,0:T(8,128)(2,1)}) custom-call(s32[2]{0:T(128)} %pad_add_fusion.here, bf16[512,1536]{1,0:T(8,128)(2,1)} %bitcast.49, bf16[768,256]{1,0:T(8,128)(2,1)} %copy-done, bf16[768,256]{1,0:T(8,128)(2,1)} %copy-done.11, bf16[768,256]{1,0:T(8,128)(2,1)} %copy-done.1, ...), custom_call_target="tpu_custom_call" | custom-call | flops 2415919104 | bytes 9437184 | tf_op jit(solution)/shard_map/pallas_call | solution.py:82
  200.0 3.0 %collective-permute-start.44 = (bf16[2,512,256]{2,1,0:T(8,128)(2,1)}, bf16[2,512,256]{2,1,0:T(8,128)(2,1)S(1)}, u32[]{:S(2)}, u32[]{:S(2)}) collective-permute-start(bf16[2,512,256]{2,1,0:T(8,128)(2,1)} %get-tuple-element.61), channel_id=1, source_target_pairs={{0,48},{1,17},{2,50},{3,19},{4,52},{5,21},{6,54},{7,23},{8,56},{9,... | collective-permute-start | bytes 1572872 | tf_op jit(solution)/shard_map/ppermute | solution.py:27
  205.7 9.5 %shard_map.140 = bf16[1536,512]{1,0:T(8,128)(2,1)} custom-call(s32[2]{0:T(128)} %pad_add_fusion.here, bf16[1536,512]{1,0:T(8,128)(2,1)} %cot, bf16[768,256]{1,0:T(8,128)(2,1)} %copy-done, bf16[768,256]{1,0:T(8,128)(2,1)} %copy-done.11, bf16[768,256]{1,0:T(8,128)(2,1)} %copy-done.1, bf16[768,256]{1,0:T(8,128)(2,1)} %copy-done.3, bf16[768,256]{1,0:T(8,128)(2,1)} %copy-done.2, ...), custom_call_target="tpu_custom_call" | custom-call | flops 3221225472 | bytes 12582912 | tf_op jit(solution)/shard_map/pallas_call | solution.py:82
  216.5 3.1 %collective-permute-start.48 = (bf16[512,256]{1,0:T(8,128)(2,1)S(1)}, bf16[512,256]{1,0:T(8,128)(2,1)S(1)}, u32[]{:S(2)}, u32[]{:S(2)}) collective-permute-start(bf16[512,256]{1,0:T(8,128)(2,1)S(1)} %fusion.9), channel_id=1, source_target_pairs={{0,64},{1,65},{2,66},{3,67},{4,68},{5,69},{6,70},{7,71},{8,72},{9,... | collective-permute-start | bytes 786440 | tf_op jit(solution)/shard_map/ppermute | solution.py:27
  221.0 4.8 %collective-permute-done.48 = bf16[512,256]{1,0:T(8,128)(2,1)S(1)} collective-permute-done((bf16[512,256]{1,0:T(8,128)(2,1)S(1)}, bf16[512,256]{1,0:T(8,128)(2,1)S(1)}, u32[]{:S(2)}, u32[]{:S(2)}) %collective-permute-start.48) | collective-permute-done | bytes 262176 | tf_op jit(solution)/shard_map/ppermute | solution.py:27
  (189 shorter events, 46.9 us)
Async XLA Ops:
  7.2 91.8 %all-gather.2.cloned.1.call-start = ((), (), s32[]{:S(2)}) async-start(), calls=%async_computation.1 | async-start | bytes 6684672 | tf_op jit(solution)/shard_map/all_gather | solution.py:278
  9.8 205.5 %reduce-scatter.2.cloned.1.call-start = ((), (), s32[]{:S(2)}) async-start(), calls=%async_computation.2 | async-start | bytes 2359296 | tf_op jit(solution)/shard_map/reduce_scatter | solution.py:336
  22.0 16.9 %collective-permute-start.2 = (bf16[768,512]{1,0:T(8,128)(2,1)}, bf16[768,512]{1,0:T(8,128)(2,1)}, u32[]{:S(2)}, u32[]{:S(2)}) collective-permute-start(bf16[768,512]{1,0:T(8,128)(2,1)} %get-tuple-element.78), channel_id=1, source_target_pairs={{0,1},{1,0},{2,3},{3,2},{4,5},{5,4},{6,7},{7,6},{8,9},{9,8},{10,11... | collective-permute-start | bytes 2359304 | tf_op jit(solution)/shard_map/ppermute | solution.py:27
  22.0 11.1 %collective-permute-start.5 = (bf16[256,512]{1,0:T(8,128)(2,1)}, bf16[256,512]{1,0:T(8,128)(2,1)S(1)}, u32[]{:S(2)}, u32[]{:S(2)}) collective-permute-start(bf16[256,512]{1,0:T(8,128)(2,1)} %refs_0_.3), channel_id=1, source_target_pairs={{0,48},{1,49},{2,50},{3,51},{4,52},{5,53},{6,54},{7,55},{8,56},{9,... | collective-permute-start | bytes 786440 | tf_op jit(solution)/shard_map/ppermute | solution.py:27
  26.2 10.7 %collective-permute-start.6 = (bf16[256,512]{1,0:T(8,128)(2,1)}, bf16[256,512]{1,0:T(8,128)(2,1)}, u32[]{:S(2)}, u32[]{:S(2)}) collective-permute-start(bf16[256,512]{1,0:T(8,128)(2,1)} %refs_0_.3), channel_id=1, source_target_pairs={{0,16},{1,17},{2,18},{3,19},{4,20},{5,21},{6,22},{7,23},{8,24},{9,... | collective-permute-start | bytes 786440 | tf_op jit(solution)/shard_map/ppermute | solution.py:27
  26.2 12.2 %collective-permute-start.1 = (bf16[256,512]{1,0:T(8,128)(2,1)}, bf16[256,512]{1,0:T(8,128)(2,1)}, u32[]{:S(2)}, u32[]{:S(2)}) collective-permute-start(bf16[256,512]{1,0:T(8,128)(2,1)} %collective-permute-done.refs_1_), channel_id=1, source_target_pairs={{0,48},{1,49},{2,50},{3,51},{4,52},{5,53},{6,54},{7,55},{8,56},{9,... | collective-permute-start | bytes 786440 | tf_op jit(solution)/shard_map/ppermute | solution.py:27
  29.5 12.3 %collective-permute-start.7 = (bf16[256,512]{1,0:T(8,128)(2,1)}, bf16[256,512]{1,0:T(8,128)(2,1)}, u32[]{:S(2)}, u32[]{:S(2)}) collective-permute-start(bf16[256,512]{1,0:T(8,128)(2,1)} %collective-permute-done.refs_1_), channel_id=1, source_target_pairs={{0,16},{1,17},{2,18},{3,19},{4,20},{5,21},{6,22},{7,23},{8,24},{9,... | collective-permute-start | bytes 786440 | tf_op jit(solution)/shard_map/ppermute | solution.py:27
  33.2 9.7 %collective-permute-start.10 = (bf16[256,512]{1,0:T(8,128)(2,1)}, bf16[256,512]{1,0:T(8,128)(2,1)S(1)}, u32[]{:S(2)}, u32[]{:S(2)}) collective-permute-start(bf16[256,512]{1,0:T(8,128)(2,1)} %refs_0_.3), channel_id=1, source_target_pairs={{0,1},{1,0},{2,3},{3,2},{4,5},{5,4},{6,7},{7,6},{8,9},{9,8},{10,11... | collective-permute-start | bytes 786440 | tf_op jit(solution)/shard_map/ppermute | solution.py:27
  36.9 9.6 %collective-permute-start.11 = (bf16[256,512]{1,0:T(8,128)(2,1)}, bf16[256,512]{1,0:T(8,128)(2,1)S(1)}, u32[]{:S(2)}, u32[]{:S(2)}) collective-permute-start(bf16[256,512]{1,0:T(8,128)(2,1)} %collective-permute-done.refs_1_), channel_id=1, source_target_pairs={{0,1},{1,0},{2,3},{3,2},{4,5},{5,4},{6,7},{7,6},{8,9},{9,8},{10,11... | collective-permute-start | bytes 786440 | tf_op jit(solution)/shard_map/ppermute | solution.py:27
  57.7 15.2 %collective-permute-start.18 = (bf16[2,768,256]{2,1,0:T(8,128)(2,1)}, bf16[2,768,256]{2,1,0:T(8,128)(2,1)S(1)}, u32[]{:S(2)}, u32[]{:S(2)}) collective-permute-start(bf16[2,768,256]{2,1,0:T(8,128)(2,1)} %shard_map.137), channel_id=1, source_target_pairs={{0,4},{1,13},{2,6},{3,15},{4,8},{5,1},{6,10},{7,3},{8,12},{9,5},{1... | collective-permute-start | bytes 2359304 | tf_op jit(solution)/shard_map/ppermute | solution.py:27
  59.3 13.6 %collective-permute-start.19 = (bf16[512,256]{1,0:T(8,128)(2,1)S(1)}, bf16[512,256]{1,0:T(8,128)(2,1)S(1)}, u32[]{:S(2)}, u32[]{:S(2)}) collective-permute-start(bf16[512,256]{1,0:T(8,128)(2,1)S(1)} %copy-done.22), channel_id=1, source_target_pairs={{0,64},{1,65},{2,66},{3,67},{4,68},{5,69},{6,70},{7,71},{8,72},{9,... | collective-permute-start | bytes 786440 | tf_op jit(solution)/shard_map/ppermute | solution.py:27
  72.1 27.8 %collective-permute-start.20 = (bf16[2,768,256]{2,1,0:T(8,128)(2,1)}, bf16[2,768,256]{2,1,0:T(8,128)(2,1)}, u32[]{:S(2)}, u32[]{:S(2)}) collective-permute-start(bf16[2,768,256]{2,1,0:T(8,128)(2,1)} %get-tuple-element.51), channel_id=1, source_target_pairs={{0,12},{1,5},{2,14},{3,7},{4,0},{5,9},{6,2},{7,11},{8,4},{9,13},{1... | collective-permute-start | bytes 2359304 | tf_op jit(solution)/shard_map/ppermute | solution.py:27
  74.3 24.6 %collective-permute-start.21 = (bf16[2,768,256]{2,1,0:T(8,128)(2,1)S(1)}, bf16[2,768,256]{2,1,0:T(8,128)(2,1)S(1)}, u32[]{:S(2)}, u32[]{:S(2)}) collective-permute-start(bf16[2,768,256]{2,1,0:T(8,128)(2,1)S(1)} %add_convert_fusion), channel_id=1, source_target_pairs={{0,4},{1,13},{2,6},{3,15},{4,8},{5,1},{6,10},{7,3},{8,12},{9,5},{1... | collective-permute-start | bytes 2359304 | tf_op jit(solution)/shard_map/ppermute | solution.py:27
  79.6 38.8 %collective-permute-start.3 = (bf16[768,128]{1,0:T(8,128)(2,1)}, bf16[768,128]{1,0:T(8,128)(2,1)}, u32[]{:S(2)}, u32[]{:S(2)}) collective-permute-start(bf16[768,128]{1,0:T(8,128)(2,1)} %constant_dynamic-slice_fusion.3), channel_id=1, source_target_pairs={{0,1},{1,0},{2,3},{3,2},{4,5},{5,4},{6,7},{7,6},{8,9},{9,8},{10,11... | collective-permute-start | bytes 589832 | tf_op jit(solution)/shard_map/ppermute | solution.py:27
  102.5 11.7 %collective-permute-start.22 = (bf16[768,256]{1,0:T(8,128)(2,1)}, bf16[768,256]{1,0:T(8,128)(2,1)}, u32[]{:S(2)}, u32[]{:S(2)}) collective-permute-start(bf16[768,256]{1,0:T(8,128)(2,1)} %fusion.8), channel_id=1, source_target_pairs={{0,2},{1,3},{2,0},{3,1},{4,6},{5,7},{6,4},{7,5},{8,10},{9,11},{10,... | collective-permute-start | bytes 1179656 | tf_op jit(solution)/shard_map/ppermute | solution.py:27
  114.4 21.0 %collective-permute-start.23 = (bf16[2,512,256]{2,1,0:T(8,128)(2,1)S(1)}, bf16[2,512,256]{2,1,0:T(8,128)(2,1)}, u32[]{:S(2)}, u32[]{:S(2)}) collective-permute-start(bf16[2,512,256]{2,1,0:T(8,128)(2,1)S(1)} %pad_maximum_fusion.refs_16_), channel_id=1, source_target_pairs={{0,48},{1,49},{2,50},{3,51},{4,52},{5,53},{6,54},{7,55},{8,56},{9,... | collective-permute-start | bytes 1572872 | tf_op jit(solution)/shard_map/ppermute | solution.py:27
  118.4 21.6 %collective-permute-start.24 = (bf16[2,512,256]{2,1,0:T(8,128)(2,1)S(1)}, bf16[2,512,256]{2,1,0:T(8,128)(2,1)}, u32[]{:S(2)}, u32[]{:S(2)}) collective-permute-start(bf16[2,512,256]{2,1,0:T(8,128)(2,1)S(1)} %pad_maximum_fusion.refs_16_), channel_id=1, source_target_pairs={{0,16},{1,17},{2,18},{3,19},{4,20},{5,21},{6,22},{7,23},{8,24},{9,... | collective-permute-start | bytes 1572872 | tf_op jit(solution)/shard_map/ppermute | solution.py:27
  120.8 19.3 %collective-permute-start.32 = (f32[128]{0:T(128)S(1)}, f32[128]{0:T(128)S(1)}, u32[]{:S(2)}, u32[]{:S(2)}) collective-permute-start(f32[128]{0:T(128)S(1)} %fusion.14), channel_id=1, source_target_pairs={{0,1},{1,0},{2,3},{3,2},{4,5},{5,4},{6,7},{7,6},{8,9},{9,8},{10,11... | collective-permute-start | bytes 1544 | tf_op jit(solution)/shard_map/ppermute | solution.py:27
  140.0 15.8 %collective-permute-start.25 = (bf16[768,256]{1,0:T(8,128)(2,1)S(1)}, bf16[768,256]{1,0:T(8,128)(2,1)S(1)}, u32[]{:S(2)}, u32[]{:S(2)}) collective-permute-start(bf16[768,256]{1,0:T(8,128)(2,1)S(1)} %get-tuple-element.58.refs_0_), channel_id=1, source_target_pairs={{0,2},{1,3},{2,0},{3,1},{4,6},{5,7},{6,4},{7,5},{8,10},{9,11},{10,... | collective-permute-start | bytes 1179656 | tf_op jit(solution)/shard_map/ppermute | solution.py:27
  140.1 21.8 %collective-permute-start.26 = (bf16[768,256]{1,0:T(8,128)(2,1)S(1)}, bf16[768,256]{1,0:T(8,128)(2,1)S(1)}, u32[]{:S(2)}, u32[]{:S(2)}) collective-permute-start(bf16[768,256]{1,0:T(8,128)(2,1)S(1)} %get-tuple-element.58.refs_0_), channel_id=1, source_target_pairs={{0,12},{1,13},{2,14},{3,15},{4,0},{5,1},{6,2},{7,3},{8,4},{9,5},{1... | collective-permute-start | bytes 1179656 | tf_op jit(solution)/shard_map/ppermute | solution.py:27
  143.4 20.6 %collective-permute-start.28 = (bf16[768,256]{1,0:T(8,128)(2,1)S(1)}, bf16[768,256]{1,0:T(8,128)(2,1)S(1)}, u32[]{:S(2)}, u32[]{:S(2)}) collective-permute-start(bf16[768,256]{1,0:T(8,128)(2,1)S(1)} %get-tuple-element.58.refs_0_), channel_id=1, source_target_pairs={{0,4},{1,5},{2,6},{3,7},{4,8},{5,9},{6,10},{7,11},{8,12},{9,13},{1... | collective-permute-start | bytes 1179656 | tf_op jit(solution)/shard_map/ppermute | solution.py:27
  145.4 14.8 %collective-permute-start.34 = (f32[5,128]{1,0:T(8,128)S(1)}, f32[5,128]{1,0:T(8,128)S(1)}, u32[]{:S(2)}, u32[]{:S(2)}) collective-permute-start(f32[5,128]{1,0:T(8,128)S(1)} %fusion.15), channel_id=1, source_target_pairs={{0,32},{1,33},{2,34},{3,35},{4,36},{5,37},{6,38},{7,39},{8,40},{9,... | collective-permute-start | bytes 7688 | tf_op jit(solution)/shard_map/ppermute | solution.py:27
  146.3 28.3 %collective-permute-start.36 = (bf16[768,256]{1,0:T(8,128)(2,1)S(1)}, bf16[768,256]{1,0:T(8,128)(2,1)S(1)}, u32[]{:S(2)}, u32[]{:S(2)}) collective-permute-start(bf16[768,256]{1,0:T(8,128)(2,1)S(1)} %get-tuple-element.58.refs_0_), channel_id=1, source_target_pairs={{0,1},{1,0},{2,3},{3,2},{4,5},{5,4},{6,7},{7,6},{8,9},{9,8},{10,11... | collective-permute-start | bytes 1179656 | tf_op jit(solution)/shard_map/ppermute | solution.py:27
  155.8 15.2 %collective-permute-start.27 = (bf16[768,256]{1,0:T(8,128)(2,1)S(1)}, bf16[768,256]{1,0:T(8,128)(2,1)S(1)}, u32[]{:S(2)}, u32[]{:S(2)}) collective-permute-start(bf16[768,256]{1,0:T(8,128)(2,1)S(1)} %collective-permute-done.25.refs_1_), channel_id=1, source_target_pairs={{0,12},{1,13},{2,14},{3,15},{4,0},{5,1},{6,2},{7,3},{8,4},{9,5},{1... | collective-permute-start | bytes 1179656 | tf_op jit(solution)/shard_map/ppermute | solution.py:27
  160.2 11.0 %collective-permute-start.29 = (bf16[768,256]{1,0:T(8,128)(2,1)S(1)}, bf16[768,256]{1,0:T(8,128)(2,1)S(1)}, u32[]{:S(2)}, u32[]{:S(2)}) collective-permute-start(bf16[768,256]{1,0:T(8,128)(2,1)S(1)} %collective-permute-done.25.refs_1_), channel_id=1, source_target_pairs={{0,4},{1,5},{2,6},{3,7},{4,8},{5,9},{6,10},{7,11},{8,12},{9,13},{1... | collective-permute-start | bytes 1179656 | tf_op jit(solution)/shard_map/ppermute | solution.py:27
  162.0 9.7 %collective-permute-start.35 = (f32[5,128]{1,0:T(8,128)S(1)}, f32[5,128]{1,0:T(8,128)S(1)}, u32[]{:S(2)}, u32[]{:S(2)}) collective-permute-start(f32[5,128]{1,0:T(8,128)S(1)} %fusion.19), channel_id=1, source_target_pairs={{0,64},{1,65},{2,66},{3,67},{4,68},{5,69},{6,70},{7,71},{8,72},{9,... | collective-permute-start | bytes 7688 | tf_op jit(solution)/shard_map/ppermute | solution.py:27
  164.0 11.5 %collective-permute-start.30 = (bf16[768,256]{1,0:T(8,128)(2,1)S(1)}, bf16[768,256]{1,0:T(8,128)(2,1)S(1)}, u32[]{:S(2)}, u32[]{:S(2)}) collective-permute-start(bf16[768,256]{1,0:T(8,128)(2,1)S(1)} %broadcast_select_fusion.2), channel_id=1, source_target_pairs={{0,4},{1,13},{2,6},{3,15},{4,8},{5,1},{6,10},{7,3},{8,12},{9,5},{1... | collective-permute-start | bytes 1179656 | tf_op jit(solution)/shard_map/ppermute | solution.py:27
  188.1 14.9 %collective-permute-start.46 = (bf16[2,512,256]{2,1,0:T(8,128)(2,1)}, bf16[2,512,256]{2,1,0:T(8,128)(2,1)S(1)}, u32[]{:S(2)}, u32[]{:S(2)}) collective-permute-start(bf16[2,512,256]{2,1,0:T(8,128)(2,1)} %shard_map.141), channel_id=1, source_target_pairs={{0,16},{1,49},{2,18},{3,51},{4,20},{5,53},{6,22},{7,55},{8,24},{9,... | collective-permute-start | bytes 1572872 | tf_op jit(solution)/shard_map/ppermute | solution.py:27
  189.6 15.4 %collective-permute-start.45 = (bf16[2,512,256]{2,1,0:T(8,128)(2,1)S(1)}, bf16[2,512,256]{2,1,0:T(8,128)(2,1)S(1)}, u32[]{:S(2)}, u32[]{:S(2)}) collective-permute-start(bf16[2,512,256]{2,1,0:T(8,128)(2,1)S(1)} %broadcast_select_fusion), channel_id=1, source_target_pairs={{0,16},{1,49},{2,18},{3,51},{4,20},{5,53},{6,22},{7,55},{8,24},{9,... | collective-permute-start | bytes 1572872 | tf_op jit(solution)/shard_map/ppermute | solution.py:27
  200.0 15.3 %collective-permute-start.44 = (bf16[2,512,256]{2,1,0:T(8,128)(2,1)}, bf16[2,512,256]{2,1,0:T(8,128)(2,1)S(1)}, u32[]{:S(2)}, u32[]{:S(2)}) collective-permute-start(bf16[2,512,256]{2,1,0:T(8,128)(2,1)} %get-tuple-element.61), channel_id=1, source_target_pairs={{0,48},{1,17},{2,50},{3,19},{4,52},{5,21},{6,54},{7,23},{8,56},{9,... | collective-permute-start | bytes 1572872 | tf_op jit(solution)/shard_map/ppermute | solution.py:27
  204.2 12.1 %collective-permute-start.47 = (bf16[2,512,256]{2,1,0:T(8,128)(2,1)S(1)}, bf16[2,512,256]{2,1,0:T(8,128)(2,1)S(1)}, u32[]{:S(2)}, u32[]{:S(2)}) collective-permute-start(bf16[2,512,256]{2,1,0:T(8,128)(2,1)S(1)} %add_convert_fusion.1), channel_id=1, source_target_pairs={{0,16},{1,49},{2,18},{3,51},{4,20},{5,53},{6,22},{7,55},{8,24},{9,... | collective-permute-start | bytes 1572872 | tf_op jit(solution)/shard_map/ppermute | solution.py:27
  216.5 9.3 %collective-permute-start.48 = (bf16[512,256]{1,0:T(8,128)(2,1)S(1)}, bf16[512,256]{1,0:T(8,128)(2,1)S(1)}, u32[]{:S(2)}, u32[]{:S(2)}) collective-permute-start(bf16[512,256]{1,0:T(8,128)(2,1)S(1)} %fusion.9), channel_id=1, source_target_pairs={{0,64},{1,65},{2,66},{3,67},{4,68},{5,69},{6,70},{7,71},{8,72},{9,... | collective-permute-start | bytes 786440 | tf_op jit(solution)/shard_map/ppermute | solution.py:27
  (56 other events, 437.2 us)
Sparse Core Ops, SparseCore 0:
  10.8 82.0 all-gather.1
  114.4 46.2 reduce-scatter.1

commit v4 on v2

--- a/solution.py
+++ b/solution.py
@@ -153,12 +153,13 @@
     load(copies)
 
 
-def win_kernel(here, left, *refs):
-    blocks, outs, (held, sems) = refs[:16], refs[16:20], refs[20:]
+def win_kernel(ways, here, left, *refs):
+    blocks, outs, (held, sems) = refs[:16], refs[16:18], refs[18:]
     row, y_lo, z, x, y_hi, core = place_of(here)
     load_act(blocks, held, sems, core)
     ahead = 1 - 2 * core
-    for out, step in zip(outs, (2, -ahead, ahead, 0)):
+    for out, (fixed, way) in zip(outs, ways):
+        step = fixed + way * ahead
         for i in range(2):
             block = (y_lo ^ i) * 4 + ((z + step) & 3)
             out[i] = jnp.dot(
@@ -166,10 +167,10 @@
             ).astype(BF16)
 
 
-def win_partial(here, left, blocks, beside):
+def win_partial(here, left, blocks, beside, ways):
     return call(
-        win_kernel, [jax.ShapeDtypeStruct((2, 512, 256), BF16)] * 4,
-        [pltpu.VMEM((8, 1536, 256), BF16)], 10 << 20, 2 * 1536 * 512 * 2048, here, [left],
+        functools.partial(win_kernel, ways), [jax.ShapeDtypeStruct((2, 512, 256), BF16)] * 2,
+        [pltpu.VMEM((8, 1536, 256), BF16)], 9 << 20, 1536 * 512 * 2048, here, [left],
         [*blocks, *beside],
     )
 
@@ -185,16 +186,16 @@
         ]
     )
     load_act(blocks, held, sems, core)
-    for at in range(0, 1536, 512):
-        total = cot[at : at + 512, :].astype(F32)
+    for at in range(0, 1536, 256):
+        total = cot[at : at + 256, :].astype(F32)
         for block in range(8):
             total = total + lax.dot_general(
-                held[hidden_slot(block, x, y_hi), at : at + 512, :],
+                held[hidden_slot(block, x, y_hi), at : at + 256, :],
                 weights[row_slot(block, y_lo, z)],
                 (((1,), (1,)), ((), ())),
                 preferred_element_type=F32,
             )
-        out[at : at + 512, :] = total.astype(BF16)
+        out[at : at + 256, :] = total.astype(BF16)
 
 
 def out_gradient(here, cot, blocks, beside, weights):
@@ -248,7 +249,6 @@
     )
     out_here = jnp.stack([weight_out, out_near])
     out_above, out_below = z_shift(out_here, -1), z_shift(out_here, 1)
-    out_blocks = [out_here, out_above, out_below, onward(out_above, out_below, core, z_split)]
 
     wide_gain = scale_wide * keep_wide.astype(F32)
     cot_float = cotangent.astype(F32)
@@ -257,6 +257,12 @@
     conv_mine = mine(grad_conv)
     conv_beside = core_swap(theirs(grad_conv))
 
+    input_turned = inputs.T
+    out_above, conv_beside, input_turned, wide_part = tie(
+        out_above, conv_beside, input_turned, wide_part
+    )
+    out_blocks = [out_here, out_above, out_below, onward(out_above, out_below, core, z_split)]
+
     gain_pair = jnp.stack([scale_mid, keep_mid.astype(F32)])
     gain_beside = core_swap(gain_pair)
     pre_mine = mine(pre_act)
@@ -272,35 +278,35 @@
     mid_gain = gain_chip[0] * gain_chip[1]
 
     out_beside = [core_swap(block) for block in out_blocks]
-    input_turned = inputs.T
-    out_beside[3], weight_in, input_turned = tie(out_beside[3], weight_in, input_turned)
+    out_beside[3], weight_in = tie(out_beside[3], weight_in)
     in_near = y_lo_swap(weight_in)
     away, there = hid_partial(
         place, conv_mine, conv_beside, out_blocks, out_beside, ((2, 0), (0, -1))
     )
     passed, back = x_split(away, 1), x_split(there, -1)
+    away, in_near = tie(away, in_near)
+    in_here = jnp.stack([weight_in, in_near])
+    in_above, in_below = z_shift(in_here, -1), z_shift(in_here, 1)
     further, own = hid_partial(
         place, conv_mine, conv_beside, out_blocks, out_beside, ((0, 1), (0, 0))
     )
-    passed, own, in_near = tie(passed, own, in_near)
-    in_here = jnp.stack([weight_in, in_near])
-    in_above, in_below = z_shift(in_here, -1), z_shift(in_here, 1)
+    passed, own, in_above, in_below = tie(passed, own, in_above, in_below)
     further = x_split(add([further, passed]).astype(BF16), 1)
-    further, hidden_full = tie(further, hidden_full)
+    in_across = onward(in_above, in_below, core, z_split)
+    further, hidden_full, in_across = tie(further, hidden_full, in_across)
+    in_blocks = [in_here, in_above, in_below, in_across]
     terms = [own, back, further]
     total = add(terms)
-    grad_hid = total[0] + y_hi_swap(total[1].astype(BF16)).astype(F32)
+    wout = dot(hidden_full, grad_conv, 0, 0).astype(BF16)
+    crossed, wout = tie(y_hi_swap(total[1].astype(BF16)), wout)
+    wout = lax.psum_scatter(wout, "row", scatter_dimension=0, tiled=True)
+    grad_hid = add([total[0], crossed])
     alive = (pre_chip > 0) & (gain_chip[1] > 0)[None, :]
     grad_pre = jnp.where(alive, grad_hid, 0.0)
     mid_part = jnp.sum(grad_pre * pre_chip, axis=0).reshape(2, 128)
     grad_act = (grad_pre * mid_gain).astype(BF16)
-    grad_act, in_above, in_below = tie(grad_act, in_above, in_below)
     act_near = y_hi_swap(grad_act)
     act_above, act_below = x_shift(grad_act, -1), x_shift(grad_act, 1)
-    in_blocks = [in_here, in_above, in_below, onward(in_above, in_below, core, z_split)]
-    wout = dot(hidden_full, grad_conv, 0, 0).astype(BF16)
-    act_above, wout = tie(act_above, wout)
-    wout = lax.psum_scatter(wout, "row", scatter_dimension=0, tiled=True)
     near_above, near_below = x_shift(act_near, -1), x_shift(act_near, 1)
     act_across = onward(act_above, act_below, core, x_split)
     near_across = onward(near_above, near_below, core, x_split)
@@ -318,11 +324,14 @@
 
     act_beside = [core_swap(block) for block in act]
     act[7], sums = tie(act[7], sums)
-    win = win_partial(place, input_turned, act, act_beside)
-    passed, back = z_split(win[0], 1), z_split(win[1], -1)
+    away, there = win_partial(place, input_turned, act, act_beside, ((2, 0), (0, -1)))
+    passed, back = z_split(away, 1), z_split(there, -1)
+    further, own = win_partial(place, input_turned, act, act_beside, ((0, 1), (0, 0)))
+    passed, own = tie(passed, own)
+    further = z_split(add([further, passed]).astype(BF16), 1)
     grad_x = out_gradient(place, cotangent, act, act_beside, in_blocks)
-    passed, grad_x = tie(passed, grad_x)
-    total = add([win[3], back, z_split(add([win[2], passed]).astype(BF16), 1)])
+    further, grad_x = tie(further, grad_x)
+    total = add([own, back, further])
     grad_win = add([total[0], y_lo_swap(total[1].astype(BF16))]) * scaling
     grad_wout = wout.astype(F32) * scaling
     grad_smid = keep_mid.astype(F32) * scaling * sums[0]

time: 215 us -> 210 us (0.977)
  starting transfers between devices: 47.8 us -> 37.6 us
  Pallas kernels: 31.8 us -> 37.1 us
  waiting for transfers between devices: 82.8 us -> 87.2 us
  other arithmetic: 22.7 us -> 19.6 us
    ppermute x42, starting transfers between devices: 47.8 us -> 37.5 us  [permute(): return lax.ppermute(v, AXES, pairs)]
    pallas_call x4 -> x5, Pallas kernels: 31.8 us -> 37.1 us  [call(): pl.pallas_call(body, out_shape=outs, in_specs=[pl.BlockSpec(memory_space=...]
    ppermute x42, waiting for transfers between devices: 82.8 us -> 87.2 us  [permute(): return lax.ppermute(v, AXES, pairs)]
  transfers between devices with their start and end apart: 44 -> 44, of which waited for: 20 -> 23; matrix products, arithmetic and copies ran while one was open for 14% -> 11% of each run, Pallas kernels for 15% -> 18%
where the time goes in v4:
time: 210 us; the launch traced here: 209 us
  waiting for transfers between devices  87.2 us (42%)
  starting transfers between devices  37.6 us (18%)
  Pallas kernels  37.1 us (18%)
  other arithmetic  19.6 us (9%)
  between operations  14.6 us (7%)
  matrix products  7.67 us (4%)
  local copies, waits for them, and re-layouts  5.54 us (3%)
    ppermute x42, waiting for transfers between devices, permute(): return lax.ppermute(v, AXES, pairs)  87.2 us
    ppermute x42, starting transfers between devices, permute(): return lax.ppermute(v, AXES, pairs)  37.5 us
    pallas_call x5, Pallas kernels, call(): pl.pallas_call(body, out_shape=outs, in_specs=[pl.BlockSpec(memory_space=...  37.1 us
    dot_general x1, matrix products, dot(): lax.dot_general(a, b, (((ca,), (cb,)), ((), ())), preferred_element_type=...  7.67 us
  transfers between devices with their start and end apart: 44, of which 23 were waited for; matrix products, arithmetic and copies ran while one was open for 11% of the time, Pallas kernels for 18%

profile of v4, /device:TPU:0, one launch (start us, length us, event | category | flops | bytes accessed | tf_op | source)
XLA Modules:
  0.0 209.2 jit_solution(15915902108914890531)
XLA Ops:
  7.9 1.8 maximum_convert_fusion
  12.2 5.8 %collective-permute-done = bf16[256,512]{1,0:T(8,128)(2,1)S(1)} collective-permute-done((bf16[256,512]{1,0:T(8,128)(2,1)}, bf16[256,512]{1,0:T(8,128)(2,1)S(1)}, u32[]{:S(2)}, u32[]{:S(2)}) %collective-permute-start) | collective-permute-done | bytes 262176 | tf_op jit(solution)/shard_map/ppermute | solution.py:27
  18.1 2.6 %fusion.1 = (f32[512]{0:T(512)S(1)}, bf16[1536,512]{1,0:T(8,128)(2,1)S(1)}) fusion(bf16[1536,512]{1,0:T(8,128)(2,1)} %cot, bf16[1536,512]{1,0:T(8,128)(2,1)} %param.12, f32[512]{0:T(512)S(1)} %convert_multiply_fusion.4), kind=kLoop, calls=%fused_computation.3 | loop fusion | flops 4718080 | bytes 4722688 | tf_op jit(solution)/shard_map/reduce_sum | solution.py:256
  22.8 4.2 %collective-permute-start.1 = (bf16[2,256,512]{2,1,0:T(8,128)(2,1)}, bf16[2,256,512]{2,1,0:T(8,128)(2,1)}, u32[]{:S(2)}, u32[]{:S(2)}) collective-permute-start(bf16[2,256,512]{2,1,0:T(8,128)(2,1)} %pad_maximum_fusion.refs_0_), channel_id=1, source_target_pairs={{0,48},{1,49},{2,50},{3,51},{4,52},{5,53},{6,54},{7,55},{8,56},{9,... | collective-permute-start | bytes 1572872 | tf_op jit(solution)/shard_map/ppermute | solution.py:27
  28.6 10.6 %collective-permute-done.1.refs_1_ = bf16[2,256,512]{2,1,0:T(8,128)(2,1)} collective-permute-done((bf16[2,256,512]{2,1,0:T(8,128)(2,1)}, bf16[2,256,512]{2,1,0:T(8,128)(2,1)}, u32[]{:S(2)}, u32[]{:S(2)}) %collective-permute-start.1) | collective-permute-done | bytes 524320 | tf_op jit(solution)/shard_map/ppermute | solution.py:27
  39.2 3.4 %collective-permute-done.5.refs_2_ = bf16[2,256,512]{2,1,0:T(8,128)(2,1)} collective-permute-done((bf16[2,256,512]{2,1,0:T(8,128)(2,1)}, bf16[2,256,512]{2,1,0:T(8,128)(2,1)}, u32[]{:S(2)}, u32[]{:S(2)}) %collective-permute-start.5) | collective-permute-done | bytes 524320 | tf_op jit(solution)/shard_map/ppermute | solution.py:27
  43.8 10.4 %collective-permute-done.6.refs_3_ = bf16[2,256,512]{2,1,0:T(8,128)(2,1)S(1)} collective-permute-done((bf16[2,256,512]{2,1,0:T(8,128)(2,1)S(1)}, bf16[2,256,512]{2,1,0:T(8,128)(2,1)S(1)}, u32[]{:S(2)}, u32[]{:S(2)}) %collective-permute-start.6) | collective-permute-done | bytes 524320 | tf_op jit(solution)/shard_map/ppermute | solution.py:27
  58.7 6.3 %shard_map.137 = (bf16[2,768,256]{2,1,0:T(8,128)(2,1)}, bf16[2,768,256]{2,1,0:T(8,128)(2,1)}) custom-call(s32[2]{0:T(128)} %pad_add_fusion.here, bf16[768,512]{1,0:T(8,128)(2,1)} %get-tuple-element.79.conv_mine, bf16[768,512]{1,0:T(8,128)(2,1)} %collective-permute-done.2.conv_beside, bf16[2,256,512]{2,1,0:T(8,128)(2,1)} %pad_maximum_fusion.refs_0_, ...), custom_call_target="tpu_custom_call" | custom-call | flops 1610612736 | bytes 7340032 | tf_op jit(solution)/shard_map/pallas_call | solution.py:89
  66.6 3.9 %collective-permute-done.12 = bf16[512,256]{1,0:T(8,128)(2,1)S(1)} collective-permute-done((bf16[512,256]{1,0:T(8,128)(2,1)S(1)}, bf16[512,256]{1,0:T(8,128)(2,1)S(1)}, u32[]{:S(2)}, u32[]{:S(2)}) %collective-permute-start.12) | collective-permute-done | bytes 262176 | tf_op jit(solution)/shard_map/ppermute | solution.py:27
  73.9 2.8 %collective-permute-start.15 = (bf16[2,768,256]{2,1,0:T(8,128)(2,1)}, bf16[2,768,256]{2,1,0:T(8,128)(2,1)}, u32[]{:S(2)}, u32[]{:S(2)}) collective-permute-start(bf16[2,768,256]{2,1,0:T(8,128)(2,1)} %get-tuple-element.54), channel_id=1, source_target_pairs={{0,12},{1,5},{2,14},{3,7},{4,0},{5,9},{6,2},{7,11},{8,4},{9,13},{1... | collective-permute-start | bytes 2359304 | tf_op jit(solution)/shard_map/ppermute | solution.py:27
  76.7 6.3 %shard_map.138 = (bf16[2,768,256]{2,1,0:T(8,128)(2,1)}, bf16[2,768,256]{2,1,0:T(8,128)(2,1)}) custom-call(s32[2]{0:T(128)} %pad_add_fusion.here, bf16[768,512]{1,0:T(8,128)(2,1)} %get-tuple-element.79.conv_mine, bf16[768,512]{1,0:T(8,128)(2,1)} %collective-permute-done.2.conv_beside, bf16[2,256,512]{2,1,0:T(8,128)(2,1)} %pad_maximum_fusion.refs_0_, ...), custom_call_target="tpu_custom_call" | custom-call | flops 1610612736 | bytes 7340032 | tf_op jit(solution)/shard_map/pallas_call | solution.py:89
  83.0 4.7 %collective-permute-done.11 = bf16[2,768,256]{2,1,0:T(8,128)(2,1)S(1)} collective-permute-done((bf16[2,768,256]{2,1,0:T(8,128)(2,1)}, bf16[2,768,256]{2,1,0:T(8,128)(2,1)S(1)}, u32[]{:S(2)}, u32[]{:S(2)}) %collective-permute-start.11) | collective-permute-done | bytes 786464 | tf_op jit(solution)/shard_map/ppermute | solution.py:27
  89.2 1.8 collective-permute-start.16
  93.8 8.7 %collective-permute-done.17.refs_19_ = bf16[2,512,256]{2,1,0:T(8,128)(2,1)S(1)} collective-permute-done((bf16[2,512,256]{2,1,0:T(8,128)(2,1)S(1)}, bf16[2,512,256]{2,1,0:T(8,128)(2,1)S(1)}, u32[]{:S(2)}, u32[]{:S(2)}) %collective-permute-start.17) | collective-permute-done | bytes 524320 | tf_op jit(solution)/shard_map/ppermute | solution.py:27
  103.9 1.9 convert_add_fusion
  106.5 5.9 %collective-permute-start.18 = (bf16[768,256]{1,0:T(8,128)(2,1)}, bf16[768,256]{1,0:T(8,128)(2,1)}, u32[]{:S(2)}, u32[]{:S(2)}) collective-permute-start(bf16[768,256]{1,0:T(8,128)(2,1)} %fusion.8), channel_id=1, source_target_pairs={{0,2},{1,3},{2,0},{3,1},{4,6},{5,7},{6,4},{7,5},{8,10},{9,11},{10,... | collective-permute-start | bytes 1179656 | tf_op jit(solution)/shard_map/ppermute | solution.py:27
  112.4 7.7 %convolution_convert_fusion = bf16[2048,512]{1,0:T(8,128)(2,1)} fusion(bf16[1536,2048]{1,0:T(8,128)(2,1)} %all-gather.2.cloned.1.call-done, bf16[1536,512]{1,0:T(8,128)(2,1)S(1)} %get-tuple-element.82), kind=kOutput, calls=%fused_computation.4 | convolution fusion | flops 3222274048 | bytes 9961472 | tf_op jit(solution)/shard_map/dot_general | solution.py:63
  121.6 2.0 collective-permute-start.19
  123.7 2.4 %collective-permute-start.20 = (bf16[768,256]{1,0:T(8,128)(2,1)S(1)}, bf16[768,256]{1,0:T(8,128)(2,1)S(1)}, u32[]{:S(2)}, u32[]{:S(2)}) collective-permute-start(bf16[768,256]{1,0:T(8,128)(2,1)S(1)} %get-tuple-element.78.refs_0_), channel_id=1, source_target_pairs={{0,12},{1,13},{2,14},{3,15},{4,0},{5,1},{6,2},{7,3},{8,4},{9,5},{1... | collective-permute-start | bytes 1179656 | tf_op jit(solution)/shard_map/ppermute | solution.py:27
  127.4 7.2 %collective-permute-done.19.refs_1_ = bf16[768,256]{1,0:T(8,128)(2,1)S(1)} collective-permute-done((bf16[768,256]{1,0:T(8,128)(2,1)S(1)}, bf16[768,256]{1,0:T(8,128)(2,1)S(1)}, u32[]{:S(2)}, u32[]{:S(2)}) %collective-permute-start.19) | collective-permute-done | bytes 393248 | tf_op jit(solution)/shard_map/ppermute | solution.py:27
  134.6 2.3 %collective-permute-start.21 = (bf16[768,256]{1,0:T(8,128)(2,1)S(1)}, bf16[768,256]{1,0:T(8,128)(2,1)S(1)}, u32[]{:S(2)}, u32[]{:S(2)}) collective-permute-start(bf16[768,256]{1,0:T(8,128)(2,1)S(1)} %collective-permute-done.19.refs_1_), channel_id=1, source_target_pairs={{0,12},{1,13},{2,14},{3,15},{4,0},{5,1},{6,2},{7,3},{8,4},{9,5},{1... | collective-permute-start | bytes 1179656 | tf_op jit(solution)/shard_map/ppermute | solution.py:27
  138.4 8.2 %collective-permute-done.21.refs_3_ = bf16[768,256]{1,0:T(8,128)(2,1)S(1)} collective-permute-done((bf16[768,256]{1,0:T(8,128)(2,1)S(1)}, bf16[768,256]{1,0:T(8,128)(2,1)S(1)}, u32[]{:S(2)}, u32[]{:S(2)}) %collective-permute-start.21) | collective-permute-done | bytes 393248 | tf_op jit(solution)/shard_map/ppermute | solution.py:27
  146.6 1.8 collective-permute-done.23.refs_5_
  150.6 2.1 %collective-permute-done.24.refs_6_ = bf16[768,256]{1,0:T(8,128)(2,1)S(1)} collective-permute-done((bf16[768,256]{1,0:T(8,128)(2,1)S(1)}, bf16[768,256]{1,0:T(8,128)(2,1)S(1)}, u32[]{:S(2)}, u32[]{:S(2)}) %collective-permute-start.24) | collective-permute-done | bytes 393248 | tf_op jit(solution)/shard_map/ppermute | solution.py:27
  153.3 4.3 %collective-permute-done.25.refs_7_ = bf16[768,256]{1,0:T(8,128)(2,1)S(1)} collective-permute-done((bf16[768,256]{1,0:T(8,128)(2,1)S(1)}, bf16[768,256]{1,0:T(8,128)(2,1)S(1)}, u32[]{:S(2)}, u32[]{:S(2)}) %collective-permute-start.25) | collective-permute-done | bytes 393248 | tf_op jit(solution)/shard_map/ppermute | solution.py:27
  159.5 7.0 %shard_map.140 = (bf16[2,512,256]{2,1,0:T(8,128)(2,1)}, bf16[2,512,256]{2,1,0:T(8,128)(2,1)}) custom-call(s32[2]{0:T(128)} %pad_add_fusion.here, bf16[512,1536]{1,0:T(8,128)(2,1)} %bitcast.50, bf16[768,256]{1,0:T(8,128)(2,1)} %copy-done, bf16[768,256]{1,0:T(8,128)(2,1)} %copy-done.5, bf16[768,256]{1,0:T(8,128)(2,1)} %copy-done.1, ...), custom_call_target="tpu_custom_call" | custom-call | flops 1610612736 | bytes 9437184 | tf_op jit(solution)/shard_map/pallas_call | solution.py:89
  166.6 7.0 %shard_map.139 = (bf16[2,512,256]{2,1,0:T(8,128)(2,1)}, bf16[2,512,256]{2,1,0:T(8,128)(2,1)}) custom-call(s32[2]{0:T(128)} %pad_add_fusion.here, bf16[512,1536]{1,0:T(8,128)(2,1)} %bitcast.51, bf16[768,256]{1,0:T(8,128)(2,1)} %copy-done, bf16[768,256]{1,0:T(8,128)(2,1)} %copy-done.5, bf16[768,256]{1,0:T(8,128)(2,1)} %copy-done.1, ...), custom_call_target="tpu_custom_call" | custom-call | flops 1610612736 | bytes 9437184 | tf_op jit(solution)/shard_map/pallas_call | solution.py:89
  173.6 3.6 %collective-permute-done.38 = bf16[2,512,256]{2,1,0:T(8,128)(2,1)S(1)} collective-permute-done((bf16[2,512,256]{2,1,0:T(8,128)(2,1)}, bf16[2,512,256]{2,1,0:T(8,128)(2,1)S(1)}, u32[]{:S(2)}, u32[]{:S(2)}) %collective-permute-start.38) | collective-permute-done | bytes 524320 | tf_op jit(solution)/shard_map/ppermute | solution.py:27
  178.7 3.2 %collective-permute-start.40 = (bf16[2,512,256]{2,1,0:T(8,128)(2,1)S(1)}, bf16[2,512,256]{2,1,0:T(8,128)(2,1)S(1)}, u32[]{:S(2)}, u32[]{:S(2)}) collective-permute-start(bf16[2,512,256]{2,1,0:T(8,128)(2,1)S(1)} %copy-done.27), channel_id=1, source_target_pairs={{0,48},{1,17},{2,50},{3,19},{4,52},{5,21},{6,54},{7,23},{8,56},{9,... | collective-permute-start | bytes 1572872 | tf_op jit(solution)/shard_map/ppermute | solution.py:27
  181.9 10.5 %shard_map.141 = bf16[1536,512]{1,0:T(8,128)(2,1)} custom-call(s32[2]{0:T(128)} %pad_add_fusion.here, bf16[1536,512]{1,0:T(8,128)(2,1)} %cot, bf16[768,256]{1,0:T(8,128)(2,1)} %copy-done, bf16[768,256]{1,0:T(8,128)(2,1)} %copy-done.5, bf16[768,256]{1,0:T(8,128)(2,1)} %copy-done.1, bf16[768,256]{1,0:T(8,128)(2,1)} %copy-done.3, bf16[768,256]{1,0:T(8,128)(2,1)} %copy-done.2, ...), custom_call_target="tpu_custom_call" | custom-call | flops 3221225472 | bytes 12582912 | tf_op jit(solution)/shard_map/pallas_call | solution.py:89
  194.8 4.9 %collective-permute-done.41 = bf16[512,256]{1,0:T(8,128)(2,1)S(1)} collective-permute-done((bf16[512,256]{1,0:T(8,128)(2,1)S(1)}, bf16[512,256]{1,0:T(8,128)(2,1)S(1)}, u32[]{:S(2)}, u32[]{:S(2)}) %collective-permute-start.41) | collective-permute-done | bytes 262176 | tf_op jit(solution)/shard_map/ppermute | solution.py:27
  200.5 1.8 convert_multiply_fusion.3
  (159 shorter events, 37.7 us)
Async XLA Ops:
  7.2 96.7 %all-gather.2.cloned.1.call-start = ((), (), s32[]{:S(2)}) async-start(), calls=%async_computation.1 | async-start | bytes 6684672 | tf_op jit(solution)/shard_map/all_gather | solution.py:245
  9.8 190.8 %reduce-scatter.2.cloned.1.call-start = ((), (), s32[]{:S(2)}) async-start(), calls=%async_computation.2 | async-start | bytes 2359296 | tf_op jit(solution)/shard_map/reduce_scatter | solution.py:302
  9.8 8.3 %collective-permute-start = (bf16[256,512]{1,0:T(8,128)(2,1)}, bf16[256,512]{1,0:T(8,128)(2,1)S(1)}, u32[]{:S(2)}, u32[]{:S(2)}) collective-permute-start(bf16[256,512]{1,0:T(8,128)(2,1)} %param.15), channel_id=1, source_target_pairs={{0,64},{1,65},{2,66},{3,67},{4,68},{5,69},{6,70},{7,71},{8,72},{9,... | collective-permute-start | bytes 786440 | tf_op jit(solution)/shard_map/ppermute | solution.py:27
  21.9 17.2 %collective-permute-start.2 = (bf16[768,512]{1,0:T(8,128)(2,1)}, bf16[768,512]{1,0:T(8,128)(2,1)}, u32[]{:S(2)}, u32[]{:S(2)}) collective-permute-start(bf16[768,512]{1,0:T(8,128)(2,1)} %get-tuple-element.80), channel_id=1, source_target_pairs={{0,1},{1,0},{2,3},{3,2},{4,5},{5,4},{6,7},{7,6},{8,9},{9,8},{10,11... | collective-permute-start | bytes 2359304 | tf_op jit(solution)/shard_map/ppermute | solution.py:27
  22.8 16.4 %collective-permute-start.1 = (bf16[2,256,512]{2,1,0:T(8,128)(2,1)}, bf16[2,256,512]{2,1,0:T(8,128)(2,1)}, u32[]{:S(2)}, u32[]{:S(2)}) collective-permute-start(bf16[2,256,512]{2,1,0:T(8,128)(2,1)} %pad_maximum_fusion.refs_0_), channel_id=1, source_target_pairs={{0,48},{1,49},{2,50},{3,51},{4,52},{5,53},{6,54},{7,55},{8,56},{9,... | collective-permute-start | bytes 1572872 | tf_op jit(solution)/shard_map/ppermute | solution.py:27
  27.0 15.6 %collective-permute-start.5 = (bf16[2,256,512]{2,1,0:T(8,128)(2,1)}, bf16[2,256,512]{2,1,0:T(8,128)(2,1)}, u32[]{:S(2)}, u32[]{:S(2)}) collective-permute-start(bf16[2,256,512]{2,1,0:T(8,128)(2,1)} %pad_maximum_fusion.refs_0_), channel_id=1, source_target_pairs={{0,16},{1,17},{2,18},{3,19},{4,20},{5,21},{6,22},{7,23},{8,24},{9,... | collective-permute-start | bytes 1572872 | tf_op jit(solution)/shard_map/ppermute | solution.py:27
  43.7 10.5 %collective-permute-start.6 = (bf16[2,256,512]{2,1,0:T(8,128)(2,1)S(1)}, bf16[2,256,512]{2,1,0:T(8,128)(2,1)S(1)}, u32[]{:S(2)}, u32[]{:S(2)}) collective-permute-start(bf16[2,256,512]{2,1,0:T(8,128)(2,1)S(1)} %broadcast_select_fusion.1), channel_id=1, source_target_pairs={{0,16},{1,49},{2,18},{3,51},{4,20},{5,53},{6,22},{7,55},{8,24},{9,... | collective-permute-start | bytes 1572872 | tf_op jit(solution)/shard_map/ppermute | solution.py:27
  56.8 13.7 %collective-permute-start.12 = (bf16[512,256]{1,0:T(8,128)(2,1)S(1)}, bf16[512,256]{1,0:T(8,128)(2,1)S(1)}, u32[]{:S(2)}, u32[]{:S(2)}) collective-permute-start(bf16[512,256]{1,0:T(8,128)(2,1)S(1)} %copy-done.21), channel_id=1, source_target_pairs={{0,64},{1,65},{2,66},{3,67},{4,68},{5,69},{6,70},{7,71},{8,72},{9,... | collective-permute-start | bytes 786440 | tf_op jit(solution)/shard_map/ppermute | solution.py:27
  65.0 22.7 %collective-permute-start.11 = (bf16[2,768,256]{2,1,0:T(8,128)(2,1)}, bf16[2,768,256]{2,1,0:T(8,128)(2,1)S(1)}, u32[]{:S(2)}, u32[]{:S(2)}) collective-permute-start(bf16[2,768,256]{2,1,0:T(8,128)(2,1)} %get-tuple-element.49), channel_id=1, source_target_pairs={{0,4},{1,13},{2,6},{3,15},{4,8},{5,1},{6,10},{7,3},{8,12},{9,5},{1... | collective-permute-start | bytes 2359304 | tf_op jit(solution)/shard_map/ppermute | solution.py:27
  70.6 17.1 %collective-permute-start.13 = (bf16[2,512,256]{2,1,0:T(8,128)(2,1)S(1)}, bf16[2,512,256]{2,1,0:T(8,128)(2,1)S(1)}, u32[]{:S(2)}, u32[]{:S(2)}) collective-permute-start(bf16[2,512,256]{2,1,0:T(8,128)(2,1)S(1)} %pad_maximum_fusion.1.refs_16_), channel_id=1, source_target_pairs={{0,48},{1,49},{2,50},{3,51},{4,52},{5,53},{6,54},{7,55},{8,56},{9,... | collective-permute-start | bytes 1572872 | tf_op jit(solution)/shard_map/ppermute | solution.py:27
  70.9 16.7 %collective-permute-start.14 = (bf16[2,512,256]{2,1,0:T(8,128)(2,1)S(1)}, bf16[2,512,256]{2,1,0:T(8,128)(2,1)}, u32[]{:S(2)}, u32[]{:S(2)}) collective-permute-start(bf16[2,512,256]{2,1,0:T(8,128)(2,1)S(1)} %pad_maximum_fusion.1.refs_16_), channel_id=1, source_target_pairs={{0,16},{1,17},{2,18},{3,19},{4,20},{5,21},{6,22},{7,23},{8,24},{9,... | collective-permute-start | bytes 1572872 | tf_op jit(solution)/shard_map/ppermute | solution.py:27
  73.9 29.9 %collective-permute-start.15 = (bf16[2,768,256]{2,1,0:T(8,128)(2,1)}, bf16[2,768,256]{2,1,0:T(8,128)(2,1)}, u32[]{:S(2)}, u32[]{:S(2)}) collective-permute-start(bf16[2,768,256]{2,1,0:T(8,128)(2,1)} %get-tuple-element.54), channel_id=1, source_target_pairs={{0,12},{1,5},{2,14},{3,7},{4,0},{5,9},{6,2},{7,11},{8,4},{9,13},{1... | collective-permute-start | bytes 2359304 | tf_op jit(solution)/shard_map/ppermute | solution.py:27
  89.2 14.6 %collective-permute-start.16 = (bf16[2,768,256]{2,1,0:T(8,128)(2,1)S(1)}, bf16[2,768,256]{2,1,0:T(8,128)(2,1)}, u32[]{:S(2)}, u32[]{:S(2)}) collective-permute-start(bf16[2,768,256]{2,1,0:T(8,128)(2,1)S(1)} %add_convert_fusion), channel_id=1, source_target_pairs={{0,4},{1,13},{2,6},{3,15},{4,8},{5,1},{6,10},{7,3},{8,12},{9,5},{1... | collective-permute-start | bytes 2359304 | tf_op jit(solution)/shard_map/ppermute | solution.py:27
  92.1 10.5 %collective-permute-start.17 = (bf16[2,512,256]{2,1,0:T(8,128)(2,1)S(1)}, bf16[2,512,256]{2,1,0:T(8,128)(2,1)S(1)}, u32[]{:S(2)}, u32[]{:S(2)}) collective-permute-start(bf16[2,512,256]{2,1,0:T(8,128)(2,1)S(1)} %broadcast_select_fusion), channel_id=1, source_target_pairs={{0,16},{1,49},{2,18},{3,51},{4,20},{5,53},{6,22},{7,55},{8,24},{9,... | collective-permute-start | bytes 1572872 | tf_op jit(solution)/shard_map/ppermute | solution.py:27
  106.5 13.6 %collective-permute-start.18 = (bf16[768,256]{1,0:T(8,128)(2,1)}, bf16[768,256]{1,0:T(8,128)(2,1)}, u32[]{:S(2)}, u32[]{:S(2)}) collective-permute-start(bf16[768,256]{1,0:T(8,128)(2,1)} %fusion.8), channel_id=1, source_target_pairs={{0,2},{1,3},{2,0},{3,1},{4,6},{5,7},{6,4},{7,5},{8,10},{9,11},{10,... | collective-permute-start | bytes 1179656 | tf_op jit(solution)/shard_map/ppermute | solution.py:27
  121.6 13.0 %collective-permute-start.19 = (bf16[768,256]{1,0:T(8,128)(2,1)S(1)}, bf16[768,256]{1,0:T(8,128)(2,1)S(1)}, u32[]{:S(2)}, u32[]{:S(2)}) collective-permute-start(bf16[768,256]{1,0:T(8,128)(2,1)S(1)} %get-tuple-element.78.refs_0_), channel_id=1, source_target_pairs={{0,2},{1,3},{2,0},{3,1},{4,6},{5,7},{6,4},{7,5},{8,10},{9,11},{10,... | collective-permute-start | bytes 1179656 | tf_op jit(solution)/shard_map/ppermute | solution.py:27
  123.7 13.2 %collective-permute-start.20 = (bf16[768,256]{1,0:T(8,128)(2,1)S(1)}, bf16[768,256]{1,0:T(8,128)(2,1)S(1)}, u32[]{:S(2)}, u32[]{:S(2)}) collective-permute-start(bf16[768,256]{1,0:T(8,128)(2,1)S(1)} %get-tuple-element.78.refs_0_), channel_id=1, source_target_pairs={{0,12},{1,13},{2,14},{3,15},{4,0},{5,1},{6,2},{7,3},{8,4},{9,5},{1... | collective-permute-start | bytes 1179656 | tf_op jit(solution)/shard_map/ppermute | solution.py:27
  126.0 12.1 %collective-permute-start.22 = (bf16[768,256]{1,0:T(8,128)(2,1)S(1)}, bf16[768,256]{1,0:T(8,128)(2,1)S(1)}, u32[]{:S(2)}, u32[]{:S(2)}) collective-permute-start(bf16[768,256]{1,0:T(8,128)(2,1)S(1)} %get-tuple-element.78.refs_0_), channel_id=1, source_target_pairs={{0,4},{1,5},{2,6},{3,7},{4,8},{5,9},{6,10},{7,11},{8,12},{9,13},{1... | collective-permute-start | bytes 1179656 | tf_op jit(solution)/shard_map/ppermute | solution.py:27
  127.3 9.6 %collective-permute-start.28 = (f32[5,128]{1,0:T(8,128)S(1)}, f32[5,128]{1,0:T(8,128)S(1)}, u32[]{:S(2)}, u32[]{:S(2)}) collective-permute-start(f32[5,128]{1,0:T(8,128)S(1)} %fusion.15), channel_id=1, source_target_pairs={{0,32},{1,33},{2,34},{3,35},{4,36},{5,37},{6,38},{7,39},{8,40},{9,... | collective-permute-start | bytes 7688 | tf_op jit(solution)/shard_map/ppermute | solution.py:27
  127.3 21.5 %collective-permute-start.30 = (bf16[768,256]{1,0:T(8,128)(2,1)S(1)}, bf16[768,256]{1,0:T(8,128)(2,1)S(1)}, u32[]{:S(2)}, u32[]{:S(2)}) collective-permute-start(bf16[768,256]{1,0:T(8,128)(2,1)S(1)} %get-tuple-element.78.refs_0_), channel_id=1, source_target_pairs={{0,1},{1,0},{2,3},{3,2},{4,5},{5,4},{6,7},{7,6},{8,9},{9,8},{10,11... | collective-permute-start | bytes 1179656 | tf_op jit(solution)/shard_map/ppermute | solution.py:27
  134.6 12.0 %collective-permute-start.21 = (bf16[768,256]{1,0:T(8,128)(2,1)S(1)}, bf16[768,256]{1,0:T(8,128)(2,1)S(1)}, u32[]{:S(2)}, u32[]{:S(2)}) collective-permute-start(bf16[768,256]{1,0:T(8,128)(2,1)S(1)} %collective-permute-done.19.refs_1_), channel_id=1, source_target_pairs={{0,12},{1,13},{2,14},{3,15},{4,0},{5,1},{6,2},{7,3},{8,4},{9,5},{1... | collective-permute-start | bytes 1179656 | tf_op jit(solution)/shard_map/ppermute | solution.py:27
  136.9 11.6 %collective-permute-start.23 = (bf16[768,256]{1,0:T(8,128)(2,1)S(1)}, bf16[768,256]{1,0:T(8,128)(2,1)S(1)}, u32[]{:S(2)}, u32[]{:S(2)}) collective-permute-start(bf16[768,256]{1,0:T(8,128)(2,1)S(1)} %collective-permute-done.19.refs_1_), channel_id=1, source_target_pairs={{0,4},{1,5},{2,6},{3,7},{4,8},{5,9},{6,10},{7,11},{8,12},{9,13},{1... | collective-permute-start | bytes 1179656 | tf_op jit(solution)/shard_map/ppermute | solution.py:27
  136.9 11.6 %collective-permute-start.29 = (f32[5,128]{1,0:T(8,128)S(1)}, f32[5,128]{1,0:T(8,128)S(1)}, u32[]{:S(2)}, u32[]{:S(2)}) collective-permute-start(f32[5,128]{1,0:T(8,128)S(1)} %fusion.19), channel_id=1, source_target_pairs={{0,64},{1,65},{2,66},{3,67},{4,68},{5,69},{6,70},{7,71},{8,72},{9,... | collective-permute-start | bytes 7688 | tf_op jit(solution)/shard_map/ppermute | solution.py:27
  138.2 14.5 %collective-permute-start.24 = (bf16[768,256]{1,0:T(8,128)(2,1)S(1)}, bf16[768,256]{1,0:T(8,128)(2,1)S(1)}, u32[]{:S(2)}, u32[]{:S(2)}) collective-permute-start(bf16[768,256]{1,0:T(8,128)(2,1)S(1)} %broadcast_select_fusion.3), channel_id=1, source_target_pairs={{0,4},{1,13},{2,6},{3,15},{4,8},{5,1},{6,10},{7,3},{8,12},{9,5},{1... | collective-permute-start | bytes 1179656 | tf_op jit(solution)/shard_map/ppermute | solution.py:27
  146.6 6.1 %collective-permute-start.31 = (bf16[768,256]{1,0:T(8,128)(2,1)S(1)}, bf16[768,256]{1,0:T(8,128)(2,1)S(1)}, u32[]{:S(2)}, u32[]{:S(2)}) collective-permute-start(bf16[768,256]{1,0:T(8,128)(2,1)S(1)} %collective-permute-done.19.refs_1_), channel_id=1, source_target_pairs={{0,1},{1,0},{2,3},{3,2},{4,5},{5,4},{6,7},{7,6},{8,9},{9,8},{10,11... | collective-permute-start | bytes 1179656 | tf_op jit(solution)/shard_map/ppermute | solution.py:27
  148.5 9.1 %collective-permute-start.25 = (bf16[768,256]{1,0:T(8,128)(2,1)S(1)}, bf16[768,256]{1,0:T(8,128)(2,1)S(1)}, u32[]{:S(2)}, u32[]{:S(2)}) collective-permute-start(bf16[768,256]{1,0:T(8,128)(2,1)S(1)} %broadcast_select_fusion.2), channel_id=1, source_target_pairs={{0,4},{1,13},{2,6},{3,15},{4,8},{5,1},{6,10},{7,3},{8,12},{9,5},{1... | collective-permute-start | bytes 1179656 | tf_op jit(solution)/shard_map/ppermute | solution.py:27
  148.8 8.8 %collective-permute-start.34 = (bf16[768,256]{1,0:T(8,128)(2,1)S(1)}, bf16[768,256]{1,0:T(8,128)(2,1)S(1)}, u32[]{:S(2)}, u32[]{:S(2)}) collective-permute-start(bf16[768,256]{1,0:T(8,128)(2,1)S(1)} %collective-permute-done.22.refs_4_), channel_id=1, source_target_pairs={{0,1},{1,0},{2,3},{3,2},{4,5},{5,4},{6,7},{7,6},{8,9},{9,8},{10,11... | collective-permute-start | bytes 1179656 | tf_op jit(solution)/shard_map/ppermute | solution.py:27
  152.7 4.9 %collective-permute-start.35 = (bf16[768,256]{1,0:T(8,128)(2,1)S(1)}, bf16[768,256]{1,0:T(8,128)(2,1)S(1)}, u32[]{:S(2)}, u32[]{:S(2)}) collective-permute-start(bf16[768,256]{1,0:T(8,128)(2,1)S(1)} %collective-permute-done.23.refs_5_), channel_id=1, source_target_pairs={{0,1},{1,0},{2,3},{3,2},{4,5},{5,4},{6,7},{7,6},{8,9},{9,8},{10,11... | collective-permute-start | bytes 1179656 | tf_op jit(solution)/shard_map/ppermute | solution.py:27
  166.6 10.7 %collective-permute-start.38 = (bf16[2,512,256]{2,1,0:T(8,128)(2,1)}, bf16[2,512,256]{2,1,0:T(8,128)(2,1)S(1)}, u32[]{:S(2)}, u32[]{:S(2)}) collective-permute-start(bf16[2,512,256]{2,1,0:T(8,128)(2,1)} %get-tuple-element.65), channel_id=1, source_target_pairs={{0,16},{1,49},{2,18},{3,51},{4,20},{5,53},{6,22},{7,55},{8,24},{9,... | collective-permute-start | bytes 1572872 | tf_op jit(solution)/shard_map/ppermute | solution.py:27
  178.4 14.5 %collective-permute-start.39 = (bf16[2,512,256]{2,1,0:T(8,128)(2,1)S(1)}, bf16[2,512,256]{2,1,0:T(8,128)(2,1)S(1)}, u32[]{:S(2)}, u32[]{:S(2)}) collective-permute-start(bf16[2,512,256]{2,1,0:T(8,128)(2,1)S(1)} %add_convert_fusion.1), channel_id=1, source_target_pairs={{0,16},{1,49},{2,18},{3,51},{4,20},{5,53},{6,22},{7,55},{8,24},{9,... | collective-permute-start | bytes 1572872 | tf_op jit(solution)/shard_map/ppermute | solution.py:27
  178.7 14.2 %collective-permute-start.40 = (bf16[2,512,256]{2,1,0:T(8,128)(2,1)S(1)}, bf16[2,512,256]{2,1,0:T(8,128)(2,1)S(1)}, u32[]{:S(2)}, u32[]{:S(2)}) collective-permute-start(bf16[2,512,256]{2,1,0:T(8,128)(2,1)S(1)} %copy-done.27), channel_id=1, source_target_pairs={{0,48},{1,17},{2,50},{3,19},{4,52},{5,21},{6,54},{7,23},{8,56},{9,... | collective-permute-start | bytes 1572872 | tf_op jit(solution)/shard_map/ppermute | solution.py:27
  193.1 6.5 %collective-permute-start.41 = (bf16[512,256]{1,0:T(8,128)(2,1)S(1)}, bf16[512,256]{1,0:T(8,128)(2,1)S(1)}, u32[]{:S(2)}, u32[]{:S(2)}) collective-permute-start(bf16[512,256]{1,0:T(8,128)(2,1)S(1)} %fusion.9), channel_id=1, source_target_pairs={{0,64},{1,65},{2,66},{3,67},{4,68},{5,69},{6,70},{7,71},{8,72},{9,... | collective-permute-start | bytes 786440 | tf_op jit(solution)/shard_map/ppermute | solution.py:27
  (41 other events, 292.2 us)
Sparse Core Ops, SparseCore 0:
  10.3 82.7 all-gather.1
  127.5 43.3 reduce-scatter.1

commit v5 on v2

v5 whole, which is shorter than its diff:
```python
import functools
import math

import jax
import jax.numpy as jnp
from jax import lax
from jax.experimental import pallas as pl
from jax.experimental.pallas import tpu as pltpu
from jax.sharding import PartitionSpec as P

F32 = jnp.float32
BF16 = jnp.bfloat16
AXES = ("row", "col")
STEPS = (0, 1, 3, 2)


def permute(v, target):
    pairs = []
    for row in range(8):
        for col in range(16):
            y_lo, z, x, y_hi, core = target(
                row // 4, row % 4, col // 4, (col // 2) % 2, col % 2
            )
            pairs.append(
                (row * 16 + col, (y_lo * 4 + z % 4) * 16 + (x % 4) * 4 + y_hi * 2 + core)
            )
    return lax.ppermute(v, AXES, pairs)


def core_swap(v):
    return permute(v, lambda yl, z, x, yh, c: (yl, z, x, yh, 1 - c))


def y_hi_swap(v):
    return permute(v, lambda yl, z, x, yh, c: (yl, z, x, 1 - yh, c))


def y_lo_swap(v):
    return permute(v, lambda yl, z, x, yh, c: (1 - yl, z, x, yh, c))


def z_flip(v, mask):
    return permute(v, lambda yl, z, x, yh, c: (yl, z ^ mask, x, yh, c))


def x_shift(v, step):
    return permute(v, lambda yl, z, x, yh, c: (yl, z, x + step, yh, c))


def z_shift(v, step):
    return permute(v, lambda yl, z, x, yh, c: (yl, z + step, x, yh, c))


def x_split(v, way):
    return permute(v, lambda yl, z, x, yh, c: (yl, z, x + way * (1 - 2 * c), yh, c))


def z_split(v, way):
    return permute(v, lambda yl, z, x, yh, c: (yl, z + way * (1 - 2 * c), x, yh, c))


def dot(a, b, ca, cb):
    return lax.dot_general(a, b, (((ca,), (cb,)), ((), ())), preferred_element_type=F32)


def onward(above, below, core, split):
    return split(jnp.where(core == 0, below, above), 1)


def place_of(v):
    row, col = v[0], v[1]
    return row, row >> 2, row & 3, col >> 2, (col >> 1) & 1, col & 1


def slot_of(step):
    step = step & 3
    return jnp.where(step >= 2, 5 - step, step)


def row_slot(block, y_lo, z):
    return slot_of((block & 3) - z) * 2 + ((block >> 2) ^ y_lo)


def hidden_slot(block, x, y_hi):
    return slot_of((block >> 1) - x) * 2 + ((block & 1) ^ y_hi)


def call(body, outs, out_space, scratch, sems, loads, flops, here, vmem_args, any_args):
    vmem = pl.BlockSpec(memory_space=pltpu.VMEM)
    return pl.pallas_call(
        body,
        out_shape=outs,
        in_specs=[pl.BlockSpec(memory_space=pltpu.SMEM)]
        + [vmem] * len(vmem_args)
        + [pl.BlockSpec(memory_space=pl.ANY)] * len(any_args),
        out_specs=[pl.BlockSpec(memory_space=out_space)] * len(outs),
        scratch_shapes=[*scratch, pltpu.SemaphoreType.DMA((sems,))],
        compiler_params=pltpu.CompilerParams(vmem_limit_bytes=60 * 1024 * 1024),
        cost_estimate=pl.CostEstimate(flops=flops, bytes_accessed=loads, transcendentals=0),
    )(here, *vmem_args, *any_args)


def send_out(whole, slots, outs, sems, first):
    copies = [
        pltpu.make_async_copy(whole.at[slot], out, sems.at[first + j])
        for j, (slot, out) in enumerate(zip(slots, outs))
    ]
    for copy in copies:
        copy.start()
    for copy in copies:
        copy.wait()


def hid_copies(own, beside, held, k, sems):
    return [
        pltpu.make_async_copy(own, held.at[k, :, pl.ds(0, 512)], sems.at[2 * k]),
        pltpu.make_async_copy(beside, held.at[k, :, pl.ds(512, 512)], sems.at[2 * k + 1]),
    ]


def hid_dot(conv, weights):
    return lax.dot_general(
        conv, weights, (((1,), (1,)), ((), ())), preferred_element_type=F32
    ).astype(BF16)


def hid_kernel(here, conv, *refs):
    blocks, out, (held, sems) = refs[:14], refs[14], refs[15:]
    copies = [hid_copies(blocks[k], blocks[7 + k], held, k, sems) for k in range(7)]
    for pair in copies:
        for copy in pair:
            copy.start()
    for k, pair in enumerate(copies):
        for copy in pair:
            copy.wait()
        out[k] = hid_dot(conv[...], held[k])


def hid_last_kernel(here, conv, done, own, beside, *refs):
    outs, (held, whole, sems) = refs[:8], refs[8:]
    copies = hid_copies(own, beside, held, 0, sems)
    copies.append(pltpu.make_async_copy(done, whole.at[pl.ds(0, 7)], sems.at[2]))
    for copy in copies:
        copy.start()
    row, y_lo, z, x, y_hi, core = place_of(here)
    ahead = 1 - 2 * core
    copies[0].wait()
    copies[1].wait()
    whole[7] = hid_dot(conv[...], held[0])
    copies[2].wait()
    slots = [
        row_slot(((x + step) & 3) * 2 + (y_hi ^ i), y_lo, z)
        for step in (2, -ahead, ahead, 0)
        for i in range(2)
    ]
    send_out(whole, slots, outs, sems, 3)


def hid_partial(here, conv, blocks, beside):
    part = jax.ShapeDtypeStruct((768, 256), BF16)
    flops = 2 * 768 * 1024 * 256
    (done,) = call(
        hid_kernel, [jax.ShapeDtypeStruct((7, 768, 256), BF16)], pltpu.VMEM,
        [pltpu.VMEM((7, 256, 1024), BF16)], 14, 8 << 20, 7 * flops, here, [conv],
        [*blocks[:7], *beside[:7]],
    )
    return call(
        hid_last_kernel, [part] * 8, pl.ANY,
        [pltpu.VMEM((1, 256, 1024), BF16), pltpu.VMEM((8, 768, 256), BF16)], 11, 6 << 20, flops,
        here, [conv], [done, blocks[7], beside[7]],
    )


def act_copies(own, beside, at, sems, first, core):
    copies = []
    for part, ref in enumerate((own, beside)):
        rows = pl.ds(pl.multiple_of((core ^ part) * 768, 768), 768)
        copies.append(pltpu.make_async_copy(ref, at(rows), sems.at[first + part]))
    return copies


def win_kernel(here, left, *refs):
    blocks, out, (held, sems) = refs[:14], refs[14], refs[15:]
    core = here[1] & 1
    copies = [
        act_copies(
            blocks[k], blocks[7 + k], lambda rows, k=k: held.at[k, rows, :], sems, 2 * k, core
        )
        for k in range(7)
    ]
    for pair in copies:
        for copy in pair:
            copy.start()
    for k, pair in enumerate(copies):
        for copy in pair:
            copy.wait()
        out[k] = jnp.dot(left[...], held[k], preferred_element_type=F32).astype(BF16)


def win_last_kernel(here, left, done, own, beside, *refs):
    outs, (held, whole, sems) = refs[:8], refs[8:]
    row, y_lo, z, x, y_hi, core = place_of(here)
    ahead = 1 - 2 * core
    copies = act_copies(own, beside, lambda rows: held.at[rows, :], sems, 0, core)
    copies.append(pltpu.make_async_copy(done, whole.at[pl.ds(0, 7)], sems.at[2]))
    for copy in copies:
        copy.start()
    copies[0].wait()
    copies[1].wait()
    whole[7] = jnp.dot(left[...], held[...], preferred_element_type=F32).astype(BF16)
    copies[2].wait()
    slots = [
        hidden_slot((y_lo ^ i) * 4 + ((z + step) & 3), x, y_hi)
        for step in (2, -ahead, ahead, 0)
        for i in range(2)
    ]
    send_out(whole, slots, outs, sems, 3)


def win_partial(here, left, blocks, beside):
    part = jax.ShapeDtypeStruct((512, 256), BF16)
    flops = 2 * 512 * 1536 * 256
    (done,) = call(
        win_kernel, [jax.ShapeDtypeStruct((7, 512, 256), BF16)], pltpu.VMEM,
        [pltpu.VMEM((7, 1536, 256), BF16)], 14, 8 << 20, 7 * flops, here, [left],
        [*blocks[:7], *beside[:7]],
    )
    return call(
        win_last_kernel, [part] * 8, pl.ANY,
        [pltpu.VMEM((1536, 256), BF16), pltpu.VMEM((8, 512, 256), BF16)], 11, 6 << 20, flops,
        here, [left], [done, blocks[7], beside[7]],
    )


def out_kernel(held_slots, here, start, *refs):
    blocks, parts, out = refs[:8], refs[8:12], refs[12]
    held, loaded, weights, sems = refs[13:]
    row, y_lo, z, x, y_hi, core = place_of(here)
    copies = [
        pltpu.make_async_copy(ref, loaded.at[pl.ds(k * 2, 2)], sems.at[8 + k])
        for k, ref in enumerate(parts)
    ]
    for k in range(4):
        copies += act_copies(
            blocks[k], blocks[4 + k],
            lambda rows, k=k: held.at[rows, pl.ds(k * 256, 256)], sems, 2 * k, core,
        )
    for copy in copies:
        copy.start()
    for copy in copies:
        copy.wait()
    for k, slot in enumerate(held_slots):
        block = ((x + STEPS[slot // 2]) & 3) * 2 + (y_hi ^ (slot & 1))
        weights[:, k * 256 : k * 256 + 256] = loaded[row_slot(block, y_lo, z)]
    for at in range(0, 1536, 256):
        total = start[at : at + 256, :].astype(F32) + lax.dot_general(
            held[at : at + 256, :], weights[...], (((1,), (1,)), ((), ())),
            preferred_element_type=F32,
        )
        out[at : at + 256, :] = total.astype(out.dtype)


def out_partial(here, start, blocks, beside, weights, slots, kind):
    return call(
        functools.partial(out_kernel, slots), [jax.ShapeDtypeStruct((1536, 512), kind)],
        pltpu.VMEM,
        [
            pltpu.VMEM((1536, 1024), BF16),
            pltpu.VMEM((8, 512, 256), BF16),
            pltpu.VMEM((512, 1024), BF16),
        ],
        12, 10 << 20, 1536 * 512 * 2048, here, [start],
        [*(blocks[k] for k in slots), *(beside[k] for k in slots), *weights],
    )[0]


def tie(*values):
    return lax.optimization_barrier(values)


def add(terms):
    return sum(term.astype(F32) for term in terms)


def local(
    inputs,
    cotangent,
    conv_out,
    pre_act,
    weight_in,
    weight_out,
    scale_mid,
    scale_wide,
    keep_mid,
    keep_wide,
):
    rows = inputs.shape[0]
    half = rows // 2
    scaling = 1.0 / math.sqrt(rows * lax.axis_size("row"))
    row, col = lax.axis_index("row"), lax.axis_index("col")
    y_lo, z = row // 4, row % 4
    x, y_hi, core = col // 4, (col // 2) % 2, col % 2
    place = jnp.stack([row, col]).astype(jnp.int32)

    def mine(v):
        return lax.dynamic_slice_in_dim(v, core * half, half, 0)

    def theirs(v):
        return lax.dynamic_slice_in_dim(v, (1 - core) * half, half, 0)

    mid_gain = scale_mid * keep_mid.astype(F32)
    hidden = jnp.maximum(pre_act.astype(F32) * mid_gain, 0.0).astype(BF16)
    hidden_full = lax.all_gather(hidden, "col", axis=1, tiled=True)
    out_above, out_below = z_shift(weight_out, -1), z_shift(weight_out, 1)
    out_near = y_lo_swap(weight_out)

    wide_gain = scale_wide * keep_wide.astype(F32)
    cot_float = cotangent.astype(F32)
    grad_conv = (cot_float * wide_gain).astype(BF16)
    wide_part = jnp.sum(cot_float * conv_out.astype(F32), axis=0)
    conv_mine = mine(grad_conv)
    conv_sent, input_turned = theirs(grad_conv), inputs.T
    out_near, conv_sent, input_turned, wide_part, pre_act = tie(
        out_near, conv_sent, input_turned, wide_part, pre_act
    )
    near_above, near_below = z_shift(out_near, -1), z_shift(out_near, 1)
    out_across = onward(out_above, out_below, core, z_split)
    conv_both = jnp.concatenate([conv_mine, core_swap(conv_sent)], axis=1)
    near_above, conv_both = tie(near_above, conv_both)
    near_across = onward(near_above, near_below, core, z_split)
    out_blocks = [
        weight_out, out_near, out_above, near_above, out_below, near_below, out_across, near_across
    ]

    gain_pair = jnp.stack([scale_mid, keep_mid.astype(F32)])
    gain_beside = core_swap(gain_pair)
    pre_mine = mine(pre_act)
    pre_beside = core_swap(theirs(pre_act))

    def chip_order(a, b):
        return jnp.concatenate(
            [jnp.where(core == 0, a, b), jnp.where(core == 0, b, a)], axis=1
        )

    pre_chip = chip_order(pre_mine, pre_beside).astype(F32)
    gain_chip = chip_order(gain_pair, gain_beside)
    mid_gain = gain_chip[0] * gain_chip[1]

    out_beside = [core_swap(block) for block in out_blocks]
    out_beside[7], weight_in = tie(out_beside[7], weight_in)
    in_near = y_lo_swap(weight_in)
    sends = hid_partial(place, conv_both, out_blocks, out_beside)
    passed = [x_split(sends[i], 1) for i in (1, 0)]
    back = [x_split(sends[2 + i], -1) for i in (1, 0)]
    passed[0], in_near = tie(passed[0], in_near)
    in_here = jnp.stack([weight_in, in_near])
    in_above, in_below = z_shift(in_here, -1), z_shift(in_here, 1)
    far = x_split(add([sends[5], passed[0]]).astype(BF16), 1)
    near = x_split(add([sends[4], passed[1]]).astype(BF16), 1)
    far, in_above, in_below = tie(far, in_above, in_below)
    in_across = onward(in_above, in_below, core, z_split)
    crossed = y_hi_swap(add([sends[7], back[0], far]).astype(BF16))
    near, hidden_full = tie(near, hidden_full)
    total = add([sends[6], back[1], near])
    wout = dot(hidden_full, grad_conv, 0, 0).astype(BF16)
    crossed, wout, in_across = tie(crossed, wout, in_across)
    in_blocks = [in_here, in_above, in_below, in_across]
    wout = lax.psum_scatter(wout, "row", scatter_dimension=0, tiled=True)
    grad_hid = add([total, crossed])
    alive = (pre_chip > 0) & (gain_chip[1] > 0)[None, :]
    grad_pre = jnp.where(alive, grad_hid, 0.0)
    mid_part = jnp.sum(grad_pre * pre_chip, axis=0).reshape(2, 128)
    grad_act = (grad_pre * mid_gain).astype(BF16)
    act_near = y_hi_swap(grad_act)
    act_above, act_below = x_shift(grad_act, -1), x_shift(grad_act, 1)
    near_above, near_below = x_shift(act_near, -1), x_shift(act_near, 1)
    act_across = onward(act_above, act_below, core, x_split)
    act = [grad_act, act_near, act_above, near_above, act_below, near_below, act_across]
    act_beside = [core_swap(block) for block in act]
    grad_x = out_partial(place, cotangent, act, act_beside, in_blocks, (0, 1, 2, 4), F32)
    near_above, grad_x = tie(near_above, grad_x)
    act.append(onward(near_above, near_below, core, x_split))
    act_beside.append(core_swap(act[7]))

    mid_own = lax.dynamic_index_in_dim(mid_part, core, 0, keepdims=False)
    mid_away = lax.dynamic_index_in_dim(mid_part, 1 - core, 0, keepdims=False)
    mid_own = mid_own + core_swap(mid_away)
    sums = jnp.concatenate([mid_own, wide_part]).reshape(5, 128)
    sums = sums + z_flip(sums, 1)
    sums = sums + z_flip(sums, 2)
    sums = sums + y_lo_swap(sums)

    act[7], sums = tie(act[7], sums)
    sends = win_partial(place, input_turned, act, act_beside)
    passed = [z_split(sends[i], 1) for i in (1, 0)]
    back = [z_split(sends[2 + i], -1) for i in (1, 0)]
    far = z_split(add([sends[5], passed[0]]).astype(BF16), 1)
    near = z_split(add([sends[4], passed[1]]).astype(BF16), 1)
    grad_x = out_partial(place, grad_x, act, act_beside, in_blocks, (3, 5, 6, 7), BF16)
    far, grad_x, wout = tie(far, grad_x, wout)
    crossed = y_lo_swap(add([sends[7], back[0], far]).astype(BF16))
    grad_win = add([sends[6], back[1], near, crossed]) * scaling
    grad_wout = wout.astype(F32) * scaling
    grad_smid = keep_mid.astype(F32) * scaling * sums[0]
    grad_swide = keep_wide.astype(F32) * scaling * sums[1:].reshape(512)
    return (grad_x, grad_win, grad_wout, grad_smid, grad_swide)


def solution(mesh):
    return jax.shard_map(
        local,
        mesh=mesh,
        in_specs=(
            P("row", "col"),
            P("row", "col"),
            P("row", "col"),
            P("row", "col"),
            P("col", "row"),
            P("row", "col"),
            P("col"),
            P("col"),
            P("col"),
            P("col"),
        ),
        out_specs=(P("row", "col"), P("col", "row"), P("row", "col"), P("col"), P("col")),
        check_vma=False,
    )
```

time: 215 us -> 226 us (1.051)
  Pallas kernels: 31.8 us -> 45.8 us
  waiting for transfers between devices: 82.8 us -> 77.9 us
  local copies, waits for them, and re-layouts: 6.1 us -> 9.82 us
    pallas_call x4 -> x6, Pallas kernels: 31.8 us -> 45.8 us  [call(): pl.pallas_call(body, out_shape=outs, in_specs=[pl.BlockSpec(memory_space=...]
    unnamed x64 -> x87, local copies, waits for them, and re-layouts: 2.53 us -> 8.82 us
    ppermute x42 -> x55, waiting for transfers between devices: 82.8 us -> 77.9 us  [permute(): return lax.ppermute(v, AXES, pairs)]
    ppermute x42 -> x55, starting transfers between devices: 47.8 us -> 48.6 us  [permute(): return lax.ppermute(v, AXES, pairs)]
  transfers between devices with their start and end apart: 44 -> 57, of which waited for: 20 -> 26; matrix products, arithmetic and copies ran while one was open for 14% -> 12% of each run, Pallas kernels for 15% -> 20%
where the time goes in v5:
time: 226 us; the launch traced here: 225 us
  waiting for transfers between devices  77.9 us (34%)
  starting transfers between devices  48.7 us (22%)
  Pallas kernels  45.8 us (20%)
  other arithmetic  20.8 us (9%)
  between operations  14.7 us (7%)
  local copies, waits for them, and re-layouts  9.82 us (4%)
  matrix products  7.67 us (3%)
    ppermute x55, waiting for transfers between devices, permute(): return lax.ppermute(v, AXES, pairs)  77.9 us
    ppermute x55, starting transfers between devices, permute(): return lax.ppermute(v, AXES, pairs)  48.6 us
    pallas_call x6, Pallas kernels, call(): pl.pallas_call(body, out_shape=outs, in_specs=[pl.BlockSpec(memory_space=...  45.8 us
    unnamed x87, local copies, waits for them, and re-layouts  8.82 us
    dot_general x1, matrix products, dot(): lax.dot_general(a, b, (((ca,), (cb,)), ((), ())), preferred_element_type=...  7.67 us
  transfers between devices with their start and end apart: 57, of which 26 were waited for; matrix products, arithmetic and copies ran while one was open for 12% of the time, Pallas kernels for 20%

profile of v5, /device:TPU:0, one launch (start us, length us, event | category | flops | bytes accessed | tf_op | source)
XLA Modules:
  0.0 225.4 jit_solution(11333470388519823442)
XLA Ops:
  12.2 2.7 %fusion.1 = (f32[512]{0:T(512)S(1)}, bf16[1536,512]{1,0:T(8,128)(2,1)S(1)}) fusion(bf16[1536,512]{1,0:T(8,128)(2,1)} %start.1, bf16[1536,512]{1,0:T(8,128)(2,1)} %param.12, f32[512]{0:T(512)S(1)} %convert_multiply_fusion.4), kind=kLoop, calls=%fused_computation.3 | loop fusion | flops 4718080 | bytes 4722688 | tf_op jit(solution)/shard_map/reduce_sum | solution.py:320
  18.8 4.2 %collective-permute-start.5 = (bf16[256,512]{1,0:T(8,128)(2,1)}, bf16[256,512]{1,0:T(8,128)(2,1)S(1)}, u32[]{:S(2)}, u32[]{:S(2)}) collective-permute-start(bf16[256,512]{1,0:T(8,128)(2,1)} %refs_0_.1), channel_id=1, source_target_pairs={{0,48},{1,49},{2,50},{3,51},{4,52},{5,53},{6,54},{7,55},{8,56},{9,... | collective-permute-start | bytes 786440 | tf_op jit(solution)/shard_map/ppermute | solution.py:27
  23.0 3.2 %collective-permute-start.3 = (bf16[256,512]{1,0:T(8,128)(2,1)}, bf16[256,512]{1,0:T(8,128)(2,1)}, u32[]{:S(2)}, u32[]{:S(2)}) collective-permute-start(bf16[256,512]{1,0:T(8,128)(2,1)} %copy-done.34), channel_id=1, source_target_pairs={{0,48},{1,49},{2,50},{3,51},{4,52},{5,53},{6,54},{7,55},{8,56},{9,... | collective-permute-start | bytes 786440 | tf_op jit(solution)/shard_map/ppermute | solution.py:27
  26.2 3.7 %collective-permute-done.5.refs_2_ = bf16[256,512]{1,0:T(8,128)(2,1)S(1)} collective-permute-done((bf16[256,512]{1,0:T(8,128)(2,1)}, bf16[256,512]{1,0:T(8,128)(2,1)S(1)}, u32[]{:S(2)}, u32[]{:S(2)}) %collective-permute-start.5) | collective-permute-done | bytes 262176 | tf_op jit(solution)/shard_map/ppermute | solution.py:27
  30.2 2.7 %collective-permute-done.6.refs_4_ = bf16[256,512]{1,0:T(8,128)(2,1)} collective-permute-done((bf16[256,512]{1,0:T(8,128)(2,1)}, bf16[256,512]{1,0:T(8,128)(2,1)}, u32[]{:S(2)}, u32[]{:S(2)}) %collective-permute-start.6) | collective-permute-done | bytes 262176 | tf_op jit(solution)/shard_map/ppermute | solution.py:27
  35.7 2.6 %collective-permute-start.11 = (bf16[256,512]{1,0:T(8,128)(2,1)S(1)}, bf16[256,512]{1,0:T(8,128)(2,1)S(1)}, u32[]{:S(2)}, u32[]{:S(2)}) collective-permute-start(bf16[256,512]{1,0:T(8,128)(2,1)S(1)} %collective-permute-done.5.refs_2_), channel_id=1, source_target_pairs={{0,1},{1,0},{2,3},{3,2},{4,5},{5,4},{6,7},{7,6},{8,9},{9,8},{10,11... | collective-permute-start | bytes 786440 | tf_op jit(solution)/shard_map/ppermute | solution.py:27
  40.8 2.5 %collective-permute-done.8.refs_6_ = bf16[256,512]{1,0:T(8,128)(2,1)} collective-permute-done((bf16[256,512]{1,0:T(8,128)(2,1)S(1)}, bf16[256,512]{1,0:T(8,128)(2,1)}, u32[]{:S(2)}, u32[]{:S(2)}) %collective-permute-start.8) | collective-permute-done | bytes 262176 | tf_op jit(solution)/shard_map/ppermute | solution.py:27
  45.9 2.5 %collective-permute-done.16.own = bf16[256,512]{1,0:T(8,128)(2,1)S(1)} collective-permute-done((bf16[256,512]{1,0:T(8,128)(2,1)S(1)}, bf16[256,512]{1,0:T(8,128)(2,1)S(1)}, u32[]{:S(2)}, u32[]{:S(2)}) %collective-permute-start.16) | collective-permute-done | bytes 262176 | tf_op jit(solution)/shard_map/ppermute | solution.py:27
  50.0 10.7 %shard_map.137.done = bf16[7,768,256]{2,1,0:T(8,128)(2,1)} custom-call(s32[2]{0:T(128)} %pad_add_fusion.here, bf16[768,1024]{1,0:T(8,128)(2,1)} %pad_maximum_fusion.conv, bf16[256,512]{1,0:T(8,128)(2,1)} %refs_0_.1, bf16[256,512]{1,0:T(8,128)(2,1)} %copy-done.34, bf16[256,512]{1,0:T(8,128)(2,1)} %copy-done.28, ...), custom_call_target="tpu_custom_call" | custom-call | flops 2818572288 | bytes 8388608 | tf_op jit(solution)/shard_map/pallas_call | solution.py:90
  61.5 5.1 %shard_map.138 = (bf16[768,256]{1,0:T(8,128)(2,1)}, bf16[768,256]{1,0:T(8,128)(2,1)}, bf16[768,256]{1,0:T(8,128)(2,1)}, bf16[768,256]{1,0:T(8,128)(2,1)}, bf16[7...) custom-call(s32[2]{0:T(128)} %pad_add_fusion.here, ...), custom_call_target="tpu_custom_call" | custom-call | flops 402653184 | bytes 6291456 | tf_op jit(solution)/shard_map/pallas_call | solution.py:90
  71.8 5.2 %collective-permute-done.23 = bf16[512,256]{1,0:T(8,128)(2,1)S(1)} collective-permute-done((bf16[512,256]{1,0:T(8,128)(2,1)S(1)}, bf16[512,256]{1,0:T(8,128)(2,1)S(1)}, u32[]{:S(2)}, u32[]{:S(2)}) %collective-permute-start.23) | collective-permute-done | bytes 262176 | tf_op jit(solution)/shard_map/ppermute | solution.py:27
  77.0 8.2 %collective-permute-done.22 = bf16[768,256]{1,0:T(8,128)(2,1)S(1)} collective-permute-done((bf16[768,256]{1,0:T(8,128)(2,1)}, bf16[768,256]{1,0:T(8,128)(2,1)S(1)}, u32[]{:S(2)}, u32[]{:S(2)}) %collective-permute-start.22) | collective-permute-done | bytes 393248 | tf_op jit(solution)/shard_map/ppermute | solution.py:27
  85.4 2.0 collective-permute-start.26
  89.0 2.2 collective-permute-done.19
  91.3 6.3 %collective-permute-done.24 = bf16[768,256]{1,0:T(8,128)(2,1)S(1)} collective-permute-done((bf16[768,256]{1,0:T(8,128)(2,1)S(1)}, bf16[768,256]{1,0:T(8,128)(2,1)S(1)}, u32[]{:S(2)}, u32[]{:S(2)}) %collective-permute-start.24) | collective-permute-done | bytes 393248 | tf_op jit(solution)/shard_map/ppermute | solution.py:27
  98.5 3.4 %collective-permute-start.27 = (bf16[768,256]{1,0:T(8,128)(2,1)S(1)}, bf16[768,256]{1,0:T(8,128)(2,1)}, u32[]{:S(2)}, u32[]{:S(2)}) collective-permute-start(bf16[768,256]{1,0:T(8,128)(2,1)S(1)} %add_convert_fusion), channel_id=1, source_target_pairs={{0,2},{1,3},{2,0},{3,1},{4,6},{5,7},{6,4},{7,5},{8,10},{9,11},{10,... | collective-permute-start | bytes 1179656 | tf_op jit(solution)/shard_map/ppermute | solution.py:27
  102.7 3.9 %collective-permute-done.20 = bf16[768,256]{1,0:T(8,128)(2,1)} collective-permute-done((bf16[768,256]{1,0:T(8,128)(2,1)S(1)}, bf16[768,256]{1,0:T(8,128)(2,1)}, u32[]{:S(2)}, u32[]{:S(2)}) %collective-permute-start.20) | collective-permute-done | bytes 393248 | tf_op jit(solution)/shard_map/ppermute | solution.py:27
  106.7 7.7 %convolution_convert_fusion = bf16[2048,512]{1,0:T(8,128)(2,1)} fusion(bf16[1536,2048]{1,0:T(8,128)(2,1)} %all-gather.2.cloned.1.call-done, bf16[1536,512]{1,0:T(8,128)(2,1)S(1)} %get-tuple-element.96), kind=kOutput, calls=%fused_computation.4 | convolution fusion | flops 3222274048 | bytes 9961472 | tf_op jit(solution)/shard_map/dot_general | solution.py:63
  117.3 6.3 %collective-permute-done.18 = bf16[768,256]{1,0:T(8,128)(2,1)S(1)} collective-permute-done((bf16[768,256]{1,0:T(8,128)(2,1)S(1)}, bf16[768,256]{1,0:T(8,128)(2,1)S(1)}, u32[]{:S(2)}, u32[]{:S(2)}) %collective-permute-start.18) | collective-permute-done | bytes 393248 | tf_op jit(solution)/shard_map/ppermute | solution.py:27
  125.3 2.1 collective-permute-start.29
  129.4 17.0 %collective-permute-done.29.refs_1_ = bf16[768,256]{1,0:T(8,128)(2,1)S(1)} collective-permute-done((bf16[768,256]{1,0:T(8,128)(2,1)S(1)}, bf16[768,256]{1,0:T(8,128)(2,1)S(1)}, u32[]{:S(2)}, u32[]{:S(2)}) %collective-permute-start.29) | collective-permute-done | bytes 393248 | tf_op jit(solution)/shard_map/ppermute | solution.py:27
  150.8 7.7 %shard_map.140.start = f32[1536,512]{1,0:T(8,128)} custom-call(s32[2]{0:T(128)} %pad_add_fusion.here, bf16[1536,512]{1,0:T(8,128)(2,1)} %start.1, bf16[768,256]{1,0:T(8,128)(2,1)} %copy-done.10, bf16[768,256]{1,0:T(8,128)(2,1)} %copy-done.13, bf16[768,256]{1,0:T(8,128)(2,1)} %copy-done.7, bf16[768,256]{1,0:T(8,128)(2,1)} %copy-done.8, ...), custom_call_target="tpu_custom_call" | custom-call | flops 1610612736 | bytes 10485760 | tf_op jit(solution)/shard_map/pallas_call | solution.py:90
  161.3 2.7 %collective-permute-done.34.refs_6_.refs_2_ = bf16[768,256]{1,0:T(8,128)(2,1)S(1)} collective-permute-done((bf16[768,256]{1,0:T(8,128)(2,1)}, bf16[768,256]{1,0:T(8,128)(2,1)S(1)}, u32[]{:S(2)}, u32[]{:S(2)}) %collective-permute-start.34) | collective-permute-done | bytes 393248 | tf_op jit(solution)/shard_map/ppermute | solution.py:27
  164.4 2.4 %collective-permute-start.45 = (f32[5,128]{1,0:T(8,128)S(1)}, f32[5,128]{1,0:T(8,128)S(1)}, u32[]{:S(2)}, u32[]{:S(2)}) collective-permute-start(f32[5,128]{1,0:T(8,128)S(1)} %fusion.9), channel_id=1, source_target_pairs={{0,32},{1,33},{2,34},{3,35},{4,36},{5,37},{6,38},{7,39},{8,40},{9,... | collective-permute-start | bytes 7688 | tf_op jit(solution)/shard_map/ppermute | solution.py:27
  166.7 2.5 %collective-permute-done.42.own.refs_3_ = bf16[768,256]{1,0:T(8,128)(2,1)S(1)} collective-permute-done((bf16[768,256]{1,0:T(8,128)(2,1)S(1)}, bf16[768,256]{1,0:T(8,128)(2,1)S(1)}, u32[]{:S(2)}, u32[]{:S(2)}) %collective-permute-start.42) | collective-permute-done | bytes 393248 | tf_op jit(solution)/shard_map/ppermute | solution.py:27
  169.5 2.0 collective-permute-start.46
  174.8 10.3 %shard_map.139.done = bf16[7,512,256]{2,1,0:T(8,128)(2,1)} custom-call(s32[2]{0:T(128)} %pad_add_fusion.here, bf16[512,1536]{1,0:T(8,128)(2,1)} %bitcast.28, bf16[768,256]{1,0:T(8,128)(2,1)} %copy-done.10, bf16[768,256]{1,0:T(8,128)(2,1)} %copy-done.13, bf16[768,256]{1,0:T(8,128)(2,1)} %copy-done.7, bf16[768,256]{1,0:T(8,128)(2,1)} %copy-done.6, ...), custom_call_target="tpu_custom_call" | custom-call | flops 2818572288 | bytes 8388608 | tf_op jit(solution)/shard_map/pallas_call | solution.py:90
  185.9 4.6 %shard_map.141 = (bf16[512,256]{1,0:T(8,128)(2,1)}, bf16[512,256]{1,0:T(8,128)(2,1)}, bf16[512,256]{1,0:T(8,128)(2,1)}, bf16[512,256]{1,0:T(8,128)(2,1)}, bf16[5...) custom-call(s32[2]{0:T(128)} %pad_add_fusion.here, ...), custom_call_target="tpu_custom_call" | custom-call | flops 402653184 | bytes 6291456 | tf_op jit(solution)/shard_map/pallas_call | solution.py:90
  191.6 2.8 %collective-permute-start.53 = (bf16[512,256]{1,0:T(8,128)(2,1)}, bf16[512,256]{1,0:T(8,128)(2,1)S(1)}, u32[]{:S(2)}, u32[]{:S(2)}) collective-permute-start(bf16[512,256]{1,0:T(8,128)(2,1)} %get-tuple-element.85), channel_id=1, source_target_pairs={{0,48},{1,17},{2,50},{3,19},{4,52},{5,21},{6,54},{7,23},{8,56},{9,... | collective-permute-start | bytes 786440 | tf_op jit(solution)/shard_map/ppermute | solution.py:27
  194.4 3.2 %collective-permute-start.50 = (bf16[512,256]{1,0:T(8,128)(2,1)}, bf16[512,256]{1,0:T(8,128)(2,1)S(1)}, u32[]{:S(2)}, u32[]{:S(2)}) collective-permute-start(bf16[512,256]{1,0:T(8,128)(2,1)} %get-tuple-element.81), channel_id=1, source_target_pairs={{0,48},{1,17},{2,50},{3,19},{4,52},{5,21},{6,54},{7,23},{8,56},{9,... | collective-permute-start | bytes 786440 | tf_op jit(solution)/shard_map/ppermute | solution.py:27
  201.0 7.5 %shard_map.142 = bf16[1536,512]{1,0:T(8,128)(2,1)} custom-call(s32[2]{0:T(128)} %pad_add_fusion.here, f32[1536,512]{1,0:T(8,128)} %shard_map.140.start, bf16[768,256]{1,0:T(8,128)(2,1)} %copy-done.6, bf16[768,256]{1,0:T(8,128)(2,1)} %copy-done.9, bf16[768,256]{1,0:T(8,128)(2,1)} %copy-done.16, bf16[768,256]{1,0:T(8,128)(2,1)} %copy-done.4, ...), custom_call_target="tpu_custom_call" | custom-call | flops 1610612736 | bytes 10485760 | tf_op jit(solution)/shard_map/pallas_call | solution.py:90
  208.6 2.4 %collective-permute-start.52 = (bf16[512,256]{1,0:T(8,128)(2,1)S(1)}, bf16[512,256]{1,0:T(8,128)(2,1)S(1)}, u32[]{:S(2)}, u32[]{:S(2)}) collective-permute-start(bf16[512,256]{1,0:T(8,128)(2,1)S(1)} %add_convert_fusion.4), channel_id=1, source_target_pairs={{0,16},{1,49},{2,18},{3,51},{4,20},{5,53},{6,22},{7,55},{8,24},{9,... | collective-permute-start | bytes 786440 | tf_op jit(solution)/shard_map/ppermute | solution.py:27
  (215 shorter events, 58.4 us)
Async XLA Ops:
  7.2 99.5 %all-gather.2.cloned.1.call-start = ((), (), s32[]{:S(2)}) async-start(), calls=%async_computation.1 | async-start | bytes 6684672 | tf_op jit(solution)/shard_map/all_gather | solution.py:313
  9.8 201.3 %reduce-scatter.2.cloned.1.call-start = ((), (), s32[]{:S(2)}) async-start(), calls=%async_computation.2 | async-start | bytes 2359296 | tf_op jit(solution)/shard_map/reduce_scatter | solution.py:368
  18.8 16.9 %collective-permute-start.4 = (bf16[768,512]{1,0:T(8,128)(2,1)}, bf16[768,512]{1,0:T(8,128)(2,1)S(1)}, u32[]{:S(2)}, u32[]{:S(2)}) collective-permute-start(bf16[768,512]{1,0:T(8,128)(2,1)} %get-tuple-element.50), channel_id=1, source_target_pairs={{0,1},{1,0},{2,3},{3,2},{4,5},{5,4},{6,7},{7,6},{8,9},{9,8},{10,11... | collective-permute-start | bytes 2359304 | tf_op jit(solution)/shard_map/ppermute | solution.py:27
  18.8 11.1 %collective-permute-start.5 = (bf16[256,512]{1,0:T(8,128)(2,1)}, bf16[256,512]{1,0:T(8,128)(2,1)S(1)}, u32[]{:S(2)}, u32[]{:S(2)}) collective-permute-start(bf16[256,512]{1,0:T(8,128)(2,1)} %refs_0_.1), channel_id=1, source_target_pairs={{0,48},{1,49},{2,50},{3,51},{4,52},{5,53},{6,54},{7,55},{8,56},{9,... | collective-permute-start | bytes 786440 | tf_op jit(solution)/shard_map/ppermute | solution.py:27
  23.0 10.0 %collective-permute-start.6 = (bf16[256,512]{1,0:T(8,128)(2,1)}, bf16[256,512]{1,0:T(8,128)(2,1)}, u32[]{:S(2)}, u32[]{:S(2)}) collective-permute-start(bf16[256,512]{1,0:T(8,128)(2,1)} %refs_0_.1), channel_id=1, source_target_pairs={{0,16},{1,17},{2,18},{3,19},{4,20},{5,21},{6,22},{7,23},{8,24},{9,... | collective-permute-start | bytes 786440 | tf_op jit(solution)/shard_map/ppermute | solution.py:27
  23.0 12.2 %collective-permute-start.3 = (bf16[256,512]{1,0:T(8,128)(2,1)}, bf16[256,512]{1,0:T(8,128)(2,1)}, u32[]{:S(2)}, u32[]{:S(2)}) collective-permute-start(bf16[256,512]{1,0:T(8,128)(2,1)} %copy-done.34), channel_id=1, source_target_pairs={{0,48},{1,49},{2,50},{3,51},{4,52},{5,53},{6,54},{7,55},{8,56},{9,... | collective-permute-start | bytes 786440 | tf_op jit(solution)/shard_map/ppermute | solution.py:27
  26.2 14.5 %collective-permute-start.9 = (bf16[256,512]{1,0:T(8,128)(2,1)}, bf16[256,512]{1,0:T(8,128)(2,1)}, u32[]{:S(2)}, u32[]{:S(2)}) collective-permute-start(bf16[256,512]{1,0:T(8,128)(2,1)} %refs_0_.1), channel_id=1, source_target_pairs={{0,1},{1,0},{2,3},{3,2},{4,5},{5,4},{6,7},{7,6},{8,9},{9,8},{10,11... | collective-permute-start | bytes 786440 | tf_op jit(solution)/shard_map/ppermute | solution.py:27
  32.9 10.4 %collective-permute-start.10 = (bf16[256,512]{1,0:T(8,128)(2,1)}, bf16[256,512]{1,0:T(8,128)(2,1)S(1)}, u32[]{:S(2)}, u32[]{:S(2)}) collective-permute-start(bf16[256,512]{1,0:T(8,128)(2,1)} %copy-done.34), channel_id=1, source_target_pairs={{0,1},{1,0},{2,3},{3,2},{4,5},{5,4},{6,7},{7,6},{8,9},{9,8},{10,11... | collective-permute-start | bytes 786440 | tf_op jit(solution)/shard_map/ppermute | solution.py:27
  48.4 12.4 %collective-permute-start.17 = (bf16[256,512]{1,0:T(8,128)(2,1)S(1)}, bf16[256,512]{1,0:T(8,128)(2,1)S(1)}, u32[]{:S(2)}, u32[]{:S(2)}) collective-permute-start(bf16[256,512]{1,0:T(8,128)(2,1)S(1)} %collective-permute-done.16.own), channel_id=1, source_target_pairs={{0,1},{1,0},{2,3},{3,2},{4,5},{5,4},{6,7},{7,6},{8,9},{9,8},{10,11... | collective-permute-start | bytes 786440 | tf_op jit(solution)/shard_map/ppermute | solution.py:27
  66.7 18.6 %collective-permute-start.22 = (bf16[768,256]{1,0:T(8,128)(2,1)}, bf16[768,256]{1,0:T(8,128)(2,1)S(1)}, u32[]{:S(2)}, u32[]{:S(2)}) collective-permute-start(bf16[768,256]{1,0:T(8,128)(2,1)} %get-tuple-element.62), channel_id=1, source_target_pairs={{0,4},{1,13},{2,6},{3,15},{4,8},{5,1},{6,10},{7,3},{8,12},{9,5},{1... | collective-permute-start | bytes 1179656 | tf_op jit(solution)/shard_map/ppermute | solution.py:27
  69.8 28.6 %collective-permute-start.21 = (bf16[768,256]{1,0:T(8,128)(2,1)}, bf16[768,256]{1,0:T(8,128)(2,1)S(1)}, u32[]{:S(2)}, u32[]{:S(2)}) collective-permute-start(bf16[768,256]{1,0:T(8,128)(2,1)} %get-tuple-element.60), channel_id=1, source_target_pairs={{0,12},{1,5},{2,14},{3,7},{4,0},{5,9},{6,2},{7,11},{8,4},{9,13},{1... | collective-permute-start | bytes 1179656 | tf_op jit(solution)/shard_map/ppermute | solution.py:27
  71.5 19.7 %collective-permute-start.19 = (bf16[768,256]{1,0:T(8,128)(2,1)}, bf16[768,256]{1,0:T(8,128)(2,1)S(1)}, u32[]{:S(2)}, u32[]{:S(2)}) collective-permute-start(bf16[768,256]{1,0:T(8,128)(2,1)} %get-tuple-element.57), channel_id=1, source_target_pairs={{0,4},{1,13},{2,6},{3,15},{4,8},{5,1},{6,10},{7,3},{8,12},{9,5},{1... | collective-permute-start | bytes 1179656 | tf_op jit(solution)/shard_map/ppermute | solution.py:27
  85.3 12.3 %collective-permute-start.25 = (bf16[2,512,256]{2,1,0:T(8,128)(2,1)S(1)}, bf16[2,512,256]{2,1,0:T(8,128)(2,1)S(1)}, u32[]{:S(2)}, u32[]{:S(2)}) collective-permute-start(bf16[2,512,256]{2,1,0:T(8,128)(2,1)S(1)} %pad_maximum_fusion.1.refs_8_), channel_id=1, source_target_pairs={{0,48},{1,49},{2,50},{3,51},{4,52},{5,53},{6,54},{7,55},{8,56},{9,... | collective-permute-start | bytes 1572872 | tf_op jit(solution)/shard_map/ppermute | solution.py:27
  85.4 12.9 %collective-permute-start.26 = (bf16[2,512,256]{2,1,0:T(8,128)(2,1)S(1)}, bf16[2,512,256]{2,1,0:T(8,128)(2,1)S(1)}, u32[]{:S(2)}, u32[]{:S(2)}) collective-permute-start(bf16[2,512,256]{2,1,0:T(8,128)(2,1)S(1)} %pad_maximum_fusion.1.refs_8_), channel_id=1, source_target_pairs={{0,16},{1,17},{2,18},{3,19},{4,20},{5,21},{6,22},{7,23},{8,24},{9,... | collective-permute-start | bytes 1572872 | tf_op jit(solution)/shard_map/ppermute | solution.py:27
  91.2 23.2 %collective-permute-start.2 = (f32[2,128]{1,0:T(2,128)S(1)}, f32[2,128]{1,0:T(2,128)}, u32[]{:S(2)}, u32[]{:S(2)}) collective-permute-start(f32[2,128]{1,0:T(2,128)S(1)} %pad_maximum_fusion.4), channel_id=1, source_target_pairs={{0,1},{1,0},{2,3},{3,2},{4,5},{5,4},{6,7},{7,6},{8,9},{9,8},{10,11... | collective-permute-start | bytes 3080 | tf_op jit(solution)/shard_map/ppermute | solution.py:27
  98.5 15.9 %collective-permute-start.27 = (bf16[768,256]{1,0:T(8,128)(2,1)S(1)}, bf16[768,256]{1,0:T(8,128)(2,1)}, u32[]{:S(2)}, u32[]{:S(2)}) collective-permute-start(bf16[768,256]{1,0:T(8,128)(2,1)S(1)} %add_convert_fusion), channel_id=1, source_target_pairs={{0,2},{1,3},{2,0},{3,1},{4,6},{5,7},{6,4},{7,5},{8,10},{9,11},{10,... | collective-permute-start | bytes 1179656 | tf_op jit(solution)/shard_map/ppermute | solution.py:27
  102.7 11.7 %collective-permute-start.28 = (bf16[2,512,256]{2,1,0:T(8,128)(2,1)}, bf16[2,512,256]{2,1,0:T(8,128)(2,1)S(1)}, u32[]{:S(2)}, u32[]{:S(2)}) collective-permute-start(bf16[2,512,256]{2,1,0:T(8,128)(2,1)} %broadcast_select_fusion), channel_id=1, source_target_pairs={{0,16},{1,49},{2,18},{3,51},{4,20},{5,53},{6,22},{7,55},{8,24},{9,... | collective-permute-start | bytes 1572872 | tf_op jit(solution)/shard_map/ppermute | solution.py:27
  125.3 21.2 %collective-permute-start.29 = (bf16[768,256]{1,0:T(8,128)(2,1)S(1)}, bf16[768,256]{1,0:T(8,128)(2,1)S(1)}, u32[]{:S(2)}, u32[]{:S(2)}) collective-permute-start(bf16[768,256]{1,0:T(8,128)(2,1)S(1)} %get-tuple-element.92.refs_0_), channel_id=1, source_target_pairs={{0,2},{1,3},{2,0},{3,1},{4,6},{5,7},{6,4},{7,5},{8,10},{9,11},{10,... | collective-permute-start | bytes 1179656 | tf_op jit(solution)/shard_map/ppermute | solution.py:27
  127.4 19.1 %collective-permute-start.30 = (bf16[768,256]{1,0:T(8,128)(2,1)S(1)}, bf16[768,256]{1,0:T(8,128)(2,1)S(1)}, u32[]{:S(2)}, u32[]{:S(2)}) collective-permute-start(bf16[768,256]{1,0:T(8,128)(2,1)S(1)} %get-tuple-element.92.refs_0_), channel_id=1, source_target_pairs={{0,12},{1,13},{2,14},{3,15},{4,0},{5,1},{6,2},{7,3},{8,4},{9,5},{1... | collective-permute-start | bytes 1179656 | tf_op jit(solution)/shard_map/ppermute | solution.py:27
  128.7 18.3 %collective-permute-start.32 = (bf16[768,256]{1,0:T(8,128)(2,1)S(1)}, bf16[768,256]{1,0:T(8,128)(2,1)S(1)}, u32[]{:S(2)}, u32[]{:S(2)}) collective-permute-start(bf16[768,256]{1,0:T(8,128)(2,1)S(1)} %get-tuple-element.92.refs_0_), channel_id=1, source_target_pairs={{0,4},{1,5},{2,6},{3,7},{4,8},{5,9},{6,10},{7,11},{8,12},{9,13},{1... | collective-permute-start | bytes 1179656 | tf_op jit(solution)/shard_map/ppermute | solution.py:27
  129.4 17.7 %collective-permute-start.35 = (bf16[768,256]{1,0:T(8,128)(2,1)S(1)}, bf16[768,256]{1,0:T(8,128)(2,1)S(1)}, u32[]{:S(2)}, u32[]{:S(2)}) collective-permute-start(bf16[768,256]{1,0:T(8,128)(2,1)S(1)} %get-tuple-element.92.refs_0_), channel_id=1, source_target_pairs={{0,1},{1,0},{2,3},{3,2},{4,5},{5,4},{6,7},{7,6},{8,9},{9,8},{10,11... | collective-permute-start | bytes 1179656 | tf_op jit(solution)/shard_map/ppermute | solution.py:27
  147.1 11.9 %collective-permute-start.31 = (bf16[768,256]{1,0:T(8,128)(2,1)S(1)}, bf16[768,256]{1,0:T(8,128)(2,1)S(1)}, u32[]{:S(2)}, u32[]{:S(2)}) collective-permute-start(bf16[768,256]{1,0:T(8,128)(2,1)S(1)} %collective-permute-done.29.refs_1_), channel_id=1, source_target_pairs={{0,12},{1,13},{2,14},{3,15},{4,0},{5,1},{6,2},{7,3},{8,4},{9,5},{1... | collective-permute-start | bytes 1179656 | tf_op jit(solution)/shard_map/ppermute | solution.py:27
  147.1 12.7 %collective-permute-start.33 = (bf16[768,256]{1,0:T(8,128)(2,1)S(1)}, bf16[768,256]{1,0:T(8,128)(2,1)S(1)}, u32[]{:S(2)}, u32[]{:S(2)}) collective-permute-start(bf16[768,256]{1,0:T(8,128)(2,1)S(1)} %collective-permute-done.29.refs_1_), channel_id=1, source_target_pairs={{0,4},{1,5},{2,6},{3,7},{4,8},{5,9},{6,10},{7,11},{8,12},{9,13},{1... | collective-permute-start | bytes 1179656 | tf_op jit(solution)/shard_map/ppermute | solution.py:27
  149.9 10.7 %collective-permute-start.43 = (f32[128]{0:T(128)S(1)}, f32[128]{0:T(128)S(1)}, u32[]{:S(2)}, u32[]{:S(2)}) collective-permute-start(f32[128]{0:T(128)S(1)} %fusion.8), channel_id=1, source_target_pairs={{0,1},{1,0},{2,3},{3,2},{4,5},{5,4},{6,7},{7,6},{8,9},{9,8},{10,11... | collective-permute-start | bytes 1544 | tf_op jit(solution)/shard_map/ppermute | solution.py:27
  149.9 14.1 %collective-permute-start.34 = (bf16[768,256]{1,0:T(8,128)(2,1)}, bf16[768,256]{1,0:T(8,128)(2,1)S(1)}, u32[]{:S(2)}, u32[]{:S(2)}) collective-permute-start(bf16[768,256]{1,0:T(8,128)(2,1)} %broadcast_select_fusion.2), channel_id=1, source_target_pairs={{0,4},{1,13},{2,6},{3,15},{4,8},{5,1},{6,10},{7,3},{8,12},{9,5},{1... | collective-permute-start | bytes 1179656 | tf_op jit(solution)/shard_map/ppermute | solution.py:27
  160.8 12.4 %collective-permute-start.38 = (bf16[768,256]{1,0:T(8,128)(2,1)S(1)}, bf16[768,256]{1,0:T(8,128)(2,1)S(1)}, u32[]{:S(2)}, u32[]{:S(2)}) collective-permute-start(bf16[768,256]{1,0:T(8,128)(2,1)S(1)} %collective-permute-done.31.refs_3_.refs_0_), channel_id=1, source_target_pairs={{0,1},{1,0},{2,3},{3,2},{4,5},{5,4},{6,7},{7,6},{8,9},{9,8},{10,11... | collective-permute-start | bytes 1179656 | tf_op jit(solution)/shard_map/ppermute | solution.py:27
  160.8 12.3 %collective-permute-start.40 = (bf16[768,256]{1,0:T(8,128)(2,1)S(1)}, bf16[768,256]{1,0:T(8,128)(2,1)S(1)}, u32[]{:S(2)}, u32[]{:S(2)}) collective-permute-start(bf16[768,256]{1,0:T(8,128)(2,1)S(1)} %collective-permute-done.33.refs_5_.refs_1_), channel_id=1, source_target_pairs={{0,1},{1,0},{2,3},{3,2},{4,5},{5,4},{6,7},{7,6},{8,9},{9,8},{10,11... | collective-permute-start | bytes 1179656 | tf_op jit(solution)/shard_map/ppermute | solution.py:27
  169.2 15.9 %collective-permute-start.47 = (bf16[768,256]{1,0:T(8,128)(2,1)S(1)}, bf16[768,256]{1,0:T(8,128)(2,1)S(1)}, u32[]{:S(2)}, u32[]{:S(2)}) collective-permute-start(bf16[768,256]{1,0:T(8,128)(2,1)S(1)} %collective-permute-done.42.own.refs_3_), channel_id=1, source_target_pairs={{0,1},{1,0},{2,3},{3,2},{4,5},{5,4},{6,7},{7,6},{8,9},{9,8},{10,11... | collective-permute-start | bytes 1179656 | tf_op jit(solution)/shard_map/ppermute | solution.py:27
  191.6 19.5 %collective-permute-start.53 = (bf16[512,256]{1,0:T(8,128)(2,1)}, bf16[512,256]{1,0:T(8,128)(2,1)S(1)}, u32[]{:S(2)}, u32[]{:S(2)}) collective-permute-start(bf16[512,256]{1,0:T(8,128)(2,1)} %get-tuple-element.85), channel_id=1, source_target_pairs={{0,48},{1,17},{2,50},{3,19},{4,52},{5,21},{6,54},{7,23},{8,56},{9,... | collective-permute-start | bytes 786440 | tf_op jit(solution)/shard_map/ppermute | solution.py:27
  194.4 14.2 %collective-permute-start.51 = (bf16[512,256]{1,0:T(8,128)(2,1)}, bf16[512,256]{1,0:T(8,128)(2,1)S(1)}, u32[]{:S(2)}, u32[]{:S(2)}) collective-permute-start(bf16[512,256]{1,0:T(8,128)(2,1)} %get-tuple-element.83), channel_id=1, source_target_pairs={{0,16},{1,49},{2,18},{3,51},{4,20},{5,53},{6,22},{7,55},{8,24},{9,... | collective-permute-start | bytes 786440 | tf_op jit(solution)/shard_map/ppermute | solution.py:27
  194.4 20.1 %collective-permute-start.50 = (bf16[512,256]{1,0:T(8,128)(2,1)}, bf16[512,256]{1,0:T(8,128)(2,1)S(1)}, u32[]{:S(2)}, u32[]{:S(2)}) collective-permute-start(bf16[512,256]{1,0:T(8,128)(2,1)} %get-tuple-element.81), channel_id=1, source_target_pairs={{0,48},{1,17},{2,50},{3,19},{4,52},{5,21},{6,54},{7,23},{8,56},{9,... | collective-permute-start | bytes 786440 | tf_op jit(solution)/shard_map/ppermute | solution.py:27
  200.3 10.7 %collective-permute-start.49 = (bf16[512,256]{1,0:T(8,128)(2,1)S(1)}, bf16[512,256]{1,0:T(8,128)(2,1)S(1)}, u32[]{:S(2)}, u32[]{:S(2)}) collective-permute-start(bf16[512,256]{1,0:T(8,128)(2,1)S(1)} %add_convert_fusion.5), channel_id=1, source_target_pairs={{0,16},{1,49},{2,18},{3,51},{4,20},{5,53},{6,22},{7,55},{8,24},{9,... | collective-permute-start | bytes 786440 | tf_op jit(solution)/shard_map/ppermute | solution.py:27
  (68 other events, 506.6 us)
Sparse Core Ops, SparseCore 0:
  10.3 78.6 all-gather.1
  114.6 45.9 reduce-scatter.1

commit v6 on v5

--- a/solution.py
+++ b/solution.py
@@ -100,74 +100,34 @@
     )(here, *vmem_args, *any_args)
 
 
-def send_out(whole, slots, outs, sems, first):
+def hid_kernel(ways, here, conv, *refs):
+    blocks, outs, (held, sems) = refs[:16], refs[16:20], refs[20:]
     copies = [
-        pltpu.make_async_copy(whole.at[slot], out, sems.at[first + j])
-        for j, (slot, out) in enumerate(zip(slots, outs))
+        pltpu.make_async_copy(
+            ref, held.at[k % 8, :, pl.ds((k // 8) * 512, 512)], sems.at[k]
+        )
+        for k, ref in enumerate(blocks)
     ]
-    for copy in copies:
-        copy.start()
-    for copy in copies:
-        copy.wait()
-
-
-def hid_copies(own, beside, held, k, sems):
-    return [
-        pltpu.make_async_copy(own, held.at[k, :, pl.ds(0, 512)], sems.at[2 * k]),
-        pltpu.make_async_copy(beside, held.at[k, :, pl.ds(512, 512)], sems.at[2 * k + 1]),
-    ]
-
-
-def hid_dot(conv, weights):
-    return lax.dot_general(
-        conv, weights, (((1,), (1,)), ((), ())), preferred_element_type=F32
-    ).astype(BF16)
-
-
-def hid_kernel(here, conv, *refs):
-    blocks, out, (held, sems) = refs[:14], refs[14], refs[15:]
-    copies = [hid_copies(blocks[k], blocks[7 + k], held, k, sems) for k in range(7)]
-    for pair in copies:
-        for copy in pair:
-            copy.start()
-    for k, pair in enumerate(copies):
-        for copy in pair:
-            copy.wait()
-        out[k] = hid_dot(conv[...], held[k])
-
-
-def hid_last_kernel(here, conv, done, own, beside, *refs):
-    outs, (held, whole, sems) = refs[:8], refs[8:]
-    copies = hid_copies(own, beside, held, 0, sems)
-    copies.append(pltpu.make_async_copy(done, whole.at[pl.ds(0, 7)], sems.at[2]))
     for copy in copies:
         copy.start()
     row, y_lo, z, x, y_hi, core = place_of(here)
     ahead = 1 - 2 * core
-    copies[0].wait()
-    copies[1].wait()
-    whole[7] = hid_dot(conv[...], held[0])
-    copies[2].wait()
-    slots = [
-        row_slot(((x + step) & 3) * 2 + (y_hi ^ i), y_lo, z)
-        for step in (2, -ahead, ahead, 0)
-        for i in range(2)
-    ]
-    send_out(whole, slots, outs, sems, 3)
-
-
-def hid_partial(here, conv, blocks, beside):
-    part = jax.ShapeDtypeStruct((768, 256), BF16)
-    flops = 2 * 768 * 1024 * 256
-    (done,) = call(
-        hid_kernel, [jax.ShapeDtypeStruct((7, 768, 256), BF16)], pltpu.VMEM,
-        [pltpu.VMEM((7, 256, 1024), BF16)], 14, 8 << 20, 7 * flops, here, [conv],
-        [*blocks[:7], *beside[:7]],
-    )
+    for copy in copies:
+        copy.wait()
+    for j, out in enumerate(outs):
+        fixed, way = ways[j // 2]
+        block = ((x + fixed + way * ahead) & 3) * 2 + (y_hi ^ (j % 2))
+        out[...] = lax.dot_general(
+            conv[...], held[row_slot(block, y_lo, z)], (((1,), (1,)), ((), ())),
+            preferred_element_type=F32,
+        ).astype(BF16)
+
+
+def hid_partial(here, conv, blocks, beside, ways):
     return call(
-        hid_last_kernel, [part] * 8, pl.ANY,
-        [pltpu.VMEM((1, 256, 1024), BF16), pltpu.VMEM((8, 768, 256), BF16)], 11, 6 << 20, flops,
-        here, [conv], [done, blocks[7], beside[7]],
+        functools.partial(hid_kernel, ways), [jax.ShapeDtypeStruct((768, 256), BF16)] * 4,
+        pltpu.VMEM, [pltpu.VMEM((8, 256, 1024), BF16)], 16, 8 << 20, 768 * 1024 * 2048, here,
+        [conv], [*blocks, *beside],
     )
 
 
@@ -180,55 +140,31 @@
 
 
 def win_kernel(here, left, *refs):
-    blocks, out, (held, sems) = refs[:14], refs[14], refs[15:]
-    core = here[1] & 1
-    copies = [
-        act_copies(
-            blocks[k], blocks[7 + k], lambda rows, k=k: held.at[k, rows, :], sems, 2 * k, core
-        )
-        for k in range(7)
-    ]
-    for pair in copies:
-        for copy in pair:
-            copy.start()
-    for k, pair in enumerate(copies):
-        for copy in pair:
-            copy.wait()
-        out[k] = jnp.dot(left[...], held[k], preferred_element_type=F32).astype(BF16)
-
-
-def win_last_kernel(here, left, done, own, beside, *refs):
-    outs, (held, whole, sems) = refs[:8], refs[8:]
+    blocks, outs, (held, sems) = refs[:16], refs[16:24], refs[24:]
     row, y_lo, z, x, y_hi, core = place_of(here)
+    copies = []
+    for k in range(8):
+        copies += act_copies(
+            blocks[k], blocks[8 + k], lambda rows, k=k: held.at[k, rows, :], sems, 2 * k, core
+        )
+    for copy in copies:
+        copy.start()
+    for copy in copies:
+        copy.wait()
     ahead = 1 - 2 * core
-    copies = act_copies(own, beside, lambda rows: held.at[rows, :], sems, 0, core)
-    copies.append(pltpu.make_async_copy(done, whole.at[pl.ds(0, 7)], sems.at[2]))
-    for copy in copies:
-        copy.start()
-    copies[0].wait()
-    copies[1].wait()
-    whole[7] = jnp.dot(left[...], held[...], preferred_element_type=F32).astype(BF16)
-    copies[2].wait()
-    slots = [
-        hidden_slot((y_lo ^ i) * 4 + ((z + step) & 3), x, y_hi)
-        for step in (2, -ahead, ahead, 0)
-        for i in range(2)
-    ]
-    send_out(whole, slots, outs, sems, 3)
+    for j, out in enumerate(outs):
+        step = (2, -ahead, ahead, 0)[j // 2]
+        block = (y_lo ^ (j % 2)) * 4 + ((z + step) & 3)
+        out[...] = jnp.dot(
+            left[...], held[hidden_slot(block, x, y_hi)], preferred_element_type=F32
+        ).astype(BF16)
 
 
 def win_partial(here, left, blocks, beside):
-    part = jax.ShapeDtypeStruct((512, 256), BF16)
-    flops = 2 * 512 * 1536 * 256
-    (done,) = call(
-        win_kernel, [jax.ShapeDtypeStruct((7, 512, 256), BF16)], pltpu.VMEM,
-        [pltpu.VMEM((7, 1536, 256), BF16)], 14, 8 << 20, 7 * flops, here, [left],
-        [*blocks[:7], *beside[:7]],
-    )
     return call(
-        win_last_kernel, [part] * 8, pl.ANY,
-        [pltpu.VMEM((1536, 256), BF16), pltpu.VMEM((8, 512, 256), BF16)], 11, 6 << 20, flops,
-        here, [left], [done, blocks[7], beside[7]],
+        win_kernel, [jax.ShapeDtypeStruct((512, 256), BF16)] * 8, pltpu.VMEM,
+        [pltpu.VMEM((8, 1536, 256), BF16)], 16, 10 << 20, 2 * 512 * 1536 * 2048, here, [left],
+        [*blocks, *beside],
     )
 
 
@@ -326,7 +262,8 @@
     near_above, near_below = z_shift(out_near, -1), z_shift(out_near, 1)
     out_across = onward(out_above, out_below, core, z_split)
     conv_both = jnp.concatenate([conv_mine, core_swap(conv_sent)], axis=1)
-    near_above, conv_both = tie(near_above, conv_both)
+    near_above, conv_both, weight_in = tie(near_above, conv_both, weight_in)
+    in_near = y_lo_swap(weight_in)
     near_across = onward(near_above, near_below, core, z_split)
     out_blocks = [
         weight_out, out_near, out_above, near_above, out_below, near_below, out_across, near_across
@@ -347,25 +284,26 @@
     mid_gain = gain_chip[0] * gain_chip[1]
 
     out_beside = [core_swap(block) for block in out_blocks]
-    out_beside[7], weight_in = tie(out_beside[7], weight_in)
-    in_near = y_lo_swap(weight_in)
-    sends = hid_partial(place, conv_both, out_blocks, out_beside)
-    passed = [x_split(sends[i], 1) for i in (1, 0)]
-    back = [x_split(sends[2 + i], -1) for i in (1, 0)]
-    passed[0], in_near = tie(passed[0], in_near)
+    ways = ((2, 0), (0, 1))
+    first = list(hid_partial(place, conv_both, out_blocks, out_beside, ways))
+    passed = [x_split(first[i], 1) for i in (1, 0)]
+    first[3], in_near = tie(first[3], in_near)
     in_here = jnp.stack([weight_in, in_near])
+    conv_both, in_here = tie(conv_both, in_here)
     in_above, in_below = z_shift(in_here, -1), z_shift(in_here, 1)
-    far = x_split(add([sends[5], passed[0]]).astype(BF16), 1)
-    near = x_split(add([sends[4], passed[1]]).astype(BF16), 1)
+    second = hid_partial(place, conv_both, out_blocks, out_beside, ((0, -1), (0, 0)))
+    passed[0], second = tie(passed[0], second)
+    back = [x_split(second[i], -1) for i in (1, 0)]
+    far = x_split(add([first[3], passed[0]]).astype(BF16), 1)
+    near = x_split(add([first[2], passed[1]]).astype(BF16), 1)
     far, in_above, in_below = tie(far, in_above, in_below)
     in_across = onward(in_above, in_below, core, z_split)
-    crossed = y_hi_swap(add([sends[7], back[0], far]).astype(BF16))
-    near, hidden_full = tie(near, hidden_full)
-    total = add([sends[6], back[1], near])
+    in_blocks = [in_here, in_above, in_below, in_across]
+    crossed = y_hi_swap(add([second[3], back[0], far]).astype(BF16))
+    near, hidden_full, in_blocks[3] = tie(near, hidden_full, in_across)
+    total = add([second[2], back[1], near])
     wout = dot(hidden_full, grad_conv, 0, 0).astype(BF16)
-    crossed, wout, in_across = tie(crossed, wout, in_across)
-    in_blocks = [in_here, in_above, in_below, in_across]
-    wout = lax.psum_scatter(wout, "row", scatter_dimension=0, tiled=True)
+    crossed, wout = tie(crossed, wout)
     grad_hid = add([total, crossed])
     alive = (pre_chip > 0) & (gain_chip[1] > 0)[None, :]
     grad_pre = jnp.where(alive, grad_hid, 0.0)
@@ -373,6 +311,8 @@
     grad_act = (grad_pre * mid_gain).astype(BF16)
     act_near = y_hi_swap(grad_act)
     act_above, act_below = x_shift(grad_act, -1), x_shift(grad_act, 1)
+    act_near, wout = tie(act_near, wout)
+    wout = lax.psum_scatter(wout, "row", scatter_dimension=0, tiled=True)
     near_above, near_below = x_shift(act_near, -1), x_shift(act_near, 1)
     act_across = onward(act_above, act_below, core, x_split)
     act = [grad_act, act_near, act_above, near_above, act_below, near_below, act_across]

time: 226 us -> 216 us (0.956)
  Pallas kernels: 45.8 us -> 36.3 us
  starting transfers between devices: 48.7 us -> 53.9 us
  local copies, waits for them, and re-layouts: 9.82 us -> 7.3 us
    pallas_call x6 -> x5, Pallas kernels: 45.8 us -> 36.3 us  [call(): pl.pallas_call(body, out_shape=outs, in_specs=[pl.BlockSpec(memory_space=...]
    ppermute x55, starting transfers between devices: 48.6 us -> 53.9 us  [permute(): return lax.ppermute(v, AXES, pairs)]
    unnamed x87 -> x89, local copies, waits for them, and re-layouts: 8.82 us -> 6.3 us
  transfers between devices with their start and end apart: 57 -> 57, of which waited for: 26 -> 23; matrix products, arithmetic and copies ran while one was open for 12% -> 11% of each run, Pallas kernels for 20% -> 17%
where the time goes in v6:
time: 216 us
  waiting for transfers between devices  76.2 us (35%)
  starting transfers between devices  53.9 us (25%)
  Pallas kernels  36.3 us (17%)
  other arithmetic  19.2 us (9%)
  between operations  14.8 us (7%)
  matrix products  7.88 us (4%)
  local copies, waits for them, and re-layouts  7.3 us (3%)
    ppermute x55, waiting for transfers between devices, permute(): return lax.ppermute(v, AXES, pairs)  76.2 us
    ppermute x55, starting transfers between devices, permute(): return lax.ppermute(v, AXES, pairs)  53.9 us
    pallas_call x5, Pallas kernels, call(): pl.pallas_call(body, out_shape=outs, in_specs=[pl.BlockSpec(memory_space=...  36.3 us
    dot_general x1, matrix products, dot(): lax.dot_general(a, b, (((ca,), (cb,)), ((), ())), preferred_element_type=...  7.88 us
    unnamed x89, local copies, waits for them, and re-layouts  6.3 us
  transfers between devices with their start and end apart: 57, of which 23 were waited for; matrix products, arithmetic and copies ran while one was open for 11% of the time, Pallas kernels for 17%

profile of v6, /device:TPU:0, one launch (start us, length us, event | category | flops | bytes accessed | tf_op | source)
XLA Modules:
  0.0 215.6 jit_solution(5992565163747264241)
XLA Ops:
  12.3 2.7 %fusion.1 = (f32[512]{0:T(512)S(1)}, bf16[1536,512]{1,0:T(8,128)(2,1)S(1)}) fusion(bf16[1536,512]{1,0:T(8,128)(2,1)} %start.1, bf16[1536,512]{1,0:T(8,128)(2,1)} %param.12, f32[512]{0:T(512)S(1)} %convert_multiply_fusion.4), kind=kLoop, calls=%fused_computation.3 | loop fusion | flops 4718080 | bytes 4722688 | tf_op jit(solution)/shard_map/reduce_sum | solution.py:256
  18.8 4.2 %collective-permute-start.5 = (bf16[256,512]{1,0:T(8,128)(2,1)}, bf16[256,512]{1,0:T(8,128)(2,1)S(1)}, u32[]{:S(2)}, u32[]{:S(2)}) collective-permute-start(bf16[256,512]{1,0:T(8,128)(2,1)} %refs_0_.3), channel_id=1, source_target_pairs={{0,48},{1,49},{2,50},{3,51},{4,52},{5,53},{6,54},{7,55},{8,56},{9,... | collective-permute-start | bytes 786440 | tf_op jit(solution)/shard_map/ppermute | solution.py:27
  23.2 3.0 %collective-permute-start.3 = (bf16[256,512]{1,0:T(8,128)(2,1)}, bf16[256,512]{1,0:T(8,128)(2,1)}, u32[]{:S(2)}, u32[]{:S(2)}) collective-permute-start(bf16[256,512]{1,0:T(8,128)(2,1)} %copy-done.35), channel_id=1, source_target_pairs={{0,48},{1,49},{2,50},{3,51},{4,52},{5,53},{6,54},{7,55},{8,56},{9,... | collective-permute-start | bytes 786440 | tf_op jit(solution)/shard_map/ppermute | solution.py:27
  26.2 3.7 %collective-permute-done.5.refs_2_ = bf16[256,512]{1,0:T(8,128)(2,1)S(1)} collective-permute-done((bf16[256,512]{1,0:T(8,128)(2,1)}, bf16[256,512]{1,0:T(8,128)(2,1)S(1)}, u32[]{:S(2)}, u32[]{:S(2)}) %collective-permute-start.5) | collective-permute-done | bytes 262176 | tf_op jit(solution)/shard_map/ppermute | solution.py:27
  30.3 2.7 %collective-permute-done.6.refs_4_ = bf16[256,512]{1,0:T(8,128)(2,1)} collective-permute-done((bf16[256,512]{1,0:T(8,128)(2,1)}, bf16[256,512]{1,0:T(8,128)(2,1)}, u32[]{:S(2)}, u32[]{:S(2)}) %collective-permute-start.6) | collective-permute-done | bytes 262176 | tf_op jit(solution)/shard_map/ppermute | solution.py:27
  35.6 4.2 %collective-permute-done.7.refs_5_ = bf16[256,512]{1,0:T(8,128)(2,1)} collective-permute-done((bf16[256,512]{1,0:T(8,128)(2,1)}, bf16[256,512]{1,0:T(8,128)(2,1)}, u32[]{:S(2)}, u32[]{:S(2)}) %collective-permute-start.7) | collective-permute-done | bytes 262176 | tf_op jit(solution)/shard_map/ppermute | solution.py:27
  43.1 5.3 %collective-permute-done.9.refs_7_ = bf16[256,512]{1,0:T(8,128)(2,1)S(1)} collective-permute-done((bf16[256,512]{1,0:T(8,128)(2,1)S(1)}, bf16[256,512]{1,0:T(8,128)(2,1)S(1)}, u32[]{:S(2)}, u32[]{:S(2)}) %collective-permute-start.9) | collective-permute-done | bytes 262176 | tf_op jit(solution)/shard_map/ppermute | solution.py:27
  52.0 6.4 %shard_map.137 = (bf16[768,256]{1,0:T(8,128)(2,1)}, bf16[768,256]{1,0:T(8,128)(2,1)}, bf16[768,256]{1,0:T(8,128)(2,1)}, bf16[768,256]{1,0:T(8,128)(2,1)}) custom-call(s32[2]{0:T(128)} %pad_add_fusion.here, bf16[768,1024]{1,0:T(8,128)(2,1)} %pad_maximum_fusion.conv, bf16[256,512]{1,0:T(8,128)(2,1)} %refs_0_.3, bf16[256,512]{1,0:T(8,128)(2,1)} %copy-done.35, ...), custom_call_target="tpu_custom_call" | custom-call | flops 1610612736 | bytes 8388608 | tf_op jit(solution)/shard_map/pallas_call | solution.py:90
  60.0 4.2 %collective-permute-done.19 = bf16[512,256]{1,0:T(8,128)(2,1)S(1)} collective-permute-done((bf16[512,256]{1,0:T(8,128)(2,1)S(1)}, bf16[512,256]{1,0:T(8,128)(2,1)S(1)}, u32[]{:S(2)}, u32[]{:S(2)}) %collective-permute-start.19) | collective-permute-done | bytes 262176 | tf_op jit(solution)/shard_map/ppermute | solution.py:27
  66.3 6.4 %shard_map.138 = (bf16[768,256]{1,0:T(8,128)(2,1)}, bf16[768,256]{1,0:T(8,128)(2,1)}, bf16[768,256]{1,0:T(8,128)(2,1)}, bf16[768,256]{1,0:T(8,128)(2,1)}) custom-call(s32[2]{0:T(128)} %pad_add_fusion.here, bf16[768,1024]{1,0:T(8,128)(2,1)} %pad_maximum_fusion.conv, bf16[256,512]{1,0:T(8,128)(2,1)} %refs_0_.3, bf16[256,512]{1,0:T(8,128)(2,1)} %copy-done.35, ...), custom_call_target="tpu_custom_call" | custom-call | flops 1610612736 | bytes 8388608 | tf_op jit(solution)/shard_map/pallas_call | solution.py:90
  77.5 2.7 %collective-permute-start.27 = (bf16[768,256]{1,0:T(8,128)(2,1)S(1)}, bf16[768,256]{1,0:T(8,128)(2,1)S(1)}, u32[]{:S(2)}, u32[]{:S(2)}) collective-permute-start(bf16[768,256]{1,0:T(8,128)(2,1)S(1)} %copy-done.34), channel_id=1, source_target_pairs={{0,12},{1,5},{2,14},{3,7},{4,0},{5,9},{6,2},{7,11},{8,4},{9,13},{1... | collective-permute-start | bytes 1179656 | tf_op jit(solution)/shard_map/ppermute | solution.py:27
  80.2 10.9 %collective-permute-done.23 = bf16[768,256]{1,0:T(8,128)(2,1)S(1)} collective-permute-done((bf16[768,256]{1,0:T(8,128)(2,1)S(1)}, bf16[768,256]{1,0:T(8,128)(2,1)S(1)}, u32[]{:S(2)}, u32[]{:S(2)}) %collective-permute-start.23) | collective-permute-done | bytes 393248 | tf_op jit(solution)/shard_map/ppermute | solution.py:27
  91.2 1.9 collective-permute-start.26
  93.0 3.8 %collective-permute-done.21 = bf16[768,256]{1,0:T(8,128)(2,1)S(1)} collective-permute-done((bf16[768,256]{1,0:T(8,128)(2,1)}, bf16[768,256]{1,0:T(8,128)(2,1)S(1)}, u32[]{:S(2)}, u32[]{:S(2)}) %collective-permute-start.21) | collective-permute-done | bytes 393248 | tf_op jit(solution)/shard_map/ppermute | solution.py:27
  97.2 3.3 %collective-permute-start.20 = (bf16[768,256]{1,0:T(8,128)(2,1)}, bf16[768,256]{1,0:T(8,128)(2,1)}, u32[]{:S(2)}, u32[]{:S(2)}) collective-permute-start(bf16[768,256]{1,0:T(8,128)(2,1)} %get-tuple-element.71), channel_id=1, source_target_pairs={{0,12},{1,5},{2,14},{3,7},{4,0},{5,9},{6,2},{7,11},{8,4},{9,13},{1... | collective-permute-start | bytes 1179656 | tf_op jit(solution)/shard_map/ppermute | solution.py:27
  100.6 2.1 collective-permute-start.28
  102.7 7.0 %collective-permute-done.22 = bf16[768,256]{1,0:T(8,128)(2,1)S(1)} collective-permute-done((bf16[768,256]{1,0:T(8,128)(2,1)S(1)}, bf16[768,256]{1,0:T(8,128)(2,1)S(1)}, u32[]{:S(2)}, u32[]{:S(2)}) %collective-permute-start.22) | collective-permute-done | bytes 393248 | tf_op jit(solution)/shard_map/ppermute | solution.py:27
  110.5 7.9 %convolution_convert_fusion = bf16[2048,512]{1,0:T(8,128)(2,1)} fusion(bf16[1536,2048]{1,0:T(8,128)(2,1)} %all-gather.2.cloned.1.call-done, bf16[1536,512]{1,0:T(8,128)(2,1)S(1)} %get-tuple-element.112), kind=kOutput, calls=%fused_computation.4 | convolution fusion | flops 3222274048 | bytes 9961472 | tf_op jit(solution)/shard_map/dot_general | solution.py:63
  120.1 2.1 collective-permute-start.29
  122.3 7.2 %collective-permute-done.29.refs_1_ = bf16[768,256]{1,0:T(8,128)(2,1)S(1)} collective-permute-done((bf16[768,256]{1,0:T(8,128)(2,1)S(1)}, bf16[768,256]{1,0:T(8,128)(2,1)S(1)}, u32[]{:S(2)}, u32[]{:S(2)}) %collective-permute-start.29) | collective-permute-done | bytes 393248 | tf_op jit(solution)/shard_map/ppermute | solution.py:27
  129.6 2.0 collective-permute-start.32
  132.1 5.2 %collective-permute-done.30.refs_2_ = bf16[768,256]{1,0:T(8,128)(2,1)S(1)} collective-permute-done((bf16[768,256]{1,0:T(8,128)(2,1)S(1)}, bf16[768,256]{1,0:T(8,128)(2,1)S(1)}, u32[]{:S(2)}, u32[]{:S(2)}) %collective-permute-start.30) | collective-permute-done | bytes 393248 | tf_op jit(solution)/shard_map/ppermute | solution.py:27
  143.1 7.5 %shard_map.139.start = f32[1536,512]{1,0:T(8,128)} custom-call(s32[2]{0:T(128)} %pad_add_fusion.here, bf16[1536,512]{1,0:T(8,128)(2,1)} %start.1, bf16[768,256]{1,0:T(8,128)(2,1)} %copy-done.8, bf16[768,256]{1,0:T(8,128)(2,1)} %copy-done.11, bf16[768,256]{1,0:T(8,128)(2,1)} %copy-done.5, bf16[768,256]{1,0:T(8,128)(2,1)} %copy-done.6, ...), custom_call_target="tpu_custom_call" | custom-call | flops 1610612736 | bytes 10485760 | tf_op jit(solution)/shard_map/pallas_call | solution.py:90
  155.7 4.9 %collective-permute-done.39.refs_7_.refs_3_ = bf16[768,256]{1,0:T(8,128)(2,1)S(1)} collective-permute-done((bf16[768,256]{1,0:T(8,128)(2,1)S(1)}, bf16[768,256]{1,0:T(8,128)(2,1)S(1)}, u32[]{:S(2)}, u32[]{:S(2)}) %collective-permute-start.39) | collective-permute-done | bytes 393248 | tf_op jit(solution)/shard_map/ppermute | solution.py:27
  160.6 3.3 %collective-permute-start.42 = (f32[5,128]{1,0:T(8,128)S(1)}, f32[5,128]{1,0:T(8,128)S(1)}, u32[]{:S(2)}, u32[]{:S(2)}) collective-permute-start(f32[5,128]{1,0:T(8,128)S(1)} %fusion.9), channel_id=1, source_target_pairs={{0,32},{1,33},{2,34},{3,35},{4,36},{5,37},{6,38},{7,39},{8,40},{9,... | collective-permute-start | bytes 7688 | tf_op jit(solution)/shard_map/ppermute | solution.py:27
  163.9 1.9 collective-permute-done.42
  167.0 2.5 %collective-permute-done.43 = f32[5,128]{1,0:T(8,128)S(1)} collective-permute-done((f32[5,128]{1,0:T(8,128)S(1)}, f32[5,128]{1,0:T(8,128)S(1)}, u32[]{:S(2)}, u32[]{:S(2)}) %collective-permute-start.43) | collective-permute-done | bytes 2592 | tf_op jit(solution)/shard_map/ppermute | solution.py:27
  171.3 8.5 %shard_map.140 = (bf16[512,256]{1,0:T(8,128)(2,1)}, bf16[512,256]{1,0:T(8,128)(2,1)}, bf16[512,256]{1,0:T(8,128)(2,1)}, bf16[512,256]{1,0:T(8,128)(2,1)}, bf16[5...) custom-call(s32[2]{0:T(128)} %pad_add_fusion.here, ...), custom_call_target="tpu_custom_call" | custom-call | flops 3221225472 | bytes 10485760 | tf_op jit(solution)/shard_map/pallas_call | solution.py:90
  185.8 3.7 %collective-permute-done.48 = bf16[512,256]{1,0:T(8,128)(2,1)S(1)} collective-permute-done((bf16[512,256]{1,0:T(8,128)(2,1)}, bf16[512,256]{1,0:T(8,128)(2,1)S(1)}, u32[]{:S(2)}, u32[]{:S(2)}) %collective-permute-start.48) | collective-permute-done | bytes 262176 | tf_op jit(solution)/shard_map/ppermute | solution.py:27
  191.2 7.4 %shard_map.141 = bf16[1536,512]{1,0:T(8,128)(2,1)} custom-call(s32[2]{0:T(128)} %pad_add_fusion.here, f32[1536,512]{1,0:T(8,128)} %shard_map.139.start, bf16[768,256]{1,0:T(8,128)(2,1)} %copy-done.4, bf16[768,256]{1,0:T(8,128)(2,1)} %copy-done.7, bf16[768,256]{1,0:T(8,128)(2,1)} %copy-done.14, bf16[768,256]{1,0:T(8,128)(2,1)} %copy-done.16, ...), custom_call_target="tpu_custom_call" | custom-call | flops 1610612736 | bytes 10485760 | tf_op jit(solution)/shard_map/pallas_call | solution.py:90
  198.8 2.4 %collective-permute-start.52 = (bf16[512,256]{1,0:T(8,128)(2,1)S(1)}, bf16[512,256]{1,0:T(8,128)(2,1)S(1)}, u32[]{:S(2)}, u32[]{:S(2)}) collective-permute-start(bf16[512,256]{1,0:T(8,128)(2,1)S(1)} %add_convert_fusion.4), channel_id=1, source_target_pairs={{0,16},{1,49},{2,18},{3,51},{4,20},{5,53},{6,22},{7,55},{8,24},{9,... | collective-permute-start | bytes 786440 | tf_op jit(solution)/shard_map/ppermute | solution.py:27
  204.4 2.1 collective-permute-done.52
  (216 shorter events, 57.5 us)
Async XLA Ops:
  7.2 103.4 %all-gather.2.cloned.1.call-start = ((), (), s32[]{:S(2)}) async-start(), calls=%async_computation.1 | async-start | bytes 6684672 | tf_op jit(solution)/shard_map/all_gather | solution.py:249
  9.8 191.4 %reduce-scatter.2.cloned.1.call-start = ((), (), s32[]{:S(2)}) async-start(), calls=%async_computation.2 | async-start | bytes 2359296 | tf_op jit(solution)/shard_map/reduce_scatter | solution.py:315
  18.8 15.2 %collective-permute-start.4 = (bf16[768,512]{1,0:T(8,128)(2,1)}, bf16[768,512]{1,0:T(8,128)(2,1)S(1)}, u32[]{:S(2)}, u32[]{:S(2)}) collective-permute-start(bf16[768,512]{1,0:T(8,128)(2,1)} %get-tuple-element.58), channel_id=1, source_target_pairs={{0,1},{1,0},{2,3},{3,2},{4,5},{5,4},{6,7},{7,6},{8,9},{9,8},{10,11... | collective-permute-start | bytes 2359304 | tf_op jit(solution)/shard_map/ppermute | solution.py:27
  18.8 11.1 %collective-permute-start.5 = (bf16[256,512]{1,0:T(8,128)(2,1)}, bf16[256,512]{1,0:T(8,128)(2,1)S(1)}, u32[]{:S(2)}, u32[]{:S(2)}) collective-permute-start(bf16[256,512]{1,0:T(8,128)(2,1)} %refs_0_.3), channel_id=1, source_target_pairs={{0,48},{1,49},{2,50},{3,51},{4,52},{5,53},{6,54},{7,55},{8,56},{9,... | collective-permute-start | bytes 786440 | tf_op jit(solution)/shard_map/ppermute | solution.py:27
  23.0 10.0 %collective-permute-start.6 = (bf16[256,512]{1,0:T(8,128)(2,1)}, bf16[256,512]{1,0:T(8,128)(2,1)}, u32[]{:S(2)}, u32[]{:S(2)}) collective-permute-start(bf16[256,512]{1,0:T(8,128)(2,1)} %refs_0_.3), channel_id=1, source_target_pairs={{0,16},{1,17},{2,18},{3,19},{4,20},{5,21},{6,22},{7,23},{8,24},{9,... | collective-permute-start | bytes 786440 | tf_op jit(solution)/shard_map/ppermute | solution.py:27
  23.0 17.8 %collective-permute-start.10 = (bf16[256,512]{1,0:T(8,128)(2,1)}, bf16[256,512]{1,0:T(8,128)(2,1)}, u32[]{:S(2)}, u32[]{:S(2)}) collective-permute-start(bf16[256,512]{1,0:T(8,128)(2,1)} %refs_0_.3), channel_id=1, source_target_pairs={{0,1},{1,0},{2,3},{3,2},{4,5},{5,4},{6,7},{7,6},{8,9},{9,8},{10,11... | collective-permute-start | bytes 786440 | tf_op jit(solution)/shard_map/ppermute | solution.py:27
  23.2 12.3 %collective-permute-start.3 = (bf16[256,512]{1,0:T(8,128)(2,1)}, bf16[256,512]{1,0:T(8,128)(2,1)}, u32[]{:S(2)}, u32[]{:S(2)}) collective-permute-start(bf16[256,512]{1,0:T(8,128)(2,1)} %copy-done.35), channel_id=1, source_target_pairs={{0,48},{1,49},{2,50},{3,51},{4,52},{5,53},{6,54},{7,55},{8,56},{9,... | collective-permute-start | bytes 786440 | tf_op jit(solution)/shard_map/ppermute | solution.py:27
  29.9 9.8 %collective-permute-start.7 = (bf16[256,512]{1,0:T(8,128)(2,1)}, bf16[256,512]{1,0:T(8,128)(2,1)}, u32[]{:S(2)}, u32[]{:S(2)}) collective-permute-start(bf16[256,512]{1,0:T(8,128)(2,1)} %copy-done.35), channel_id=1, source_target_pairs={{0,16},{1,17},{2,18},{3,19},{4,20},{5,21},{6,22},{7,23},{8,24},{9,... | collective-permute-start | bytes 786440 | tf_op jit(solution)/shard_map/ppermute | solution.py:27
  49.1 10.9 %collective-permute-start.2 = (f32[2,128]{1,0:T(2,128)S(1)}, f32[2,128]{1,0:T(2,128)S(1)}, u32[]{:S(2)}, u32[]{:S(2)}) collective-permute-start(f32[2,128]{1,0:T(2,128)S(1)} %pad_maximum_fusion.4), channel_id=1, source_target_pairs={{0,1},{1,0},{2,3},{3,2},{4,5},{5,4},{6,7},{7,6},{8,9},{9,8},{10,11... | collective-permute-start | bytes 3080 | tf_op jit(solution)/shard_map/ppermute | solution.py:27
  49.6 14.5 %collective-permute-start.19 = (bf16[512,256]{1,0:T(8,128)(2,1)S(1)}, bf16[512,256]{1,0:T(8,128)(2,1)S(1)}, u32[]{:S(2)}, u32[]{:S(2)}) collective-permute-start(bf16[512,256]{1,0:T(8,128)(2,1)S(1)} %copy-done.27), channel_id=1, source_target_pairs={{0,64},{1,65},{2,66},{3,67},{4,68},{5,69},{6,70},{7,71},{8,72},{9,... | collective-permute-start | bytes 786440 | tf_op jit(solution)/shard_map/ppermute | solution.py:27
  58.4 14.4 %collective-permute-start.18 = (bf16[768,256]{1,0:T(8,128)(2,1)}, bf16[768,256]{1,0:T(8,128)(2,1)}, u32[]{:S(2)}, u32[]{:S(2)}) collective-permute-start(bf16[768,256]{1,0:T(8,128)(2,1)} %get-tuple-element.61), channel_id=1, source_target_pairs={{0,4},{1,13},{2,6},{3,15},{4,8},{5,1},{6,10},{7,3},{8,12},{9,5},{1... | collective-permute-start | bytes 1179656 | tf_op jit(solution)/shard_map/ppermute | solution.py:27
  64.2 13.2 %collective-permute-start.24 = (bf16[2,512,256]{2,1,0:T(8,128)(2,1)S(1)}, bf16[2,512,256]{2,1,0:T(8,128)(2,1)S(1)}, u32[]{:S(2)}, u32[]{:S(2)}) collective-permute-start(bf16[2,512,256]{2,1,0:T(8,128)(2,1)S(1)} %pad_maximum_fusion.1.refs_8_), channel_id=1, source_target_pairs={{0,48},{1,49},{2,50},{3,51},{4,52},{5,53},{6,54},{7,55},{8,56},{9,... | collective-permute-start | bytes 1572872 | tf_op jit(solution)/shard_map/ppermute | solution.py:27
  64.8 15.4 %collective-permute-start.25 = (bf16[2,512,256]{2,1,0:T(8,128)(2,1)S(1)}, bf16[2,512,256]{2,1,0:T(8,128)(2,1)S(1)}, u32[]{:S(2)}, u32[]{:S(2)}) collective-permute-start(bf16[2,512,256]{2,1,0:T(8,128)(2,1)S(1)} %pad_maximum_fusion.1.refs_8_), channel_id=1, source_target_pairs={{0,16},{1,17},{2,18},{3,19},{4,20},{5,21},{6,22},{7,23},{8,24},{9,... | collective-permute-start | bytes 1572872 | tf_op jit(solution)/shard_map/ppermute | solution.py:27
  74.0 17.1 %collective-permute-start.23 = (bf16[768,256]{1,0:T(8,128)(2,1)S(1)}, bf16[768,256]{1,0:T(8,128)(2,1)S(1)}, u32[]{:S(2)}, u32[]{:S(2)}) collective-permute-start(bf16[768,256]{1,0:T(8,128)(2,1)S(1)} %add_convert_fusion.1), channel_id=1, source_target_pairs={{0,4},{1,13},{2,6},{3,15},{4,8},{5,1},{6,10},{7,3},{8,12},{9,5},{1... | collective-permute-start | bytes 1179656 | tf_op jit(solution)/shard_map/ppermute | solution.py:27
  75.8 21.1 %collective-permute-start.21 = (bf16[768,256]{1,0:T(8,128)(2,1)}, bf16[768,256]{1,0:T(8,128)(2,1)S(1)}, u32[]{:S(2)}, u32[]{:S(2)}) collective-permute-start(bf16[768,256]{1,0:T(8,128)(2,1)} %get-tuple-element.73), channel_id=1, source_target_pairs={{0,4},{1,13},{2,6},{3,15},{4,8},{5,1},{6,10},{7,3},{8,12},{9,5},{1... | collective-permute-start | bytes 1179656 | tf_op jit(solution)/shard_map/ppermute | solution.py:27
  77.4 19.7 %collective-permute-start.1 = (bf16[768,128]{1,0:T(8,128)(2,1)S(1)}, bf16[768,128]{1,0:T(8,128)(2,1)S(1)}, u32[]{:S(2)}, u32[]{:S(2)}) collective-permute-start(bf16[768,128]{1,0:T(8,128)(2,1)S(1)} %constant_dynamic-slice_fusion.3), channel_id=1, source_target_pairs={{0,1},{1,0},{2,3},{3,2},{4,5},{5,4},{6,7},{7,6},{8,9},{9,8},{10,11... | collective-permute-start | bytes 589832 | tf_op jit(solution)/shard_map/ppermute | solution.py:27
  77.5 23.0 %collective-permute-start.27 = (bf16[768,256]{1,0:T(8,128)(2,1)S(1)}, bf16[768,256]{1,0:T(8,128)(2,1)S(1)}, u32[]{:S(2)}, u32[]{:S(2)}) collective-permute-start(bf16[768,256]{1,0:T(8,128)(2,1)S(1)} %copy-done.34), channel_id=1, source_target_pairs={{0,12},{1,5},{2,14},{3,7},{4,0},{5,9},{6,2},{7,11},{8,4},{9,13},{1... | collective-permute-start | bytes 1179656 | tf_op jit(solution)/shard_map/ppermute | solution.py:27
  91.2 19.4 %collective-permute-start.26 = (bf16[2,512,256]{2,1,0:T(8,128)(2,1)S(1)}, bf16[2,512,256]{2,1,0:T(8,128)(2,1)S(1)}, u32[]{:S(2)}, u32[]{:S(2)}) collective-permute-start(bf16[2,512,256]{2,1,0:T(8,128)(2,1)S(1)} %broadcast_select_fusion), channel_id=1, source_target_pairs={{0,16},{1,49},{2,18},{3,51},{4,20},{5,53},{6,22},{7,55},{8,24},{9,... | collective-permute-start | bytes 1572872 | tf_op jit(solution)/shard_map/ppermute | solution.py:27
  97.0 12.8 %collective-permute-start.22 = (bf16[768,256]{1,0:T(8,128)(2,1)S(1)}, bf16[768,256]{1,0:T(8,128)(2,1)S(1)}, u32[]{:S(2)}, u32[]{:S(2)}) collective-permute-start(bf16[768,256]{1,0:T(8,128)(2,1)S(1)} %add_convert_fusion.2), channel_id=1, source_target_pairs={{0,4},{1,13},{2,6},{3,15},{4,8},{5,1},{6,10},{7,3},{8,12},{9,5},{1... | collective-permute-start | bytes 1179656 | tf_op jit(solution)/shard_map/ppermute | solution.py:27
  97.2 21.2 %collective-permute-start.20 = (bf16[768,256]{1,0:T(8,128)(2,1)}, bf16[768,256]{1,0:T(8,128)(2,1)}, u32[]{:S(2)}, u32[]{:S(2)}) collective-permute-start(bf16[768,256]{1,0:T(8,128)(2,1)} %get-tuple-element.71), channel_id=1, source_target_pairs={{0,12},{1,5},{2,14},{3,7},{4,0},{5,9},{6,2},{7,11},{8,4},{9,13},{1... | collective-permute-start | bytes 1179656 | tf_op jit(solution)/shard_map/ppermute | solution.py:27
  100.6 17.8 %collective-permute-start.28 = (bf16[768,256]{1,0:T(8,128)(2,1)S(1)}, bf16[768,256]{1,0:T(8,128)(2,1)}, u32[]{:S(2)}, u32[]{:S(2)}) collective-permute-start(bf16[768,256]{1,0:T(8,128)(2,1)S(1)} %add_convert_fusion), channel_id=1, source_target_pairs={{0,2},{1,3},{2,0},{3,1},{4,6},{5,7},{6,4},{7,5},{8,10},{9,11},{10,... | collective-permute-start | bytes 1179656 | tf_op jit(solution)/shard_map/ppermute | solution.py:27
  131.6 9.9 %collective-permute-start.36 = (bf16[768,256]{1,0:T(8,128)(2,1)S(1)}, bf16[768,256]{1,0:T(8,128)(2,1)S(1)}, u32[]{:S(2)}, u32[]{:S(2)}) collective-permute-start(bf16[768,256]{1,0:T(8,128)(2,1)S(1)} %collective-permute-done.29.refs_1_), channel_id=1, source_target_pairs={{0,1},{1,0},{2,3},{3,2},{4,5},{5,4},{6,7},{7,6},{8,9},{9,8},{10,11... | collective-permute-start | bytes 1179656 | tf_op jit(solution)/shard_map/ppermute | solution.py:27
  138.7 12.0 %collective-permute-start.31 = (bf16[768,256]{1,0:T(8,128)(2,1)S(1)}, bf16[768,256]{1,0:T(8,128)(2,1)S(1)}, u32[]{:S(2)}, u32[]{:S(2)}) collective-permute-start(bf16[768,256]{1,0:T(8,128)(2,1)S(1)} %collective-permute-done.29.refs_1_), channel_id=1, source_target_pairs={{0,12},{1,13},{2,14},{3,15},{4,0},{5,1},{6,2},{7,3},{8,4},{9,5},{1... | collective-permute-start | bytes 1179656 | tf_op jit(solution)/shard_map/ppermute | solution.py:27
  139.1 12.4 %collective-permute-start.33 = (bf16[768,256]{1,0:T(8,128)(2,1)S(1)}, bf16[768,256]{1,0:T(8,128)(2,1)S(1)}, u32[]{:S(2)}, u32[]{:S(2)}) collective-permute-start(bf16[768,256]{1,0:T(8,128)(2,1)S(1)} %collective-permute-done.29.refs_1_), channel_id=1, source_target_pairs={{0,4},{1,5},{2,6},{3,7},{4,8},{5,9},{6,10},{7,11},{8,12},{9,13},{1... | collective-permute-start | bytes 1179656 | tf_op jit(solution)/shard_map/ppermute | solution.py:27
  141.5 14.2 %collective-permute-start.34 = (bf16[768,256]{1,0:T(8,128)(2,1)}, bf16[768,256]{1,0:T(8,128)(2,1)S(1)}, u32[]{:S(2)}, u32[]{:S(2)}) collective-permute-start(bf16[768,256]{1,0:T(8,128)(2,1)} %broadcast_select_fusion.2), channel_id=1, source_target_pairs={{0,4},{1,13},{2,6},{3,15},{4,8},{5,1},{6,10},{7,3},{8,12},{9,5},{1... | collective-permute-start | bytes 1179656 | tf_op jit(solution)/shard_map/ppermute | solution.py:27
  154.9 14.7 %collective-permute-start.44 = (bf16[768,256]{1,0:T(8,128)(2,1)S(1)}, bf16[768,256]{1,0:T(8,128)(2,1)S(1)}, u32[]{:S(2)}, u32[]{:S(2)}) collective-permute-start(bf16[768,256]{1,0:T(8,128)(2,1)S(1)} %collective-permute-done.31.refs_3_.refs_0_), channel_id=1, source_target_pairs={{0,1},{1,0},{2,3},{3,2},{4,5},{5,4},{6,7},{7,6},{8,9},{9,8},{10,11... | collective-permute-start | bytes 1179656 | tf_op jit(solution)/shard_map/ppermute | solution.py:27
  154.9 14.7 %collective-permute-start.45 = (bf16[768,256]{1,0:T(8,128)(2,1)S(1)}, bf16[768,256]{1,0:T(8,128)(2,1)S(1)}, u32[]{:S(2)}, u32[]{:S(2)}) collective-permute-start(bf16[768,256]{1,0:T(8,128)(2,1)S(1)} %collective-permute-done.33.refs_5_.refs_1_), channel_id=1, source_target_pairs={{0,1},{1,0},{2,3},{3,2},{4,5},{5,4},{6,7},{7,6},{8,9},{9,8},{10,11... | collective-permute-start | bytes 1179656 | tf_op jit(solution)/shard_map/ppermute | solution.py:27
  155.7 13.8 %collective-permute-start.46 = (bf16[768,256]{1,0:T(8,128)(2,1)S(1)}, bf16[768,256]{1,0:T(8,128)(2,1)S(1)}, u32[]{:S(2)}, u32[]{:S(2)}) collective-permute-start(bf16[768,256]{1,0:T(8,128)(2,1)S(1)} %collective-permute-done.34.refs_6_.refs_2_), channel_id=1, source_target_pairs={{0,1},{1,0},{2,3},{3,2},{4,5},{5,4},{6,7},{7,6},{8,9},{9,8},{10,11... | collective-permute-start | bytes 1179656 | tf_op jit(solution)/shard_map/ppermute | solution.py:27
  182.1 16.6 %collective-permute-start.51 = (bf16[512,256]{1,0:T(8,128)(2,1)}, bf16[512,256]{1,0:T(8,128)(2,1)S(1)}, u32[]{:S(2)}, u32[]{:S(2)}) collective-permute-start(bf16[512,256]{1,0:T(8,128)(2,1)} %get-tuple-element.99), channel_id=1, source_target_pairs={{0,16},{1,49},{2,18},{3,51},{4,20},{5,53},{6,22},{7,55},{8,24},{9,... | collective-permute-start | bytes 786440 | tf_op jit(solution)/shard_map/ppermute | solution.py:27
  183.7 17.5 %collective-permute-start.53 = (bf16[512,256]{1,0:T(8,128)(2,1)}, bf16[512,256]{1,0:T(8,128)(2,1)S(1)}, u32[]{:S(2)}, u32[]{:S(2)}) collective-permute-start(bf16[512,256]{1,0:T(8,128)(2,1)} %get-tuple-element.101), channel_id=1, source_target_pairs={{0,48},{1,17},{2,50},{3,19},{4,52},{5,21},{6,54},{7,23},{8,56},{9,... | collective-permute-start | bytes 786440 | tf_op jit(solution)/shard_map/ppermute | solution.py:27
  185.3 19.1 %collective-permute-start.50 = (bf16[512,256]{1,0:T(8,128)(2,1)}, bf16[512,256]{1,0:T(8,128)(2,1)S(1)}, u32[]{:S(2)}, u32[]{:S(2)}) collective-permute-start(bf16[512,256]{1,0:T(8,128)(2,1)} %get-tuple-element.97), channel_id=1, source_target_pairs={{0,48},{1,17},{2,50},{3,19},{4,52},{5,21},{6,54},{7,23},{8,56},{9,... | collective-permute-start | bytes 786440 | tf_op jit(solution)/shard_map/ppermute | solution.py:27
  190.5 10.7 %collective-permute-start.49 = (bf16[512,256]{1,0:T(8,128)(2,1)S(1)}, bf16[512,256]{1,0:T(8,128)(2,1)S(1)}, u32[]{:S(2)}, u32[]{:S(2)}) collective-permute-start(bf16[512,256]{1,0:T(8,128)(2,1)S(1)} %add_convert_fusion.5), channel_id=1, source_target_pairs={{0,16},{1,49},{2,18},{3,51},{4,20},{5,53},{6,22},{7,55},{8,24},{9,... | collective-permute-start | bytes 786440 | tf_op jit(solution)/shard_map/ppermute | solution.py:27
  (69 other events, 551.7 us)
Sparse Core Ops, SparseCore 0:
  10.3 83.5 all-gather.1
  129.7 40.0 reduce-scatter.1

commit v7 on v6

--- a/solution.py
+++ b/solution.py
@@ -101,7 +101,7 @@
 
 
 def hid_kernel(ways, here, conv, *refs):
-    blocks, outs, (held, sems) = refs[:16], refs[16:20], refs[20:]
+    blocks, outs, (held, sems) = refs[:16], refs[16:18], refs[18:]
     copies = [
         pltpu.make_async_copy(
             ref, held.at[k % 8, :, pl.ds((k // 8) * 512, 512)], sems.at[k]
@@ -114,10 +114,10 @@
     ahead = 1 - 2 * core
     for copy in copies:
         copy.wait()
-    for j, out in enumerate(outs):
+    for j in range(4):
         fixed, way = ways[j // 2]
         block = ((x + fixed + way * ahead) & 3) * 2 + (y_hi ^ (j % 2))
-        out[...] = lax.dot_general(
+        outs[j // 2][j % 2] = lax.dot_general(
             conv[...], held[row_slot(block, y_lo, z)], (((1,), (1,)), ((), ())),
             preferred_element_type=F32,
         ).astype(BF16)
@@ -125,7 +125,7 @@
 
 def hid_partial(here, conv, blocks, beside, ways):
     return call(
-        functools.partial(hid_kernel, ways), [jax.ShapeDtypeStruct((768, 256), BF16)] * 4,
+        functools.partial(hid_kernel, ways), [jax.ShapeDtypeStruct((2, 768, 256), BF16)] * 2,
         pltpu.VMEM, [pltpu.VMEM((8, 256, 1024), BF16)], 16, 8 << 20, 768 * 1024 * 2048, here,
         [conv], [*blocks, *beside],
     )
@@ -140,7 +140,7 @@
 
 
 def win_kernel(here, left, *refs):
-    blocks, outs, (held, sems) = refs[:16], refs[16:24], refs[24:]
+    blocks, outs, (held, sems) = refs[:16], refs[16:20], refs[20:]
     row, y_lo, z, x, y_hi, core = place_of(here)
     copies = []
     for k in range(8):
@@ -152,61 +152,55 @@
     for copy in copies:
         copy.wait()
     ahead = 1 - 2 * core
-    for j, out in enumerate(outs):
+    for j in range(8):
         step = (2, -ahead, ahead, 0)[j // 2]
         block = (y_lo ^ (j % 2)) * 4 + ((z + step) & 3)
-        out[...] = jnp.dot(
+        outs[j // 2][j % 2] = jnp.dot(
             left[...], held[hidden_slot(block, x, y_hi)], preferred_element_type=F32
         ).astype(BF16)
 
 
 def win_partial(here, left, blocks, beside):
     return call(
-        win_kernel, [jax.ShapeDtypeStruct((512, 256), BF16)] * 8, pltpu.VMEM,
+        win_kernel, [jax.ShapeDtypeStruct((2, 512, 256), BF16)] * 4, pltpu.VMEM,
         [pltpu.VMEM((8, 1536, 256), BF16)], 16, 10 << 20, 2 * 512 * 1536 * 2048, here, [left],
         [*blocks, *beside],
     )
 
 
-def out_kernel(held_slots, here, start, *refs):
-    blocks, parts, out = refs[:8], refs[8:12], refs[12]
-    held, loaded, weights, sems = refs[13:]
+def out_kernel(here, cot, *refs):
+    blocks, parts, out = refs[:16], refs[16:20], refs[20]
+    held, weights, sems = refs[21:]
     row, y_lo, z, x, y_hi, core = place_of(here)
     copies = [
-        pltpu.make_async_copy(ref, loaded.at[pl.ds(k * 2, 2)], sems.at[8 + k])
+        pltpu.make_async_copy(ref, weights.at[pl.ds(k * 2, 2)], sems.at[16 + k])
         for k, ref in enumerate(parts)
     ]
-    for k in range(4):
+    for k in range(8):
         copies += act_copies(
-            blocks[k], blocks[4 + k],
-            lambda rows, k=k: held.at[rows, pl.ds(k * 256, 256)], sems, 2 * k, core,
+            blocks[k], blocks[8 + k], lambda rows, k=k: held.at[k, rows, :], sems, 2 * k, core
         )
     for copy in copies:
         copy.start()
     for copy in copies:
         copy.wait()
-    for k, slot in enumerate(held_slots):
-        block = ((x + STEPS[slot // 2]) & 3) * 2 + (y_hi ^ (slot & 1))
-        weights[:, k * 256 : k * 256 + 256] = loaded[row_slot(block, y_lo, z)]
     for at in range(0, 1536, 256):
-        total = start[at : at + 256, :].astype(F32) + lax.dot_general(
-            held[at : at + 256, :], weights[...], (((1,), (1,)), ((), ())),
-            preferred_element_type=F32,
-        )
-        out[at : at + 256, :] = total.astype(out.dtype)
-
-
-def out_partial(here, start, blocks, beside, weights, slots, kind):
+        total = cot[at : at + 256, :].astype(F32)
+        for block in range(8):
+            total = total + lax.dot_general(
+                held[hidden_slot(block, x, y_hi), at : at + 256, :],
+                weights[row_slot(block, y_lo, z)],
+                (((1,), (1,)), ((), ())),
+                preferred_element_type=F32,
+            )
+        out[at : at + 256, :] = total.astype(BF16)
+
+
+def out_gradient(here, cot, blocks, beside, weights):
     return call(
-        functools.partial(out_kernel, slots), [jax.ShapeDtypeStruct((1536, 512), kind)],
-        pltpu.VMEM,
-        [
-            pltpu.VMEM((1536, 1024), BF16),
-            pltpu.VMEM((8, 512, 256), BF16),
-            pltpu.VMEM((512, 1024), BF16),
-        ],
-        12, 10 << 20, 1536 * 512 * 2048, here, [start],
-        [*(blocks[k] for k in slots), *(beside[k] for k in slots), *weights],
+        out_kernel, [jax.ShapeDtypeStruct((1536, 512), BF16)], pltpu.VMEM,
+        [pltpu.VMEM((8, 1536, 256), BF16), pltpu.VMEM((8, 512, 256), BF16)], 20, 12 << 20,
+        2 * 1536 * 512 * 2048, here, [cot], [*blocks, *beside, *weights],
     )[0]
 
 
@@ -284,27 +278,22 @@
     mid_gain = gain_chip[0] * gain_chip[1]
 
     out_beside = [core_swap(block) for block in out_blocks]
-    ways = ((2, 0), (0, 1))
-    first = list(hid_partial(place, conv_both, out_blocks, out_beside, ways))
-    passed = [x_split(first[i], 1) for i in (1, 0)]
-    first[3], in_near = tie(first[3], in_near)
+    away, there = hid_partial(place, conv_both, out_blocks, out_beside, ((2, 0), (0, -1)))
+    passed, back = x_split(away, 1), x_split(there, -1)
+    away, in_near = tie(away, in_near)
     in_here = jnp.stack([weight_in, in_near])
     conv_both, in_here = tie(conv_both, in_here)
     in_above, in_below = z_shift(in_here, -1), z_shift(in_here, 1)
-    second = hid_partial(place, conv_both, out_blocks, out_beside, ((0, -1), (0, 0)))
-    passed[0], second = tie(passed[0], second)
-    back = [x_split(second[i], -1) for i in (1, 0)]
-    far = x_split(add([first[3], passed[0]]).astype(BF16), 1)
-    near = x_split(add([first[2], passed[1]]).astype(BF16), 1)
-    far, in_above, in_below = tie(far, in_above, in_below)
+    further, own = hid_partial(place, conv_both, out_blocks, out_beside, ((0, 1), (0, 0)))
+    passed, own, in_above, in_below = tie(passed, own, in_above, in_below)
+    further = x_split(add([further, passed]).astype(BF16), 1)
     in_across = onward(in_above, in_below, core, z_split)
+    wout = dot(hidden_full, grad_conv, 0, 0).astype(BF16)
+    further, wout = tie(further, wout)
+    total = add([own, back, further])
+    crossed, in_across = tie(y_hi_swap(total[1].astype(BF16)), in_across)
     in_blocks = [in_here, in_above, in_below, in_across]
-    crossed = y_hi_swap(add([second[3], back[0], far]).astype(BF16))
-    near, hidden_full, in_blocks[3] = tie(near, hidden_full, in_across)
-    total = add([second[2], back[1], near])
-    wout = dot(hidden_full, grad_conv, 0, 0).astype(BF16)
-    crossed, wout = tie(crossed, wout)
-    grad_hid = add([total, crossed])
+    grad_hid = add([total[0], crossed])
     alive = (pre_chip > 0) & (gain_chip[1] > 0)[None, :]
     grad_pre = jnp.where(alive, grad_hid, 0.0)
     mid_part = jnp.sum(grad_pre * pre_chip, axis=0).reshape(2, 128)
@@ -314,33 +303,32 @@
     act_near, wout = tie(act_near, wout)
     wout = lax.psum_scatter(wout, "row", scatter_dimension=0, tiled=True)
     near_above, near_below = x_shift(act_near, -1), x_shift(act_near, 1)
-    act_across = onward(act_above, act_below, core, x_split)
-    act = [grad_act, act_near, act_above, near_above, act_below, near_below, act_across]
-    act_beside = [core_swap(block) for block in act]
-    grad_x = out_partial(place, cotangent, act, act_beside, in_blocks, (0, 1, 2, 4), F32)
-    near_above, grad_x = tie(near_above, grad_x)
-    act.append(onward(near_above, near_below, core, x_split))
-    act_beside.append(core_swap(act[7]))
 
     mid_own = lax.dynamic_index_in_dim(mid_part, core, 0, keepdims=False)
     mid_away = lax.dynamic_index_in_dim(mid_part, 1 - core, 0, keepdims=False)
     mid_own = mid_own + core_swap(mid_away)
     sums = jnp.concatenate([mid_own, wide_part]).reshape(5, 128)
     sums = sums + z_flip(sums, 1)
+    near_above, sums = tie(near_above, sums)
     sums = sums + z_flip(sums, 2)
     sums = sums + y_lo_swap(sums)
 
-    act[7], sums = tie(act[7], sums)
-    sends = win_partial(place, input_turned, act, act_beside)
-    passed = [z_split(sends[i], 1) for i in (1, 0)]
-    back = [z_split(sends[2 + i], -1) for i in (1, 0)]
-    far = z_split(add([sends[5], passed[0]]).astype(BF16), 1)
-    near = z_split(add([sends[4], passed[1]]).astype(BF16), 1)
-    grad_x = out_partial(place, grad_x, act, act_beside, in_blocks, (3, 5, 6, 7), BF16)
-    far, grad_x, wout = tie(far, grad_x, wout)
-    crossed = y_lo_swap(add([sends[7], back[0], far]).astype(BF16))
-    grad_win = add([sends[6], back[1], near, crossed]) * scaling
+    act_across = onward(act_above, act_below, core, x_split)
+    near_across = onward(near_above, near_below, core, x_split)
+    act = [
+        grad_act, act_near, act_above, near_above, act_below, near_below, act_across, near_across
+    ]
+    act_beside = [core_swap(block) for block in act]
+
+    away, there, further, own = win_partial(place, input_turned, act, act_beside)
+    passed, back = z_split(away, 1), z_split(there, -1)
+    grad_x = out_gradient(place, cotangent, act, act_beside, in_blocks)
+    passed, grad_x = tie(passed, grad_x)
+    further = z_split(add([further, passed]).astype(BF16), 1)
     grad_wout = wout.astype(F32) * scaling
+    further, grad_wout, sums = tie(further, grad_wout, sums)
+    total = add([own, back, further])
+    grad_win = add([total[0], y_lo_swap(total[1].astype(BF16))]) * scaling
     grad_smid = keep_mid.astype(F32) * scaling * sums[0]
     grad_swide = keep_wide.astype(F32) * scaling * sums[1:].reshape(512)
     return (grad_x, grad_win, grad_wout, grad_smid, grad_swide)

time: 216 us -> 217 us (level)
  waiting for transfers between devices: 76.2 us -> 95.6 us
  starting transfers between devices: 53.9 us -> 41.1 us
  Pallas kernels: 36.3 us -> 31.1 us
    ppermute x55 -> x49, starting transfers between devices: 53.9 us -> 41 us  [permute(): return lax.ppermute(v, AXES, pairs)]
    all_gather x1, waiting for transfers between devices: 0.01 us -> 12.3 us  [local(): hidden_full = lax.all_gather(hidden, 'col', axis=1, tiled=True)]
    ppermute x55 -> x49, waiting for transfers between devices: 76.2 us -> 83.2 us  [permute(): return lax.ppermute(v, AXES, pairs)]
    pallas_call x5 -> x4, Pallas kernels: 36.3 us -> 31.1 us  [call(): pl.pallas_call(body, out_shape=outs, in_specs=[pl.BlockSpec(memory_space=...]
    convert_element_type x6 -> x2, other arithmetic: 2.61 us -> 0.31 us  [the longest x1 0.19 us: local(): further = x_split(add([further, passed]).astype(BF16), 1)]
    unnamed x89 -> x75, local copies, waits for them, and re-layouts: 6.3 us -> 4.91 us
  transfers between devices with their start and end apart: 57 -> 51, of which waited for: 23 -> 18; matrix products, arithmetic and copies ran while one was open for 11% -> 12% of each run, Pallas kernels for 17% -> 14%
where the time goes in v7:
time: 217 us; the launch traced here: 216 us
  waiting for transfers between devices  95.6 us (44%)
  starting transfers between devices  41.1 us (19%)
  Pallas kernels  31.1 us (14%)
  other arithmetic  19.6 us (9%)
  between operations  14.6 us (7%)
  matrix products  7.69 us (4%)
  local copies, waits for them, and re-layouts  6.66 us (3%)
    ppermute x49, waiting for transfers between devices, permute(): return lax.ppermute(v, AXES, pairs)  83.2 us
    ppermute x49, starting transfers between devices, permute(): return lax.ppermute(v, AXES, pairs)  41 us
    pallas_call x4, Pallas kernels, call(): pl.pallas_call(body, out_shape=outs, in_specs=[pl.BlockSpec(memory_space=...  31.1 us
    all_gather x1, waiting for transfers between devices, local(): hidden_full = lax.all_gather(hidden, 'col', axis=1, tiled=True)  12.3 us
    dot_general x1, matrix products, dot(): lax.dot_general(a, b, (((ca,), (cb,)), ((), ())), preferred_element_type=...  7.69 us
    unnamed x75, local copies, waits for them, and re-layouts  4.91 us
  transfers between devices with their start and end apart: 51, of which 18 were waited for; matrix products, arithmetic and copies ran while one was open for 12% of the time, Pallas kernels for 14%

profile of v7, /device:TPU:0, one launch (start us, length us, event | category | flops | bytes accessed | tf_op | source)
XLA Modules:
  0.0 216.3 jit_solution(2828909149836107576)
XLA Ops:
  7.9 1.9 maximum_convert_fusion
  9.8 1.7 collective-permute-start
  12.3 2.7 %fusion.1 = (f32[512]{0:T(512)S(1)}, bf16[1536,512]{1,0:T(8,128)(2,1)S(1)}) fusion(bf16[1536,512]{1,0:T(8,128)(2,1)} %cot.1, bf16[1536,512]{1,0:T(8,128)(2,1)} %param.12, f32[512]{0:T(512)S(1)} %convert_multiply_fusion.4), kind=kLoop, calls=%fused_computation.3 | loop fusion | flops 4718080 | bytes 4722688 | tf_op jit(solution)/shard_map/reduce_sum | solution.py:250
  18.2 2.1 collective-permute-start.6
  20.3 2.1 collective-permute-start.5
  22.6 7.2 %collective-permute-done.6.refs_4_ = bf16[256,512]{1,0:T(8,128)(2,1)} collective-permute-done((bf16[256,512]{1,0:T(8,128)(2,1)}, bf16[256,512]{1,0:T(8,128)(2,1)}, u32[]{:S(2)}, u32[]{:S(2)}) %collective-permute-start.6) | collective-permute-done | bytes 262176 | tf_op jit(solution)/shard_map/ppermute | solution.py:27
  29.9 1.9 collective-permute-start.3
  35.2 4.1 %collective-permute-done.3.refs_3_ = bf16[256,512]{1,0:T(8,128)(2,1)S(1)} collective-permute-done((bf16[256,512]{1,0:T(8,128)(2,1)}, bf16[256,512]{1,0:T(8,128)(2,1)S(1)}, u32[]{:S(2)}, u32[]{:S(2)}) %collective-permute-start.3) | collective-permute-done | bytes 262176 | tf_op jit(solution)/shard_map/ppermute | solution.py:27
  41.1 1.8 collective-permute-start.11
  43.4 5.2 %collective-permute-done.9.refs_7_ = bf16[256,512]{1,0:T(8,128)(2,1)S(1)} collective-permute-done((bf16[256,512]{1,0:T(8,128)(2,1)S(1)}, bf16[256,512]{1,0:T(8,128)(2,1)S(1)}, u32[]{:S(2)}, u32[]{:S(2)}) %collective-permute-start.9) | collective-permute-done | bytes 262176 | tf_op jit(solution)/shard_map/ppermute | solution.py:27
  51.9 6.4 %shard_map.137 = (bf16[2,768,256]{2,1,0:T(8,128)(2,1)}, bf16[2,768,256]{2,1,0:T(8,128)(2,1)}) custom-call(s32[2]{0:T(128)} %pad_add_fusion.here, bf16[768,1024]{1,0:T(8,128)(2,1)} %pad_maximum_fusion.conv, bf16[256,512]{1,0:T(8,128)(2,1)} %refs_0_.3, bf16[256,512]{1,0:T(8,128)(2,1)} %collective-permute-done.refs_1_, ...), custom_call_target="tpu_custom_call" | custom-call | flops 1610612736 | bytes 8388608 | tf_op jit(solution)/shard_map/pallas_call | solution.py:90
  61.1 2.9 %collective-permute-done.19 = bf16[512,256]{1,0:T(8,128)(2,1)S(1)} collective-permute-done((bf16[512,256]{1,0:T(8,128)(2,1)S(1)}, bf16[512,256]{1,0:T(8,128)(2,1)S(1)}, u32[]{:S(2)}, u32[]{:S(2)}) %collective-permute-start.19) | collective-permute-done | bytes 262176 | tf_op jit(solution)/shard_map/ppermute | solution.py:27
  64.2 3.2 %collective-permute-start.20 = (bf16[2,512,256]{2,1,0:T(8,128)(2,1)S(1)}, bf16[2,512,256]{2,1,0:T(8,128)(2,1)}, u32[]{:S(2)}, u32[]{:S(2)}) collective-permute-start(bf16[2,512,256]{2,1,0:T(8,128)(2,1)S(1)} %pad_maximum_fusion.1.refs_16_), channel_id=1, source_target_pairs={{0,48},{1,49},{2,50},{3,51},{4,52},{5,53},{6,54},{7,55},{8,56},{9,... | collective-permute-start | bytes 1572872 | tf_op jit(solution)/shard_map/ppermute | solution.py:27
  68.6 2.8 %collective-permute-start.22 = (bf16[2,768,256]{2,1,0:T(8,128)(2,1)}, bf16[2,768,256]{2,1,0:T(8,128)(2,1)}, u32[]{:S(2)}, u32[]{:S(2)}) collective-permute-start(bf16[2,768,256]{2,1,0:T(8,128)(2,1)} %get-tuple-element.54), channel_id=1, source_target_pairs={{0,12},{1,5},{2,14},{3,7},{4,0},{5,9},{6,2},{7,11},{8,4},{9,13},{1... | collective-permute-start | bytes 2359304 | tf_op jit(solution)/shard_map/ppermute | solution.py:27
  71.4 6.5 %shard_map.138 = (bf16[2,768,256]{2,1,0:T(8,128)(2,1)}, bf16[2,768,256]{2,1,0:T(8,128)(2,1)}) custom-call(s32[2]{0:T(128)} %pad_add_fusion.here, bf16[768,1024]{1,0:T(8,128)(2,1)} %pad_maximum_fusion.conv, bf16[256,512]{1,0:T(8,128)(2,1)} %refs_0_.3, bf16[256,512]{1,0:T(8,128)(2,1)} %collective-permute-done.refs_1_, ...), custom_call_target="tpu_custom_call" | custom-call | flops 1610612736 | bytes 8388608 | tf_op jit(solution)/shard_map/pallas_call | solution.py:90
  81.8 12.3 %all-gather.2.cloned.1.call-done = bf16[1536,2048]{1,0:T(8,128)(2,1)} async-done(((bf16[1536,128]{1,0:T(8,128)(2,1)}), bf16[1536,2048]{1,0:T(8,128)(2,1)}) %all-gather.2.cloned.1.call-update) | async-done | bytes 6291472 | tf_op jit(solution)/shard_map/all_gather | solution.py:243
  94.1 7.7 %convolution_convert_fusion = bf16[2048,512]{1,0:T(8,128)(2,1)} fusion(bf16[1536,2048]{1,0:T(8,128)(2,1)} %all-gather.2.cloned.1.call-done, bf16[1536,512]{1,0:T(8,128)(2,1)S(1)} %get-tuple-element.84), kind=kOutput, calls=%fused_computation.4 | convolution fusion | flops 3222274048 | bytes 9961472 | tf_op jit(solution)/shard_map/dot_general | solution.py:63
  104.7 11.7 %collective-permute-done.24 = bf16[768,256]{1,0:T(8,128)(2,1)S(1)} collective-permute-done((bf16[768,256]{1,0:T(8,128)(2,1)S(1)}, bf16[768,256]{1,0:T(8,128)(2,1)S(1)}, u32[]{:S(2)}, u32[]{:S(2)}) %collective-permute-start.24) | collective-permute-done | bytes 393248 | tf_op jit(solution)/shard_map/ppermute | solution.py:27
  117.1 11.7 %collective-permute-done.26.refs_1_ = bf16[768,256]{1,0:T(8,128)(2,1)S(1)} collective-permute-done((bf16[768,256]{1,0:T(8,128)(2,1)S(1)}, bf16[768,256]{1,0:T(8,128)(2,1)S(1)}, u32[]{:S(2)}, u32[]{:S(2)}) %collective-permute-start.26) | collective-permute-done | bytes 393248 | tf_op jit(solution)/shard_map/ppermute | solution.py:27
  129.5 2.8 %collective-permute-start.27 = (bf16[768,256]{1,0:T(8,128)(2,1)S(1)}, bf16[768,256]{1,0:T(8,128)(2,1)S(1)}, u32[]{:S(2)}, u32[]{:S(2)}) collective-permute-start(bf16[768,256]{1,0:T(8,128)(2,1)S(1)} %get-tuple-element.80.refs_0_), channel_id=1, source_target_pairs={{0,12},{1,13},{2,14},{3,15},{4,0},{5,1},{6,2},{7,3},{8,4},{9,5},{1... | collective-permute-start | bytes 1179656 | tf_op jit(solution)/shard_map/ppermute | solution.py:27
  132.6 3.4 %collective-permute-done.30 = f32[5,128]{1,0:T(8,128)S(1)} collective-permute-done((f32[5,128]{1,0:T(8,128)S(1)}, f32[5,128]{1,0:T(8,128)S(1)}, u32[]{:S(2)}, u32[]{:S(2)}) %collective-permute-start.30) | collective-permute-done | bytes 2592 | tf_op jit(solution)/shard_map/ppermute | solution.py:27
  137.2 5.0 %collective-permute-done.31.refs_4_ = bf16[768,256]{1,0:T(8,128)(2,1)S(1)} collective-permute-done((bf16[768,256]{1,0:T(8,128)(2,1)S(1)}, bf16[768,256]{1,0:T(8,128)(2,1)S(1)}, u32[]{:S(2)}, u32[]{:S(2)}) %collective-permute-start.31) | collective-permute-done | bytes 393248 | tf_op jit(solution)/shard_map/ppermute | solution.py:27
  143.9 6.2 %collective-permute-done.28.refs_3_ = bf16[768,256]{1,0:T(8,128)(2,1)S(1)} collective-permute-done((bf16[768,256]{1,0:T(8,128)(2,1)S(1)}, bf16[768,256]{1,0:T(8,128)(2,1)S(1)}, u32[]{:S(2)}, u32[]{:S(2)}) %collective-permute-start.28) | collective-permute-done | bytes 393248 | tf_op jit(solution)/shard_map/ppermute | solution.py:27
  151.3 2.9 %collective-permute-start.36 = (bf16[768,256]{1,0:T(8,128)(2,1)S(1)}, bf16[768,256]{1,0:T(8,128)(2,1)S(1)}, u32[]{:S(2)}, u32[]{:S(2)}) collective-permute-start(bf16[768,256]{1,0:T(8,128)(2,1)S(1)} %collective-permute-done.26.refs_1_), channel_id=1, source_target_pairs={{0,1},{1,0},{2,3},{3,2},{4,5},{5,4},{6,7},{7,6},{8,9},{9,8},{10,11... | collective-permute-start | bytes 1179656 | tf_op jit(solution)/shard_map/ppermute | solution.py:27
  154.9 4.8 %collective-permute-done.34.refs_7_ = bf16[768,256]{1,0:T(8,128)(2,1)S(1)} collective-permute-done((bf16[768,256]{1,0:T(8,128)(2,1)S(1)}, bf16[768,256]{1,0:T(8,128)(2,1)S(1)}, u32[]{:S(2)}, u32[]{:S(2)}) %collective-permute-start.34) | collective-permute-done | bytes 393248 | tf_op jit(solution)/shard_map/ppermute | solution.py:27
  161.7 8.6 %shard_map.139 = (bf16[2,512,256]{2,1,0:T(8,128)(2,1)}, bf16[2,512,256]{2,1,0:T(8,128)(2,1)}, bf16[2,512,256]{2,1,0:T(8,128)(2,1)}, bf16[2,512,256]{2,1,0:T(8,128)(2,1)}) custom-call(s32[2]{0:T(128)} %pad_add_fusion.here, bf16[512,1536]{1,0:T(8,128)(2,1)} %bitcast.46, bf16[768,256]{1,0:T(8,128)(2,1)} %copy-done.8, bf16[768,256]{1,0:T(8,128)(2,1)} %copy-done.19, ...), custom_call_target="tpu_custom_call" | custom-call | flops 3221225472 | bytes 10485760 | tf_op jit(solution)/shard_map/pallas_call | solution.py:90
  170.5 9.5 %shard_map.140 = bf16[1536,512]{1,0:T(8,128)(2,1)} custom-call(s32[2]{0:T(128)} %pad_add_fusion.here, bf16[1536,512]{1,0:T(8,128)(2,1)} %cot.1, bf16[768,256]{1,0:T(8,128)(2,1)} %copy-done.8, bf16[768,256]{1,0:T(8,128)(2,1)} %copy-done.19, bf16[768,256]{1,0:T(8,128)(2,1)} %copy-done.10, bf16[768,256]{1,0:T(8,128)(2,1)} %copy-done.12, ...), custom_call_target="tpu_custom_call" | custom-call | flops 3221225472 | bytes 12582912 | tf_op jit(solution)/shard_map/pallas_call | solution.py:90
  181.6 2.9 %collective-permute-start.44 = (bf16[2,512,256]{2,1,0:T(8,128)(2,1)S(1)}, bf16[2,512,256]{2,1,0:T(8,128)(2,1)S(1)}, u32[]{:S(2)}, u32[]{:S(2)}) collective-permute-start(bf16[2,512,256]{2,1,0:T(8,128)(2,1)S(1)} %copy-done.18), channel_id=1, source_target_pairs={{0,48},{1,17},{2,50},{3,19},{4,52},{5,21},{6,54},{7,23},{8,56},{9,... | collective-permute-start | bytes 1572872 | tf_op jit(solution)/shard_map/ppermute | solution.py:27
  185.3 11.2 %collective-permute-done.46 = f32[5,128]{1,0:T(8,128)S(1)} collective-permute-done((f32[5,128]{1,0:T(8,128)S(1)}, f32[5,128]{1,0:T(8,128)S(1)}, u32[]{:S(2)}, u32[]{:S(2)}) %collective-permute-start.46) | collective-permute-done | bytes 2592 | tf_op jit(solution)/shard_map/ppermute | solution.py:27
  197.4 2.7 %collective-permute-done.47 = f32[5,128]{1,0:T(8,128)S(1)} collective-permute-done((f32[5,128]{1,0:T(8,128)S(1)}, f32[5,128]{1,0:T(8,128)S(1)}, u32[]{:S(2)}, u32[]{:S(2)}) %collective-permute-start.47) | collective-permute-done | bytes 2592 | tf_op jit(solution)/shard_map/ppermute | solution.py:27
  200.1 1.8 convert_multiply_fusion.3
  204.2 4.4 %collective-permute-done.48 = bf16[512,256]{1,0:T(8,128)(2,1)S(1)} collective-permute-done((bf16[512,256]{1,0:T(8,128)(2,1)S(1)}, bf16[512,256]{1,0:T(8,128)(2,1)S(1)}, u32[]{:S(2)}, u32[]{:S(2)}) %collective-permute-start.48) | collective-permute-done | bytes 262176 | tf_op jit(solution)/shard_map/ppermute | solution.py:27
  (189 shorter events, 39.5 us)
Async XLA Ops:
  7.2 87.0 %all-gather.2.cloned.1.call-start = ((), (), s32[]{:S(2)}) async-start(), calls=%async_computation.1 | async-start | bytes 6684672 | tf_op jit(solution)/shard_map/all_gather | solution.py:243
  9.8 190.3 %reduce-scatter.2.cloned.1.call-start = ((), (), s32[]{:S(2)}) async-start(), calls=%async_computation.2 | async-start | bytes 2359296 | tf_op jit(solution)/shard_map/reduce_scatter | solution.py:304
  18.2 15.4 %collective-permute-start.4 = (bf16[768,512]{1,0:T(8,128)(2,1)}, bf16[768,512]{1,0:T(8,128)(2,1)S(1)}, u32[]{:S(2)}, u32[]{:S(2)}) collective-permute-start(bf16[768,512]{1,0:T(8,128)(2,1)} %get-tuple-element.44), channel_id=1, source_target_pairs={{0,1},{1,0},{2,3},{3,2},{4,5},{5,4},{6,7},{7,6},{8,9},{9,8},{10,11... | collective-permute-start | bytes 2359304 | tf_op jit(solution)/shard_map/ppermute | solution.py:27
  18.2 11.7 %collective-permute-start.6 = (bf16[256,512]{1,0:T(8,128)(2,1)}, bf16[256,512]{1,0:T(8,128)(2,1)}, u32[]{:S(2)}, u32[]{:S(2)}) collective-permute-start(bf16[256,512]{1,0:T(8,128)(2,1)} %refs_0_.3), channel_id=1, source_target_pairs={{0,16},{1,17},{2,18},{3,19},{4,20},{5,21},{6,22},{7,23},{8,24},{9,... | collective-permute-start | bytes 786440 | tf_op jit(solution)/shard_map/ppermute | solution.py:27
  20.3 11.5 %collective-permute-start.5 = (bf16[256,512]{1,0:T(8,128)(2,1)}, bf16[256,512]{1,0:T(8,128)(2,1)}, u32[]{:S(2)}, u32[]{:S(2)}) collective-permute-start(bf16[256,512]{1,0:T(8,128)(2,1)} %refs_0_.3), channel_id=1, source_target_pairs={{0,48},{1,49},{2,50},{3,51},{4,52},{5,53},{6,54},{7,55},{8,56},{9,... | collective-permute-start | bytes 786440 | tf_op jit(solution)/shard_map/ppermute | solution.py:27
  22.4 18.7 %collective-permute-start.10 = (bf16[256,512]{1,0:T(8,128)(2,1)}, bf16[256,512]{1,0:T(8,128)(2,1)}, u32[]{:S(2)}, u32[]{:S(2)}) collective-permute-start(bf16[256,512]{1,0:T(8,128)(2,1)} %refs_0_.3), channel_id=1, source_target_pairs={{0,1},{1,0},{2,3},{3,2},{4,5},{5,4},{6,7},{7,6},{8,9},{9,8},{10,11... | collective-permute-start | bytes 786440 | tf_op jit(solution)/shard_map/ppermute | solution.py:27
  22.6 16.7 %collective-permute-start.7 = (bf16[256,512]{1,0:T(8,128)(2,1)}, bf16[256,512]{1,0:T(8,128)(2,1)}, u32[]{:S(2)}, u32[]{:S(2)}) collective-permute-start(bf16[256,512]{1,0:T(8,128)(2,1)} %collective-permute-done.refs_1_), channel_id=1, source_target_pairs={{0,16},{1,17},{2,18},{3,19},{4,20},{5,21},{6,22},{7,23},{8,24},{9,... | collective-permute-start | bytes 786440 | tf_op jit(solution)/shard_map/ppermute | solution.py:27
  29.9 9.4 %collective-permute-start.3 = (bf16[256,512]{1,0:T(8,128)(2,1)}, bf16[256,512]{1,0:T(8,128)(2,1)S(1)}, u32[]{:S(2)}, u32[]{:S(2)}) collective-permute-start(bf16[256,512]{1,0:T(8,128)(2,1)} %collective-permute-done.refs_1_), channel_id=1, source_target_pairs={{0,48},{1,49},{2,50},{3,51},{4,52},{5,53},{6,54},{7,55},{8,56},{9,... | collective-permute-start | bytes 786440 | tf_op jit(solution)/shard_map/ppermute | solution.py:27
  33.5 9.4 %collective-permute-start.8 = (bf16[256,512]{1,0:T(8,128)(2,1)}, bf16[256,512]{1,0:T(8,128)(2,1)}, u32[]{:S(2)}, u32[]{:S(2)}) collective-permute-start(bf16[256,512]{1,0:T(8,128)(2,1)} %broadcast_select_fusion.4), channel_id=1, source_target_pairs={{0,16},{1,49},{2,18},{3,51},{4,20},{5,53},{6,22},{7,55},{8,24},{9,... | collective-permute-start | bytes 786440 | tf_op jit(solution)/shard_map/ppermute | solution.py:27
  33.6 9.3 %collective-permute-start.14 = (bf16[256,512]{1,0:T(8,128)(2,1)}, bf16[256,512]{1,0:T(8,128)(2,1)}, u32[]{:S(2)}, u32[]{:S(2)}) collective-permute-start(bf16[256,512]{1,0:T(8,128)(2,1)} %collective-permute-done.6.refs_4_), channel_id=1, source_target_pairs={{0,1},{1,0},{2,3},{3,2},{4,5},{5,4},{6,7},{7,6},{8,9},{9,8},{10,11... | collective-permute-start | bytes 786440 | tf_op jit(solution)/shard_map/ppermute | solution.py:27
  49.3 14.7 %collective-permute-start.19 = (bf16[512,256]{1,0:T(8,128)(2,1)S(1)}, bf16[512,256]{1,0:T(8,128)(2,1)S(1)}, u32[]{:S(2)}, u32[]{:S(2)}) collective-permute-start(bf16[512,256]{1,0:T(8,128)(2,1)S(1)} %copy-done.13), channel_id=1, source_target_pairs={{0,64},{1,65},{2,66},{3,67},{4,68},{5,69},{6,70},{7,71},{8,72},{9,... | collective-permute-start | bytes 786440 | tf_op jit(solution)/shard_map/ppermute | solution.py:27
  58.3 20.7 %collective-permute-start.18 = (bf16[2,768,256]{2,1,0:T(8,128)(2,1)}, bf16[2,768,256]{2,1,0:T(8,128)(2,1)S(1)}, u32[]{:S(2)}, u32[]{:S(2)}) collective-permute-start(bf16[2,768,256]{2,1,0:T(8,128)(2,1)} %get-tuple-element.47), channel_id=1, source_target_pairs={{0,4},{1,13},{2,6},{3,15},{4,8},{5,1},{6,10},{7,3},{8,12},{9,5},{1... | collective-permute-start | bytes 2359304 | tf_op jit(solution)/shard_map/ppermute | solution.py:27
  64.1 14.9 %collective-permute-start.21 = (bf16[2,512,256]{2,1,0:T(8,128)(2,1)S(1)}, bf16[2,512,256]{2,1,0:T(8,128)(2,1)S(1)}, u32[]{:S(2)}, u32[]{:S(2)}) collective-permute-start(bf16[2,512,256]{2,1,0:T(8,128)(2,1)S(1)} %pad_maximum_fusion.1.refs_16_), channel_id=1, source_target_pairs={{0,16},{1,17},{2,18},{3,19},{4,20},{5,21},{6,22},{7,23},{8,24},{9,... | collective-permute-start | bytes 1572872 | tf_op jit(solution)/shard_map/ppermute | solution.py:27
  64.2 14.8 %collective-permute-start.20 = (bf16[2,512,256]{2,1,0:T(8,128)(2,1)S(1)}, bf16[2,512,256]{2,1,0:T(8,128)(2,1)}, u32[]{:S(2)}, u32[]{:S(2)}) collective-permute-start(bf16[2,512,256]{2,1,0:T(8,128)(2,1)S(1)} %pad_maximum_fusion.1.refs_16_), channel_id=1, source_target_pairs={{0,48},{1,49},{2,50},{3,51},{4,52},{5,53},{6,54},{7,55},{8,56},{9,... | collective-permute-start | bytes 1572872 | tf_op jit(solution)/shard_map/ppermute | solution.py:27
  68.6 35.0 %collective-permute-start.1 = (bf16[768,128]{1,0:T(8,128)(2,1)}, bf16[768,128]{1,0:T(8,128)(2,1)}, u32[]{:S(2)}, u32[]{:S(2)}) collective-permute-start(bf16[768,128]{1,0:T(8,128)(2,1)} %constant_dynamic-slice_fusion.3), channel_id=1, source_target_pairs={{0,1},{1,0},{2,3},{3,2},{4,5},{5,4},{6,7},{7,6},{8,9},{9,8},{10,11... | collective-permute-start | bytes 589832 | tf_op jit(solution)/shard_map/ppermute | solution.py:27
  68.6 33.2 %collective-permute-start.22 = (bf16[2,768,256]{2,1,0:T(8,128)(2,1)}, bf16[2,768,256]{2,1,0:T(8,128)(2,1)}, u32[]{:S(2)}, u32[]{:S(2)}) collective-permute-start(bf16[2,768,256]{2,1,0:T(8,128)(2,1)} %get-tuple-element.54), channel_id=1, source_target_pairs={{0,12},{1,5},{2,14},{3,7},{4,0},{5,9},{6,2},{7,11},{8,4},{9,13},{1... | collective-permute-start | bytes 2359304 | tf_op jit(solution)/shard_map/ppermute | solution.py:27
  79.9 24.8 %collective-permute-start.25 = (bf16[2,512,256]{2,1,0:T(8,128)(2,1)}, bf16[2,512,256]{2,1,0:T(8,128)(2,1)}, u32[]{:S(2)}, u32[]{:S(2)}) collective-permute-start(bf16[2,512,256]{2,1,0:T(8,128)(2,1)} %broadcast_select_fusion), channel_id=1, source_target_pairs={{0,16},{1,49},{2,18},{3,51},{4,20},{5,53},{6,22},{7,55},{8,24},{9,... | collective-permute-start | bytes 1572872 | tf_op jit(solution)/shard_map/ppermute | solution.py:27
  80.3 21.5 %collective-permute-start.23 = (bf16[2,768,256]{2,1,0:T(8,128)(2,1)S(1)}, bf16[2,768,256]{2,1,0:T(8,128)(2,1)}, u32[]{:S(2)}, u32[]{:S(2)}) collective-permute-start(bf16[2,768,256]{2,1,0:T(8,128)(2,1)S(1)} %add_convert_fusion), channel_id=1, source_target_pairs={{0,4},{1,13},{2,6},{3,15},{4,8},{5,1},{6,10},{7,3},{8,12},{9,5},{1... | collective-permute-start | bytes 2359304 | tf_op jit(solution)/shard_map/ppermute | solution.py:27
  103.5 12.9 %collective-permute-start.24 = (bf16[768,256]{1,0:T(8,128)(2,1)S(1)}, bf16[768,256]{1,0:T(8,128)(2,1)S(1)}, u32[]{:S(2)}, u32[]{:S(2)}) collective-permute-start(bf16[768,256]{1,0:T(8,128)(2,1)S(1)} %fusion.8), channel_id=1, source_target_pairs={{0,2},{1,3},{2,0},{3,1},{4,6},{5,7},{6,4},{7,5},{8,10},{9,11},{10,... | collective-permute-start | bytes 1179656 | tf_op jit(solution)/shard_map/ppermute | solution.py:27
  116.7 12.1 %collective-permute-start.26 = (bf16[768,256]{1,0:T(8,128)(2,1)S(1)}, bf16[768,256]{1,0:T(8,128)(2,1)S(1)}, u32[]{:S(2)}, u32[]{:S(2)}) collective-permute-start(bf16[768,256]{1,0:T(8,128)(2,1)S(1)} %get-tuple-element.80.refs_0_), channel_id=1, source_target_pairs={{0,2},{1,3},{2,0},{3,1},{4,6},{5,7},{6,4},{7,5},{8,10},{9,11},{10,... | collective-permute-start | bytes 1179656 | tf_op jit(solution)/shard_map/ppermute | solution.py:27
  129.0 13.2 %collective-permute-start.31 = (bf16[768,256]{1,0:T(8,128)(2,1)S(1)}, bf16[768,256]{1,0:T(8,128)(2,1)S(1)}, u32[]{:S(2)}, u32[]{:S(2)}) collective-permute-start(bf16[768,256]{1,0:T(8,128)(2,1)S(1)} %get-tuple-element.80.refs_0_), channel_id=1, source_target_pairs={{0,4},{1,5},{2,6},{3,7},{4,8},{5,9},{6,10},{7,11},{8,12},{9,13},{1... | collective-permute-start | bytes 1179656 | tf_op jit(solution)/shard_map/ppermute | solution.py:27
  129.5 12.7 %collective-permute-start.27 = (bf16[768,256]{1,0:T(8,128)(2,1)S(1)}, bf16[768,256]{1,0:T(8,128)(2,1)S(1)}, u32[]{:S(2)}, u32[]{:S(2)}) collective-permute-start(bf16[768,256]{1,0:T(8,128)(2,1)S(1)} %get-tuple-element.80.refs_0_), channel_id=1, source_target_pairs={{0,12},{1,13},{2,14},{3,15},{4,0},{5,1},{6,2},{7,3},{8,4},{9,5},{1... | collective-permute-start | bytes 1179656 | tf_op jit(solution)/shard_map/ppermute | solution.py:27
  132.4 19.0 %collective-permute-start.35 = (bf16[768,256]{1,0:T(8,128)(2,1)S(1)}, bf16[768,256]{1,0:T(8,128)(2,1)S(1)}, u32[]{:S(2)}, u32[]{:S(2)}) collective-permute-start(bf16[768,256]{1,0:T(8,128)(2,1)S(1)} %get-tuple-element.80.refs_0_), channel_id=1, source_target_pairs={{0,1},{1,0},{2,3},{3,2},{4,5},{5,4},{6,7},{7,6},{8,9},{9,8},{10,11... | collective-permute-start | bytes 1179656 | tf_op jit(solution)/shard_map/ppermute | solution.py:27
  132.5 17.7 %collective-permute-start.32 = (bf16[768,256]{1,0:T(8,128)(2,1)S(1)}, bf16[768,256]{1,0:T(8,128)(2,1)S(1)}, u32[]{:S(2)}, u32[]{:S(2)}) collective-permute-start(bf16[768,256]{1,0:T(8,128)(2,1)S(1)} %collective-permute-done.26.refs_1_), channel_id=1, source_target_pairs={{0,4},{1,5},{2,6},{3,7},{4,8},{5,9},{6,10},{7,11},{8,12},{9,13},{1... | collective-permute-start | bytes 1179656 | tf_op jit(solution)/shard_map/ppermute | solution.py:27
  136.0 14.2 %collective-permute-start.28 = (bf16[768,256]{1,0:T(8,128)(2,1)S(1)}, bf16[768,256]{1,0:T(8,128)(2,1)S(1)}, u32[]{:S(2)}, u32[]{:S(2)}) collective-permute-start(bf16[768,256]{1,0:T(8,128)(2,1)S(1)} %collective-permute-done.26.refs_1_), channel_id=1, source_target_pairs={{0,12},{1,13},{2,14},{3,15},{4,0},{5,1},{6,2},{7,3},{8,4},{9,5},{1... | collective-permute-start | bytes 1179656 | tf_op jit(solution)/shard_map/ppermute | solution.py:27
  142.2 12.2 %collective-permute-start.33 = (bf16[768,256]{1,0:T(8,128)(2,1)S(1)}, bf16[768,256]{1,0:T(8,128)(2,1)S(1)}, u32[]{:S(2)}, u32[]{:S(2)}) collective-permute-start(bf16[768,256]{1,0:T(8,128)(2,1)S(1)} %broadcast_select_fusion.2), channel_id=1, source_target_pairs={{0,4},{1,13},{2,6},{3,15},{4,8},{5,1},{6,10},{7,3},{8,12},{9,5},{1... | collective-permute-start | bytes 1179656 | tf_op jit(solution)/shard_map/ppermute | solution.py:27
  142.9 11.4 %collective-permute-start.39 = (bf16[768,256]{1,0:T(8,128)(2,1)S(1)}, bf16[768,256]{1,0:T(8,128)(2,1)S(1)}, u32[]{:S(2)}, u32[]{:S(2)}) collective-permute-start(bf16[768,256]{1,0:T(8,128)(2,1)S(1)} %collective-permute-done.31.refs_4_), channel_id=1, source_target_pairs={{0,1},{1,0},{2,3},{3,2},{4,5},{5,4},{6,7},{7,6},{8,9},{9,8},{10,11... | collective-permute-start | bytes 1179656 | tf_op jit(solution)/shard_map/ppermute | solution.py:27
  150.2 9.5 %collective-permute-start.34 = (bf16[768,256]{1,0:T(8,128)(2,1)S(1)}, bf16[768,256]{1,0:T(8,128)(2,1)S(1)}, u32[]{:S(2)}, u32[]{:S(2)}) collective-permute-start(bf16[768,256]{1,0:T(8,128)(2,1)S(1)} %broadcast_select_fusion.1), channel_id=1, source_target_pairs={{0,4},{1,13},{2,6},{3,15},{4,8},{5,1},{6,10},{7,3},{8,12},{9,5},{1... | collective-permute-start | bytes 1179656 | tf_op jit(solution)/shard_map/ppermute | solution.py:27
  170.3 10.7 %collective-permute-start.43 = (bf16[2,512,256]{2,1,0:T(8,128)(2,1)}, bf16[2,512,256]{2,1,0:T(8,128)(2,1)S(1)}, u32[]{:S(2)}, u32[]{:S(2)}) collective-permute-start(bf16[2,512,256]{2,1,0:T(8,128)(2,1)} %get-tuple-element.65), channel_id=1, source_target_pairs={{0,16},{1,49},{2,18},{3,51},{4,20},{5,53},{6,22},{7,55},{8,24},{9,... | collective-permute-start | bytes 1572872 | tf_op jit(solution)/shard_map/ppermute | solution.py:27
  181.1 20.8 %collective-permute-start.45 = (bf16[2,512,256]{2,1,0:T(8,128)(2,1)S(1)}, bf16[2,512,256]{2,1,0:T(8,128)(2,1)S(1)}, u32[]{:S(2)}, u32[]{:S(2)}) collective-permute-start(bf16[2,512,256]{2,1,0:T(8,128)(2,1)S(1)} %add_convert_fusion.1), channel_id=1, source_target_pairs={{0,16},{1,49},{2,18},{3,51},{4,20},{5,53},{6,22},{7,55},{8,24},{9,... | collective-permute-start | bytes 1572872 | tf_op jit(solution)/shard_map/ppermute | solution.py:27
  181.6 20.4 %collective-permute-start.44 = (bf16[2,512,256]{2,1,0:T(8,128)(2,1)S(1)}, bf16[2,512,256]{2,1,0:T(8,128)(2,1)S(1)}, u32[]{:S(2)}, u32[]{:S(2)}) collective-permute-start(bf16[2,512,256]{2,1,0:T(8,128)(2,1)S(1)} %copy-done.18), channel_id=1, source_target_pairs={{0,48},{1,17},{2,50},{3,19},{4,52},{5,21},{6,54},{7,23},{8,56},{9,... | collective-permute-start | bytes 1572872 | tf_op jit(solution)/shard_map/ppermute | solution.py:27
  184.4 12.0 %collective-permute-start.46 = (f32[5,128]{1,0:T(8,128)S(1)}, f32[5,128]{1,0:T(8,128)S(1)}, u32[]{:S(2)}, u32[]{:S(2)}) collective-permute-start(f32[5,128]{1,0:T(8,128)S(1)} %fusion.15), channel_id=1, source_target_pairs={{0,32},{1,33},{2,34},{3,35},{4,36},{5,37},{6,38},{7,39},{8,40},{9,... | collective-permute-start | bytes 7688 | tf_op jit(solution)/shard_map/ppermute | solution.py:27
  (56 other events, 423.4 us)
Sparse Core Ops, SparseCore 0:
  10.3 83.8 all-gather.1
  128.9 41.6 reduce-scatter.1

commit v8 on v7

--- a/solution.py
+++ b/solution.py
@@ -288,10 +288,9 @@
     passed, own, in_above, in_below = tie(passed, own, in_above, in_below)
     further = x_split(add([further, passed]).astype(BF16), 1)
     in_across = onward(in_above, in_below, core, z_split)
+    total = add([own, back, further])
     wout = dot(hidden_full, grad_conv, 0, 0).astype(BF16)
-    further, wout = tie(further, wout)
-    total = add([own, back, further])
-    crossed, in_across = tie(y_hi_swap(total[1].astype(BF16)), in_across)
+    crossed, wout, in_across = tie(y_hi_swap(total[1].astype(BF16)), wout, in_across)
     in_blocks = [in_here, in_above, in_below, in_across]
     grad_hid = add([total[0], crossed])
     alive = (pre_chip > 0) & (gain_chip[1] > 0)[None, :]
@@ -309,7 +308,6 @@
     mid_own = mid_own + core_swap(mid_away)
     sums = jnp.concatenate([mid_own, wide_part]).reshape(5, 128)
     sums = sums + z_flip(sums, 1)
-    near_above, sums = tie(near_above, sums)
     sums = sums + z_flip(sums, 2)
     sums = sums + y_lo_swap(sums)
 
@@ -319,6 +317,7 @@
         grad_act, act_near, act_above, near_above, act_below, near_below, act_across, near_across
     ]
     act_beside = [core_swap(block) for block in act]
+    act[7], sums = tie(act[7], sums)
 
     away, there, further, own = win_partial(place, input_turned, act, act_beside)
     passed, back = z_split(away, 1), z_split(there, -1)
@@ -326,7 +325,7 @@
     passed, grad_x = tie(passed, grad_x)
     further = z_split(add([further, passed]).astype(BF16), 1)
     grad_wout = wout.astype(F32) * scaling
-    further, grad_wout, sums = tie(further, grad_wout, sums)
+    further, grad_wout = tie(further, grad_wout)
     total = add([own, back, further])
     grad_win = add([total[0], y_lo_swap(total[1].astype(BF16))]) * scaling
     grad_smid = keep_mid.astype(F32) * scaling * sums[0]

time: 217 us -> 214 us (0.986)
  waiting for transfers between devices: 95.6 us -> 78.3 us
  starting transfers between devices: 41.1 us -> 53.5 us
    ppermute x49, starting transfers between devices: 41 us -> 53.4 us  [permute(): return lax.ppermute(v, AXES, pairs)]
    all_gather x1, waiting for transfers between devices: 12.3 us -> 0.01 us  [local(): hidden_full = lax.all_gather(hidden, 'col', axis=1, tiled=True)]
    ppermute x49, waiting for transfers between devices: 83.2 us -> 78.2 us  [permute(): return lax.ppermute(v, AXES, pairs)]
    unnamed x75 -> x71, local copies, waits for them, and re-layouts: 4.91 us -> 5.46 us
  transfers between devices with their start and end apart: 51 -> 51, of which waited for: 18 -> 22; matrix products, arithmetic and copies ran while one was open for 12% -> 13% of each run, Pallas kernels for 14% -> 15%
where the time goes in v8:
time: 214 us; the launch traced here: 213 us
  waiting for transfers between devices  78.3 us (37%)
  starting transfers between devices  53.5 us (25%)
  Pallas kernels  31.2 us (15%)
  other arithmetic  20.5 us (10%)
  between operations  14.6 us (7%)
  matrix products  7.68 us (4%)
  local copies, waits for them, and re-layouts  7.28 us (3%)
    ppermute x49, waiting for transfers between devices, permute(): return lax.ppermute(v, AXES, pairs)  78.2 us
    ppermute x49, starting transfers between devices, permute(): return lax.ppermute(v, AXES, pairs)  53.4 us
    pallas_call x4, Pallas kernels, call(): pl.pallas_call(body, out_shape=outs, in_specs=[pl.BlockSpec(memory_space=...  31.2 us
    dot_general x1, matrix products, dot(): lax.dot_general(a, b, (((ca,), (cb,)), ((), ())), preferred_element_type=...  7.68 us
    unnamed x71, local copies, waits for them, and re-layouts  5.46 us
  transfers between devices with their start and end apart: 51, of which 22 were waited for; matrix products, arithmetic and copies ran while one was open for 13% of the time, Pallas kernels for 15%

profile of v8, /device:TPU:0, one launch (start us, length us, event | category | flops | bytes accessed | tf_op | source)
XLA Modules:
  0.0 213.0 jit_solution(483306545384370283)
XLA Ops:
  12.3 2.7 %fusion.1 = (f32[512]{0:T(512)S(1)}, bf16[1536,512]{1,0:T(8,128)(2,1)S(1)}) fusion(bf16[1536,512]{1,0:T(8,128)(2,1)} %cot.1, bf16[1536,512]{1,0:T(8,128)(2,1)} %param.12, f32[512]{0:T(512)S(1)} %convert_multiply_fusion.4), kind=kLoop, calls=%fused_computation.3 | loop fusion | flops 4718080 | bytes 4722688 | tf_op jit(solution)/shard_map/reduce_sum | solution.py:250
  18.2 2.1 collective-permute-start.6
  20.3 2.1 collective-permute-start.5
  22.6 7.2 %collective-permute-done.6.refs_4_ = bf16[256,512]{1,0:T(8,128)(2,1)} collective-permute-done((bf16[256,512]{1,0:T(8,128)(2,1)}, bf16[256,512]{1,0:T(8,128)(2,1)}, u32[]{:S(2)}, u32[]{:S(2)}) %collective-permute-start.6) | collective-permute-done | bytes 262176 | tf_op jit(solution)/shard_map/ppermute | solution.py:27
  29.9 1.9 collective-permute-start.3
  34.5 4.9 %collective-permute-done.3.refs_3_ = bf16[256,512]{1,0:T(8,128)(2,1)} collective-permute-done((bf16[256,512]{1,0:T(8,128)(2,1)}, bf16[256,512]{1,0:T(8,128)(2,1)}, u32[]{:S(2)}, u32[]{:S(2)}) %collective-permute-start.3) | collective-permute-done | bytes 262176 | tf_op jit(solution)/shard_map/ppermute | solution.py:27
  40.5 3.4 %collective-permute-start.11 = (bf16[256,512]{1,0:T(8,128)(2,1)}, bf16[256,512]{1,0:T(8,128)(2,1)S(1)}, u32[]{:S(2)}, u32[]{:S(2)}) collective-permute-start(bf16[256,512]{1,0:T(8,128)(2,1)} %collective-permute-done.refs_1_), channel_id=1, source_target_pairs={{0,1},{1,0},{2,3},{3,2},{4,5},{5,4},{6,7},{7,6},{8,9},{9,8},{10,11... | collective-permute-start | bytes 786440 | tf_op jit(solution)/shard_map/ppermute | solution.py:27
  44.5 3.5 %collective-permute-done.9.refs_7_ = bf16[256,512]{1,0:T(8,128)(2,1)S(1)} collective-permute-done((bf16[256,512]{1,0:T(8,128)(2,1)S(1)}, bf16[256,512]{1,0:T(8,128)(2,1)S(1)}, u32[]{:S(2)}, u32[]{:S(2)}) %collective-permute-start.9) | collective-permute-done | bytes 262176 | tf_op jit(solution)/shard_map/ppermute | solution.py:27
  51.8 6.4 %shard_map.137 = (bf16[2,768,256]{2,1,0:T(8,128)(2,1)}, bf16[2,768,256]{2,1,0:T(8,128)(2,1)}) custom-call(s32[2]{0:T(128)} %pad_add_fusion.here, bf16[768,1024]{1,0:T(8,128)(2,1)} %pad_maximum_fusion.conv, bf16[256,512]{1,0:T(8,128)(2,1)} %refs_0_.3, bf16[256,512]{1,0:T(8,128)(2,1)} %collective-permute-done.refs_1_, bf16[256,512]{1,0:T(8,128)(2,1)} %copy-done.13, ...), custom_call_target="tpu_custom_call" | custom-call | flops 1610612736 | bytes 8388608 | tf_op jit(solution)/shard_map/pallas_call | solution.py:90
  59.8 3.6 %collective-permute-done.19 = bf16[512,256]{1,0:T(8,128)(2,1)S(1)} collective-permute-done((bf16[512,256]{1,0:T(8,128)(2,1)S(1)}, bf16[512,256]{1,0:T(8,128)(2,1)S(1)}, u32[]{:S(2)}, u32[]{:S(2)}) %collective-permute-start.19) | collective-permute-done | bytes 262176 | tf_op jit(solution)/shard_map/ppermute | solution.py:27
  63.6 3.2 %collective-permute-start.20 = (bf16[2,512,256]{2,1,0:T(8,128)(2,1)S(1)}, bf16[2,512,256]{2,1,0:T(8,128)(2,1)}, u32[]{:S(2)}, u32[]{:S(2)}) collective-permute-start(bf16[2,512,256]{2,1,0:T(8,128)(2,1)S(1)} %pad_maximum_fusion.1.refs_16_), channel_id=1, source_target_pairs={{0,48},{1,49},{2,50},{3,51},{4,52},{5,53},{6,54},{7,55},{8,56},{9,... | collective-permute-start | bytes 1572872 | tf_op jit(solution)/shard_map/ppermute | solution.py:27
  68.1 3.0 %collective-permute-start.22 = (bf16[2,768,256]{2,1,0:T(8,128)(2,1)}, bf16[2,768,256]{2,1,0:T(8,128)(2,1)S(1)}, u32[]{:S(2)}, u32[]{:S(2)}) collective-permute-start(bf16[2,768,256]{2,1,0:T(8,128)(2,1)} %get-tuple-element.52), channel_id=1, source_target_pairs={{0,12},{1,5},{2,14},{3,7},{4,0},{5,9},{6,2},{7,11},{8,4},{9,13},{1... | collective-permute-start | bytes 2359304 | tf_op jit(solution)/shard_map/ppermute | solution.py:27
  71.1 6.6 %shard_map.138 = (bf16[2,768,256]{2,1,0:T(8,128)(2,1)}, bf16[2,768,256]{2,1,0:T(8,128)(2,1)}) custom-call(s32[2]{0:T(128)} %pad_add_fusion.here, bf16[768,1024]{1,0:T(8,128)(2,1)} %pad_maximum_fusion.conv, bf16[256,512]{1,0:T(8,128)(2,1)} %refs_0_.3, bf16[256,512]{1,0:T(8,128)(2,1)} %collective-permute-done.refs_1_, bf16[256,512]{1,0:T(8,128)(2,1)} %copy-done.13, ...), custom_call_target="tpu_custom_call" | custom-call | flops 1610612736 | bytes 8388608 | tf_op jit(solution)/shard_map/pallas_call | solution.py:90
  83.0 2.1 broadcast_select_fusion
  85.0 7.7 %collective-permute-done.22 = bf16[2,768,256]{2,1,0:T(8,128)(2,1)S(1)} collective-permute-done((bf16[2,768,256]{2,1,0:T(8,128)(2,1)}, bf16[2,768,256]{2,1,0:T(8,128)(2,1)S(1)}, u32[]{:S(2)}, u32[]{:S(2)}) %collective-permute-start.22) | collective-permute-done | bytes 786464 | tf_op jit(solution)/shard_map/ppermute | solution.py:27
  93.6 4.2 %collective-permute-done.23 = bf16[2,768,256]{2,1,0:T(8,128)(2,1)S(1)} collective-permute-done((bf16[2,768,256]{2,1,0:T(8,128)(2,1)S(1)}, bf16[2,768,256]{2,1,0:T(8,128)(2,1)S(1)}, u32[]{:S(2)}, u32[]{:S(2)}) %collective-permute-start.23) | collective-permute-done | bytes 786464 | tf_op jit(solution)/shard_map/ppermute | solution.py:27
  100.0 3.2 %collective-permute-start.24 = (bf16[768,256]{1,0:T(8,128)(2,1)}, bf16[768,256]{1,0:T(8,128)(2,1)}, u32[]{:S(2)}, u32[]{:S(2)}) collective-permute-start(bf16[768,256]{1,0:T(8,128)(2,1)} %fusion.8), channel_id=1, source_target_pairs={{0,2},{1,3},{2,0},{3,1},{4,6},{5,7},{6,4},{7,5},{8,10},{9,11},{10,... | collective-permute-start | bytes 1179656 | tf_op jit(solution)/shard_map/ppermute | solution.py:27
  103.2 7.7 %convolution_convert_fusion = bf16[2048,512]{1,0:T(8,128)(2,1)} fusion(bf16[1536,2048]{1,0:T(8,128)(2,1)} %all-gather.2.cloned.1.call-done, bf16[1536,512]{1,0:T(8,128)(2,1)S(1)} %get-tuple-element.80), kind=kOutput, calls=%fused_computation.4 | convolution fusion | flops 3222274048 | bytes 9961472 | tf_op jit(solution)/shard_map/dot_general | solution.py:63
  110.9 1.9 collective-permute-done.24
  114.1 2.8 %collective-permute-start.26 = (bf16[768,256]{1,0:T(8,128)(2,1)S(1)}, bf16[768,256]{1,0:T(8,128)(2,1)S(1)}, u32[]{:S(2)}, u32[]{:S(2)}) collective-permute-start(bf16[768,256]{1,0:T(8,128)(2,1)S(1)} %get-tuple-element.76.refs_0_), channel_id=1, source_target_pairs={{0,2},{1,3},{2,0},{3,1},{4,6},{5,7},{6,4},{7,5},{8,10},{9,11},{10,... | collective-permute-start | bytes 1179656 | tf_op jit(solution)/shard_map/ppermute | solution.py:27
  117.0 8.9 %collective-permute-done.26.refs_1_ = bf16[768,256]{1,0:T(8,128)(2,1)S(1)} collective-permute-done((bf16[768,256]{1,0:T(8,128)(2,1)S(1)}, bf16[768,256]{1,0:T(8,128)(2,1)S(1)}, u32[]{:S(2)}, u32[]{:S(2)}) %collective-permute-start.26) | collective-permute-done | bytes 393248 | tf_op jit(solution)/shard_map/ppermute | solution.py:27
  130.8 3.4 %collective-permute-start.35 = (f32[5,128]{1,0:T(8,128)S(1)}, f32[5,128]{1,0:T(8,128)S(1)}, u32[]{:S(2)}, u32[]{:S(2)}) collective-permute-start(f32[5,128]{1,0:T(8,128)S(1)} %fusion.15), channel_id=1, source_target_pairs={{0,32},{1,33},{2,34},{3,35},{4,36},{5,37},{6,38},{7,39},{8,40},{9,... | collective-permute-start | bytes 7688 | tf_op jit(solution)/shard_map/ppermute | solution.py:27
  135.9 3.2 %collective-permute-start.28 = (bf16[768,256]{1,0:T(8,128)(2,1)S(1)}, bf16[768,256]{1,0:T(8,128)(2,1)S(1)}, u32[]{:S(2)}, u32[]{:S(2)}) collective-permute-start(bf16[768,256]{1,0:T(8,128)(2,1)S(1)} %collective-permute-done.26.refs_1_), channel_id=1, source_target_pairs={{0,12},{1,13},{2,14},{3,15},{4,0},{5,1},{6,2},{7,3},{8,4},{9,5},{1... | collective-permute-start | bytes 1179656 | tf_op jit(solution)/shard_map/ppermute | solution.py:27
  142.6 5.9 %collective-permute-done.30.refs_5_ = bf16[768,256]{1,0:T(8,128)(2,1)S(1)} collective-permute-done((bf16[768,256]{1,0:T(8,128)(2,1)S(1)}, bf16[768,256]{1,0:T(8,128)(2,1)S(1)}, u32[]{:S(2)}, u32[]{:S(2)}) %collective-permute-start.30) | collective-permute-done | bytes 393248 | tf_op jit(solution)/shard_map/ppermute | solution.py:27
  153.5 4.9 %collective-permute-done.32.refs_7_ = bf16[768,256]{1,0:T(8,128)(2,1)S(1)} collective-permute-done((bf16[768,256]{1,0:T(8,128)(2,1)S(1)}, bf16[768,256]{1,0:T(8,128)(2,1)S(1)}, u32[]{:S(2)}, u32[]{:S(2)}) %collective-permute-start.32) | collective-permute-done | bytes 393248 | tf_op jit(solution)/shard_map/ppermute | solution.py:27
  160.4 8.6 %shard_map.139 = (bf16[2,512,256]{2,1,0:T(8,128)(2,1)}, bf16[2,512,256]{2,1,0:T(8,128)(2,1)}, bf16[2,512,256]{2,1,0:T(8,128)(2,1)}, bf16[2,512,256]{2,1,0:T(8,128)(2,1)}) custom-call(s32[2]{0:T(128)} %pad_add_fusion.here, bf16[512,1536]{1,0:T(8,128)(2,1)} %bitcast.48, bf16[768,256]{1,0:T(8,128)(2,1)} %copy-done.7, bf16[768,256]{1,0:T(8,128)(2,1)} %copy-done.18, ...), custom_call_target="tpu_custom_call" | custom-call | flops 3221225472 | bytes 10485760 | tf_op jit(solution)/shard_map/pallas_call | solution.py:90
  169.0 2.1 collective-permute-start.45
  171.1 9.5 %shard_map.140 = bf16[1536,512]{1,0:T(8,128)(2,1)} custom-call(s32[2]{0:T(128)} %pad_add_fusion.here, bf16[1536,512]{1,0:T(8,128)(2,1)} %cot.1, bf16[768,256]{1,0:T(8,128)(2,1)} %copy-done.7, bf16[768,256]{1,0:T(8,128)(2,1)} %copy-done.18, bf16[768,256]{1,0:T(8,128)(2,1)} %copy-done.9, bf16[768,256]{1,0:T(8,128)(2,1)} %copy-done.11, ...), custom_call_target="tpu_custom_call" | custom-call | flops 3221225472 | bytes 12582912 | tf_op jit(solution)/shard_map/pallas_call | solution.py:90
  181.9 2.2 %collective-permute-start.46 = (bf16[2,512,256]{2,1,0:T(8,128)(2,1)S(1)}, bf16[2,512,256]{2,1,0:T(8,128)(2,1)S(1)}, u32[]{:S(2)}, u32[]{:S(2)}) collective-permute-start(bf16[2,512,256]{2,1,0:T(8,128)(2,1)S(1)} %copy-done.17), channel_id=1, source_target_pairs={{0,48},{1,17},{2,50},{3,19},{4,52},{5,21},{6,54},{7,23},{8,56},{9,... | collective-permute-start | bytes 1572872 | tf_op jit(solution)/shard_map/ppermute | solution.py:27
  185.9 10.6 %collective-permute-done.47 = bf16[2,512,256]{2,1,0:T(8,128)(2,1)S(1)} collective-permute-done((bf16[2,512,256]{2,1,0:T(8,128)(2,1)S(1)}, bf16[2,512,256]{2,1,0:T(8,128)(2,1)S(1)}, u32[]{:S(2)}, u32[]{:S(2)}) %collective-permute-start.47) | collective-permute-done | bytes 524320 | tf_op jit(solution)/shard_map/ppermute | solution.py:27
  196.8 2.0 collective-permute-start.48
  199.9 5.5 %collective-permute-done.48 = bf16[512,256]{1,0:T(8,128)(2,1)S(1)} collective-permute-done((bf16[512,256]{1,0:T(8,128)(2,1)S(1)}, bf16[512,256]{1,0:T(8,128)(2,1)S(1)}, u32[]{:S(2)}, u32[]{:S(2)}) %collective-permute-start.48) | collective-permute-done | bytes 262176 | tf_op jit(solution)/shard_map/ppermute | solution.py:27
  (185 shorter events, 51.3 us)
Async XLA Ops:
  7.2 96.0 %all-gather.2.cloned.1.call-start = ((), (), s32[]{:S(2)}) async-start(), calls=%async_computation.1 | async-start | bytes 6684672 | tf_op jit(solution)/shard_map/all_gather | solution.py:243
  9.8 174.3 %reduce-scatter.2.cloned.1.call-start = ((), (), s32[]{:S(2)}) async-start(), calls=%async_computation.2 | async-start | bytes 2359296 | tf_op jit(solution)/shard_map/reduce_scatter | solution.py:303
  9.8 8.4 %collective-permute-start = (bf16[256,512]{1,0:T(8,128)(2,1)}, bf16[256,512]{1,0:T(8,128)(2,1)}, u32[]{:S(2)}, u32[]{:S(2)}) collective-permute-start(bf16[256,512]{1,0:T(8,128)(2,1)} %refs_0_.3), channel_id=1, source_target_pairs={{0,64},{1,65},{2,66},{3,67},{4,68},{5,69},{6,70},{7,71},{8,72},{9,... | collective-permute-start | bytes 786440 | tf_op jit(solution)/shard_map/ppermute | solution.py:27
  18.2 14.9 %collective-permute-start.4 = (bf16[768,512]{1,0:T(8,128)(2,1)}, bf16[768,512]{1,0:T(8,128)(2,1)S(1)}, u32[]{:S(2)}, u32[]{:S(2)}) collective-permute-start(bf16[768,512]{1,0:T(8,128)(2,1)} %get-tuple-element.42), channel_id=1, source_target_pairs={{0,1},{1,0},{2,3},{3,2},{4,5},{5,4},{6,7},{7,6},{8,9},{9,8},{10,11... | collective-permute-start | bytes 2359304 | tf_op jit(solution)/shard_map/ppermute | solution.py:27
  18.2 11.7 %collective-permute-start.6 = (bf16[256,512]{1,0:T(8,128)(2,1)}, bf16[256,512]{1,0:T(8,128)(2,1)}, u32[]{:S(2)}, u32[]{:S(2)}) collective-permute-start(bf16[256,512]{1,0:T(8,128)(2,1)} %refs_0_.3), channel_id=1, source_target_pairs={{0,16},{1,17},{2,18},{3,19},{4,20},{5,21},{6,22},{7,23},{8,24},{9,... | collective-permute-start | bytes 786440 | tf_op jit(solution)/shard_map/ppermute | solution.py:27
  20.3 11.5 %collective-permute-start.5 = (bf16[256,512]{1,0:T(8,128)(2,1)}, bf16[256,512]{1,0:T(8,128)(2,1)S(1)}, u32[]{:S(2)}, u32[]{:S(2)}) collective-permute-start(bf16[256,512]{1,0:T(8,128)(2,1)} %refs_0_.3), channel_id=1, source_target_pairs={{0,48},{1,49},{2,50},{3,51},{4,52},{5,53},{6,54},{7,55},{8,56},{9,... | collective-permute-start | bytes 786440 | tf_op jit(solution)/shard_map/ppermute | solution.py:27
  22.4 18.1 %collective-permute-start.10 = (bf16[256,512]{1,0:T(8,128)(2,1)}, bf16[256,512]{1,0:T(8,128)(2,1)}, u32[]{:S(2)}, u32[]{:S(2)}) collective-permute-start(bf16[256,512]{1,0:T(8,128)(2,1)} %refs_0_.3), channel_id=1, source_target_pairs={{0,1},{1,0},{2,3},{3,2},{4,5},{5,4},{6,7},{7,6},{8,9},{9,8},{10,11... | collective-permute-start | bytes 786440 | tf_op jit(solution)/shard_map/ppermute | solution.py:27
  22.6 16.8 %collective-permute-start.7 = (bf16[256,512]{1,0:T(8,128)(2,1)}, bf16[256,512]{1,0:T(8,128)(2,1)}, u32[]{:S(2)}, u32[]{:S(2)}) collective-permute-start(bf16[256,512]{1,0:T(8,128)(2,1)} %collective-permute-done.refs_1_), channel_id=1, source_target_pairs={{0,16},{1,17},{2,18},{3,19},{4,20},{5,21},{6,22},{7,23},{8,24},{9,... | collective-permute-start | bytes 786440 | tf_op jit(solution)/shard_map/ppermute | solution.py:27
  29.9 9.5 %collective-permute-start.3 = (bf16[256,512]{1,0:T(8,128)(2,1)}, bf16[256,512]{1,0:T(8,128)(2,1)}, u32[]{:S(2)}, u32[]{:S(2)}) collective-permute-start(bf16[256,512]{1,0:T(8,128)(2,1)} %collective-permute-done.refs_1_), channel_id=1, source_target_pairs={{0,48},{1,49},{2,50},{3,51},{4,52},{5,53},{6,54},{7,55},{8,56},{9,... | collective-permute-start | bytes 786440 | tf_op jit(solution)/shard_map/ppermute | solution.py:27
  32.9 11.1 %collective-permute-start.8 = (bf16[256,512]{1,0:T(8,128)(2,1)S(1)}, bf16[256,512]{1,0:T(8,128)(2,1)}, u32[]{:S(2)}, u32[]{:S(2)}) collective-permute-start(bf16[256,512]{1,0:T(8,128)(2,1)S(1)} %broadcast_select_fusion.4), channel_id=1, source_target_pairs={{0,16},{1,49},{2,18},{3,51},{4,20},{5,53},{6,22},{7,55},{8,24},{9,... | collective-permute-start | bytes 786440 | tf_op jit(solution)/shard_map/ppermute | solution.py:27
  33.0 10.8 %collective-permute-start.14 = (bf16[256,512]{1,0:T(8,128)(2,1)}, bf16[256,512]{1,0:T(8,128)(2,1)S(1)}, u32[]{:S(2)}, u32[]{:S(2)}) collective-permute-start(bf16[256,512]{1,0:T(8,128)(2,1)} %collective-permute-done.6.refs_4_), channel_id=1, source_target_pairs={{0,1},{1,0},{2,3},{3,2},{4,5},{5,4},{6,7},{7,6},{8,9},{9,8},{10,11... | collective-permute-start | bytes 786440 | tf_op jit(solution)/shard_map/ppermute | solution.py:27
  48.8 14.7 %collective-permute-start.19 = (bf16[512,256]{1,0:T(8,128)(2,1)S(1)}, bf16[512,256]{1,0:T(8,128)(2,1)S(1)}, u32[]{:S(2)}, u32[]{:S(2)}) collective-permute-start(bf16[512,256]{1,0:T(8,128)(2,1)S(1)} %copy-done.12), channel_id=1, source_target_pairs={{0,64},{1,65},{2,66},{3,67},{4,68},{5,69},{6,70},{7,71},{8,72},{9,... | collective-permute-start | bytes 786440 | tf_op jit(solution)/shard_map/ppermute | solution.py:27
  58.3 20.2 %collective-permute-start.18 = (bf16[2,768,256]{2,1,0:T(8,128)(2,1)}, bf16[2,768,256]{2,1,0:T(8,128)(2,1)S(1)}, u32[]{:S(2)}, u32[]{:S(2)}) collective-permute-start(bf16[2,768,256]{2,1,0:T(8,128)(2,1)} %get-tuple-element.45), channel_id=1, source_target_pairs={{0,4},{1,13},{2,6},{3,15},{4,8},{5,1},{6,10},{7,3},{8,12},{9,5},{1... | collective-permute-start | bytes 2359304 | tf_op jit(solution)/shard_map/ppermute | solution.py:27
  63.5 14.9 %collective-permute-start.21 = (bf16[2,512,256]{2,1,0:T(8,128)(2,1)S(1)}, bf16[2,512,256]{2,1,0:T(8,128)(2,1)}, u32[]{:S(2)}, u32[]{:S(2)}) collective-permute-start(bf16[2,512,256]{2,1,0:T(8,128)(2,1)S(1)} %pad_maximum_fusion.1.refs_16_), channel_id=1, source_target_pairs={{0,16},{1,17},{2,18},{3,19},{4,20},{5,21},{6,22},{7,23},{8,24},{9,... | collective-permute-start | bytes 1572872 | tf_op jit(solution)/shard_map/ppermute | solution.py:27
  63.6 14.9 %collective-permute-start.20 = (bf16[2,512,256]{2,1,0:T(8,128)(2,1)S(1)}, bf16[2,512,256]{2,1,0:T(8,128)(2,1)}, u32[]{:S(2)}, u32[]{:S(2)}) collective-permute-start(bf16[2,512,256]{2,1,0:T(8,128)(2,1)S(1)} %pad_maximum_fusion.1.refs_16_), channel_id=1, source_target_pairs={{0,48},{1,49},{2,50},{3,51},{4,52},{5,53},{6,54},{7,55},{8,56},{9,... | collective-permute-start | bytes 1572872 | tf_op jit(solution)/shard_map/ppermute | solution.py:27
  68.1 24.7 %collective-permute-start.22 = (bf16[2,768,256]{2,1,0:T(8,128)(2,1)}, bf16[2,768,256]{2,1,0:T(8,128)(2,1)S(1)}, u32[]{:S(2)}, u32[]{:S(2)}) collective-permute-start(bf16[2,768,256]{2,1,0:T(8,128)(2,1)} %get-tuple-element.52), channel_id=1, source_target_pairs={{0,12},{1,5},{2,14},{3,7},{4,0},{5,9},{6,2},{7,11},{8,4},{9,13},{1... | collective-permute-start | bytes 2359304 | tf_op jit(solution)/shard_map/ppermute | solution.py:27
  79.8 18.0 %collective-permute-start.23 = (bf16[2,768,256]{2,1,0:T(8,128)(2,1)S(1)}, bf16[2,768,256]{2,1,0:T(8,128)(2,1)S(1)}, u32[]{:S(2)}, u32[]{:S(2)}) collective-permute-start(bf16[2,768,256]{2,1,0:T(8,128)(2,1)S(1)} %add_convert_fusion), channel_id=1, source_target_pairs={{0,4},{1,13},{2,6},{3,15},{4,8},{5,1},{6,10},{7,3},{8,12},{9,5},{1... | collective-permute-start | bytes 2359304 | tf_op jit(solution)/shard_map/ppermute | solution.py:27
  85.0 25.8 %collective-permute-start.25 = (bf16[2,512,256]{2,1,0:T(8,128)(2,1)}, bf16[2,512,256]{2,1,0:T(8,128)(2,1)}, u32[]{:S(2)}, u32[]{:S(2)}) collective-permute-start(bf16[2,512,256]{2,1,0:T(8,128)(2,1)} %broadcast_select_fusion), channel_id=1, source_target_pairs={{0,16},{1,49},{2,18},{3,51},{4,20},{5,53},{6,22},{7,55},{8,24},{9,... | collective-permute-start | bytes 1572872 | tf_op jit(solution)/shard_map/ppermute | solution.py:27
  100.0 12.8 %collective-permute-start.24 = (bf16[768,256]{1,0:T(8,128)(2,1)}, bf16[768,256]{1,0:T(8,128)(2,1)}, u32[]{:S(2)}, u32[]{:S(2)}) collective-permute-start(bf16[768,256]{1,0:T(8,128)(2,1)} %fusion.8), channel_id=1, source_target_pairs={{0,2},{1,3},{2,0},{3,1},{4,6},{5,7},{6,4},{7,5},{8,10},{9,11},{10,... | collective-permute-start | bytes 1179656 | tf_op jit(solution)/shard_map/ppermute | solution.py:27
  114.1 11.7 %collective-permute-start.26 = (bf16[768,256]{1,0:T(8,128)(2,1)S(1)}, bf16[768,256]{1,0:T(8,128)(2,1)S(1)}, u32[]{:S(2)}, u32[]{:S(2)}) collective-permute-start(bf16[768,256]{1,0:T(8,128)(2,1)S(1)} %get-tuple-element.76.refs_0_), channel_id=1, source_target_pairs={{0,2},{1,3},{2,0},{3,1},{4,6},{5,7},{6,4},{7,5},{8,10},{9,11},{10,... | collective-permute-start | bytes 1179656 | tf_op jit(solution)/shard_map/ppermute | solution.py:27
  127.2 13.2 %collective-permute-start.29 = (bf16[768,256]{1,0:T(8,128)(2,1)S(1)}, bf16[768,256]{1,0:T(8,128)(2,1)S(1)}, u32[]{:S(2)}, u32[]{:S(2)}) collective-permute-start(bf16[768,256]{1,0:T(8,128)(2,1)S(1)} %get-tuple-element.76.refs_0_), channel_id=1, source_target_pairs={{0,4},{1,5},{2,6},{3,7},{4,8},{5,9},{6,10},{7,11},{8,12},{9,13},{1... | collective-permute-start | bytes 1179656 | tf_op jit(solution)/shard_map/ppermute | solution.py:27
  128.9 13.2 %collective-permute-start.27 = (bf16[768,256]{1,0:T(8,128)(2,1)S(1)}, bf16[768,256]{1,0:T(8,128)(2,1)S(1)}, u32[]{:S(2)}, u32[]{:S(2)}) collective-permute-start(bf16[768,256]{1,0:T(8,128)(2,1)S(1)} %get-tuple-element.76.refs_0_), channel_id=1, source_target_pairs={{0,12},{1,13},{2,14},{3,15},{4,0},{5,1},{6,2},{7,3},{8,4},{9,5},{1... | collective-permute-start | bytes 1179656 | tf_op jit(solution)/shard_map/ppermute | solution.py:27
  134.2 16.8 %collective-permute-start.37 = (bf16[768,256]{1,0:T(8,128)(2,1)S(1)}, bf16[768,256]{1,0:T(8,128)(2,1)S(1)}, u32[]{:S(2)}, u32[]{:S(2)}) collective-permute-start(bf16[768,256]{1,0:T(8,128)(2,1)S(1)} %get-tuple-element.76.refs_0_), channel_id=1, source_target_pairs={{0,1},{1,0},{2,3},{3,2},{4,5},{5,4},{6,7},{7,6},{8,9},{9,8},{10,11... | collective-permute-start | bytes 1179656 | tf_op jit(solution)/shard_map/ppermute | solution.py:27
  134.2 14.3 %collective-permute-start.30 = (bf16[768,256]{1,0:T(8,128)(2,1)S(1)}, bf16[768,256]{1,0:T(8,128)(2,1)S(1)}, u32[]{:S(2)}, u32[]{:S(2)}) collective-permute-start(bf16[768,256]{1,0:T(8,128)(2,1)S(1)} %collective-permute-done.26.refs_1_), channel_id=1, source_target_pairs={{0,4},{1,5},{2,6},{3,7},{4,8},{5,9},{6,10},{7,11},{8,12},{9,13},{1... | collective-permute-start | bytes 1179656 | tf_op jit(solution)/shard_map/ppermute | solution.py:27
  135.9 13.4 %collective-permute-start.28 = (bf16[768,256]{1,0:T(8,128)(2,1)S(1)}, bf16[768,256]{1,0:T(8,128)(2,1)S(1)}, u32[]{:S(2)}, u32[]{:S(2)}) collective-permute-start(bf16[768,256]{1,0:T(8,128)(2,1)S(1)} %collective-permute-done.26.refs_1_), channel_id=1, source_target_pairs={{0,12},{1,13},{2,14},{3,15},{4,0},{5,1},{6,2},{7,3},{8,4},{9,5},{1... | collective-permute-start | bytes 1179656 | tf_op jit(solution)/shard_map/ppermute | solution.py:27
  140.4 9.0 %collective-permute-start.36 = (f32[5,128]{1,0:T(8,128)S(1)}, f32[5,128]{1,0:T(8,128)S(1)}, u32[]{:S(2)}, u32[]{:S(2)}) collective-permute-start(f32[5,128]{1,0:T(8,128)S(1)} %fusion.19), channel_id=1, source_target_pairs={{0,64},{1,65},{2,66},{3,67},{4,68},{5,69},{6,70},{7,71},{8,72},{9,... | collective-permute-start | bytes 7688 | tf_op jit(solution)/shard_map/ppermute | solution.py:27
  142.2 10.8 %collective-permute-start.31 = (bf16[768,256]{1,0:T(8,128)(2,1)S(1)}, bf16[768,256]{1,0:T(8,128)(2,1)S(1)}, u32[]{:S(2)}, u32[]{:S(2)}) collective-permute-start(bf16[768,256]{1,0:T(8,128)(2,1)S(1)} %broadcast_select_fusion.2), channel_id=1, source_target_pairs={{0,4},{1,13},{2,6},{3,15},{4,8},{5,1},{6,10},{7,3},{8,12},{9,5},{1... | collective-permute-start | bytes 1179656 | tf_op jit(solution)/shard_map/ppermute | solution.py:27
  149.4 9.1 %collective-permute-start.32 = (bf16[768,256]{1,0:T(8,128)(2,1)S(1)}, bf16[768,256]{1,0:T(8,128)(2,1)S(1)}, u32[]{:S(2)}, u32[]{:S(2)}) collective-permute-start(bf16[768,256]{1,0:T(8,128)(2,1)S(1)} %broadcast_select_fusion.1), channel_id=1, source_target_pairs={{0,4},{1,13},{2,6},{3,15},{4,8},{5,1},{6,10},{7,3},{8,12},{9,5},{1... | collective-permute-start | bytes 1179656 | tf_op jit(solution)/shard_map/ppermute | solution.py:27
  169.0 11.7 %collective-permute-start.45 = (bf16[2,512,256]{2,1,0:T(8,128)(2,1)}, bf16[2,512,256]{2,1,0:T(8,128)(2,1)S(1)}, u32[]{:S(2)}, u32[]{:S(2)}) collective-permute-start(bf16[2,512,256]{2,1,0:T(8,128)(2,1)} %get-tuple-element.62), channel_id=1, source_target_pairs={{0,16},{1,49},{2,18},{3,51},{4,20},{5,53},{6,22},{7,55},{8,24},{9,... | collective-permute-start | bytes 1572872 | tf_op jit(solution)/shard_map/ppermute | solution.py:27
  180.8 15.7 %collective-permute-start.47 = (bf16[2,512,256]{2,1,0:T(8,128)(2,1)S(1)}, bf16[2,512,256]{2,1,0:T(8,128)(2,1)S(1)}, u32[]{:S(2)}, u32[]{:S(2)}) collective-permute-start(bf16[2,512,256]{2,1,0:T(8,128)(2,1)S(1)} %add_convert_fusion.1), channel_id=1, source_target_pairs={{0,16},{1,49},{2,18},{3,51},{4,20},{5,53},{6,22},{7,55},{8,24},{9,... | collective-permute-start | bytes 1572872 | tf_op jit(solution)/shard_map/ppermute | solution.py:27
  181.9 14.6 %collective-permute-start.46 = (bf16[2,512,256]{2,1,0:T(8,128)(2,1)S(1)}, bf16[2,512,256]{2,1,0:T(8,128)(2,1)S(1)}, u32[]{:S(2)}, u32[]{:S(2)}) collective-permute-start(bf16[2,512,256]{2,1,0:T(8,128)(2,1)S(1)} %copy-done.17), channel_id=1, source_target_pairs={{0,48},{1,17},{2,50},{3,19},{4,52},{5,21},{6,54},{7,23},{8,56},{9,... | collective-permute-start | bytes 1572872 | tf_op jit(solution)/shard_map/ppermute | solution.py:27
  196.8 8.6 %collective-permute-start.48 = (bf16[512,256]{1,0:T(8,128)(2,1)S(1)}, bf16[512,256]{1,0:T(8,128)(2,1)S(1)}, u32[]{:S(2)}, u32[]{:S(2)}) collective-permute-start(bf16[512,256]{1,0:T(8,128)(2,1)S(1)} %fusion.9), channel_id=1, source_target_pairs={{0,64},{1,65},{2,66},{3,67},{4,68},{5,69},{6,70},{7,71},{8,72},{9,... | collective-permute-start | bytes 786440 | tf_op jit(solution)/shard_map/ppermute | solution.py:27
  (54 other events, 376.1 us)
Sparse Core Ops, SparseCore 0:
  10.3 83.8 all-gather.1
  126.0 42.7 reduce-scatter.1

commit v9 on v8

--- a/solution.py
+++ b/solution.py
@@ -285,7 +285,7 @@
     conv_both, in_here = tie(conv_both, in_here)
     in_above, in_below = z_shift(in_here, -1), z_shift(in_here, 1)
     further, own = hid_partial(place, conv_both, out_blocks, out_beside, ((0, 1), (0, 0)))
-    passed, own, in_above, in_below = tie(passed, own, in_above, in_below)
+    passed, back, own, in_above, in_below = tie(passed, back, own, in_above, in_below)
     further = x_split(add([further, passed]).astype(BF16), 1)
     in_across = onward(in_above, in_below, core, z_split)
     total = add([own, back, further])
@@ -299,7 +299,9 @@
     grad_act = (grad_pre * mid_gain).astype(BF16)
     act_near = y_hi_swap(grad_act)
     act_above, act_below = x_shift(grad_act, -1), x_shift(grad_act, 1)
-    act_near, wout = tie(act_near, wout)
+    act_near, act_above, act_below, wout, mid_part = tie(
+        act_near, act_above, act_below, wout, mid_part
+    )
     wout = lax.psum_scatter(wout, "row", scatter_dimension=0, tiled=True)
     near_above, near_below = x_shift(act_near, -1), x_shift(act_near, 1)
 
@@ -308,21 +310,22 @@
     mid_own = mid_own + core_swap(mid_away)
     sums = jnp.concatenate([mid_own, wide_part]).reshape(5, 128)
     sums = sums + z_flip(sums, 1)
+
+    act_across = onward(act_above, act_below, core, x_split)
+    near_above, near_below, act_across, sums = tie(near_above, near_below, act_across, sums)
     sums = sums + z_flip(sums, 2)
-    sums = sums + y_lo_swap(sums)
-
-    act_across = onward(act_above, act_below, core, x_split)
     near_across = onward(near_above, near_below, core, x_split)
     act = [
         grad_act, act_near, act_above, near_above, act_below, near_below, act_across, near_across
     ]
     act_beside = [core_swap(block) for block in act]
     act[7], sums = tie(act[7], sums)
+    sums = sums + y_lo_swap(sums)
 
     away, there, further, own = win_partial(place, input_turned, act, act_beside)
     passed, back = z_split(away, 1), z_split(there, -1)
     grad_x = out_gradient(place, cotangent, act, act_beside, in_blocks)
-    passed, grad_x = tie(passed, grad_x)
+    passed, back, grad_x, sums = tie(passed, back, grad_x, sums)
     further = z_split(add([further, passed]).astype(BF16), 1)
     grad_wout = wout.astype(F32) * scaling
     further, grad_wout = tie(further, grad_wout)

time: 214 us -> 204 us (0.953)
  starting transfers between devices: 53.5 us -> 44.4 us
    ppermute x49, starting transfers between devices: 53.4 us -> 44.4 us  [permute(): return lax.ppermute(v, AXES, pairs)]
    unnamed x71 -> x77, local copies, waits for them, and re-layouts: 5.46 us -> 4.96 us
  transfers between devices with their start and end apart: 51 -> 51, of which waited for: 22 -> 24; matrix products, arithmetic and copies ran while one was open for 13% -> 13% of each run, Pallas kernels for 15% -> 15%
where the time goes in v9:
time: 204 us; the launch traced here: 203 us
  waiting for transfers between devices  78.3 us (38%)
  starting transfers between devices  44.4 us (22%)
  Pallas kernels  31.2 us (15%)
  other arithmetic  20.3 us (10%)
  between operations  14.6 us (7%)
  matrix products  7.69 us (4%)
  local copies, waits for them, and re-layouts  6.77 us (3%)
    ppermute x49, waiting for transfers between devices, permute(): return lax.ppermute(v, AXES, pairs)  78.3 us
    ppermute x49, starting transfers between devices, permute(): return lax.ppermute(v, AXES, pairs)  44.4 us
    pallas_call x4, Pallas kernels, call(): pl.pallas_call(body, out_shape=outs, in_specs=[pl.BlockSpec(memory_space=...  31.2 us
    dot_general x1, matrix products, dot(): lax.dot_general(a, b, (((ca,), (cb,)), ((), ())), preferred_element_type=...  7.69 us
    unnamed x77, local copies, waits for them, and re-layouts  4.96 us
  transfers between devices with their start and end apart: 51, of which 24 were waited for; matrix products, arithmetic and copies ran while one was open for 13% of the time, Pallas kernels for 15%

profile of v9, /device:TPU:0, one launch (start us, length us, event | category | flops | bytes accessed | tf_op | source)
XLA Modules:
  0.0 203.3 jit_solution(6681776829995018737)
XLA Ops:
  12.3 2.7 %fusion.1 = (f32[512]{0:T(512)S(1)}, bf16[1536,512]{1,0:T(8,128)(2,1)S(1)}) fusion(bf16[1536,512]{1,0:T(8,128)(2,1)} %cot.1, bf16[1536,512]{1,0:T(8,128)(2,1)} %param.12, f32[512]{0:T(512)S(1)} %convert_multiply_fusion.4), kind=kLoop, calls=%fused_computation.3 | loop fusion | flops 4718080 | bytes 4722688 | tf_op jit(solution)/shard_map/reduce_sum | solution.py:250
  18.2 2.1 %collective-permute-start.6 = (bf16[256,512]{1,0:T(8,128)(2,1)}, bf16[256,512]{1,0:T(8,128)(2,1)}, u32[]{:S(2)}, u32[]{:S(2)}) collective-permute-start(bf16[256,512]{1,0:T(8,128)(2,1)} %refs_0_.3), channel_id=1, source_target_pairs={{0,16},{1,17},{2,18},{3,19},{4,20},{5,21},{6,22},{7,23},{8,24},{9,... | collective-permute-start | bytes 786440 | tf_op jit(solution)/shard_map/ppermute | solution.py:27
  20.3 2.1 %collective-permute-start.5 = (bf16[256,512]{1,0:T(8,128)(2,1)}, bf16[256,512]{1,0:T(8,128)(2,1)S(1)}, u32[]{:S(2)}, u32[]{:S(2)}) collective-permute-start(bf16[256,512]{1,0:T(8,128)(2,1)} %refs_0_.3), channel_id=1, source_target_pairs={{0,48},{1,49},{2,50},{3,51},{4,52},{5,53},{6,54},{7,55},{8,56},{9,... | collective-permute-start | bytes 786440 | tf_op jit(solution)/shard_map/ppermute | solution.py:27
  22.6 7.2 %collective-permute-done.6.refs_4_ = bf16[256,512]{1,0:T(8,128)(2,1)} collective-permute-done((bf16[256,512]{1,0:T(8,128)(2,1)}, bf16[256,512]{1,0:T(8,128)(2,1)}, u32[]{:S(2)}, u32[]{:S(2)}) %collective-permute-start.6) | collective-permute-done | bytes 262176 | tf_op jit(solution)/shard_map/ppermute | solution.py:27
  29.9 1.9 collective-permute-start.3
  34.5 4.9 %collective-permute-done.3.refs_3_ = bf16[256,512]{1,0:T(8,128)(2,1)} collective-permute-done((bf16[256,512]{1,0:T(8,128)(2,1)}, bf16[256,512]{1,0:T(8,128)(2,1)}, u32[]{:S(2)}, u32[]{:S(2)}) %collective-permute-start.3) | collective-permute-done | bytes 262176 | tf_op jit(solution)/shard_map/ppermute | solution.py:27
  40.5 3.4 %collective-permute-start.11 = (bf16[256,512]{1,0:T(8,128)(2,1)}, bf16[256,512]{1,0:T(8,128)(2,1)S(1)}, u32[]{:S(2)}, u32[]{:S(2)}) collective-permute-start(bf16[256,512]{1,0:T(8,128)(2,1)} %collective-permute-done.refs_1_), channel_id=1, source_target_pairs={{0,1},{1,0},{2,3},{3,2},{4,5},{5,4},{6,7},{7,6},{8,9},{9,8},{10,11... | collective-permute-start | bytes 786440 | tf_op jit(solution)/shard_map/ppermute | solution.py:27
  44.5 3.5 %collective-permute-done.9.refs_7_ = bf16[256,512]{1,0:T(8,128)(2,1)S(1)} collective-permute-done((bf16[256,512]{1,0:T(8,128)(2,1)S(1)}, bf16[256,512]{1,0:T(8,128)(2,1)S(1)}, u32[]{:S(2)}, u32[]{:S(2)}) %collective-permute-start.9) | collective-permute-done | bytes 262176 | tf_op jit(solution)/shard_map/ppermute | solution.py:27
  51.3 6.5 %shard_map.137 = (bf16[2,768,256]{2,1,0:T(8,128)(2,1)}, bf16[2,768,256]{2,1,0:T(8,128)(2,1)}) custom-call(s32[2]{0:T(128)} %pad_add_fusion.here, bf16[768,1024]{1,0:T(8,128)(2,1)} %pad_maximum_fusion.conv, bf16[256,512]{1,0:T(8,128)(2,1)} %refs_0_.3, bf16[256,512]{1,0:T(8,128)(2,1)} %collective-permute-done.refs_1_, bf16[256,512]{1,0:T(8,128)(2,1)} %copy-done.14, ...), custom_call_target="tpu_custom_call" | custom-call | flops 1610612736 | bytes 8388608 | tf_op jit(solution)/shard_map/pallas_call | solution.py:90
  57.8 2.8 %collective-permute-start.19 = (bf16[2,768,256]{2,1,0:T(8,128)(2,1)}, bf16[2,768,256]{2,1,0:T(8,128)(2,1)S(1)}, u32[]{:S(2)}, u32[]{:S(2)}) collective-permute-start(bf16[2,768,256]{2,1,0:T(8,128)(2,1)} %get-tuple-element.56), channel_id=1, source_target_pairs={{0,12},{1,5},{2,14},{3,7},{4,0},{5,9},{6,2},{7,11},{8,4},{9,13},{1... | collective-permute-start | bytes 2359304 | tf_op jit(solution)/shard_map/ppermute | solution.py:27
  60.6 2.8 %collective-permute-done.20 = bf16[512,256]{1,0:T(8,128)(2,1)S(1)} collective-permute-done((bf16[512,256]{1,0:T(8,128)(2,1)S(1)}, bf16[512,256]{1,0:T(8,128)(2,1)S(1)}, u32[]{:S(2)}, u32[]{:S(2)}) %collective-permute-start.20) | collective-permute-done | bytes 262176 | tf_op jit(solution)/shard_map/ppermute | solution.py:27
  65.2 3.2 %collective-permute-start.21 = (bf16[2,512,256]{2,1,0:T(8,128)(2,1)S(1)}, bf16[2,512,256]{2,1,0:T(8,128)(2,1)}, u32[]{:S(2)}, u32[]{:S(2)}) collective-permute-start(bf16[2,512,256]{2,1,0:T(8,128)(2,1)S(1)} %pad_maximum_fusion.1.refs_16_), channel_id=1, source_target_pairs={{0,48},{1,49},{2,50},{3,51},{4,52},{5,53},{6,54},{7,55},{8,56},{9,... | collective-permute-start | bytes 1572872 | tf_op jit(solution)/shard_map/ppermute | solution.py:27
  69.9 6.5 %shard_map.138 = (bf16[2,768,256]{2,1,0:T(8,128)(2,1)}, bf16[2,768,256]{2,1,0:T(8,128)(2,1)}) custom-call(s32[2]{0:T(128)} %pad_add_fusion.here, bf16[768,1024]{1,0:T(8,128)(2,1)} %pad_maximum_fusion.conv, bf16[256,512]{1,0:T(8,128)(2,1)} %refs_0_.3, bf16[256,512]{1,0:T(8,128)(2,1)} %collective-permute-done.refs_1_, bf16[256,512]{1,0:T(8,128)(2,1)} %copy-done.14, ...), custom_call_target="tpu_custom_call" | custom-call | flops 1610612736 | bytes 8388608 | tf_op jit(solution)/shard_map/pallas_call | solution.py:90
  76.4 3.7 %collective-permute-done.22.refs_18_ = bf16[2,512,256]{2,1,0:T(8,128)(2,1)} collective-permute-done((bf16[2,512,256]{2,1,0:T(8,128)(2,1)S(1)}, bf16[2,512,256]{2,1,0:T(8,128)(2,1)}, u32[]{:S(2)}, u32[]{:S(2)}) %collective-permute-start.22) | collective-permute-done | bytes 524320 | tf_op jit(solution)/shard_map/ppermute | solution.py:27
  80.1 2.4 %collective-permute-done.19 = bf16[2,768,256]{2,1,0:T(8,128)(2,1)S(1)} collective-permute-done((bf16[2,768,256]{2,1,0:T(8,128)(2,1)}, bf16[2,768,256]{2,1,0:T(8,128)(2,1)S(1)}, u32[]{:S(2)}, u32[]{:S(2)}) %collective-permute-start.19) | collective-permute-done | bytes 786464 | tf_op jit(solution)/shard_map/ppermute | solution.py:27
  90.2 8.2 %collective-permute-done.23 = bf16[2,768,256]{2,1,0:T(8,128)(2,1)S(1)} collective-permute-done((bf16[2,768,256]{2,1,0:T(8,128)(2,1)S(1)}, bf16[2,768,256]{2,1,0:T(8,128)(2,1)S(1)}, u32[]{:S(2)}, u32[]{:S(2)}) %collective-permute-start.23) | collective-permute-done | bytes 786464 | tf_op jit(solution)/shard_map/ppermute | solution.py:27
  99.4 3.9 %collective-permute-start.24 = (bf16[768,256]{1,0:T(8,128)(2,1)}, bf16[768,256]{1,0:T(8,128)(2,1)}, u32[]{:S(2)}, u32[]{:S(2)}) collective-permute-start(bf16[768,256]{1,0:T(8,128)(2,1)} %fusion.8), channel_id=1, source_target_pairs={{0,2},{1,3},{2,0},{3,1},{4,6},{5,7},{6,4},{7,5},{8,10},{9,11},{10,... | collective-permute-start | bytes 1179656 | tf_op jit(solution)/shard_map/ppermute | solution.py:27
  103.4 7.7 %convolution_convert_fusion = bf16[2048,512]{1,0:T(8,128)(2,1)} fusion(bf16[1536,2048]{1,0:T(8,128)(2,1)} %all-gather.2.cloned.1.call-done, bf16[1536,512]{1,0:T(8,128)(2,1)S(1)} %get-tuple-element.100), kind=kOutput, calls=%fused_computation.4 | convolution fusion | flops 3222274048 | bytes 9961472 | tf_op jit(solution)/shard_map/dot_general | solution.py:63
  113.6 3.2 %collective-permute-start.27 = (bf16[768,256]{1,0:T(8,128)(2,1)S(1)}, bf16[768,256]{1,0:T(8,128)(2,1)S(1)}, u32[]{:S(2)}, u32[]{:S(2)}) collective-permute-start(bf16[768,256]{1,0:T(8,128)(2,1)S(1)} %get-tuple-element.96.refs_0_), channel_id=1, source_target_pairs={{0,12},{1,13},{2,14},{3,15},{4,0},{5,1},{6,2},{7,3},{8,4},{9,5},{1... | collective-permute-start | bytes 1179656 | tf_op jit(solution)/shard_map/ppermute | solution.py:27
  118.0 6.4 %collective-permute-done.28.refs_4_ = bf16[768,256]{1,0:T(8,128)(2,1)S(1)} collective-permute-done((bf16[768,256]{1,0:T(8,128)(2,1)S(1)}, bf16[768,256]{1,0:T(8,128)(2,1)S(1)}, u32[]{:S(2)}, u32[]{:S(2)}) %collective-permute-start.28) | collective-permute-done | bytes 393248 | tf_op jit(solution)/shard_map/ppermute | solution.py:27
  124.8 2.6 %collective-permute-done.26.refs_1_ = bf16[768,256]{1,0:T(8,128)(2,1)S(1)} collective-permute-done((bf16[768,256]{1,0:T(8,128)(2,1)S(1)}, bf16[768,256]{1,0:T(8,128)(2,1)S(1)}, u32[]{:S(2)}, u32[]{:S(2)}) %collective-permute-start.26) | collective-permute-done | bytes 393248 | tf_op jit(solution)/shard_map/ppermute | solution.py:27
  128.1 2.6 %collective-permute-start.29 = (bf16[768,256]{1,0:T(8,128)(2,1)S(1)}, bf16[768,256]{1,0:T(8,128)(2,1)S(1)}, u32[]{:S(2)}, u32[]{:S(2)}) collective-permute-start(bf16[768,256]{1,0:T(8,128)(2,1)S(1)} %collective-permute-done.26.refs_1_), channel_id=1, source_target_pairs={{0,12},{1,13},{2,14},{3,15},{4,0},{5,1},{6,2},{7,3},{8,4},{9,5},{1... | collective-permute-start | bytes 1179656 | tf_op jit(solution)/shard_map/ppermute | solution.py:27
  132.2 3.3 %collective-permute-done.33 = f32[5,128]{1,0:T(8,128)S(1)} collective-permute-done((f32[5,128]{1,0:T(8,128)S(1)}, f32[5,128]{1,0:T(8,128)S(1)}, u32[]{:S(2)}, u32[]{:S(2)}) %collective-permute-start.33) | collective-permute-done | bytes 2592 | tf_op jit(solution)/shard_map/ppermute | solution.py:27
  135.5 5.5 %collective-permute-done.31.refs_6_ = bf16[768,256]{1,0:T(8,128)(2,1)S(1)} collective-permute-done((bf16[768,256]{1,0:T(8,128)(2,1)S(1)}, bf16[768,256]{1,0:T(8,128)(2,1)S(1)}, u32[]{:S(2)}, u32[]{:S(2)}) %collective-permute-start.31) | collective-permute-done | bytes 393248 | tf_op jit(solution)/shard_map/ppermute | solution.py:27
  145.6 3.0 %collective-permute-done.35 = f32[5,128]{1,0:T(8,128)S(1)} collective-permute-done((f32[5,128]{1,0:T(8,128)S(1)}, f32[5,128]{1,0:T(8,128)S(1)}, u32[]{:S(2)}, u32[]{:S(2)}) %collective-permute-start.35) | collective-permute-done | bytes 2592 | tf_op jit(solution)/shard_map/ppermute | solution.py:27
  148.6 2.7 %collective-permute-done.34.refs_7_ = bf16[768,256]{1,0:T(8,128)(2,1)S(1)} collective-permute-done((bf16[768,256]{1,0:T(8,128)(2,1)S(1)}, bf16[768,256]{1,0:T(8,128)(2,1)S(1)}, u32[]{:S(2)}, u32[]{:S(2)}) %collective-permute-start.34) | collective-permute-done | bytes 393248 | tf_op jit(solution)/shard_map/ppermute | solution.py:27
  153.2 8.6 %shard_map.139 = (bf16[2,512,256]{2,1,0:T(8,128)(2,1)}, bf16[2,512,256]{2,1,0:T(8,128)(2,1)}, bf16[2,512,256]{2,1,0:T(8,128)(2,1)}, bf16[2,512,256]{2,1,0:T(8,128)(2,1)}) custom-call(s32[2]{0:T(128)} %pad_add_fusion.here, bf16[512,1536]{1,0:T(8,128)(2,1)} %bitcast.46, bf16[768,256]{1,0:T(8,128)(2,1)} %copy-done.8, bf16[768,256]{1,0:T(8,128)(2,1)} %copy-done.19, ...), custom_call_target="tpu_custom_call" | custom-call | flops 3221225472 | bytes 10485760 | tf_op jit(solution)/shard_map/pallas_call | solution.py:90
  161.9 3.2 %collective-permute-start.45 = (bf16[2,512,256]{2,1,0:T(8,128)(2,1)}, bf16[2,512,256]{2,1,0:T(8,128)(2,1)S(1)}, u32[]{:S(2)}, u32[]{:S(2)}) collective-permute-start(bf16[2,512,256]{2,1,0:T(8,128)(2,1)} %get-tuple-element.81), channel_id=1, source_target_pairs={{0,48},{1,17},{2,50},{3,19},{4,52},{5,21},{6,54},{7,23},{8,56},{9,... | collective-permute-start | bytes 1572872 | tf_op jit(solution)/shard_map/ppermute | solution.py:27
  165.9 2.8 %collective-permute-done.46 = f32[5,128]{1,0:T(8,128)S(1)} collective-permute-done((f32[5,128]{1,0:T(8,128)S(1)}, f32[5,128]{1,0:T(8,128)S(1)}, u32[]{:S(2)}, u32[]{:S(2)}) %collective-permute-start.46) | collective-permute-done | bytes 2592 | tf_op jit(solution)/shard_map/ppermute | solution.py:27
  168.7 9.6 %shard_map.140 = bf16[1536,512]{1,0:T(8,128)(2,1)} custom-call(s32[2]{0:T(128)} %pad_add_fusion.here, bf16[1536,512]{1,0:T(8,128)(2,1)} %cot.1, bf16[768,256]{1,0:T(8,128)(2,1)} %copy-done.8, bf16[768,256]{1,0:T(8,128)(2,1)} %copy-done.19, bf16[768,256]{1,0:T(8,128)(2,1)} %copy-done.10, bf16[768,256]{1,0:T(8,128)(2,1)} %copy-done.12, ...), custom_call_target="tpu_custom_call" | custom-call | flops 3221225472 | bytes 12582912 | tf_op jit(solution)/shard_map/pallas_call | solution.py:90
  180.4 8.5 %collective-permute-done.47 = bf16[2,512,256]{2,1,0:T(8,128)(2,1)S(1)} collective-permute-done((bf16[2,512,256]{2,1,0:T(8,128)(2,1)S(1)}, bf16[2,512,256]{2,1,0:T(8,128)(2,1)S(1)}, u32[]{:S(2)}, u32[]{:S(2)}) %collective-permute-start.47) | collective-permute-done | bytes 524320 | tf_op jit(solution)/shard_map/ppermute | solution.py:27
  191.2 4.5 %collective-permute-done.48 = bf16[512,256]{1,0:T(8,128)(2,1)S(1)} collective-permute-done((bf16[512,256]{1,0:T(8,128)(2,1)S(1)}, bf16[512,256]{1,0:T(8,128)(2,1)S(1)}, u32[]{:S(2)}, u32[]{:S(2)}) %collective-permute-start.48) | collective-permute-done | bytes 262176 | tf_op jit(solution)/shard_map/ppermute | solution.py:27
  (191 shorter events, 46.7 us)
Async XLA Ops:
  7.2 96.2 %all-gather.2.cloned.1.call-start = ((), (), s32[]{:S(2)}) async-start(), calls=%async_computation.1 | async-start | bytes 6684672 | tf_op jit(solution)/shard_map/all_gather | solution.py:243
  9.8 168.8 %reduce-scatter.2.cloned.1.call-start = ((), (), s32[]{:S(2)}) async-start(), calls=%async_computation.2 | async-start | bytes 2359296 | tf_op jit(solution)/shard_map/reduce_scatter | solution.py:305
  9.8 8.4 %collective-permute-start = (bf16[256,512]{1,0:T(8,128)(2,1)}, bf16[256,512]{1,0:T(8,128)(2,1)}, u32[]{:S(2)}, u32[]{:S(2)}) collective-permute-start(bf16[256,512]{1,0:T(8,128)(2,1)} %refs_0_.3), channel_id=1, source_target_pairs={{0,64},{1,65},{2,66},{3,67},{4,68},{5,69},{6,70},{7,71},{8,72},{9,... | collective-permute-start | bytes 786440 | tf_op jit(solution)/shard_map/ppermute | solution.py:27
  18.2 14.9 %collective-permute-start.4 = (bf16[768,512]{1,0:T(8,128)(2,1)}, bf16[768,512]{1,0:T(8,128)(2,1)S(1)}, u32[]{:S(2)}, u32[]{:S(2)}) collective-permute-start(bf16[768,512]{1,0:T(8,128)(2,1)} %get-tuple-element.52), channel_id=1, source_target_pairs={{0,1},{1,0},{2,3},{3,2},{4,5},{5,4},{6,7},{7,6},{8,9},{9,8},{10,11... | collective-permute-start | bytes 2359304 | tf_op jit(solution)/shard_map/ppermute | solution.py:27
  18.2 11.7 %collective-permute-start.6 = (bf16[256,512]{1,0:T(8,128)(2,1)}, bf16[256,512]{1,0:T(8,128)(2,1)}, u32[]{:S(2)}, u32[]{:S(2)}) collective-permute-start(bf16[256,512]{1,0:T(8,128)(2,1)} %refs_0_.3), channel_id=1, source_target_pairs={{0,16},{1,17},{2,18},{3,19},{4,20},{5,21},{6,22},{7,23},{8,24},{9,... | collective-permute-start | bytes 786440 | tf_op jit(solution)/shard_map/ppermute | solution.py:27
  20.3 11.5 %collective-permute-start.5 = (bf16[256,512]{1,0:T(8,128)(2,1)}, bf16[256,512]{1,0:T(8,128)(2,1)S(1)}, u32[]{:S(2)}, u32[]{:S(2)}) collective-permute-start(bf16[256,512]{1,0:T(8,128)(2,1)} %refs_0_.3), channel_id=1, source_target_pairs={{0,48},{1,49},{2,50},{3,51},{4,52},{5,53},{6,54},{7,55},{8,56},{9,... | collective-permute-start | bytes 786440 | tf_op jit(solution)/shard_map/ppermute | solution.py:27
  22.4 18.1 %collective-permute-start.10 = (bf16[256,512]{1,0:T(8,128)(2,1)}, bf16[256,512]{1,0:T(8,128)(2,1)}, u32[]{:S(2)}, u32[]{:S(2)}) collective-permute-start(bf16[256,512]{1,0:T(8,128)(2,1)} %refs_0_.3), channel_id=1, source_target_pairs={{0,1},{1,0},{2,3},{3,2},{4,5},{5,4},{6,7},{7,6},{8,9},{9,8},{10,11... | collective-permute-start | bytes 786440 | tf_op jit(solution)/shard_map/ppermute | solution.py:27
  22.6 16.8 %collective-permute-start.7 = (bf16[256,512]{1,0:T(8,128)(2,1)}, bf16[256,512]{1,0:T(8,128)(2,1)}, u32[]{:S(2)}, u32[]{:S(2)}) collective-permute-start(bf16[256,512]{1,0:T(8,128)(2,1)} %collective-permute-done.refs_1_), channel_id=1, source_target_pairs={{0,16},{1,17},{2,18},{3,19},{4,20},{5,21},{6,22},{7,23},{8,24},{9,... | collective-permute-start | bytes 786440 | tf_op jit(solution)/shard_map/ppermute | solution.py:27
  29.9 9.5 %collective-permute-start.3 = (bf16[256,512]{1,0:T(8,128)(2,1)}, bf16[256,512]{1,0:T(8,128)(2,1)}, u32[]{:S(2)}, u32[]{:S(2)}) collective-permute-start(bf16[256,512]{1,0:T(8,128)(2,1)} %collective-permute-done.refs_1_), channel_id=1, source_target_pairs={{0,48},{1,49},{2,50},{3,51},{4,52},{5,53},{6,54},{7,55},{8,56},{9,... | collective-permute-start | bytes 786440 | tf_op jit(solution)/shard_map/ppermute | solution.py:27
  32.9 11.1 %collective-permute-start.8 = (bf16[256,512]{1,0:T(8,128)(2,1)S(1)}, bf16[256,512]{1,0:T(8,128)(2,1)}, u32[]{:S(2)}, u32[]{:S(2)}) collective-permute-start(bf16[256,512]{1,0:T(8,128)(2,1)S(1)} %broadcast_select_fusion.4), channel_id=1, source_target_pairs={{0,16},{1,49},{2,18},{3,51},{4,20},{5,53},{6,22},{7,55},{8,24},{9,... | collective-permute-start | bytes 786440 | tf_op jit(solution)/shard_map/ppermute | solution.py:27
  33.0 10.8 %collective-permute-start.14 = (bf16[256,512]{1,0:T(8,128)(2,1)}, bf16[256,512]{1,0:T(8,128)(2,1)S(1)}, u32[]{:S(2)}, u32[]{:S(2)}) collective-permute-start(bf16[256,512]{1,0:T(8,128)(2,1)} %collective-permute-done.6.refs_4_), channel_id=1, source_target_pairs={{0,1},{1,0},{2,3},{3,2},{4,5},{5,4},{6,7},{7,6},{8,9},{9,8},{10,11... | collective-permute-start | bytes 786440 | tf_op jit(solution)/shard_map/ppermute | solution.py:27
  40.5 8.2 %collective-permute-start.11 = (bf16[256,512]{1,0:T(8,128)(2,1)}, bf16[256,512]{1,0:T(8,128)(2,1)S(1)}, u32[]{:S(2)}, u32[]{:S(2)}) collective-permute-start(bf16[256,512]{1,0:T(8,128)(2,1)} %collective-permute-done.refs_1_), channel_id=1, source_target_pairs={{0,1},{1,0},{2,3},{3,2},{4,5},{5,4},{6,7},{7,6},{8,9},{9,8},{10,11... | collective-permute-start | bytes 786440 | tf_op jit(solution)/shard_map/ppermute | solution.py:27
  48.7 14.7 %collective-permute-start.20 = (bf16[512,256]{1,0:T(8,128)(2,1)S(1)}, bf16[512,256]{1,0:T(8,128)(2,1)S(1)}, u32[]{:S(2)}, u32[]{:S(2)}) collective-permute-start(bf16[512,256]{1,0:T(8,128)(2,1)S(1)} %copy-done.13), channel_id=1, source_target_pairs={{0,64},{1,65},{2,66},{3,67},{4,68},{5,69},{6,70},{7,71},{8,72},{9,... | collective-permute-start | bytes 786440 | tf_op jit(solution)/shard_map/ppermute | solution.py:27
  57.8 24.8 %collective-permute-start.19 = (bf16[2,768,256]{2,1,0:T(8,128)(2,1)}, bf16[2,768,256]{2,1,0:T(8,128)(2,1)S(1)}, u32[]{:S(2)}, u32[]{:S(2)}) collective-permute-start(bf16[2,768,256]{2,1,0:T(8,128)(2,1)} %get-tuple-element.56), channel_id=1, source_target_pairs={{0,12},{1,5},{2,14},{3,7},{4,0},{5,9},{6,2},{7,11},{8,4},{9,13},{1... | collective-permute-start | bytes 2359304 | tf_op jit(solution)/shard_map/ppermute | solution.py:27
  60.6 22.5 %collective-permute-start.18 = (bf16[2,768,256]{2,1,0:T(8,128)(2,1)}, bf16[2,768,256]{2,1,0:T(8,128)(2,1)S(1)}, u32[]{:S(2)}, u32[]{:S(2)}) collective-permute-start(bf16[2,768,256]{2,1,0:T(8,128)(2,1)} %get-tuple-element.55), channel_id=1, source_target_pairs={{0,4},{1,13},{2,6},{3,15},{4,8},{5,1},{6,10},{7,3},{8,12},{9,5},{1... | collective-permute-start | bytes 2359304 | tf_op jit(solution)/shard_map/ppermute | solution.py:27
  65.1 15.0 %collective-permute-start.22 = (bf16[2,512,256]{2,1,0:T(8,128)(2,1)S(1)}, bf16[2,512,256]{2,1,0:T(8,128)(2,1)}, u32[]{:S(2)}, u32[]{:S(2)}) collective-permute-start(bf16[2,512,256]{2,1,0:T(8,128)(2,1)S(1)} %pad_maximum_fusion.1.refs_16_), channel_id=1, source_target_pairs={{0,16},{1,17},{2,18},{3,19},{4,20},{5,21},{6,22},{7,23},{8,24},{9,... | collective-permute-start | bytes 1572872 | tf_op jit(solution)/shard_map/ppermute | solution.py:27
  65.2 14.9 %collective-permute-start.21 = (bf16[2,512,256]{2,1,0:T(8,128)(2,1)S(1)}, bf16[2,512,256]{2,1,0:T(8,128)(2,1)}, u32[]{:S(2)}, u32[]{:S(2)}) collective-permute-start(bf16[2,512,256]{2,1,0:T(8,128)(2,1)S(1)} %pad_maximum_fusion.1.refs_16_), channel_id=1, source_target_pairs={{0,48},{1,49},{2,50},{3,51},{4,52},{5,53},{6,54},{7,55},{8,56},{9,... | collective-permute-start | bytes 1572872 | tf_op jit(solution)/shard_map/ppermute | solution.py:27
  84.9 13.5 %collective-permute-start.23 = (bf16[2,768,256]{2,1,0:T(8,128)(2,1)S(1)}, bf16[2,768,256]{2,1,0:T(8,128)(2,1)S(1)}, u32[]{:S(2)}, u32[]{:S(2)}) collective-permute-start(bf16[2,768,256]{2,1,0:T(8,128)(2,1)S(1)} %add_convert_fusion), channel_id=1, source_target_pairs={{0,4},{1,13},{2,6},{3,15},{4,8},{5,1},{6,10},{7,3},{8,12},{9,5},{1... | collective-permute-start | bytes 2359304 | tf_op jit(solution)/shard_map/ppermute | solution.py:27
  90.2 20.9 %collective-permute-start.25 = (bf16[2,512,256]{2,1,0:T(8,128)(2,1)}, bf16[2,512,256]{2,1,0:T(8,128)(2,1)}, u32[]{:S(2)}, u32[]{:S(2)}) collective-permute-start(bf16[2,512,256]{2,1,0:T(8,128)(2,1)} %broadcast_select_fusion), channel_id=1, source_target_pairs={{0,16},{1,49},{2,18},{3,51},{4,20},{5,53},{6,22},{7,55},{8,24},{9,... | collective-permute-start | bytes 1572872 | tf_op jit(solution)/shard_map/ppermute | solution.py:27
  99.4 12.7 %collective-permute-start.24 = (bf16[768,256]{1,0:T(8,128)(2,1)}, bf16[768,256]{1,0:T(8,128)(2,1)}, u32[]{:S(2)}, u32[]{:S(2)}) collective-permute-start(bf16[768,256]{1,0:T(8,128)(2,1)} %fusion.8), channel_id=1, source_target_pairs={{0,2},{1,3},{2,0},{3,1},{4,6},{5,7},{6,4},{7,5},{8,10},{9,11},{10,... | collective-permute-start | bytes 1179656 | tf_op jit(solution)/shard_map/ppermute | solution.py:27
  113.5 10.9 %collective-permute-start.28 = (bf16[768,256]{1,0:T(8,128)(2,1)S(1)}, bf16[768,256]{1,0:T(8,128)(2,1)S(1)}, u32[]{:S(2)}, u32[]{:S(2)}) collective-permute-start(bf16[768,256]{1,0:T(8,128)(2,1)S(1)} %get-tuple-element.96.refs_0_), channel_id=1, source_target_pairs={{0,4},{1,5},{2,6},{3,7},{4,8},{5,9},{6,10},{7,11},{8,12},{9,13},{1... | collective-permute-start | bytes 1179656 | tf_op jit(solution)/shard_map/ppermute | solution.py:27
  113.6 11.2 %collective-permute-start.27 = (bf16[768,256]{1,0:T(8,128)(2,1)S(1)}, bf16[768,256]{1,0:T(8,128)(2,1)S(1)}, u32[]{:S(2)}, u32[]{:S(2)}) collective-permute-start(bf16[768,256]{1,0:T(8,128)(2,1)S(1)} %get-tuple-element.96.refs_0_), channel_id=1, source_target_pairs={{0,12},{1,13},{2,14},{3,15},{4,0},{5,1},{6,2},{7,3},{8,4},{9,5},{1... | collective-permute-start | bytes 1179656 | tf_op jit(solution)/shard_map/ppermute | solution.py:27
  116.8 10.5 %collective-permute-start.26 = (bf16[768,256]{1,0:T(8,128)(2,1)S(1)}, bf16[768,256]{1,0:T(8,128)(2,1)S(1)}, u32[]{:S(2)}, u32[]{:S(2)}) collective-permute-start(bf16[768,256]{1,0:T(8,128)(2,1)S(1)} %get-tuple-element.96.refs_0_), channel_id=1, source_target_pairs={{0,2},{1,3},{2,0},{3,1},{4,6},{5,7},{6,4},{7,5},{8,10},{9,11},{10,... | collective-permute-start | bytes 1179656 | tf_op jit(solution)/shard_map/ppermute | solution.py:27
  127.4 14.8 %collective-permute-start.30 = (bf16[768,256]{1,0:T(8,128)(2,1)S(1)}, bf16[768,256]{1,0:T(8,128)(2,1)S(1)}, u32[]{:S(2)}, u32[]{:S(2)}) collective-permute-start(bf16[768,256]{1,0:T(8,128)(2,1)S(1)} %collective-permute-done.26.refs_1_), channel_id=1, source_target_pairs={{0,4},{1,5},{2,6},{3,7},{4,8},{5,9},{6,10},{7,11},{8,12},{9,13},{1... | collective-permute-start | bytes 1179656 | tf_op jit(solution)/shard_map/ppermute | solution.py:27
  128.1 14.0 %collective-permute-start.29 = (bf16[768,256]{1,0:T(8,128)(2,1)S(1)}, bf16[768,256]{1,0:T(8,128)(2,1)S(1)}, u32[]{:S(2)}, u32[]{:S(2)}) collective-permute-start(bf16[768,256]{1,0:T(8,128)(2,1)S(1)} %collective-permute-done.26.refs_1_), channel_id=1, source_target_pairs={{0,12},{1,13},{2,14},{3,15},{4,0},{5,1},{6,2},{7,3},{8,4},{9,5},{1... | collective-permute-start | bytes 1179656 | tf_op jit(solution)/shard_map/ppermute | solution.py:27
  130.8 10.2 %collective-permute-start.31 = (bf16[768,256]{1,0:T(8,128)(2,1)S(1)}, bf16[768,256]{1,0:T(8,128)(2,1)S(1)}, u32[]{:S(2)}, u32[]{:S(2)}) collective-permute-start(bf16[768,256]{1,0:T(8,128)(2,1)S(1)} %broadcast_select_fusion.2), channel_id=1, source_target_pairs={{0,4},{1,13},{2,6},{3,15},{4,8},{5,1},{6,10},{7,3},{8,12},{9,5},{1... | collective-permute-start | bytes 1179656 | tf_op jit(solution)/shard_map/ppermute | solution.py:27
  131.9 12.6 %collective-permute-start.36 = (bf16[768,256]{1,0:T(8,128)(2,1)S(1)}, bf16[768,256]{1,0:T(8,128)(2,1)S(1)}, u32[]{:S(2)}, u32[]{:S(2)}) collective-permute-start(bf16[768,256]{1,0:T(8,128)(2,1)S(1)} %get-tuple-element.96.refs_0_), channel_id=1, source_target_pairs={{0,1},{1,0},{2,3},{3,2},{4,5},{5,4},{6,7},{7,6},{8,9},{9,8},{10,11... | collective-permute-start | bytes 1179656 | tf_op jit(solution)/shard_map/ppermute | solution.py:27
  135.5 9.5 %collective-permute-start.38 = (bf16[768,256]{1,0:T(8,128)(2,1)S(1)}, bf16[768,256]{1,0:T(8,128)(2,1)S(1)}, u32[]{:S(2)}, u32[]{:S(2)}) collective-permute-start(bf16[768,256]{1,0:T(8,128)(2,1)S(1)} %collective-permute-done.27.refs_2_), channel_id=1, source_target_pairs={{0,1},{1,0},{2,3},{3,2},{4,5},{5,4},{6,7},{7,6},{8,9},{9,8},{10,11... | collective-permute-start | bytes 1179656 | tf_op jit(solution)/shard_map/ppermute | solution.py:27
  142.2 9.1 %collective-permute-start.34 = (bf16[768,256]{1,0:T(8,128)(2,1)S(1)}, bf16[768,256]{1,0:T(8,128)(2,1)S(1)}, u32[]{:S(2)}, u32[]{:S(2)}) collective-permute-start(bf16[768,256]{1,0:T(8,128)(2,1)S(1)} %broadcast_select_fusion.1), channel_id=1, source_target_pairs={{0,4},{1,13},{2,6},{3,15},{4,8},{5,1},{6,10},{7,3},{8,12},{9,5},{1... | collective-permute-start | bytes 1179656 | tf_op jit(solution)/shard_map/ppermute | solution.py:27
  161.8 16.5 %collective-permute-start.44 = (bf16[2,512,256]{2,1,0:T(8,128)(2,1)}, bf16[2,512,256]{2,1,0:T(8,128)(2,1)S(1)}, u32[]{:S(2)}, u32[]{:S(2)}) collective-permute-start(bf16[2,512,256]{2,1,0:T(8,128)(2,1)} %get-tuple-element.80), channel_id=1, source_target_pairs={{0,16},{1,49},{2,18},{3,51},{4,20},{5,53},{6,22},{7,55},{8,24},{9,... | collective-permute-start | bytes 1572872 | tf_op jit(solution)/shard_map/ppermute | solution.py:27
  161.9 16.5 %collective-permute-start.45 = (bf16[2,512,256]{2,1,0:T(8,128)(2,1)}, bf16[2,512,256]{2,1,0:T(8,128)(2,1)S(1)}, u32[]{:S(2)}, u32[]{:S(2)}) collective-permute-start(bf16[2,512,256]{2,1,0:T(8,128)(2,1)} %get-tuple-element.81), channel_id=1, source_target_pairs={{0,48},{1,17},{2,50},{3,19},{4,52},{5,21},{6,54},{7,23},{8,56},{9,... | collective-permute-start | bytes 1572872 | tf_op jit(solution)/shard_map/ppermute | solution.py:27
  178.5 10.5 %collective-permute-start.47 = (bf16[2,512,256]{2,1,0:T(8,128)(2,1)S(1)}, bf16[2,512,256]{2,1,0:T(8,128)(2,1)S(1)}, u32[]{:S(2)}, u32[]{:S(2)}) collective-permute-start(bf16[2,512,256]{2,1,0:T(8,128)(2,1)S(1)} %add_convert_fusion.1), channel_id=1, source_target_pairs={{0,16},{1,49},{2,18},{3,51},{4,20},{5,53},{6,22},{7,55},{8,24},{9,... | collective-permute-start | bytes 1572872 | tf_op jit(solution)/shard_map/ppermute | solution.py:27
  (57 other events, 359.4 us)
Sparse Core Ops, SparseCore 0:
  10.3 82.9 all-gather.1
  127.5 41.1 reduce-scatter.1

commit v10 on v9

--- a/solution.py
+++ b/solution.py
@@ -250,15 +250,18 @@
     wide_part = jnp.sum(cot_float * conv_out.astype(F32), axis=0)
     conv_mine = mine(grad_conv)
     conv_sent, input_turned = theirs(grad_conv), inputs.T
-    out_near, conv_sent, input_turned, wide_part, pre_act = tie(
-        out_near, conv_sent, input_turned, wide_part, pre_act
+    out_near, out_above, out_below, conv_sent, pre_act, weight_in = tie(
+        out_near, out_above, out_below, conv_sent, pre_act, weight_in
     )
     near_above, near_below = z_shift(out_near, -1), z_shift(out_near, 1)
     out_across = onward(out_above, out_below, core, z_split)
+    in_near = y_lo_swap(weight_in)
     conv_both = jnp.concatenate([conv_mine, core_swap(conv_sent)], axis=1)
-    near_above, conv_both, weight_in = tie(near_above, conv_both, weight_in)
-    in_near = y_lo_swap(weight_in)
+    near_above, near_below, out_across, conv_both, in_near, input_turned, wide_part, place = tie(
+        near_above, near_below, out_across, conv_both, in_near, input_turned, wide_part, place
+    )
     near_across = onward(near_above, near_below, core, z_split)
+    in_here = jnp.stack([weight_in, in_near])
     out_blocks = [
         weight_out, out_near, out_above, near_above, out_below, near_below, out_across, near_across
     ]
@@ -278,21 +281,21 @@
     mid_gain = gain_chip[0] * gain_chip[1]
 
     out_beside = [core_swap(block) for block in out_blocks]
+    near_across, in_here = tie(near_across, in_here)
+    out_blocks[7] = near_across
     away, there = hid_partial(place, conv_both, out_blocks, out_beside, ((2, 0), (0, -1)))
     passed, back = x_split(away, 1), x_split(there, -1)
-    away, in_near = tie(away, in_near)
-    in_here = jnp.stack([weight_in, in_near])
-    conv_both, in_here = tie(conv_both, in_here)
     in_above, in_below = z_shift(in_here, -1), z_shift(in_here, 1)
     further, own = hid_partial(place, conv_both, out_blocks, out_beside, ((0, 1), (0, 0)))
     passed, back, own, in_above, in_below = tie(passed, back, own, in_above, in_below)
-    further = x_split(add([further, passed]).astype(BF16), 1)
+    far = x_split(add([further[1], passed[1]]).astype(BF16), 1)
+    near = x_split(add([further[0], passed[0]]).astype(BF16), 1)
     in_across = onward(in_above, in_below, core, z_split)
-    total = add([own, back, further])
     wout = dot(hidden_full, grad_conv, 0, 0).astype(BF16)
-    crossed, wout, in_across = tie(y_hi_swap(total[1].astype(BF16)), wout, in_across)
+    crossed = y_hi_swap(add([own[1], back[1], far]).astype(BF16))
+    crossed, near, wout, in_across = tie(crossed, near, wout, in_across)
     in_blocks = [in_here, in_above, in_below, in_across]
-    grad_hid = add([total[0], crossed])
+    grad_hid = add([own[0], back[0], near, crossed])
     alive = (pre_chip > 0) & (gain_chip[1] > 0)[None, :]
     grad_pre = jnp.where(alive, grad_hid, 0.0)
     mid_part = jnp.sum(grad_pre * pre_chip, axis=0).reshape(2, 128)
@@ -325,12 +328,13 @@
     away, there, further, own = win_partial(place, input_turned, act, act_beside)
     passed, back = z_split(away, 1), z_split(there, -1)
     grad_x = out_gradient(place, cotangent, act, act_beside, in_blocks)
-    passed, back, grad_x, sums = tie(passed, back, grad_x, sums)
-    further = z_split(add([further, passed]).astype(BF16), 1)
+    passed, back, grad_x = tie(passed, back, grad_x)
+    far = z_split(add([further[1], passed[1]]).astype(BF16), 1)
+    near = z_split(add([further[0], passed[0]]).astype(BF16), 1)
     grad_wout = wout.astype(F32) * scaling
-    further, grad_wout = tie(further, grad_wout)
-    total = add([own, back, further])
-    grad_win = add([total[0], y_lo_swap(total[1].astype(BF16))]) * scaling
+    far, grad_wout, sums = tie(far, grad_wout, sums)
+    crossed = y_lo_swap(add([own[1], back[1], far]).astype(BF16))
+    grad_win = add([own[0], back[0], near, crossed]) * scaling
     grad_smid = keep_mid.astype(F32) * scaling * sums[0]
     grad_swide = keep_wide.astype(F32) * scaling * sums[1:].reshape(512)
     return (grad_x, grad_win, grad_wout, grad_smid, grad_swide)

time: 204 us -> 198 us (0.971)
  waiting for transfers between devices: 78.3 us -> 55.7 us
  starting transfers between devices: 44.4 us -> 59.4 us
  other arithmetic: 20.3 us -> 22.5 us
    ppermute x49 -> x51, waiting for transfers between devices: 78.3 us -> 55.6 us  [permute(): return lax.ppermute(v, AXES, pairs)]
    ppermute x49 -> x51, starting transfers between devices: 44.4 us -> 59.3 us  [permute(): return lax.ppermute(v, AXES, pairs)]
  transfers between devices with their start and end apart: 51 -> 53, of which waited for: 24 -> 21; matrix products, arithmetic and copies ran while one was open for 13% -> 14% of each run, Pallas kernels for 15% -> 16%
where the time goes in v10:
time: 198 us; the launch traced here: 197 us
  starting transfers between devices  59.4 us (30%)
  waiting for transfers between devices  55.7 us (28%)
  Pallas kernels  31.1 us (16%)
  other arithmetic  22.5 us (11%)
  between operations  14.7 us (7%)
  matrix products  7.66 us (4%)
  local copies, waits for them, and re-layouts  6.54 us (3%)
    ppermute x51, starting transfers between devices, permute(): return lax.ppermute(v, AXES, pairs)  59.3 us
    ppermute x51, waiting for transfers between devices, permute(): return lax.ppermute(v, AXES, pairs)  55.6 us
    pallas_call x4, Pallas kernels, call(): pl.pallas_call(body, out_shape=outs, in_specs=[pl.BlockSpec(memory_space=...  31.1 us
    dot_general x1, matrix products, dot(): lax.dot_general(a, b, (((ca,), (cb,)), ((), ())), preferred_element_type=...  7.66 us
    unnamed x77, local copies, waits for them, and re-layouts  6.4 us
  transfers between devices with their start and end apart: 53, of which 21 were waited for; matrix products, arithmetic and copies ran while one was open for 14% of the time, Pallas kernels for 16%

profile of v10, /device:TPU:0, one launch (start us, length us, event | category | flops | bytes accessed | tf_op | source)
XLA Modules:
  0.0 197.5 jit_solution(5095835424074988615)
XLA Ops:
  9.8 2.1 %collective-permute-start.2 = (bf16[256,512]{1,0:T(8,128)(2,1)}, bf16[256,512]{1,0:T(8,128)(2,1)S(1)}, u32[]{:S(2)}, u32[]{:S(2)}) collective-permute-start(bf16[256,512]{1,0:T(8,128)(2,1)} %refs_0_.3), channel_id=1, source_target_pairs={{0,16},{1,17},{2,18},{3,19},{4,20},{5,21},{6,22},{7,23},{8,24},{9,... | collective-permute-start | bytes 786440 | tf_op jit(solution)/shard_map/ppermute | solution.py:27
  11.9 2.2 %collective-permute-start.1 = (bf16[256,512]{1,0:T(8,128)(2,1)}, bf16[256,512]{1,0:T(8,128)(2,1)}, u32[]{:S(2)}, u32[]{:S(2)}) collective-permute-start(bf16[256,512]{1,0:T(8,128)(2,1)} %refs_0_.3), channel_id=1, source_target_pairs={{0,48},{1,49},{2,50},{3,51},{4,52},{5,53},{6,54},{7,55},{8,56},{9,... | collective-permute-start | bytes 786440 | tf_op jit(solution)/shard_map/ppermute | solution.py:27
  16.4 2.6 %fusion.1 = (f32[512]{0:T(512)S(1)}, bf16[1536,512]{1,0:T(8,128)(2,1)S(1)}) fusion(bf16[1536,512]{1,0:T(8,128)(2,1)} %cot.1, bf16[1536,512]{1,0:T(8,128)(2,1)} %param.12, f32[512]{0:T(512)S(1)} %convert_multiply_fusion.4), kind=kLoop, calls=%fused_computation.3 | loop fusion | flops 4718080 | bytes 4722688 | tf_op jit(solution)/shard_map/reduce_sum | solution.py:250
  22.2 2.7 %copy.15 = bf16[1536,512]{0,1:T(8,128)(2,1)} copy(bf16[1536,512]{1,0:T(8,128)(2,1)} %param.10) | data formatting | bytes 3145728 | tf_op args[0]
  24.9 3.2 %collective-permute-start.3 = (bf16[256,512]{1,0:T(8,128)(2,1)}, bf16[256,512]{1,0:T(8,128)(2,1)S(1)}, u32[]{:S(2)}, u32[]{:S(2)}) collective-permute-start(bf16[256,512]{1,0:T(8,128)(2,1)} %collective-permute-done.refs_1_), channel_id=1, source_target_pairs={{0,48},{1,49},{2,50},{3,51},{4,52},{5,53},{6,54},{7,55},{8,56},{9,... | collective-permute-start | bytes 786440 | tf_op jit(solution)/shard_map/ppermute | solution.py:27
  31.6 2.5 %pad_maximum_fusion.conv = bf16[768,1024]{1,0:T(8,128)(2,1)} fusion(bf16[768,512]{1,0:T(8,128)(2,1)} %collective-permute-done.6, bf16[768,512]{1,0:T(8,128)(2,1)S(1)} %get-tuple-element.113), kind=kLoop, calls=%fused_computation.5 | loop fusion | flops 3145728 | bytes 3145728 | tf_op jit(solution)/shard_map/concatenate | solution.py:259
  34.1 3.7 %collective-permute-done.5.refs_6_ = bf16[256,512]{1,0:T(8,128)(2,1)S(1)} collective-permute-done((bf16[256,512]{1,0:T(8,128)(2,1)S(1)}, bf16[256,512]{1,0:T(8,128)(2,1)S(1)}, u32[]{:S(2)}, u32[]{:S(2)}) %collective-permute-start.5) | collective-permute-done | bytes 262176 | tf_op jit(solution)/shard_map/ppermute | solution.py:27
  41.6 4.5 %collective-permute-done.10.refs_7_ = bf16[256,512]{1,0:T(8,128)(2,1)S(1)} collective-permute-done((bf16[256,512]{1,0:T(8,128)(2,1)S(1)}, bf16[256,512]{1,0:T(8,128)(2,1)S(1)}, u32[]{:S(2)}, u32[]{:S(2)}) %collective-permute-start.10) | collective-permute-done | bytes 262176 | tf_op jit(solution)/shard_map/ppermute | solution.py:27
  49.7 6.4 %shard_map.137 = (bf16[2,768,256]{2,1,0:T(8,128)(2,1)}, bf16[2,768,256]{2,1,0:T(8,128)(2,1)}) custom-call(s32[2]{0:T(128)} %pad_add_fusion.here, bf16[768,1024]{1,0:T(8,128)(2,1)} %pad_maximum_fusion.conv, bf16[256,512]{1,0:T(8,128)(2,1)} %refs_0_.3, bf16[256,512]{1,0:T(8,128)(2,1)} %collective-permute-done.refs_1_, ...), custom_call_target="tpu_custom_call" | custom-call | flops 1610612736 | bytes 8388608 | tf_op jit(solution)/shard_map/pallas_call | solution.py:90
  59.6 3.2 %collective-permute-start.21 = (bf16[2,512,256]{2,1,0:T(8,128)(2,1)}, bf16[2,512,256]{2,1,0:T(8,128)(2,1)}, u32[]{:S(2)}, u32[]{:S(2)}) collective-permute-start(bf16[2,512,256]{2,1,0:T(8,128)(2,1)} %pad_maximum_fusion.1.refs_16_), channel_id=1, source_target_pairs={{0,48},{1,49},{2,50},{3,51},{4,52},{5,53},{6,54},{7,55},{8,56},{9,... | collective-permute-start | bytes 1572872 | tf_op jit(solution)/shard_map/ppermute | solution.py:27
  63.1 6.4 %shard_map.138 = (bf16[2,768,256]{2,1,0:T(8,128)(2,1)}, bf16[2,768,256]{2,1,0:T(8,128)(2,1)}) custom-call(s32[2]{0:T(128)} %pad_add_fusion.here, bf16[768,1024]{1,0:T(8,128)(2,1)} %pad_maximum_fusion.conv, bf16[256,512]{1,0:T(8,128)(2,1)} %refs_0_.3, bf16[256,512]{1,0:T(8,128)(2,1)} %collective-permute-done.refs_1_, ...), custom_call_target="tpu_custom_call" | custom-call | flops 1610612736 | bytes 8388608 | tf_op jit(solution)/shard_map/pallas_call | solution.py:90
  69.6 4.6 %collective-permute-done.22.refs_18_ = bf16[2,512,256]{2,1,0:T(8,128)(2,1)} collective-permute-done((bf16[2,512,256]{2,1,0:T(8,128)(2,1)}, bf16[2,512,256]{2,1,0:T(8,128)(2,1)}, u32[]{:S(2)}, u32[]{:S(2)}) %collective-permute-start.22) | collective-permute-done | bytes 524320 | tf_op jit(solution)/shard_map/ppermute | solution.py:27
  74.2 6.5 %collective-permute-done.19 = bf16[2,768,256]{2,1,0:T(8,128)(2,1)S(1)} collective-permute-done((bf16[2,768,256]{2,1,0:T(8,128)(2,1)}, bf16[2,768,256]{2,1,0:T(8,128)(2,1)S(1)}, u32[]{:S(2)}, u32[]{:S(2)}) %collective-permute-start.19) | collective-permute-done | bytes 786464 | tf_op jit(solution)/shard_map/ppermute | solution.py:27
  86.6 2.4 %collective-permute-start.25 = (bf16[768,256]{1,0:T(8,128)(2,1)}, bf16[768,256]{1,0:T(8,128)(2,1)}, u32[]{:S(2)}, u32[]{:S(2)}) collective-permute-start(bf16[768,256]{1,0:T(8,128)(2,1)} %get-tuple-element.109), channel_id=1, source_target_pairs={{0,4},{1,13},{2,6},{3,15},{4,8},{5,1},{6,10},{7,3},{8,12},{9,5},{1... | collective-permute-start | bytes 1179656 | tf_op jit(solution)/shard_map/ppermute | solution.py:27
  90.9 2.5 %collective-permute-done.23 = bf16[768,256]{1,0:T(8,128)(2,1)S(1)} collective-permute-done((bf16[768,256]{1,0:T(8,128)(2,1)S(1)}, bf16[768,256]{1,0:T(8,128)(2,1)S(1)}, u32[]{:S(2)}, u32[]{:S(2)}) %collective-permute-start.23) | collective-permute-done | bytes 393248 | tf_op jit(solution)/shard_map/ppermute | solution.py:27
  94.3 5.9 %collective-permute-start.24 = (bf16[768,256]{1,0:T(8,128)(2,1)}, bf16[768,256]{1,0:T(8,128)(2,1)}, u32[]{:S(2)}, u32[]{:S(2)}) collective-permute-start(bf16[768,256]{1,0:T(8,128)(2,1)} %fusion.3), channel_id=1, source_target_pairs={{0,2},{1,3},{2,0},{3,1},{4,6},{5,7},{6,4},{7,5},{8,10},{9,11},{10,... | collective-permute-start | bytes 1179656 | tf_op jit(solution)/shard_map/ppermute | solution.py:27
  100.2 7.7 %convolution_convert_fusion = bf16[2048,512]{1,0:T(8,128)(2,1)} fusion(bf16[1536,2048]{1,0:T(8,128)(2,1)} %all-gather.2.cloned.1.call-done, bf16[1536,512]{1,0:T(8,128)(2,1)S(1)} %get-tuple-element.112), kind=kOutput, calls=%fused_computation.4 | convolution fusion | flops 3222274048 | bytes 9961472 | tf_op jit(solution)/shard_map/dot_general | solution.py:63
  110.7 3.2 %collective-permute-start.28 = (bf16[768,256]{1,0:T(8,128)(2,1)S(1)}, bf16[768,256]{1,0:T(8,128)(2,1)S(1)}, u32[]{:S(2)}, u32[]{:S(2)}) collective-permute-start(bf16[768,256]{1,0:T(8,128)(2,1)S(1)} %get-tuple-element.108.refs_0_), channel_id=1, source_target_pairs={{0,12},{1,13},{2,14},{3,15},{4,0},{5,1},{6,2},{7,3},{8,4},{9,5},{1... | collective-permute-start | bytes 1179656 | tf_op jit(solution)/shard_map/ppermute | solution.py:27
  113.9 3.2 %collective-permute-start.27 = (bf16[768,256]{1,0:T(8,128)(2,1)S(1)}, bf16[768,256]{1,0:T(8,128)(2,1)S(1)}, u32[]{:S(2)}, u32[]{:S(2)}) collective-permute-start(bf16[768,256]{1,0:T(8,128)(2,1)S(1)} %get-tuple-element.108.refs_0_), channel_id=1, source_target_pairs={{0,2},{1,3},{2,0},{3,1},{4,6},{5,7},{6,4},{7,5},{8,10},{9,11},{10,... | collective-permute-start | bytes 1179656 | tf_op jit(solution)/shard_map/ppermute | solution.py:27
  117.1 4.3 %collective-permute-done.29.refs_4_ = bf16[768,256]{1,0:T(8,128)(2,1)S(1)} collective-permute-done((bf16[768,256]{1,0:T(8,128)(2,1)S(1)}, bf16[768,256]{1,0:T(8,128)(2,1)S(1)}, u32[]{:S(2)}, u32[]{:S(2)}) %collective-permute-start.29) | collective-permute-done | bytes 393248 | tf_op jit(solution)/shard_map/ppermute | solution.py:27
  121.5 3.0 %collective-permute-done.27.refs_1_ = bf16[768,256]{1,0:T(8,128)(2,1)S(1)} collective-permute-done((bf16[768,256]{1,0:T(8,128)(2,1)S(1)}, bf16[768,256]{1,0:T(8,128)(2,1)S(1)}, u32[]{:S(2)}, u32[]{:S(2)}) %collective-permute-start.27) | collective-permute-done | bytes 393248 | tf_op jit(solution)/shard_map/ppermute | solution.py:27
  124.6 3.2 %collective-permute-start.30 = (bf16[768,256]{1,0:T(8,128)(2,1)S(1)}, bf16[768,256]{1,0:T(8,128)(2,1)S(1)}, u32[]{:S(2)}, u32[]{:S(2)}) collective-permute-start(bf16[768,256]{1,0:T(8,128)(2,1)S(1)} %collective-permute-done.27.refs_1_), channel_id=1, source_target_pairs={{0,12},{1,13},{2,14},{3,15},{4,0},{5,1},{6,2},{7,3},{8,4},{9,5},{1... | collective-permute-start | bytes 1179656 | tf_op jit(solution)/shard_map/ppermute | solution.py:27
  129.3 3.3 %collective-permute-done.34 = f32[5,128]{1,0:T(8,128)S(1)} collective-permute-done((f32[5,128]{1,0:T(8,128)S(1)}, f32[5,128]{1,0:T(8,128)S(1)}, u32[]{:S(2)}, u32[]{:S(2)}) %collective-permute-start.34) | collective-permute-done | bytes 2592 | tf_op jit(solution)/shard_map/ppermute | solution.py:27
  132.6 5.4 %collective-permute-done.32.refs_6_ = bf16[768,256]{1,0:T(8,128)(2,1)S(1)} collective-permute-done((bf16[768,256]{1,0:T(8,128)(2,1)S(1)}, bf16[768,256]{1,0:T(8,128)(2,1)S(1)}, u32[]{:S(2)}, u32[]{:S(2)}) %collective-permute-start.32) | collective-permute-done | bytes 393248 | tf_op jit(solution)/shard_map/ppermute | solution.py:27
  138.4 2.8 %collective-permute-start.38 = (bf16[768,256]{1,0:T(8,128)(2,1)S(1)}, bf16[768,256]{1,0:T(8,128)(2,1)S(1)}, u32[]{:S(2)}, u32[]{:S(2)}) collective-permute-start(bf16[768,256]{1,0:T(8,128)(2,1)S(1)} %collective-permute-done.27.refs_1_), channel_id=1, source_target_pairs={{0,1},{1,0},{2,3},{3,2},{4,5},{5,4},{6,7},{7,6},{8,9},{9,8},{10,11... | collective-permute-start | bytes 1179656 | tf_op jit(solution)/shard_map/ppermute | solution.py:27
  149.2 8.6 %shard_map.139 = (bf16[2,512,256]{2,1,0:T(8,128)(2,1)}, bf16[2,512,256]{2,1,0:T(8,128)(2,1)}, bf16[2,512,256]{2,1,0:T(8,128)(2,1)}, bf16[2,512,256]{2,1,0:T(8,128)(2,1)}) custom-call(s32[2]{0:T(128)} %pad_add_fusion.here, bf16[512,1536]{1,0:T(8,128)(2,1)} %bitcast.58, bf16[768,256]{1,0:T(8,128)(2,1)} %copy-done.8, bf16[768,256]{1,0:T(8,128)(2,1)} %copy-done.16, ...), custom_call_target="tpu_custom_call" | custom-call | flops 3221225472 | bytes 10485760 | tf_op jit(solution)/shard_map/pallas_call | solution.py:90
  159.6 2.6 %collective-permute-start.46 = (bf16[2,512,256]{2,1,0:T(8,128)(2,1)}, bf16[2,512,256]{2,1,0:T(8,128)(2,1)S(1)}, u32[]{:S(2)}, u32[]{:S(2)}) collective-permute-start(bf16[2,512,256]{2,1,0:T(8,128)(2,1)} %get-tuple-element.93), channel_id=1, source_target_pairs={{0,48},{1,17},{2,50},{3,19},{4,52},{5,21},{6,54},{7,23},{8,56},{9,... | collective-permute-start | bytes 1572872 | tf_op jit(solution)/shard_map/ppermute | solution.py:27
  162.2 9.6 %shard_map.140 = bf16[1536,512]{1,0:T(8,128)(2,1)} custom-call(s32[2]{0:T(128)} %pad_add_fusion.here, bf16[1536,512]{1,0:T(8,128)(2,1)} %cot.1, bf16[768,256]{1,0:T(8,128)(2,1)} %copy-done.8, bf16[768,256]{1,0:T(8,128)(2,1)} %copy-done.16, bf16[768,256]{1,0:T(8,128)(2,1)} %copy-done.5, bf16[768,256]{1,0:T(8,128)(2,1)} %copy-done.7, ...), custom_call_target="tpu_custom_call" | custom-call | flops 3221225472 | bytes 12582912 | tf_op jit(solution)/shard_map/pallas_call | solution.py:90
  171.8 2.5 %collective-permute-done.45 = bf16[2,512,256]{2,1,0:T(8,128)(2,1)S(1)} collective-permute-done((bf16[2,512,256]{2,1,0:T(8,128)(2,1)}, bf16[2,512,256]{2,1,0:T(8,128)(2,1)S(1)}, u32[]{:S(2)}, u32[]{:S(2)}) %collective-permute-start.45) | collective-permute-done | bytes 524320 | tf_op jit(solution)/shard_map/ppermute | solution.py:27
  174.6 3.0 %collective-permute-start.49 = (f32[5,128]{1,0:T(8,128)S(1)}, f32[5,128]{1,0:T(8,128)S(1)}, u32[]{:S(2)}, u32[]{:S(2)}) collective-permute-start(f32[5,128]{1,0:T(8,128)S(1)} %add.108), channel_id=1, source_target_pairs={{0,64},{1,65},{2,66},{3,67},{4,68},{5,69},{6,70},{7,71},{8,72},{9,... | collective-permute-start | bytes 7688 | tf_op jit(solution)/shard_map/ppermute | solution.py:27
  182.4 2.9 %collective-permute-start.50 = (bf16[512,256]{1,0:T(8,128)(2,1)S(1)}, bf16[512,256]{1,0:T(8,128)(2,1)S(1)}, u32[]{:S(2)}, u32[]{:S(2)}) collective-permute-start(bf16[512,256]{1,0:T(8,128)(2,1)S(1)} %fusion.7), channel_id=1, source_target_pairs={{0,64},{1,65},{2,66},{3,67},{4,68},{5,69},{6,70},{7,71},{8,72},{9,... | collective-permute-start | bytes 786440 | tf_op jit(solution)/shard_map/ppermute | solution.py:27
  186.7 3.0 %collective-permute-done.50 = bf16[512,256]{1,0:T(8,128)(2,1)S(1)} collective-permute-done((bf16[512,256]{1,0:T(8,128)(2,1)S(1)}, bf16[512,256]{1,0:T(8,128)(2,1)S(1)}, u32[]{:S(2)}, u32[]{:S(2)}) %collective-permute-start.50) | collective-permute-done | bytes 262176 | tf_op jit(solution)/shard_map/ppermute | solution.py:27
  (193 shorter events, 52.9 us)
Async XLA Ops:
  7.2 93.1 %all-gather.2.cloned.1.call-start = ((), (), s32[]{:S(2)}) async-start(), calls=%async_computation.1 | async-start | bytes 6684672 | tf_op jit(solution)/shard_map/all_gather | solution.py:243
  9.8 170.7 %reduce-scatter.2.cloned.1.call-start = ((), (), s32[]{:S(2)}) async-start(), calls=%async_computation.2 | async-start | bytes 2359296 | tf_op jit(solution)/shard_map/reduce_scatter | solution.py:308
  9.8 10.7 %collective-permute-start.2 = (bf16[256,512]{1,0:T(8,128)(2,1)}, bf16[256,512]{1,0:T(8,128)(2,1)S(1)}, u32[]{:S(2)}, u32[]{:S(2)}) collective-permute-start(bf16[256,512]{1,0:T(8,128)(2,1)} %refs_0_.3), channel_id=1, source_target_pairs={{0,16},{1,17},{2,18},{3,19},{4,20},{5,21},{6,22},{7,23},{8,24},{9,... | collective-permute-start | bytes 786440 | tf_op jit(solution)/shard_map/ppermute | solution.py:27
  11.9 8.6 %collective-permute-start.1 = (bf16[256,512]{1,0:T(8,128)(2,1)}, bf16[256,512]{1,0:T(8,128)(2,1)}, u32[]{:S(2)}, u32[]{:S(2)}) collective-permute-start(bf16[256,512]{1,0:T(8,128)(2,1)} %refs_0_.3), channel_id=1, source_target_pairs={{0,48},{1,49},{2,50},{3,51},{4,52},{5,53},{6,54},{7,55},{8,56},{9,... | collective-permute-start | bytes 786440 | tf_op jit(solution)/shard_map/ppermute | solution.py:27
  22.2 9.3 %collective-permute-start.6 = (bf16[768,512]{1,0:T(8,128)(2,1)S(1)}, bf16[768,512]{1,0:T(8,128)(2,1)}, u32[]{:S(2)}, u32[]{:S(2)}) collective-permute-start(bf16[768,512]{1,0:T(8,128)(2,1)S(1)} %get-tuple-element.58), channel_id=1, source_target_pairs={{0,1},{1,0},{2,3},{3,2},{4,5},{5,4},{6,7},{7,6},{8,9},{9,8},{10,11... | collective-permute-start | bytes 2359304 | tf_op jit(solution)/shard_map/ppermute | solution.py:27
  24.9 13.4 %collective-permute-start.4 = (bf16[256,512]{1,0:T(8,128)(2,1)}, bf16[256,512]{1,0:T(8,128)(2,1)S(1)}, u32[]{:S(2)}, u32[]{:S(2)}) collective-permute-start(bf16[256,512]{1,0:T(8,128)(2,1)} %collective-permute-done.refs_1_), channel_id=1, source_target_pairs={{0,16},{1,17},{2,18},{3,19},{4,20},{5,21},{6,22},{7,23},{8,24},{9,... | collective-permute-start | bytes 786440 | tf_op jit(solution)/shard_map/ppermute | solution.py:27
  24.9 13.4 %collective-permute-start.3 = (bf16[256,512]{1,0:T(8,128)(2,1)}, bf16[256,512]{1,0:T(8,128)(2,1)S(1)}, u32[]{:S(2)}, u32[]{:S(2)}) collective-permute-start(bf16[256,512]{1,0:T(8,128)(2,1)} %collective-permute-done.refs_1_), channel_id=1, source_target_pairs={{0,48},{1,49},{2,50},{3,51},{4,52},{5,53},{6,54},{7,55},{8,56},{9,... | collective-permute-start | bytes 786440 | tf_op jit(solution)/shard_map/ppermute | solution.py:27
  29.1 8.7 %collective-permute-start.5 = (bf16[256,512]{1,0:T(8,128)(2,1)S(1)}, bf16[256,512]{1,0:T(8,128)(2,1)S(1)}, u32[]{:S(2)}, u32[]{:S(2)}) collective-permute-start(bf16[256,512]{1,0:T(8,128)(2,1)S(1)} %broadcast_select_fusion.4), channel_id=1, source_target_pairs={{0,16},{1,49},{2,18},{3,51},{4,20},{5,53},{6,22},{7,55},{8,24},{9,... | collective-permute-start | bytes 786440 | tf_op jit(solution)/shard_map/ppermute | solution.py:27
  29.2 8.6 %collective-permute-start.7 = (bf16[512,256]{1,0:T(8,128)(2,1)S(1)}, bf16[512,256]{1,0:T(8,128)(2,1)S(1)}, u32[]{:S(2)}, u32[]{:S(2)}) collective-permute-start(bf16[512,256]{1,0:T(8,128)(2,1)S(1)} %copy-done.9), channel_id=1, source_target_pairs={{0,64},{1,65},{2,66},{3,67},{4,68},{5,69},{6,70},{7,71},{8,72},{9,... | collective-permute-start | bytes 786440 | tf_op jit(solution)/shard_map/ppermute | solution.py:27
  31.5 9.4 %collective-permute-start.11 = (bf16[256,512]{1,0:T(8,128)(2,1)}, bf16[256,512]{1,0:T(8,128)(2,1)S(1)}, u32[]{:S(2)}, u32[]{:S(2)}) collective-permute-start(bf16[256,512]{1,0:T(8,128)(2,1)} %refs_0_.3), channel_id=1, source_target_pairs={{0,1},{1,0},{2,3},{3,2},{4,5},{5,4},{6,7},{7,6},{8,9},{9,8},{10,11... | collective-permute-start | bytes 786440 | tf_op jit(solution)/shard_map/ppermute | solution.py:27
  46.9 12.5 %collective-permute-start.9 = (f32[2,128]{1,0:T(2,128)S(1)}, f32[2,128]{1,0:T(2,128)S(1)}, u32[]{:S(2)}, u32[]{:S(2)}) collective-permute-start(f32[2,128]{1,0:T(2,128)S(1)} %pad_maximum_fusion.4), channel_id=1, source_target_pairs={{0,1},{1,0},{2,3},{3,2},{4,5},{5,4},{6,7},{7,6},{8,9},{9,8},{10,11... | collective-permute-start | bytes 3080 | tf_op jit(solution)/shard_map/ppermute | solution.py:27
  56.2 24.5 %collective-permute-start.19 = (bf16[2,768,256]{2,1,0:T(8,128)(2,1)}, bf16[2,768,256]{2,1,0:T(8,128)(2,1)S(1)}, u32[]{:S(2)}, u32[]{:S(2)}) collective-permute-start(bf16[2,768,256]{2,1,0:T(8,128)(2,1)} %get-tuple-element.69), channel_id=1, source_target_pairs={{0,4},{1,13},{2,6},{3,15},{4,8},{5,1},{6,10},{7,3},{8,12},{9,5},{1... | collective-permute-start | bytes 2359304 | tf_op jit(solution)/shard_map/ppermute | solution.py:27
  57.7 24.2 %collective-permute-start.20 = (bf16[2,768,256]{2,1,0:T(8,128)(2,1)}, bf16[2,768,256]{2,1,0:T(8,128)(2,1)S(1)}, u32[]{:S(2)}, u32[]{:S(2)}) collective-permute-start(bf16[2,768,256]{2,1,0:T(8,128)(2,1)} %get-tuple-element.70), channel_id=1, source_target_pairs={{0,12},{1,5},{2,14},{3,7},{4,0},{5,9},{6,2},{7,11},{8,4},{9,13},{1... | collective-permute-start | bytes 2359304 | tf_op jit(solution)/shard_map/ppermute | solution.py:27
  59.5 14.7 %collective-permute-start.22 = (bf16[2,512,256]{2,1,0:T(8,128)(2,1)}, bf16[2,512,256]{2,1,0:T(8,128)(2,1)}, u32[]{:S(2)}, u32[]{:S(2)}) collective-permute-start(bf16[2,512,256]{2,1,0:T(8,128)(2,1)} %pad_maximum_fusion.1.refs_16_), channel_id=1, source_target_pairs={{0,16},{1,17},{2,18},{3,19},{4,20},{5,21},{6,22},{7,23},{8,24},{9,... | collective-permute-start | bytes 1572872 | tf_op jit(solution)/shard_map/ppermute | solution.py:27
  59.6 14.6 %collective-permute-start.21 = (bf16[2,512,256]{2,1,0:T(8,128)(2,1)}, bf16[2,512,256]{2,1,0:T(8,128)(2,1)}, u32[]{:S(2)}, u32[]{:S(2)}) collective-permute-start(bf16[2,512,256]{2,1,0:T(8,128)(2,1)} %pad_maximum_fusion.1.refs_16_), channel_id=1, source_target_pairs={{0,48},{1,49},{2,50},{3,51},{4,52},{5,53},{6,54},{7,55},{8,56},{9,... | collective-permute-start | bytes 1572872 | tf_op jit(solution)/shard_map/ppermute | solution.py:27
  62.9 22.7 %collective-permute-start.8 = (bf16[768,128]{1,0:T(8,128)(2,1)S(1)}, bf16[768,128]{1,0:T(8,128)(2,1)}, u32[]{:S(2)}, u32[]{:S(2)}) collective-permute-start(bf16[768,128]{1,0:T(8,128)(2,1)S(1)} %constant_dynamic-slice_fusion.2), channel_id=1, source_target_pairs={{0,1},{1,0},{2,3},{3,2},{4,5},{5,4},{6,7},{7,6},{8,9},{9,8},{10,11... | collective-permute-start | bytes 589832 | tf_op jit(solution)/shard_map/ppermute | solution.py:27
  84.0 9.4 %collective-permute-start.23 = (bf16[768,256]{1,0:T(8,128)(2,1)S(1)}, bf16[768,256]{1,0:T(8,128)(2,1)S(1)}, u32[]{:S(2)}, u32[]{:S(2)}) collective-permute-start(bf16[768,256]{1,0:T(8,128)(2,1)S(1)} %get-tuple-element.110), channel_id=1, source_target_pairs={{0,4},{1,13},{2,6},{3,15},{4,8},{5,1},{6,10},{7,3},{8,12},{9,5},{1... | collective-permute-start | bytes 1179656 | tf_op jit(solution)/shard_map/ppermute | solution.py:27
  86.6 21.3 %collective-permute-start.25 = (bf16[768,256]{1,0:T(8,128)(2,1)}, bf16[768,256]{1,0:T(8,128)(2,1)}, u32[]{:S(2)}, u32[]{:S(2)}) collective-permute-start(bf16[768,256]{1,0:T(8,128)(2,1)} %get-tuple-element.109), channel_id=1, source_target_pairs={{0,4},{1,13},{2,6},{3,15},{4,8},{5,1},{6,10},{7,3},{8,12},{9,5},{1... | collective-permute-start | bytes 1179656 | tf_op jit(solution)/shard_map/ppermute | solution.py:27
  90.9 17.0 %collective-permute-start.26 = (bf16[2,512,256]{2,1,0:T(8,128)(2,1)}, bf16[2,512,256]{2,1,0:T(8,128)(2,1)}, u32[]{:S(2)}, u32[]{:S(2)}) collective-permute-start(bf16[2,512,256]{2,1,0:T(8,128)(2,1)} %broadcast_select_fusion), channel_id=1, source_target_pairs={{0,16},{1,49},{2,18},{3,51},{4,20},{5,53},{6,22},{7,55},{8,24},{9,... | collective-permute-start | bytes 1572872 | tf_op jit(solution)/shard_map/ppermute | solution.py:27
  94.3 14.7 %collective-permute-start.24 = (bf16[768,256]{1,0:T(8,128)(2,1)}, bf16[768,256]{1,0:T(8,128)(2,1)}, u32[]{:S(2)}, u32[]{:S(2)}) collective-permute-start(bf16[768,256]{1,0:T(8,128)(2,1)} %fusion.3), channel_id=1, source_target_pairs={{0,2},{1,3},{2,0},{3,1},{4,6},{5,7},{6,4},{7,5},{8,10},{9,11},{10,... | collective-permute-start | bytes 1179656 | tf_op jit(solution)/shard_map/ppermute | solution.py:27
  110.6 10.9 %collective-permute-start.29 = (bf16[768,256]{1,0:T(8,128)(2,1)S(1)}, bf16[768,256]{1,0:T(8,128)(2,1)S(1)}, u32[]{:S(2)}, u32[]{:S(2)}) collective-permute-start(bf16[768,256]{1,0:T(8,128)(2,1)S(1)} %get-tuple-element.108.refs_0_), channel_id=1, source_target_pairs={{0,4},{1,5},{2,6},{3,7},{4,8},{5,9},{6,10},{7,11},{8,12},{9,13},{1... | collective-permute-start | bytes 1179656 | tf_op jit(solution)/shard_map/ppermute | solution.py:27
  110.7 10.8 %collective-permute-start.28 = (bf16[768,256]{1,0:T(8,128)(2,1)S(1)}, bf16[768,256]{1,0:T(8,128)(2,1)S(1)}, u32[]{:S(2)}, u32[]{:S(2)}) collective-permute-start(bf16[768,256]{1,0:T(8,128)(2,1)S(1)} %get-tuple-element.108.refs_0_), channel_id=1, source_target_pairs={{0,12},{1,13},{2,14},{3,15},{4,0},{5,1},{6,2},{7,3},{8,4},{9,5},{1... | collective-permute-start | bytes 1179656 | tf_op jit(solution)/shard_map/ppermute | solution.py:27
  113.9 10.5 %collective-permute-start.27 = (bf16[768,256]{1,0:T(8,128)(2,1)S(1)}, bf16[768,256]{1,0:T(8,128)(2,1)S(1)}, u32[]{:S(2)}, u32[]{:S(2)}) collective-permute-start(bf16[768,256]{1,0:T(8,128)(2,1)S(1)} %get-tuple-element.108.refs_0_), channel_id=1, source_target_pairs={{0,2},{1,3},{2,0},{3,1},{4,6},{5,7},{6,4},{7,5},{8,10},{9,11},{10,... | collective-permute-start | bytes 1179656 | tf_op jit(solution)/shard_map/ppermute | solution.py:27
  124.5 13.6 %collective-permute-start.31 = (bf16[768,256]{1,0:T(8,128)(2,1)S(1)}, bf16[768,256]{1,0:T(8,128)(2,1)S(1)}, u32[]{:S(2)}, u32[]{:S(2)}) collective-permute-start(bf16[768,256]{1,0:T(8,128)(2,1)S(1)} %collective-permute-done.27.refs_1_), channel_id=1, source_target_pairs={{0,4},{1,5},{2,6},{3,7},{4,8},{5,9},{6,10},{7,11},{8,12},{9,13},{1... | collective-permute-start | bytes 1179656 | tf_op jit(solution)/shard_map/ppermute | solution.py:27
  124.6 13.5 %collective-permute-start.30 = (bf16[768,256]{1,0:T(8,128)(2,1)S(1)}, bf16[768,256]{1,0:T(8,128)(2,1)S(1)}, u32[]{:S(2)}, u32[]{:S(2)}) collective-permute-start(bf16[768,256]{1,0:T(8,128)(2,1)S(1)} %collective-permute-done.27.refs_1_), channel_id=1, source_target_pairs={{0,12},{1,13},{2,14},{3,15},{4,0},{5,1},{6,2},{7,3},{8,4},{9,5},{1... | collective-permute-start | bytes 1179656 | tf_op jit(solution)/shard_map/ppermute | solution.py:27
  127.8 10.2 %collective-permute-start.32 = (bf16[768,256]{1,0:T(8,128)(2,1)S(1)}, bf16[768,256]{1,0:T(8,128)(2,1)S(1)}, u32[]{:S(2)}, u32[]{:S(2)}) collective-permute-start(bf16[768,256]{1,0:T(8,128)(2,1)S(1)} %broadcast_select_fusion.2), channel_id=1, source_target_pairs={{0,4},{1,13},{2,6},{3,15},{4,8},{5,1},{6,10},{7,3},{8,12},{9,5},{1... | collective-permute-start | bytes 1179656 | tf_op jit(solution)/shard_map/ppermute | solution.py:27
  129.0 9.3 %collective-permute-start.37 = (bf16[768,256]{1,0:T(8,128)(2,1)S(1)}, bf16[768,256]{1,0:T(8,128)(2,1)S(1)}, u32[]{:S(2)}, u32[]{:S(2)}) collective-permute-start(bf16[768,256]{1,0:T(8,128)(2,1)S(1)} %get-tuple-element.108.refs_0_), channel_id=1, source_target_pairs={{0,1},{1,0},{2,3},{3,2},{4,5},{5,4},{6,7},{7,6},{8,9},{9,8},{10,11... | collective-permute-start | bytes 1179656 | tf_op jit(solution)/shard_map/ppermute | solution.py:27
  132.6 8.6 %collective-permute-start.39 = (bf16[768,256]{1,0:T(8,128)(2,1)S(1)}, bf16[768,256]{1,0:T(8,128)(2,1)S(1)}, u32[]{:S(2)}, u32[]{:S(2)}) collective-permute-start(bf16[768,256]{1,0:T(8,128)(2,1)S(1)} %collective-permute-done.28.refs_2_), channel_id=1, source_target_pairs={{0,1},{1,0},{2,3},{3,2},{4,5},{5,4},{6,7},{7,6},{8,9},{9,8},{10,11... | collective-permute-start | bytes 1179656 | tf_op jit(solution)/shard_map/ppermute | solution.py:27
  138.2 9.1 %collective-permute-start.35 = (bf16[768,256]{1,0:T(8,128)(2,1)S(1)}, bf16[768,256]{1,0:T(8,128)(2,1)S(1)}, u32[]{:S(2)}, u32[]{:S(2)}) collective-permute-start(bf16[768,256]{1,0:T(8,128)(2,1)S(1)} %broadcast_select_fusion.1), channel_id=1, source_target_pairs={{0,4},{1,13},{2,6},{3,15},{4,8},{5,1},{6,10},{7,3},{8,12},{9,5},{1... | collective-permute-start | bytes 1179656 | tf_op jit(solution)/shard_map/ppermute | solution.py:27
  138.4 8.9 %collective-permute-start.38 = (bf16[768,256]{1,0:T(8,128)(2,1)S(1)}, bf16[768,256]{1,0:T(8,128)(2,1)S(1)}, u32[]{:S(2)}, u32[]{:S(2)}) collective-permute-start(bf16[768,256]{1,0:T(8,128)(2,1)S(1)} %collective-permute-done.27.refs_1_), channel_id=1, source_target_pairs={{0,1},{1,0},{2,3},{3,2},{4,5},{5,4},{6,7},{7,6},{8,9},{9,8},{10,11... | collective-permute-start | bytes 1179656 | tf_op jit(solution)/shard_map/ppermute | solution.py:27
  157.8 16.5 %collective-permute-start.45 = (bf16[2,512,256]{2,1,0:T(8,128)(2,1)}, bf16[2,512,256]{2,1,0:T(8,128)(2,1)S(1)}, u32[]{:S(2)}, u32[]{:S(2)}) collective-permute-start(bf16[2,512,256]{2,1,0:T(8,128)(2,1)} %get-tuple-element.92), channel_id=1, source_target_pairs={{0,16},{1,49},{2,18},{3,51},{4,20},{5,53},{6,22},{7,55},{8,24},{9,... | collective-permute-start | bytes 1572872 | tf_op jit(solution)/shard_map/ppermute | solution.py:27
  159.6 14.8 %collective-permute-start.46 = (bf16[2,512,256]{2,1,0:T(8,128)(2,1)}, bf16[2,512,256]{2,1,0:T(8,128)(2,1)S(1)}, u32[]{:S(2)}, u32[]{:S(2)}) collective-permute-start(bf16[2,512,256]{2,1,0:T(8,128)(2,1)} %get-tuple-element.93), channel_id=1, source_target_pairs={{0,48},{1,17},{2,50},{3,19},{4,52},{5,21},{6,54},{7,23},{8,56},{9,... | collective-permute-start | bytes 1572872 | tf_op jit(solution)/shard_map/ppermute | solution.py:27
  (59 other events, 408.6 us)
Sparse Core Ops, SparseCore 0:
  10.3 78.2 all-gather.1
  124.6 41.6 reduce-scatter.1

commit v11 on v10

--- a/solution.py
+++ b/solution.py
@@ -241,7 +241,6 @@
     mid_gain = scale_mid * keep_mid.astype(F32)
     hidden = jnp.maximum(pre_act.astype(F32) * mid_gain, 0.0).astype(BF16)
     hidden_full = lax.all_gather(hidden, "col", axis=1, tiled=True)
-    out_above, out_below = z_shift(weight_out, -1), z_shift(weight_out, 1)
     out_near = y_lo_swap(weight_out)
 
     wide_gain = scale_wide * keep_wide.astype(F32)
@@ -249,6 +248,8 @@
     grad_conv = (cot_float * wide_gain).astype(BF16)
     wide_part = jnp.sum(cot_float * conv_out.astype(F32), axis=0)
     conv_mine = mine(grad_conv)
+    weight_out, grad_conv = tie(weight_out, grad_conv)
+    out_above, out_below = z_shift(weight_out, -1), z_shift(weight_out, 1)
     conv_sent, input_turned = theirs(grad_conv), inputs.T
     out_near, out_above, out_below, conv_sent, pre_act, weight_in = tie(
         out_near, out_above, out_below, conv_sent, pre_act, weight_in
@@ -257,11 +258,10 @@
     out_across = onward(out_above, out_below, core, z_split)
     in_near = y_lo_swap(weight_in)
     conv_both = jnp.concatenate([conv_mine, core_swap(conv_sent)], axis=1)
-    near_above, near_below, out_across, conv_both, in_near, input_turned, wide_part, place = tie(
-        near_above, near_below, out_across, conv_both, in_near, input_turned, wide_part, place
+    near_above, near_below, out_across, conv_both, in_near, wide_part, place = tie(
+        near_above, near_below, out_across, conv_both, in_near, wide_part, place
     )
     near_across = onward(near_above, near_below, core, z_split)
-    in_here = jnp.stack([weight_in, in_near])
     out_blocks = [
         weight_out, out_near, out_above, near_above, out_below, near_below, out_across, near_across
     ]
@@ -281,10 +281,13 @@
     mid_gain = gain_chip[0] * gain_chip[1]
 
     out_beside = [core_swap(block) for block in out_blocks]
-    near_across, in_here = tie(near_across, in_here)
+    near_across, input_turned = tie(near_across, input_turned)
     out_blocks[7] = near_across
     away, there = hid_partial(place, conv_both, out_blocks, out_beside, ((2, 0), (0, -1)))
     passed, back = x_split(away, 1), x_split(there, -1)
+    away, in_near = tie(away, in_near)
+    in_here = jnp.stack([weight_in, in_near])
+    conv_both, in_here = tie(conv_both, in_here)
     in_above, in_below = z_shift(in_here, -1), z_shift(in_here, 1)
     further, own = hid_partial(place, conv_both, out_blocks, out_beside, ((0, 1), (0, 0)))
     passed, back, own, in_above, in_below = tie(passed, back, own, in_above, in_below)
@@ -323,17 +326,17 @@
     ]
     act_beside = [core_swap(block) for block in act]
     act[7], sums = tie(act[7], sums)
-    sums = sums + y_lo_swap(sums)
 
     away, there, further, own = win_partial(place, input_turned, act, act_beside)
     passed, back = z_split(away, 1), z_split(there, -1)
     grad_x = out_gradient(place, cotangent, act, act_beside, in_blocks)
-    passed, back, grad_x = tie(passed, back, grad_x)
+    grad_wout = wout.astype(F32) * scaling
+    passed, back, grad_x, grad_wout = tie(passed, back, grad_x, grad_wout)
     far = z_split(add([further[1], passed[1]]).astype(BF16), 1)
     near = z_split(add([further[0], passed[0]]).astype(BF16), 1)
-    grad_wout = wout.astype(F32) * scaling
-    far, grad_wout, sums = tie(far, grad_wout, sums)
-    crossed = y_lo_swap(add([own[1], back[1], far]).astype(BF16))
+    crossed, sums = tie(add([own[1], back[1], far]).astype(BF16), sums)
+    crossed = y_lo_swap(crossed)
+    sums = sums + y_lo_swap(sums)
     grad_win = add([own[0], back[0], near, crossed]) * scaling
     grad_smid = keep_mid.astype(F32) * scaling * sums[0]
     grad_swide = keep_wide.astype(F32) * scaling * sums[1:].reshape(512)

time: 198 us -> 201 us (1.015)
  waiting for transfers between devices: 55.7 us -> 68.8 us
  starting transfers between devices: 59.4 us -> 47.2 us
  other arithmetic: 22.5 us -> 25.2 us
    ppermute x51, waiting for transfers between devices: 55.6 us -> 68.7 us  [permute(): return lax.ppermute(v, AXES, pairs)]
    ppermute x51, starting transfers between devices: 59.3 us -> 47.1 us  [permute(): return lax.ppermute(v, AXES, pairs)]
    unnamed x77 -> x67, local copies, waits for them, and re-layouts: 6.4 us -> 4.51 us
  transfers between devices with their start and end apart: 53 -> 53, of which waited for: 21 -> 21; matrix products, arithmetic and copies ran while one was open for 14% -> 15% of each run, Pallas kernels for 16% -> 16%
where the time goes in v11:
time: 201 us; the launch traced here: 200 us
  waiting for transfers between devices  68.8 us (34%)
  starting transfers between devices  47.2 us (23%)
  Pallas kernels  31.2 us (16%)
  other arithmetic  25.2 us (13%)
  between operations  14.6 us (7%)
  matrix products  7.64 us (4%)
  local copies, waits for them, and re-layouts  5.52 us (3%)
    ppermute x51, waiting for transfers between devices, permute(): return lax.ppermute(v, AXES, pairs)  68.7 us
    ppermute x51, starting transfers between devices, permute(): return lax.ppermute(v, AXES, pairs)  47.1 us
    pallas_call x4, Pallas kernels, call(): pl.pallas_call(body, out_shape=outs, in_specs=[pl.BlockSpec(memory_space=...  31.2 us
    dot_general x1, matrix products, dot(): lax.dot_general(a, b, (((ca,), (cb,)), ((), ())), preferred_element_type=...  7.64 us
    select_n x5, other arithmetic, onward(): return split(jnp.where(core == 0, below, above), 1)  4.66 us
    unnamed x67, local copies, waits for them, and re-layouts  4.51 us
  transfers between devices with their start and end apart: 53, of which 21 were waited for; matrix products, arithmetic and copies ran while one was open for 15% of the time, Pallas kernels for 16%

profile of v11, /device:TPU:0, one launch (start us, length us, event | category | flops | bytes accessed | tf_op | source)
XLA Modules:
  0.0 200.1 jit_solution(14250078403263425188)
XLA Ops:
  12.3 2.6 %fusion.1 = (f32[512]{0:T(512)S(1)}, bf16[1536,512]{1,0:T(8,128)(2,1)S(1)}) fusion(bf16[1536,512]{1,0:T(8,128)(2,1)} %cot.1, bf16[1536,512]{1,0:T(8,128)(2,1)} %param.12, f32[512]{0:T(512)S(1)} %convert_multiply_fusion.4), kind=kLoop, calls=%fused_computation.3 | loop fusion | flops 4718080 | bytes 4722688 | tf_op jit(solution)/shard_map/reduce_sum | solution.py:249
  14.9 2.0 collective-permute-start.2
  16.9 2.2 %collective-permute-start.1 = (bf16[256,512]{1,0:T(8,128)(2,1)S(1)}, bf16[256,512]{1,0:T(8,128)(2,1)}, u32[]{:S(2)}, u32[]{:S(2)}) collective-permute-start(bf16[256,512]{1,0:T(8,128)(2,1)S(1)} %copy-done.24), channel_id=1, source_target_pairs={{0,48},{1,49},{2,50},{3,51},{4,52},{5,53},{6,54},{7,55},{8,56},{9,... | collective-permute-start | bytes 786440 | tf_op jit(solution)/shard_map/ppermute | solution.py:27
  20.0 5.1 %collective-permute-done.2.refs_4_ = bf16[256,512]{1,0:T(8,128)(2,1)} collective-permute-done((bf16[256,512]{1,0:T(8,128)(2,1)S(1)}, bf16[256,512]{1,0:T(8,128)(2,1)}, u32[]{:S(2)}, u32[]{:S(2)}) %collective-permute-start.2) | collective-permute-done | bytes 262176 | tf_op jit(solution)/shard_map/ppermute | solution.py:27
  26.5 2.0 %collective-permute-start.3 = (bf16[256,512]{1,0:T(8,128)(2,1)}, bf16[256,512]{1,0:T(8,128)(2,1)}, u32[]{:S(2)}, u32[]{:S(2)}) collective-permute-start(bf16[256,512]{1,0:T(8,128)(2,1)} %collective-permute-done.refs_1_), channel_id=1, source_target_pairs={{0,48},{1,49},{2,50},{3,51},{4,52},{5,53},{6,54},{7,55},{8,56},{9,... | collective-permute-start | bytes 786440 | tf_op jit(solution)/shard_map/ppermute | solution.py:27
  31.9 2.5 %pad_maximum_fusion.conv = bf16[768,1024]{1,0:T(8,128)(2,1)} fusion(bf16[768,512]{1,0:T(8,128)(2,1)} %collective-permute-done.6, bf16[768,512]{1,0:T(8,128)(2,1)S(1)} %constant_dynamic-slice_fusion.3), kind=kLoop, calls=%fused_computation.5 | loop fusion | flops 3145728 | bytes 3145728 | tf_op jit(solution)/shard_map/concatenate | solution.py:260
  34.3 4.0 %collective-permute-done.5.refs_6_ = bf16[256,512]{1,0:T(8,128)(2,1)S(1)} collective-permute-done((bf16[256,512]{1,0:T(8,128)(2,1)S(1)}, bf16[256,512]{1,0:T(8,128)(2,1)S(1)}, u32[]{:S(2)}, u32[]{:S(2)}) %collective-permute-start.5) | collective-permute-done | bytes 262176 | tf_op jit(solution)/shard_map/ppermute | solution.py:27
  46.0 3.1 %collective-permute-done.8.refs_7_ = bf16[256,512]{1,0:T(8,128)(2,1)} collective-permute-done((bf16[256,512]{1,0:T(8,128)(2,1)}, bf16[256,512]{1,0:T(8,128)(2,1)}, u32[]{:S(2)}, u32[]{:S(2)}) %collective-permute-start.8) | collective-permute-done | bytes 262176 | tf_op jit(solution)/shard_map/ppermute | solution.py:27
  51.6 6.4 %shard_map.137 = (bf16[2,768,256]{2,1,0:T(8,128)(2,1)}, bf16[2,768,256]{2,1,0:T(8,128)(2,1)}) custom-call(s32[2]{0:T(128)} %pad_add_fusion.here, bf16[768,1024]{1,0:T(8,128)(2,1)} %pad_maximum_fusion.conv, bf16[256,512]{1,0:T(8,128)(2,1)} %refs_0_.1, bf16[256,512]{1,0:T(8,128)(2,1)} %collective-permute-done.refs_1_, ...), custom_call_target="tpu_custom_call" | custom-call | flops 1610612736 | bytes 8388608 | tf_op jit(solution)/shard_map/pallas_call | solution.py:90
  58.0 2.8 %collective-permute-start.20 = (bf16[2,768,256]{2,1,0:T(8,128)(2,1)}, bf16[2,768,256]{2,1,0:T(8,128)(2,1)S(1)}, u32[]{:S(2)}, u32[]{:S(2)}) collective-permute-start(bf16[2,768,256]{2,1,0:T(8,128)(2,1)} %get-tuple-element.75), channel_id=1, source_target_pairs={{0,12},{1,5},{2,14},{3,7},{4,0},{5,9},{6,2},{7,11},{8,4},{9,13},{1... | collective-permute-start | bytes 2359304 | tf_op jit(solution)/shard_map/ppermute | solution.py:27
  62.7 3.2 %collective-permute-start.21 = (bf16[2,512,256]{2,1,0:T(8,128)(2,1)}, bf16[2,512,256]{2,1,0:T(8,128)(2,1)}, u32[]{:S(2)}, u32[]{:S(2)}) collective-permute-start(bf16[2,512,256]{2,1,0:T(8,128)(2,1)} %pad_maximum_fusion.1.refs_16_), channel_id=1, source_target_pairs={{0,48},{1,49},{2,50},{3,51},{4,52},{5,53},{6,54},{7,55},{8,56},{9,... | collective-permute-start | bytes 1572872 | tf_op jit(solution)/shard_map/ppermute | solution.py:27
  66.2 6.5 %shard_map.138 = (bf16[2,768,256]{2,1,0:T(8,128)(2,1)}, bf16[2,768,256]{2,1,0:T(8,128)(2,1)}) custom-call(s32[2]{0:T(128)} %pad_add_fusion.here, bf16[768,1024]{1,0:T(8,128)(2,1)} %pad_maximum_fusion.conv, bf16[256,512]{1,0:T(8,128)(2,1)} %refs_0_.1, bf16[256,512]{1,0:T(8,128)(2,1)} %collective-permute-done.refs_1_, ...), custom_call_target="tpu_custom_call" | custom-call | flops 1610612736 | bytes 8388608 | tf_op jit(solution)/shard_map/pallas_call | solution.py:90
  72.8 5.3 %collective-permute-done.22.refs_18_ = bf16[2,512,256]{2,1,0:T(8,128)(2,1)} collective-permute-done((bf16[2,512,256]{2,1,0:T(8,128)(2,1)}, bf16[2,512,256]{2,1,0:T(8,128)(2,1)}, u32[]{:S(2)}, u32[]{:S(2)}) %collective-permute-start.22) | collective-permute-done | bytes 524320 | tf_op jit(solution)/shard_map/ppermute | solution.py:27
  78.1 8.0 %collective-permute-done.20 = bf16[2,768,256]{2,1,0:T(8,128)(2,1)S(1)} collective-permute-done((bf16[2,768,256]{2,1,0:T(8,128)(2,1)}, bf16[2,768,256]{2,1,0:T(8,128)(2,1)S(1)}, u32[]{:S(2)}, u32[]{:S(2)}) %collective-permute-start.20) | collective-permute-done | bytes 786464 | tf_op jit(solution)/shard_map/ppermute | solution.py:27
  87.5 2.0 %fusion.11 = (bf16[768,256]{1,0:T(8,128)(2,1)}, bf16[768,256]{1,0:T(8,128)(2,1)S(1)}) fusion(bf16[2,768,256]{2,1,0:T(8,128)(2,1)S(1)} %collective-permute-done.19, bf16[2,768,256]{2,1,0:T(8,128)(2,1)} %get-tuple-element.83), kind=kLoop, calls=%fused_computation.30 | loop fusion | flops 1572864 | bytes 2359296 | tf_op jit(solution)/shard_map/convert_element_type | solution.py:295
  94.4 4.2 %collective-permute-done.23 = bf16[768,256]{1,0:T(8,128)(2,1)S(1)} collective-permute-done((bf16[768,256]{1,0:T(8,128)(2,1)S(1)}, bf16[768,256]{1,0:T(8,128)(2,1)S(1)}, u32[]{:S(2)}, u32[]{:S(2)}) %collective-permute-start.23) | collective-permute-done | bytes 393248 | tf_op jit(solution)/shard_map/ppermute | solution.py:27
  99.4 2.9 %collective-permute-start.24 = (bf16[768,256]{1,0:T(8,128)(2,1)}, bf16[768,256]{1,0:T(8,128)(2,1)}, u32[]{:S(2)}, u32[]{:S(2)}) collective-permute-start(bf16[768,256]{1,0:T(8,128)(2,1)} %fusion.3), channel_id=1, source_target_pairs={{0,2},{1,3},{2,0},{3,1},{4,6},{5,7},{6,4},{7,5},{8,10},{9,11},{10,... | collective-permute-start | bytes 1179656 | tf_op jit(solution)/shard_map/ppermute | solution.py:27
  102.3 7.6 %convolution_convert_fusion = bf16[2048,512]{1,0:T(8,128)(2,1)} fusion(bf16[1536,2048]{1,0:T(8,128)(2,1)} %all-gather.2.cloned.1.call-done, bf16[1536,512]{1,0:T(8,128)(2,1)S(1)} %get-tuple-element.60), kind=kOutput, calls=%fused_computation.4 | convolution fusion | flops 3222274048 | bytes 9961472 | tf_op jit(solution)/shard_map/dot_general | solution.py:63
  112.7 2.3 %collective-permute-start.28 = (bf16[768,256]{1,0:T(8,128)(2,1)S(1)}, bf16[768,256]{1,0:T(8,128)(2,1)S(1)}, u32[]{:S(2)}, u32[]{:S(2)}) collective-permute-start(bf16[768,256]{1,0:T(8,128)(2,1)S(1)} %get-tuple-element.116.refs_0_), channel_id=1, source_target_pairs={{0,12},{1,13},{2,14},{3,15},{4,0},{5,1},{6,2},{7,3},{8,4},{9,5},{1... | collective-permute-start | bytes 1179656 | tf_op jit(solution)/shard_map/ppermute | solution.py:27
  115.0 3.2 %collective-permute-start.27 = (bf16[768,256]{1,0:T(8,128)(2,1)S(1)}, bf16[768,256]{1,0:T(8,128)(2,1)S(1)}, u32[]{:S(2)}, u32[]{:S(2)}) collective-permute-start(bf16[768,256]{1,0:T(8,128)(2,1)S(1)} %get-tuple-element.116.refs_0_), channel_id=1, source_target_pairs={{0,2},{1,3},{2,0},{3,1},{4,6},{5,7},{6,4},{7,5},{8,10},{9,11},{10,... | collective-permute-start | bytes 1179656 | tf_op jit(solution)/shard_map/ppermute | solution.py:27
  118.2 5.0 %collective-permute-done.29.refs_4_ = bf16[768,256]{1,0:T(8,128)(2,1)S(1)} collective-permute-done((bf16[768,256]{1,0:T(8,128)(2,1)S(1)}, bf16[768,256]{1,0:T(8,128)(2,1)S(1)}, u32[]{:S(2)}, u32[]{:S(2)}) %collective-permute-start.29) | collective-permute-done | bytes 393248 | tf_op jit(solution)/shard_map/ppermute | solution.py:27
  123.2 3.0 %collective-permute-done.27.refs_1_ = bf16[768,256]{1,0:T(8,128)(2,1)S(1)} collective-permute-done((bf16[768,256]{1,0:T(8,128)(2,1)S(1)}, bf16[768,256]{1,0:T(8,128)(2,1)S(1)}, u32[]{:S(2)}, u32[]{:S(2)}) %collective-permute-start.27) | collective-permute-done | bytes 393248 | tf_op jit(solution)/shard_map/ppermute | solution.py:27
  126.4 3.2 %collective-permute-start.30 = (bf16[768,256]{1,0:T(8,128)(2,1)S(1)}, bf16[768,256]{1,0:T(8,128)(2,1)S(1)}, u32[]{:S(2)}, u32[]{:S(2)}) collective-permute-start(bf16[768,256]{1,0:T(8,128)(2,1)S(1)} %collective-permute-done.27.refs_1_), channel_id=1, source_target_pairs={{0,12},{1,13},{2,14},{3,15},{4,0},{5,1},{6,2},{7,3},{8,4},{9,5},{1... | collective-permute-start | bytes 1179656 | tf_op jit(solution)/shard_map/ppermute | solution.py:27
  131.1 3.3 %collective-permute-done.34 = f32[5,128]{1,0:T(8,128)S(1)} collective-permute-done((f32[5,128]{1,0:T(8,128)S(1)}, f32[5,128]{1,0:T(8,128)S(1)}, u32[]{:S(2)}, u32[]{:S(2)}) %collective-permute-start.34) | collective-permute-done | bytes 2592 | tf_op jit(solution)/shard_map/ppermute | solution.py:27
  134.4 6.2 %collective-permute-done.32.refs_6_ = bf16[768,256]{1,0:T(8,128)(2,1)S(1)} collective-permute-done((bf16[768,256]{1,0:T(8,128)(2,1)S(1)}, bf16[768,256]{1,0:T(8,128)(2,1)S(1)}, u32[]{:S(2)}, u32[]{:S(2)}) %collective-permute-start.32) | collective-permute-done | bytes 393248 | tf_op jit(solution)/shard_map/ppermute | solution.py:27
  141.2 2.6 %collective-permute-start.38 = (bf16[768,256]{1,0:T(8,128)(2,1)S(1)}, bf16[768,256]{1,0:T(8,128)(2,1)S(1)}, u32[]{:S(2)}, u32[]{:S(2)}) collective-permute-start(bf16[768,256]{1,0:T(8,128)(2,1)S(1)} %collective-permute-done.27.refs_1_), channel_id=1, source_target_pairs={{0,1},{1,0},{2,3},{3,2},{4,5},{5,4},{6,7},{7,6},{8,9},{9,8},{10,11... | collective-permute-start | bytes 1179656 | tf_op jit(solution)/shard_map/ppermute | solution.py:27
  147.6 2.1 %collective-permute-done.35.refs_7_ = bf16[768,256]{1,0:T(8,128)(2,1)S(1)} collective-permute-done((bf16[768,256]{1,0:T(8,128)(2,1)S(1)}, bf16[768,256]{1,0:T(8,128)(2,1)S(1)}, u32[]{:S(2)}, u32[]{:S(2)}) %collective-permute-start.35) | collective-permute-done | bytes 393248 | tf_op jit(solution)/shard_map/ppermute | solution.py:27
  151.7 8.6 %shard_map.139 = (bf16[2,512,256]{2,1,0:T(8,128)(2,1)}, bf16[2,512,256]{2,1,0:T(8,128)(2,1)}, bf16[2,512,256]{2,1,0:T(8,128)(2,1)}, bf16[2,512,256]{2,1,0:T(8,128)(2,1)}) custom-call(s32[2]{0:T(128)} %pad_add_fusion.here, bf16[512,1536]{1,0:T(8,128)(2,1)} %bitcast.58, bf16[768,256]{1,0:T(8,128)(2,1)} %copy-done.9, bf16[768,256]{1,0:T(8,128)(2,1)} %copy-done.14, ...), custom_call_target="tpu_custom_call" | custom-call | flops 3221225472 | bytes 10485760 | tf_op jit(solution)/shard_map/pallas_call | solution.py:90
  160.8 2.8 %collective-permute-start.46 = (bf16[2,512,256]{2,1,0:T(8,128)(2,1)}, bf16[2,512,256]{2,1,0:T(8,128)(2,1)S(1)}, u32[]{:S(2)}, u32[]{:S(2)}) collective-permute-start(bf16[2,512,256]{2,1,0:T(8,128)(2,1)} %get-tuple-element.101), channel_id=1, source_target_pairs={{0,48},{1,17},{2,50},{3,19},{4,52},{5,21},{6,54},{7,23},{8,56},{9,... | collective-permute-start | bytes 1572872 | tf_op jit(solution)/shard_map/ppermute | solution.py:27
  163.6 9.6 %shard_map.140 = bf16[1536,512]{1,0:T(8,128)(2,1)} custom-call(s32[2]{0:T(128)} %pad_add_fusion.here, bf16[1536,512]{1,0:T(8,128)(2,1)} %cot.1, bf16[768,256]{1,0:T(8,128)(2,1)} %copy-done.9, bf16[768,256]{1,0:T(8,128)(2,1)} %copy-done.14, bf16[768,256]{1,0:T(8,128)(2,1)} %copy-done.6, bf16[768,256]{1,0:T(8,128)(2,1)} %copy-done.8, ...), custom_call_target="tpu_custom_call" | custom-call | flops 3221225472 | bytes 12582912 | tf_op jit(solution)/shard_map/pallas_call | solution.py:90
  176.8 7.6 %collective-permute-done.48 = bf16[512,256]{1,0:T(8,128)(2,1)S(1)} collective-permute-done((bf16[512,256]{1,0:T(8,128)(2,1)S(1)}, bf16[512,256]{1,0:T(8,128)(2,1)S(1)}, u32[]{:S(2)}, u32[]{:S(2)}) %collective-permute-start.48) | collective-permute-done | bytes 262176 | tf_op jit(solution)/shard_map/ppermute | solution.py:27
  189.4 2.8 %collective-permute-done.47 = bf16[512,256]{1,0:T(8,128)(2,1)S(1)} collective-permute-done((bf16[512,256]{1,0:T(8,128)(2,1)S(1)}, bf16[512,256]{1,0:T(8,128)(2,1)S(1)}, u32[]{:S(2)}, u32[]{:S(2)}) %collective-permute-start.47) | collective-permute-done | bytes 262176 | tf_op jit(solution)/shard_map/ppermute | solution.py:27
  (184 shorter events, 50.6 us)
Async XLA Ops:
  7.2 95.2 %all-gather.2.cloned.1.call-start = ((), (), s32[]{:S(2)}) async-start(), calls=%async_computation.1 | async-start | bytes 6684672 | tf_op jit(solution)/shard_map/all_gather | solution.py:243
  9.8 163.5 %reduce-scatter.2.cloned.1.call-start = ((), (), s32[]{:S(2)}) async-start(), calls=%async_computation.2 | async-start | bytes 2359296 | tf_op jit(solution)/shard_map/reduce_scatter | solution.py:311
  9.8 10.2 %collective-permute-start = (bf16[256,512]{1,0:T(8,128)(2,1)}, bf16[256,512]{1,0:T(8,128)(2,1)}, u32[]{:S(2)}, u32[]{:S(2)}) collective-permute-start(bf16[256,512]{1,0:T(8,128)(2,1)} %refs_0_.1), channel_id=1, source_target_pairs={{0,64},{1,65},{2,66},{3,67},{4,68},{5,69},{6,70},{7,71},{8,72},{9,... | collective-permute-start | bytes 786440 | tf_op jit(solution)/shard_map/ppermute | solution.py:27
  14.9 10.2 %collective-permute-start.2 = (bf16[256,512]{1,0:T(8,128)(2,1)S(1)}, bf16[256,512]{1,0:T(8,128)(2,1)}, u32[]{:S(2)}, u32[]{:S(2)}) collective-permute-start(bf16[256,512]{1,0:T(8,128)(2,1)S(1)} %copy-done.24), channel_id=1, source_target_pairs={{0,16},{1,17},{2,18},{3,19},{4,20},{5,21},{6,22},{7,23},{8,24},{9,... | collective-permute-start | bytes 786440 | tf_op jit(solution)/shard_map/ppermute | solution.py:27
  16.9 8.3 %collective-permute-start.1 = (bf16[256,512]{1,0:T(8,128)(2,1)S(1)}, bf16[256,512]{1,0:T(8,128)(2,1)}, u32[]{:S(2)}, u32[]{:S(2)}) collective-permute-start(bf16[256,512]{1,0:T(8,128)(2,1)S(1)} %copy-done.24), channel_id=1, source_target_pairs={{0,48},{1,49},{2,50},{3,51},{4,52},{5,53},{6,54},{7,55},{8,56},{9,... | collective-permute-start | bytes 786440 | tf_op jit(solution)/shard_map/ppermute | solution.py:27
  25.2 14.3 %collective-permute-start.4 = (bf16[256,512]{1,0:T(8,128)(2,1)}, bf16[256,512]{1,0:T(8,128)(2,1)}, u32[]{:S(2)}, u32[]{:S(2)}) collective-permute-start(bf16[256,512]{1,0:T(8,128)(2,1)} %collective-permute-done.refs_1_), channel_id=1, source_target_pairs={{0,16},{1,17},{2,18},{3,19},{4,20},{5,21},{6,22},{7,23},{8,24},{9,... | collective-permute-start | bytes 786440 | tf_op jit(solution)/shard_map/ppermute | solution.py:27
  26.5 13.0 %collective-permute-start.3 = (bf16[256,512]{1,0:T(8,128)(2,1)}, bf16[256,512]{1,0:T(8,128)(2,1)}, u32[]{:S(2)}, u32[]{:S(2)}) collective-permute-start(bf16[256,512]{1,0:T(8,128)(2,1)} %collective-permute-done.refs_1_), channel_id=1, source_target_pairs={{0,48},{1,49},{2,50},{3,51},{4,52},{5,53},{6,54},{7,55},{8,56},{9,... | collective-permute-start | bytes 786440 | tf_op jit(solution)/shard_map/ppermute | solution.py:27
  29.5 8.8 %collective-permute-start.5 = (bf16[256,512]{1,0:T(8,128)(2,1)S(1)}, bf16[256,512]{1,0:T(8,128)(2,1)S(1)}, u32[]{:S(2)}, u32[]{:S(2)}) collective-permute-start(bf16[256,512]{1,0:T(8,128)(2,1)S(1)} %broadcast_select_fusion.4), channel_id=1, source_target_pairs={{0,16},{1,49},{2,18},{3,51},{4,20},{5,53},{6,22},{7,55},{8,24},{9,... | collective-permute-start | bytes 786440 | tf_op jit(solution)/shard_map/ppermute | solution.py:27
  29.6 9.0 %collective-permute-start.7 = (bf16[512,256]{1,0:T(8,128)(2,1)S(1)}, bf16[512,256]{1,0:T(8,128)(2,1)S(1)}, u32[]{:S(2)}, u32[]{:S(2)}) collective-permute-start(bf16[512,256]{1,0:T(8,128)(2,1)S(1)} %copy-done.10), channel_id=1, source_target_pairs={{0,64},{1,65},{2,66},{3,67},{4,68},{5,69},{6,70},{7,71},{8,72},{9,... | collective-permute-start | bytes 786440 | tf_op jit(solution)/shard_map/ppermute | solution.py:27
  30.8 14.6 %collective-permute-start.11 = (bf16[256,512]{1,0:T(8,128)(2,1)}, bf16[256,512]{1,0:T(8,128)(2,1)}, u32[]{:S(2)}, u32[]{:S(2)}) collective-permute-start(bf16[256,512]{1,0:T(8,128)(2,1)} %refs_0_.1), channel_id=1, source_target_pairs={{0,1},{1,0},{2,3},{3,2},{4,5},{5,4},{6,7},{7,6},{8,9},{9,8},{10,11... | collective-permute-start | bytes 786440 | tf_op jit(solution)/shard_map/ppermute | solution.py:27
  49.2 11.7 %collective-permute-start.10 = (f32[2,128]{1,0:T(2,128)S(1)}, f32[2,128]{1,0:T(2,128)S(1)}, u32[]{:S(2)}, u32[]{:S(2)}) collective-permute-start(f32[2,128]{1,0:T(2,128)S(1)} %pad_maximum_fusion.4), channel_id=1, source_target_pairs={{0,1},{1,0},{2,3},{3,2},{4,5},{5,4},{6,7},{7,6},{8,9},{9,8},{10,11... | collective-permute-start | bytes 3080 | tf_op jit(solution)/shard_map/ppermute | solution.py:27
  58.0 28.1 %collective-permute-start.20 = (bf16[2,768,256]{2,1,0:T(8,128)(2,1)}, bf16[2,768,256]{2,1,0:T(8,128)(2,1)S(1)}, u32[]{:S(2)}, u32[]{:S(2)}) collective-permute-start(bf16[2,768,256]{2,1,0:T(8,128)(2,1)} %get-tuple-element.75), channel_id=1, source_target_pairs={{0,12},{1,5},{2,14},{3,7},{4,0},{5,9},{6,2},{7,11},{8,4},{9,13},{1... | collective-permute-start | bytes 2359304 | tf_op jit(solution)/shard_map/ppermute | solution.py:27
  60.8 26.7 %collective-permute-start.19 = (bf16[2,768,256]{2,1,0:T(8,128)(2,1)}, bf16[2,768,256]{2,1,0:T(8,128)(2,1)S(1)}, u32[]{:S(2)}, u32[]{:S(2)}) collective-permute-start(bf16[2,768,256]{2,1,0:T(8,128)(2,1)} %get-tuple-element.74), channel_id=1, source_target_pairs={{0,4},{1,13},{2,6},{3,15},{4,8},{5,1},{6,10},{7,3},{8,12},{9,5},{1... | collective-permute-start | bytes 2359304 | tf_op jit(solution)/shard_map/ppermute | solution.py:27
  62.7 15.4 %collective-permute-start.22 = (bf16[2,512,256]{2,1,0:T(8,128)(2,1)}, bf16[2,512,256]{2,1,0:T(8,128)(2,1)}, u32[]{:S(2)}, u32[]{:S(2)}) collective-permute-start(bf16[2,512,256]{2,1,0:T(8,128)(2,1)} %pad_maximum_fusion.1.refs_16_), channel_id=1, source_target_pairs={{0,16},{1,17},{2,18},{3,19},{4,20},{5,21},{6,22},{7,23},{8,24},{9,... | collective-permute-start | bytes 1572872 | tf_op jit(solution)/shard_map/ppermute | solution.py:27
  62.7 15.4 %collective-permute-start.21 = (bf16[2,512,256]{2,1,0:T(8,128)(2,1)}, bf16[2,512,256]{2,1,0:T(8,128)(2,1)}, u32[]{:S(2)}, u32[]{:S(2)}) collective-permute-start(bf16[2,512,256]{2,1,0:T(8,128)(2,1)} %pad_maximum_fusion.1.refs_16_), channel_id=1, source_target_pairs={{0,48},{1,49},{2,50},{3,51},{4,52},{5,53},{6,54},{7,55},{8,56},{9,... | collective-permute-start | bytes 1572872 | tf_op jit(solution)/shard_map/ppermute | solution.py:27
  66.0 23.6 %collective-permute-start.9 = (bf16[768,128]{1,0:T(8,128)(2,1)S(1)}, bf16[768,128]{1,0:T(8,128)(2,1)}, u32[]{:S(2)}, u32[]{:S(2)}) collective-permute-start(bf16[768,128]{1,0:T(8,128)(2,1)S(1)} %constant_dynamic-slice_fusion.2), channel_id=1, source_target_pairs={{0,1},{1,0},{2,3},{3,2},{4,5},{5,4},{6,7},{7,6},{8,9},{9,8},{10,11... | collective-permute-start | bytes 589832 | tf_op jit(solution)/shard_map/ppermute | solution.py:27
  89.6 9.0 %collective-permute-start.23 = (bf16[768,256]{1,0:T(8,128)(2,1)S(1)}, bf16[768,256]{1,0:T(8,128)(2,1)S(1)}, u32[]{:S(2)}, u32[]{:S(2)}) collective-permute-start(bf16[768,256]{1,0:T(8,128)(2,1)S(1)} %get-tuple-element.118), channel_id=1, source_target_pairs={{0,4},{1,13},{2,6},{3,15},{4,8},{5,1},{6,10},{7,3},{8,12},{9,5},{1... | collective-permute-start | bytes 1179656 | tf_op jit(solution)/shard_map/ppermute | solution.py:27
  90.7 19.3 %collective-permute-start.25 = (bf16[768,256]{1,0:T(8,128)(2,1)}, bf16[768,256]{1,0:T(8,128)(2,1)}, u32[]{:S(2)}, u32[]{:S(2)}) collective-permute-start(bf16[768,256]{1,0:T(8,128)(2,1)} %get-tuple-element.117), channel_id=1, source_target_pairs={{0,4},{1,13},{2,6},{3,15},{4,8},{5,1},{6,10},{7,3},{8,12},{9,5},{1... | collective-permute-start | bytes 1179656 | tf_op jit(solution)/shard_map/ppermute | solution.py:27
  94.4 15.6 %collective-permute-start.26 = (bf16[2,512,256]{2,1,0:T(8,128)(2,1)}, bf16[2,512,256]{2,1,0:T(8,128)(2,1)}, u32[]{:S(2)}, u32[]{:S(2)}) collective-permute-start(bf16[2,512,256]{2,1,0:T(8,128)(2,1)} %broadcast_select_fusion), channel_id=1, source_target_pairs={{0,16},{1,49},{2,18},{3,51},{4,20},{5,53},{6,22},{7,55},{8,24},{9,... | collective-permute-start | bytes 1572872 | tf_op jit(solution)/shard_map/ppermute | solution.py:27
  99.4 10.5 %collective-permute-start.24 = (bf16[768,256]{1,0:T(8,128)(2,1)}, bf16[768,256]{1,0:T(8,128)(2,1)}, u32[]{:S(2)}, u32[]{:S(2)}) collective-permute-start(bf16[768,256]{1,0:T(8,128)(2,1)} %fusion.3), channel_id=1, source_target_pairs={{0,2},{1,3},{2,0},{3,1},{4,6},{5,7},{6,4},{7,5},{8,10},{9,11},{10,... | collective-permute-start | bytes 1179656 | tf_op jit(solution)/shard_map/ppermute | solution.py:27
  111.6 11.6 %collective-permute-start.29 = (bf16[768,256]{1,0:T(8,128)(2,1)S(1)}, bf16[768,256]{1,0:T(8,128)(2,1)S(1)}, u32[]{:S(2)}, u32[]{:S(2)}) collective-permute-start(bf16[768,256]{1,0:T(8,128)(2,1)S(1)} %get-tuple-element.116.refs_0_), channel_id=1, source_target_pairs={{0,4},{1,5},{2,6},{3,7},{4,8},{5,9},{6,10},{7,11},{8,12},{9,13},{1... | collective-permute-start | bytes 1179656 | tf_op jit(solution)/shard_map/ppermute | solution.py:27
  112.7 10.5 %collective-permute-start.28 = (bf16[768,256]{1,0:T(8,128)(2,1)S(1)}, bf16[768,256]{1,0:T(8,128)(2,1)S(1)}, u32[]{:S(2)}, u32[]{:S(2)}) collective-permute-start(bf16[768,256]{1,0:T(8,128)(2,1)S(1)} %get-tuple-element.116.refs_0_), channel_id=1, source_target_pairs={{0,12},{1,13},{2,14},{3,15},{4,0},{5,1},{6,2},{7,3},{8,4},{9,5},{1... | collective-permute-start | bytes 1179656 | tf_op jit(solution)/shard_map/ppermute | solution.py:27
  115.0 11.3 %collective-permute-start.27 = (bf16[768,256]{1,0:T(8,128)(2,1)S(1)}, bf16[768,256]{1,0:T(8,128)(2,1)S(1)}, u32[]{:S(2)}, u32[]{:S(2)}) collective-permute-start(bf16[768,256]{1,0:T(8,128)(2,1)S(1)} %get-tuple-element.116.refs_0_), channel_id=1, source_target_pairs={{0,2},{1,3},{2,0},{3,1},{4,6},{5,7},{6,4},{7,5},{8,10},{9,11},{10,... | collective-permute-start | bytes 1179656 | tf_op jit(solution)/shard_map/ppermute | solution.py:27
  126.3 14.3 %collective-permute-start.31 = (bf16[768,256]{1,0:T(8,128)(2,1)S(1)}, bf16[768,256]{1,0:T(8,128)(2,1)S(1)}, u32[]{:S(2)}, u32[]{:S(2)}) collective-permute-start(bf16[768,256]{1,0:T(8,128)(2,1)S(1)} %collective-permute-done.27.refs_1_), channel_id=1, source_target_pairs={{0,4},{1,5},{2,6},{3,7},{4,8},{5,9},{6,10},{7,11},{8,12},{9,13},{1... | collective-permute-start | bytes 1179656 | tf_op jit(solution)/shard_map/ppermute | solution.py:27
  126.4 14.3 %collective-permute-start.30 = (bf16[768,256]{1,0:T(8,128)(2,1)S(1)}, bf16[768,256]{1,0:T(8,128)(2,1)S(1)}, u32[]{:S(2)}, u32[]{:S(2)}) collective-permute-start(bf16[768,256]{1,0:T(8,128)(2,1)S(1)} %collective-permute-done.27.refs_1_), channel_id=1, source_target_pairs={{0,12},{1,13},{2,14},{3,15},{4,0},{5,1},{6,2},{7,3},{8,4},{9,5},{1... | collective-permute-start | bytes 1179656 | tf_op jit(solution)/shard_map/ppermute | solution.py:27
  129.6 10.9 %collective-permute-start.32 = (bf16[768,256]{1,0:T(8,128)(2,1)S(1)}, bf16[768,256]{1,0:T(8,128)(2,1)S(1)}, u32[]{:S(2)}, u32[]{:S(2)}) collective-permute-start(bf16[768,256]{1,0:T(8,128)(2,1)S(1)} %broadcast_select_fusion.2), channel_id=1, source_target_pairs={{0,4},{1,13},{2,6},{3,15},{4,8},{5,1},{6,10},{7,3},{8,12},{9,5},{1... | collective-permute-start | bytes 1179656 | tf_op jit(solution)/shard_map/ppermute | solution.py:27
  130.8 10.3 %collective-permute-start.37 = (bf16[768,256]{1,0:T(8,128)(2,1)S(1)}, bf16[768,256]{1,0:T(8,128)(2,1)S(1)}, u32[]{:S(2)}, u32[]{:S(2)}) collective-permute-start(bf16[768,256]{1,0:T(8,128)(2,1)S(1)} %get-tuple-element.116.refs_0_), channel_id=1, source_target_pairs={{0,1},{1,0},{2,3},{3,2},{4,5},{5,4},{6,7},{7,6},{8,9},{9,8},{10,11... | collective-permute-start | bytes 1179656 | tf_op jit(solution)/shard_map/ppermute | solution.py:27
  134.4 9.4 %collective-permute-start.39 = (bf16[768,256]{1,0:T(8,128)(2,1)S(1)}, bf16[768,256]{1,0:T(8,128)(2,1)S(1)}, u32[]{:S(2)}, u32[]{:S(2)}) collective-permute-start(bf16[768,256]{1,0:T(8,128)(2,1)S(1)} %collective-permute-done.28.refs_2_), channel_id=1, source_target_pairs={{0,1},{1,0},{2,3},{3,2},{4,5},{5,4},{6,7},{7,6},{8,9},{9,8},{10,11... | collective-permute-start | bytes 1179656 | tf_op jit(solution)/shard_map/ppermute | solution.py:27
  140.7 9.1 %collective-permute-start.35 = (bf16[768,256]{1,0:T(8,128)(2,1)S(1)}, bf16[768,256]{1,0:T(8,128)(2,1)S(1)}, u32[]{:S(2)}, u32[]{:S(2)}) collective-permute-start(bf16[768,256]{1,0:T(8,128)(2,1)S(1)} %broadcast_select_fusion.1), channel_id=1, source_target_pairs={{0,4},{1,13},{2,6},{3,15},{4,8},{5,1},{6,10},{7,3},{8,12},{9,5},{1... | collective-permute-start | bytes 1179656 | tf_op jit(solution)/shard_map/ppermute | solution.py:27
  141.2 8.6 %collective-permute-start.38 = (bf16[768,256]{1,0:T(8,128)(2,1)S(1)}, bf16[768,256]{1,0:T(8,128)(2,1)S(1)}, u32[]{:S(2)}, u32[]{:S(2)}) collective-permute-start(bf16[768,256]{1,0:T(8,128)(2,1)S(1)} %collective-permute-done.27.refs_1_), channel_id=1, source_target_pairs={{0,1},{1,0},{2,3},{3,2},{4,5},{5,4},{6,7},{7,6},{8,9},{9,8},{10,11... | collective-permute-start | bytes 1179656 | tf_op jit(solution)/shard_map/ppermute | solution.py:27
  160.3 16.3 %collective-permute-start.45 = (bf16[2,512,256]{2,1,0:T(8,128)(2,1)}, bf16[2,512,256]{2,1,0:T(8,128)(2,1)S(1)}, u32[]{:S(2)}, u32[]{:S(2)}) collective-permute-start(bf16[2,512,256]{2,1,0:T(8,128)(2,1)} %get-tuple-element.100), channel_id=1, source_target_pairs={{0,16},{1,49},{2,18},{3,51},{4,20},{5,53},{6,22},{7,55},{8,24},{9,... | collective-permute-start | bytes 1572872 | tf_op jit(solution)/shard_map/ppermute | solution.py:27
  160.8 15.8 %collective-permute-start.46 = (bf16[2,512,256]{2,1,0:T(8,128)(2,1)}, bf16[2,512,256]{2,1,0:T(8,128)(2,1)S(1)}, u32[]{:S(2)}, u32[]{:S(2)}) collective-permute-start(bf16[2,512,256]{2,1,0:T(8,128)(2,1)} %get-tuple-element.101), channel_id=1, source_target_pairs={{0,48},{1,17},{2,50},{3,19},{4,52},{5,21},{6,54},{7,23},{8,56},{9,... | collective-permute-start | bytes 1572872 | tf_op jit(solution)/shard_map/ppermute | solution.py:27
  (54 other events, 362.4 us)
Sparse Core Ops, SparseCore 0:
  10.3 79.1 all-gather.1
  126.4 40.7 reduce-scatter.1

commit v12 on v11

--- a/solution.py
+++ b/solution.py
@@ -241,6 +241,7 @@
     mid_gain = scale_mid * keep_mid.astype(F32)
     hidden = jnp.maximum(pre_act.astype(F32) * mid_gain, 0.0).astype(BF16)
     hidden_full = lax.all_gather(hidden, "col", axis=1, tiled=True)
+    out_above, out_below = z_shift(weight_out, -1), z_shift(weight_out, 1)
     out_near = y_lo_swap(weight_out)
 
     wide_gain = scale_wide * keep_wide.astype(F32)
@@ -248,8 +249,6 @@
     grad_conv = (cot_float * wide_gain).astype(BF16)
     wide_part = jnp.sum(cot_float * conv_out.astype(F32), axis=0)
     conv_mine = mine(grad_conv)
-    weight_out, grad_conv = tie(weight_out, grad_conv)
-    out_above, out_below = z_shift(weight_out, -1), z_shift(weight_out, 1)
     conv_sent, input_turned = theirs(grad_conv), inputs.T
     out_near, out_above, out_below, conv_sent, pre_act, weight_in = tie(
         out_near, out_above, out_below, conv_sent, pre_act, weight_in

time: 201 us -> 194 us (0.965)
  waiting for transfers between devices: 68.8 us -> 54.2 us
  starting transfers between devices: 47.2 us -> 54.8 us
    ppermute x51, waiting for transfers between devices: 68.7 us -> 54.1 us  [permute(): return lax.ppermute(v, AXES, pairs)]
    ppermute x51, starting transfers between devices: 47.1 us -> 54.7 us  [permute(): return lax.ppermute(v, AXES, pairs)]
    unnamed x67 -> x75, local copies, waits for them, and re-layouts: 4.51 us -> 7.15 us
  transfers between devices with their start and end apart: 53 -> 53, of which waited for: 21 -> 24; matrix products, arithmetic and copies ran while one was open for 15% -> 15% of each run, Pallas kernels for 16% -> 16%
where the time goes in v12:
time: 194 us; the launch traced here: 193 us
  starting transfers between devices  54.8 us (28%)
  waiting for transfers between devices  54.2 us (28%)
  Pallas kernels  31.2 us (16%)
  other arithmetic  23.4 us (12%)
  between operations  14.6 us (8%)
  matrix products  7.66 us (4%)
  local copies, waits for them, and re-layouts  7.29 us (4%)
    ppermute x51, starting transfers between devices, permute(): return lax.ppermute(v, AXES, pairs)  54.7 us
    ppermute x51, waiting for transfers between devices, permute(): return lax.ppermute(v, AXES, pairs)  54.1 us
    pallas_call x4, Pallas kernels, call(): pl.pallas_call(body, out_shape=outs, in_specs=[pl.BlockSpec(memory_space=...  31.2 us
    dot_general x1, matrix products, dot(): lax.dot_general(a, b, (((ca,), (cb,)), ((), ())), preferred_element_type=...  7.66 us
    unnamed x75, local copies, waits for them, and re-layouts  7.15 us
  transfers between devices with their start and end apart: 53, of which 24 were waited for; matrix products, arithmetic and copies ran while one was open for 15% of the time, Pallas kernels for 16%

profile of v12, /device:TPU:0, one launch (start us, length us, event | category | flops | bytes accessed | tf_op | source)
XLA Modules:
  0.0 193.1 jit_solution(14981548936001151727)
XLA Ops:
  9.8 2.1 %collective-permute-start.2 = (bf16[256,512]{1,0:T(8,128)(2,1)}, bf16[256,512]{1,0:T(8,128)(2,1)}, u32[]{:S(2)}, u32[]{:S(2)}) collective-permute-start(bf16[256,512]{1,0:T(8,128)(2,1)} %refs_0_.3), channel_id=1, source_target_pairs={{0,16},{1,17},{2,18},{3,19},{4,20},{5,21},{6,22},{7,23},{8,24},{9,... | collective-permute-start | bytes 786440 | tf_op jit(solution)/shard_map/ppermute | solution.py:27
  11.9 2.2 %collective-permute-start.1 = (bf16[256,512]{1,0:T(8,128)(2,1)}, bf16[256,512]{1,0:T(8,128)(2,1)}, u32[]{:S(2)}, u32[]{:S(2)}) collective-permute-start(bf16[256,512]{1,0:T(8,128)(2,1)} %refs_0_.3), channel_id=1, source_target_pairs={{0,48},{1,49},{2,50},{3,51},{4,52},{5,53},{6,54},{7,55},{8,56},{9,... | collective-permute-start | bytes 786440 | tf_op jit(solution)/shard_map/ppermute | solution.py:27
  16.4 2.6 %fusion.1 = (f32[512]{0:T(512)S(1)}, bf16[1536,512]{1,0:T(8,128)(2,1)S(1)}) fusion(bf16[1536,512]{1,0:T(8,128)(2,1)} %cot.1, bf16[1536,512]{1,0:T(8,128)(2,1)} %param.12, f32[512]{0:T(512)S(1)} %convert_multiply_fusion.4), kind=kLoop, calls=%fused_computation.3 | loop fusion | flops 4718080 | bytes 4722688 | tf_op jit(solution)/shard_map/reduce_sum | solution.py:250
  22.2 3.2 %collective-permute-start.3 = (bf16[256,512]{1,0:T(8,128)(2,1)}, bf16[256,512]{1,0:T(8,128)(2,1)S(1)}, u32[]{:S(2)}, u32[]{:S(2)}) collective-permute-start(bf16[256,512]{1,0:T(8,128)(2,1)} %collective-permute-done.refs_1_), channel_id=1, source_target_pairs={{0,48},{1,49},{2,50},{3,51},{4,52},{5,53},{6,54},{7,55},{8,56},{9,... | collective-permute-start | bytes 786440 | tf_op jit(solution)/shard_map/ppermute | solution.py:27
  28.8 2.5 %pad_maximum_fusion.conv = bf16[768,1024]{1,0:T(8,128)(2,1)} fusion(bf16[768,512]{1,0:T(8,128)(2,1)} %collective-permute-done.6, bf16[768,512]{1,0:T(8,128)(2,1)S(1)} %get-tuple-element.117), kind=kLoop, calls=%fused_computation.5 | loop fusion | flops 3145728 | bytes 3145728 | tf_op jit(solution)/shard_map/concatenate | solution.py:259
  31.2 3.9 %collective-permute-done.5.refs_6_ = bf16[256,512]{1,0:T(8,128)(2,1)S(1)} collective-permute-done((bf16[256,512]{1,0:T(8,128)(2,1)S(1)}, bf16[256,512]{1,0:T(8,128)(2,1)S(1)}, u32[]{:S(2)}, u32[]{:S(2)}) %collective-permute-start.5) | collective-permute-done | bytes 262176 | tf_op jit(solution)/shard_map/ppermute | solution.py:27
  38.0 2.7 %copy.15 = bf16[1536,512]{0,1:T(8,128)(2,1)} copy(bf16[1536,512]{1,0:T(8,128)(2,1)} %param.10) | data formatting | bytes 3145728 | tf_op args[0]
  47.1 6.5 %shard_map.137 = (bf16[2,768,256]{2,1,0:T(8,128)(2,1)}, bf16[2,768,256]{2,1,0:T(8,128)(2,1)}) custom-call(s32[2]{0:T(128)} %pad_add_fusion.here, bf16[768,1024]{1,0:T(8,128)(2,1)} %pad_maximum_fusion.conv, bf16[256,512]{1,0:T(8,128)(2,1)} %refs_0_.3, bf16[256,512]{1,0:T(8,128)(2,1)} %collective-permute-done.refs_1_, ...), custom_call_target="tpu_custom_call" | custom-call | flops 1610612736 | bytes 8388608 | tf_op jit(solution)/shard_map/pallas_call | solution.py:90
  53.7 2.8 %collective-permute-start.20 = (bf16[2,768,256]{2,1,0:T(8,128)(2,1)}, bf16[2,768,256]{2,1,0:T(8,128)(2,1)S(1)}, u32[]{:S(2)}, u32[]{:S(2)}) collective-permute-start(bf16[2,768,256]{2,1,0:T(8,128)(2,1)} %get-tuple-element.71), channel_id=1, source_target_pairs={{0,12},{1,5},{2,14},{3,7},{4,0},{5,9},{6,2},{7,11},{8,4},{9,13},{1... | collective-permute-start | bytes 2359304 | tf_op jit(solution)/shard_map/ppermute | solution.py:27
  58.7 2.8 %collective-permute-start.21 = (bf16[2,512,256]{2,1,0:T(8,128)(2,1)}, bf16[2,512,256]{2,1,0:T(8,128)(2,1)}, u32[]{:S(2)}, u32[]{:S(2)}) collective-permute-start(bf16[2,512,256]{2,1,0:T(8,128)(2,1)} %pad_maximum_fusion.1.refs_16_), channel_id=1, source_target_pairs={{0,48},{1,49},{2,50},{3,51},{4,52},{5,53},{6,54},{7,55},{8,56},{9,... | collective-permute-start | bytes 1572872 | tf_op jit(solution)/shard_map/ppermute | solution.py:27
  61.9 6.4 %shard_map.138 = (bf16[2,768,256]{2,1,0:T(8,128)(2,1)}, bf16[2,768,256]{2,1,0:T(8,128)(2,1)}) custom-call(s32[2]{0:T(128)} %pad_add_fusion.here, bf16[768,1024]{1,0:T(8,128)(2,1)} %pad_maximum_fusion.conv, bf16[256,512]{1,0:T(8,128)(2,1)} %refs_0_.3, bf16[256,512]{1,0:T(8,128)(2,1)} %collective-permute-done.refs_1_, ...), custom_call_target="tpu_custom_call" | custom-call | flops 1610612736 | bytes 8388608 | tf_op jit(solution)/shard_map/pallas_call | solution.py:90
  68.3 5.3 %collective-permute-done.22.refs_18_ = bf16[2,512,256]{2,1,0:T(8,128)(2,1)} collective-permute-done((bf16[2,512,256]{2,1,0:T(8,128)(2,1)}, bf16[2,512,256]{2,1,0:T(8,128)(2,1)}, u32[]{:S(2)}, u32[]{:S(2)}) %collective-permute-start.22) | collective-permute-done | bytes 524320 | tf_op jit(solution)/shard_map/ppermute | solution.py:27
  73.6 4.6 %collective-permute-done.20 = bf16[2,768,256]{2,1,0:T(8,128)(2,1)S(1)} collective-permute-done((bf16[2,768,256]{2,1,0:T(8,128)(2,1)}, bf16[2,768,256]{2,1,0:T(8,128)(2,1)S(1)}, u32[]{:S(2)}, u32[]{:S(2)}) %collective-permute-start.20) | collective-permute-done | bytes 786464 | tf_op jit(solution)/shard_map/ppermute | solution.py:27
  78.9 2.1 %fusion.11 = (bf16[768,256]{1,0:T(8,128)(2,1)}, bf16[768,256]{1,0:T(8,128)(2,1)S(1)}) fusion(bf16[2,768,256]{2,1,0:T(8,128)(2,1)S(1)} %collective-permute-done.19, bf16[2,768,256]{2,1,0:T(8,128)(2,1)} %get-tuple-element.79), kind=kLoop, calls=%fused_computation.30 | loop fusion | flops 1572864 | bytes 2359296 | tf_op jit(solution)/shard_map/convert_element_type | solution.py:294
  84.7 1.9 broadcast_select_fusion
  86.9 3.0 %collective-permute-done.23 = bf16[768,256]{1,0:T(8,128)(2,1)S(1)} collective-permute-done((bf16[768,256]{1,0:T(8,128)(2,1)S(1)}, bf16[768,256]{1,0:T(8,128)(2,1)S(1)}, u32[]{:S(2)}, u32[]{:S(2)}) %collective-permute-start.23) | collective-permute-done | bytes 393248 | tf_op jit(solution)/shard_map/ppermute | solution.py:27
  90.8 5.1 %collective-permute-start.24 = (bf16[768,256]{1,0:T(8,128)(2,1)}, bf16[768,256]{1,0:T(8,128)(2,1)}, u32[]{:S(2)}, u32[]{:S(2)}) collective-permute-start(bf16[768,256]{1,0:T(8,128)(2,1)} %fusion.3), channel_id=1, source_target_pairs={{0,2},{1,3},{2,0},{3,1},{4,6},{5,7},{6,4},{7,5},{8,10},{9,11},{10,... | collective-permute-start | bytes 1179656 | tf_op jit(solution)/shard_map/ppermute | solution.py:27
  96.0 7.7 %convolution_convert_fusion = bf16[2048,512]{1,0:T(8,128)(2,1)} fusion(bf16[1536,2048]{1,0:T(8,128)(2,1)} %all-gather.2.cloned.1.call-done, bf16[1536,512]{1,0:T(8,128)(2,1)S(1)} %get-tuple-element.116), kind=kOutput, calls=%fused_computation.4 | convolution fusion | flops 3222274048 | bytes 9961472 | tf_op jit(solution)/shard_map/dot_general | solution.py:63
  106.0 2.5 %collective-permute-start.28 = (bf16[768,256]{1,0:T(8,128)(2,1)S(1)}, bf16[768,256]{1,0:T(8,128)(2,1)S(1)}, u32[]{:S(2)}, u32[]{:S(2)}) collective-permute-start(bf16[768,256]{1,0:T(8,128)(2,1)S(1)} %get-tuple-element.112.refs_0_), channel_id=1, source_target_pairs={{0,12},{1,13},{2,14},{3,15},{4,0},{5,1},{6,2},{7,3},{8,4},{9,5},{1... | collective-permute-start | bytes 1179656 | tf_op jit(solution)/shard_map/ppermute | solution.py:27
  108.5 2.3 %collective-permute-start.27 = (bf16[768,256]{1,0:T(8,128)(2,1)S(1)}, bf16[768,256]{1,0:T(8,128)(2,1)S(1)}, u32[]{:S(2)}, u32[]{:S(2)}) collective-permute-start(bf16[768,256]{1,0:T(8,128)(2,1)S(1)} %get-tuple-element.112.refs_0_), channel_id=1, source_target_pairs={{0,2},{1,3},{2,0},{3,1},{4,6},{5,7},{6,4},{7,5},{8,10},{9,11},{10,... | collective-permute-start | bytes 1179656 | tf_op jit(solution)/shard_map/ppermute | solution.py:27
  110.8 3.7 %collective-permute-done.29.refs_4_ = bf16[768,256]{1,0:T(8,128)(2,1)S(1)} collective-permute-done((bf16[768,256]{1,0:T(8,128)(2,1)S(1)}, bf16[768,256]{1,0:T(8,128)(2,1)S(1)}, u32[]{:S(2)}, u32[]{:S(2)}) %collective-permute-start.29) | collective-permute-done | bytes 393248 | tf_op jit(solution)/shard_map/ppermute | solution.py:27
  115.1 2.7 %collective-permute-done.27.refs_1_ = bf16[768,256]{1,0:T(8,128)(2,1)S(1)} collective-permute-done((bf16[768,256]{1,0:T(8,128)(2,1)S(1)}, bf16[768,256]{1,0:T(8,128)(2,1)S(1)}, u32[]{:S(2)}, u32[]{:S(2)}) %collective-permute-start.27) | collective-permute-done | bytes 393248 | tf_op jit(solution)/shard_map/ppermute | solution.py:27
  118.4 2.7 %collective-permute-start.30 = (bf16[768,256]{1,0:T(8,128)(2,1)S(1)}, bf16[768,256]{1,0:T(8,128)(2,1)S(1)}, u32[]{:S(2)}, u32[]{:S(2)}) collective-permute-start(bf16[768,256]{1,0:T(8,128)(2,1)S(1)} %collective-permute-done.27.refs_1_), channel_id=1, source_target_pairs={{0,12},{1,13},{2,14},{3,15},{4,0},{5,1},{6,2},{7,3},{8,4},{9,5},{1... | collective-permute-start | bytes 1179656 | tf_op jit(solution)/shard_map/ppermute | solution.py:27
  124.0 2.0 %collective-permute-done.34 = f32[5,128]{1,0:T(8,128)S(1)} collective-permute-done((f32[5,128]{1,0:T(8,128)S(1)}, f32[5,128]{1,0:T(8,128)S(1)}, u32[]{:S(2)}, u32[]{:S(2)}) %collective-permute-start.34) | collective-permute-done | bytes 2592 | tf_op jit(solution)/shard_map/ppermute | solution.py:27
  126.0 5.1 %collective-permute-done.32.refs_6_ = bf16[768,256]{1,0:T(8,128)(2,1)S(1)} collective-permute-done((bf16[768,256]{1,0:T(8,128)(2,1)S(1)}, bf16[768,256]{1,0:T(8,128)(2,1)S(1)}, u32[]{:S(2)}, u32[]{:S(2)}) %collective-permute-start.32) | collective-permute-done | bytes 393248 | tf_op jit(solution)/shard_map/ppermute | solution.py:27
  132.0 4.3 %collective-permute-start.36 = (f32[5,128]{1,0:T(8,128)S(1)}, f32[5,128]{1,0:T(8,128)S(1)}, u32[]{:S(2)}, u32[]{:S(2)}) collective-permute-start(f32[5,128]{1,0:T(8,128)S(1)} %fusion.19), channel_id=1, source_target_pairs={{0,32},{1,33},{2,34},{3,35},{4,36},{5,37},{6,38},{7,39},{8,40},{9,... | collective-permute-start | bytes 7688 | tf_op jit(solution)/shard_map/ppermute | solution.py:27
  138.3 2.0 %collective-permute-done.35.refs_7_ = bf16[768,256]{1,0:T(8,128)(2,1)S(1)} collective-permute-done((bf16[768,256]{1,0:T(8,128)(2,1)S(1)}, bf16[768,256]{1,0:T(8,128)(2,1)S(1)}, u32[]{:S(2)}, u32[]{:S(2)}) %collective-permute-start.35) | collective-permute-done | bytes 393248 | tf_op jit(solution)/shard_map/ppermute | solution.py:27
  142.3 8.7 %shard_map.139 = (bf16[2,512,256]{2,1,0:T(8,128)(2,1)}, bf16[2,512,256]{2,1,0:T(8,128)(2,1)}, bf16[2,512,256]{2,1,0:T(8,128)(2,1)}, bf16[2,512,256]{2,1,0:T(8,128)(2,1)}) custom-call(s32[2]{0:T(128)} %pad_add_fusion.here, bf16[512,1536]{1,0:T(8,128)(2,1)} %bitcast.58, bf16[768,256]{1,0:T(8,128)(2,1)} %copy-done.8, bf16[768,256]{1,0:T(8,128)(2,1)} %copy-done.16, ...), custom_call_target="tpu_custom_call" | custom-call | flops 3221225472 | bytes 10485760 | tf_op jit(solution)/shard_map/pallas_call | solution.py:90
  151.0 3.2 %collective-permute-start.45 = (bf16[2,512,256]{2,1,0:T(8,128)(2,1)}, bf16[2,512,256]{2,1,0:T(8,128)(2,1)S(1)}, u32[]{:S(2)}, u32[]{:S(2)}) collective-permute-start(bf16[2,512,256]{2,1,0:T(8,128)(2,1)} %get-tuple-element.96), channel_id=1, source_target_pairs={{0,16},{1,49},{2,18},{3,51},{4,20},{5,53},{6,22},{7,55},{8,24},{9,... | collective-permute-start | bytes 1572872 | tf_op jit(solution)/shard_map/ppermute | solution.py:27
  154.8 9.6 %shard_map.140 = bf16[1536,512]{1,0:T(8,128)(2,1)} custom-call(s32[2]{0:T(128)} %pad_add_fusion.here, bf16[1536,512]{1,0:T(8,128)(2,1)} %cot.1, bf16[768,256]{1,0:T(8,128)(2,1)} %copy-done.8, bf16[768,256]{1,0:T(8,128)(2,1)} %copy-done.16, bf16[768,256]{1,0:T(8,128)(2,1)} %copy-done.5, bf16[768,256]{1,0:T(8,128)(2,1)} %copy-done.7, ...), custom_call_target="tpu_custom_call" | custom-call | flops 3221225472 | bytes 12582912 | tf_op jit(solution)/shard_map/pallas_call | solution.py:90
  169.4 6.3 %collective-permute-done.48 = bf16[512,256]{1,0:T(8,128)(2,1)S(1)} collective-permute-done((bf16[512,256]{1,0:T(8,128)(2,1)S(1)}, bf16[512,256]{1,0:T(8,128)(2,1)S(1)}, u32[]{:S(2)}, u32[]{:S(2)}) %collective-permute-start.48) | collective-permute-done | bytes 262176 | tf_op jit(solution)/shard_map/ppermute | solution.py:27
  180.6 4.5 %collective-permute-done.47 = bf16[512,256]{1,0:T(8,128)(2,1)S(1)} collective-permute-done((bf16[512,256]{1,0:T(8,128)(2,1)S(1)}, bf16[512,256]{1,0:T(8,128)(2,1)S(1)}, u32[]{:S(2)}, u32[]{:S(2)}) %collective-permute-start.47) | collective-permute-done | bytes 262176 | tf_op jit(solution)/shard_map/ppermute | solution.py:27
  (191 shorter events, 51.5 us)
Async XLA Ops:
  7.2 88.8 %all-gather.2.cloned.1.call-start = ((), (), s32[]{:S(2)}) async-start(), calls=%async_computation.1 | async-start | bytes 6684672 | tf_op jit(solution)/shard_map/all_gather | solution.py:243
  9.8 154.6 %reduce-scatter.2.cloned.1.call-start = ((), (), s32[]{:S(2)}) async-start(), calls=%async_computation.2 | async-start | bytes 2359296 | tf_op jit(solution)/shard_map/reduce_scatter | solution.py:310
  9.8 10.8 %collective-permute-start.2 = (bf16[256,512]{1,0:T(8,128)(2,1)}, bf16[256,512]{1,0:T(8,128)(2,1)}, u32[]{:S(2)}, u32[]{:S(2)}) collective-permute-start(bf16[256,512]{1,0:T(8,128)(2,1)} %refs_0_.3), channel_id=1, source_target_pairs={{0,16},{1,17},{2,18},{3,19},{4,20},{5,21},{6,22},{7,23},{8,24},{9,... | collective-permute-start | bytes 786440 | tf_op jit(solution)/shard_map/ppermute | solution.py:27
  11.9 8.7 %collective-permute-start.1 = (bf16[256,512]{1,0:T(8,128)(2,1)}, bf16[256,512]{1,0:T(8,128)(2,1)}, u32[]{:S(2)}, u32[]{:S(2)}) collective-permute-start(bf16[256,512]{1,0:T(8,128)(2,1)} %refs_0_.3), channel_id=1, source_target_pairs={{0,48},{1,49},{2,50},{3,51},{4,52},{5,53},{6,54},{7,55},{8,56},{9,... | collective-permute-start | bytes 786440 | tf_op jit(solution)/shard_map/ppermute | solution.py:27
  14.1 8.1 %collective-permute-start = (bf16[256,512]{1,0:T(8,128)(2,1)}, bf16[256,512]{1,0:T(8,128)(2,1)}, u32[]{:S(2)}, u32[]{:S(2)}) collective-permute-start(bf16[256,512]{1,0:T(8,128)(2,1)} %refs_0_.3), channel_id=1, source_target_pairs={{0,64},{1,65},{2,66},{3,67},{4,68},{5,69},{6,70},{7,71},{8,72},{9,... | collective-permute-start | bytes 786440 | tf_op jit(solution)/shard_map/ppermute | solution.py:27
  22.2 13.5 %collective-permute-start.4 = (bf16[256,512]{1,0:T(8,128)(2,1)}, bf16[256,512]{1,0:T(8,128)(2,1)S(1)}, u32[]{:S(2)}, u32[]{:S(2)}) collective-permute-start(bf16[256,512]{1,0:T(8,128)(2,1)} %collective-permute-done.refs_1_), channel_id=1, source_target_pairs={{0,16},{1,17},{2,18},{3,19},{4,20},{5,21},{6,22},{7,23},{8,24},{9,... | collective-permute-start | bytes 786440 | tf_op jit(solution)/shard_map/ppermute | solution.py:27
  22.2 13.5 %collective-permute-start.3 = (bf16[256,512]{1,0:T(8,128)(2,1)}, bf16[256,512]{1,0:T(8,128)(2,1)S(1)}, u32[]{:S(2)}, u32[]{:S(2)}) collective-permute-start(bf16[256,512]{1,0:T(8,128)(2,1)} %collective-permute-done.refs_1_), channel_id=1, source_target_pairs={{0,48},{1,49},{2,50},{3,51},{4,52},{5,53},{6,54},{7,55},{8,56},{9,... | collective-permute-start | bytes 786440 | tf_op jit(solution)/shard_map/ppermute | solution.py:27
  26.4 8.7 %collective-permute-start.5 = (bf16[256,512]{1,0:T(8,128)(2,1)S(1)}, bf16[256,512]{1,0:T(8,128)(2,1)S(1)}, u32[]{:S(2)}, u32[]{:S(2)}) collective-permute-start(bf16[256,512]{1,0:T(8,128)(2,1)S(1)} %broadcast_select_fusion.4), channel_id=1, source_target_pairs={{0,16},{1,49},{2,18},{3,51},{4,20},{5,53},{6,22},{7,55},{8,24},{9,... | collective-permute-start | bytes 786440 | tf_op jit(solution)/shard_map/ppermute | solution.py:27
  26.5 9.0 %collective-permute-start.7 = (bf16[512,256]{1,0:T(8,128)(2,1)S(1)}, bf16[512,256]{1,0:T(8,128)(2,1)}, u32[]{:S(2)}, u32[]{:S(2)}) collective-permute-start(bf16[512,256]{1,0:T(8,128)(2,1)S(1)} %copy-done.9), channel_id=1, source_target_pairs={{0,64},{1,65},{2,66},{3,67},{4,68},{5,69},{6,70},{7,71},{8,72},{9,... | collective-permute-start | bytes 786440 | tf_op jit(solution)/shard_map/ppermute | solution.py:27
  28.8 13.5 %collective-permute-start.11 = (bf16[256,512]{1,0:T(8,128)(2,1)}, bf16[256,512]{1,0:T(8,128)(2,1)S(1)}, u32[]{:S(2)}, u32[]{:S(2)}) collective-permute-start(bf16[256,512]{1,0:T(8,128)(2,1)} %refs_0_.3), channel_id=1, source_target_pairs={{0,1},{1,0},{2,3},{3,2},{4,5},{5,4},{6,7},{7,6},{8,9},{9,8},{10,11... | collective-permute-start | bytes 786440 | tf_op jit(solution)/shard_map/ppermute | solution.py:27
  44.3 12.2 %collective-permute-start.10 = (f32[2,128]{1,0:T(2,128)S(1)}, f32[2,128]{1,0:T(2,128)S(1)}, u32[]{:S(2)}, u32[]{:S(2)}) collective-permute-start(f32[2,128]{1,0:T(2,128)S(1)} %pad_maximum_fusion.4), channel_id=1, source_target_pairs={{0,1},{1,0},{2,3},{3,2},{4,5},{5,4},{6,7},{7,6},{8,9},{9,8},{10,11... | collective-permute-start | bytes 3080 | tf_op jit(solution)/shard_map/ppermute | solution.py:27
  53.7 24.6 %collective-permute-start.20 = (bf16[2,768,256]{2,1,0:T(8,128)(2,1)}, bf16[2,768,256]{2,1,0:T(8,128)(2,1)S(1)}, u32[]{:S(2)}, u32[]{:S(2)}) collective-permute-start(bf16[2,768,256]{2,1,0:T(8,128)(2,1)} %get-tuple-element.71), channel_id=1, source_target_pairs={{0,12},{1,5},{2,14},{3,7},{4,0},{5,9},{6,2},{7,11},{8,4},{9,13},{1... | collective-permute-start | bytes 2359304 | tf_op jit(solution)/shard_map/ppermute | solution.py:27
  56.5 22.4 %collective-permute-start.19 = (bf16[2,768,256]{2,1,0:T(8,128)(2,1)}, bf16[2,768,256]{2,1,0:T(8,128)(2,1)S(1)}, u32[]{:S(2)}, u32[]{:S(2)}) collective-permute-start(bf16[2,768,256]{2,1,0:T(8,128)(2,1)} %get-tuple-element.70), channel_id=1, source_target_pairs={{0,4},{1,13},{2,6},{3,15},{4,8},{5,1},{6,10},{7,3},{8,12},{9,5},{1... | collective-permute-start | bytes 2359304 | tf_op jit(solution)/shard_map/ppermute | solution.py:27
  58.3 15.3 %collective-permute-start.22 = (bf16[2,512,256]{2,1,0:T(8,128)(2,1)}, bf16[2,512,256]{2,1,0:T(8,128)(2,1)}, u32[]{:S(2)}, u32[]{:S(2)}) collective-permute-start(bf16[2,512,256]{2,1,0:T(8,128)(2,1)} %pad_maximum_fusion.1.refs_16_), channel_id=1, source_target_pairs={{0,16},{1,17},{2,18},{3,19},{4,20},{5,21},{6,22},{7,23},{8,24},{9,... | collective-permute-start | bytes 1572872 | tf_op jit(solution)/shard_map/ppermute | solution.py:27
  58.7 14.9 %collective-permute-start.21 = (bf16[2,512,256]{2,1,0:T(8,128)(2,1)}, bf16[2,512,256]{2,1,0:T(8,128)(2,1)}, u32[]{:S(2)}, u32[]{:S(2)}) collective-permute-start(bf16[2,512,256]{2,1,0:T(8,128)(2,1)} %pad_maximum_fusion.1.refs_16_), channel_id=1, source_target_pairs={{0,48},{1,49},{2,50},{3,51},{4,52},{5,53},{6,54},{7,55},{8,56},{9,... | collective-permute-start | bytes 1572872 | tf_op jit(solution)/shard_map/ppermute | solution.py:27
  61.6 20.5 %collective-permute-start.9 = (bf16[768,128]{1,0:T(8,128)(2,1)S(1)}, bf16[768,128]{1,0:T(8,128)(2,1)}, u32[]{:S(2)}, u32[]{:S(2)}) collective-permute-start(bf16[768,128]{1,0:T(8,128)(2,1)S(1)} %constant_dynamic-slice_fusion.2), channel_id=1, source_target_pairs={{0,1},{1,0},{2,3},{3,2},{4,5},{5,4},{6,7},{7,6},{8,9},{9,8},{10,11... | collective-permute-start | bytes 589832 | tf_op jit(solution)/shard_map/ppermute | solution.py:27
  80.9 9.0 %collective-permute-start.23 = (bf16[768,256]{1,0:T(8,128)(2,1)S(1)}, bf16[768,256]{1,0:T(8,128)(2,1)S(1)}, u32[]{:S(2)}, u32[]{:S(2)}) collective-permute-start(bf16[768,256]{1,0:T(8,128)(2,1)S(1)} %get-tuple-element.114), channel_id=1, source_target_pairs={{0,4},{1,13},{2,6},{3,15},{4,8},{5,1},{6,10},{7,3},{8,12},{9,5},{1... | collective-permute-start | bytes 1179656 | tf_op jit(solution)/shard_map/ppermute | solution.py:27
  83.1 20.5 %collective-permute-start.25 = (bf16[768,256]{1,0:T(8,128)(2,1)}, bf16[768,256]{1,0:T(8,128)(2,1)}, u32[]{:S(2)}, u32[]{:S(2)}) collective-permute-start(bf16[768,256]{1,0:T(8,128)(2,1)} %get-tuple-element.113), channel_id=1, source_target_pairs={{0,4},{1,13},{2,6},{3,15},{4,8},{5,1},{6,10},{7,3},{8,12},{9,5},{1... | collective-permute-start | bytes 1179656 | tf_op jit(solution)/shard_map/ppermute | solution.py:27
  86.6 17.0 %collective-permute-start.26 = (bf16[2,512,256]{2,1,0:T(8,128)(2,1)}, bf16[2,512,256]{2,1,0:T(8,128)(2,1)}, u32[]{:S(2)}, u32[]{:S(2)}) collective-permute-start(bf16[2,512,256]{2,1,0:T(8,128)(2,1)} %broadcast_select_fusion), channel_id=1, source_target_pairs={{0,16},{1,49},{2,18},{3,51},{4,20},{5,53},{6,22},{7,55},{8,24},{9,... | collective-permute-start | bytes 1572872 | tf_op jit(solution)/shard_map/ppermute | solution.py:27
  90.8 12.8 %collective-permute-start.24 = (bf16[768,256]{1,0:T(8,128)(2,1)}, bf16[768,256]{1,0:T(8,128)(2,1)}, u32[]{:S(2)}, u32[]{:S(2)}) collective-permute-start(bf16[768,256]{1,0:T(8,128)(2,1)} %fusion.3), channel_id=1, source_target_pairs={{0,2},{1,3},{2,0},{3,1},{4,6},{5,7},{6,4},{7,5},{8,10},{9,11},{10,... | collective-permute-start | bytes 1179656 | tf_op jit(solution)/shard_map/ppermute | solution.py:27
  105.2 9.3 %collective-permute-start.29 = (bf16[768,256]{1,0:T(8,128)(2,1)S(1)}, bf16[768,256]{1,0:T(8,128)(2,1)S(1)}, u32[]{:S(2)}, u32[]{:S(2)}) collective-permute-start(bf16[768,256]{1,0:T(8,128)(2,1)S(1)} %get-tuple-element.112.refs_0_), channel_id=1, source_target_pairs={{0,4},{1,5},{2,6},{3,7},{4,8},{5,9},{6,10},{7,11},{8,12},{9,13},{1... | collective-permute-start | bytes 1179656 | tf_op jit(solution)/shard_map/ppermute | solution.py:27
  106.0 9.1 %collective-permute-start.28 = (bf16[768,256]{1,0:T(8,128)(2,1)S(1)}, bf16[768,256]{1,0:T(8,128)(2,1)S(1)}, u32[]{:S(2)}, u32[]{:S(2)}) collective-permute-start(bf16[768,256]{1,0:T(8,128)(2,1)S(1)} %get-tuple-element.112.refs_0_), channel_id=1, source_target_pairs={{0,12},{1,13},{2,14},{3,15},{4,0},{5,1},{6,2},{7,3},{8,4},{9,5},{1... | collective-permute-start | bytes 1179656 | tf_op jit(solution)/shard_map/ppermute | solution.py:27
  108.5 9.3 %collective-permute-start.27 = (bf16[768,256]{1,0:T(8,128)(2,1)S(1)}, bf16[768,256]{1,0:T(8,128)(2,1)S(1)}, u32[]{:S(2)}, u32[]{:S(2)}) collective-permute-start(bf16[768,256]{1,0:T(8,128)(2,1)S(1)} %get-tuple-element.112.refs_0_), channel_id=1, source_target_pairs={{0,2},{1,3},{2,0},{3,1},{4,6},{5,7},{6,4},{7,5},{8,10},{9,11},{10,... | collective-permute-start | bytes 1179656 | tf_op jit(solution)/shard_map/ppermute | solution.py:27
  117.8 13.3 %collective-permute-start.31 = (bf16[768,256]{1,0:T(8,128)(2,1)S(1)}, bf16[768,256]{1,0:T(8,128)(2,1)S(1)}, u32[]{:S(2)}, u32[]{:S(2)}) collective-permute-start(bf16[768,256]{1,0:T(8,128)(2,1)S(1)} %collective-permute-done.27.refs_1_), channel_id=1, source_target_pairs={{0,4},{1,5},{2,6},{3,7},{4,8},{5,9},{6,10},{7,11},{8,12},{9,13},{1... | collective-permute-start | bytes 1179656 | tf_op jit(solution)/shard_map/ppermute | solution.py:27
  118.4 12.7 %collective-permute-start.30 = (bf16[768,256]{1,0:T(8,128)(2,1)S(1)}, bf16[768,256]{1,0:T(8,128)(2,1)S(1)}, u32[]{:S(2)}, u32[]{:S(2)}) collective-permute-start(bf16[768,256]{1,0:T(8,128)(2,1)S(1)} %collective-permute-done.27.refs_1_), channel_id=1, source_target_pairs={{0,12},{1,13},{2,14},{3,15},{4,0},{5,1},{6,2},{7,3},{8,4},{9,5},{1... | collective-permute-start | bytes 1179656 | tf_op jit(solution)/shard_map/ppermute | solution.py:27
  121.2 9.9 %collective-permute-start.32 = (bf16[768,256]{1,0:T(8,128)(2,1)S(1)}, bf16[768,256]{1,0:T(8,128)(2,1)S(1)}, u32[]{:S(2)}, u32[]{:S(2)}) collective-permute-start(bf16[768,256]{1,0:T(8,128)(2,1)S(1)} %broadcast_select_fusion.2), channel_id=1, source_target_pairs={{0,4},{1,13},{2,6},{3,15},{4,8},{5,1},{6,10},{7,3},{8,12},{9,5},{1... | collective-permute-start | bytes 1179656 | tf_op jit(solution)/shard_map/ppermute | solution.py:27
  124.0 12.3 %collective-permute-start.37 = (bf16[768,256]{1,0:T(8,128)(2,1)S(1)}, bf16[768,256]{1,0:T(8,128)(2,1)S(1)}, u32[]{:S(2)}, u32[]{:S(2)}) collective-permute-start(bf16[768,256]{1,0:T(8,128)(2,1)S(1)} %get-tuple-element.112.refs_0_), channel_id=1, source_target_pairs={{0,1},{1,0},{2,3},{3,2},{4,5},{5,4},{6,7},{7,6},{8,9},{9,8},{10,11... | collective-permute-start | bytes 1179656 | tf_op jit(solution)/shard_map/ppermute | solution.py:27
  126.0 11.1 %collective-permute-start.39 = (bf16[768,256]{1,0:T(8,128)(2,1)S(1)}, bf16[768,256]{1,0:T(8,128)(2,1)S(1)}, u32[]{:S(2)}, u32[]{:S(2)}) collective-permute-start(bf16[768,256]{1,0:T(8,128)(2,1)S(1)} %collective-permute-done.28.refs_2_), channel_id=1, source_target_pairs={{0,1},{1,0},{2,3},{3,2},{4,5},{5,4},{6,7},{7,6},{8,9},{9,8},{10,11... | collective-permute-start | bytes 1179656 | tf_op jit(solution)/shard_map/ppermute | solution.py:27
  131.2 9.2 %collective-permute-start.35 = (bf16[768,256]{1,0:T(8,128)(2,1)S(1)}, bf16[768,256]{1,0:T(8,128)(2,1)S(1)}, u32[]{:S(2)}, u32[]{:S(2)}) collective-permute-start(bf16[768,256]{1,0:T(8,128)(2,1)S(1)} %broadcast_select_fusion.1), channel_id=1, source_target_pairs={{0,4},{1,13},{2,6},{3,15},{4,8},{5,1},{6,10},{7,3},{8,12},{9,5},{1... | collective-permute-start | bytes 1179656 | tf_op jit(solution)/shard_map/ppermute | solution.py:27
  151.0 16.6 %collective-permute-start.45 = (bf16[2,512,256]{2,1,0:T(8,128)(2,1)}, bf16[2,512,256]{2,1,0:T(8,128)(2,1)S(1)}, u32[]{:S(2)}, u32[]{:S(2)}) collective-permute-start(bf16[2,512,256]{2,1,0:T(8,128)(2,1)} %get-tuple-element.96), channel_id=1, source_target_pairs={{0,16},{1,49},{2,18},{3,51},{4,20},{5,53},{6,22},{7,55},{8,24},{9,... | collective-permute-start | bytes 1572872 | tf_op jit(solution)/shard_map/ppermute | solution.py:27
  154.2 13.7 %collective-permute-start.46 = (bf16[2,512,256]{2,1,0:T(8,128)(2,1)}, bf16[2,512,256]{2,1,0:T(8,128)(2,1)S(1)}, u32[]{:S(2)}, u32[]{:S(2)}) collective-permute-start(bf16[2,512,256]{2,1,0:T(8,128)(2,1)} %get-tuple-element.97), channel_id=1, source_target_pairs={{0,48},{1,17},{2,50},{3,19},{4,52},{5,21},{6,54},{7,23},{8,56},{9,... | collective-permute-start | bytes 1572872 | tf_op jit(solution)/shard_map/ppermute | solution.py:27
  177.5 7.9 %collective-permute-start.49 = (bf16[512,256]{1,0:T(8,128)(2,1)S(1)}, bf16[512,256]{1,0:T(8,128)(2,1)S(1)}, u32[]{:S(2)}, u32[]{:S(2)}) collective-permute-start(bf16[512,256]{1,0:T(8,128)(2,1)S(1)} %fusion.7), channel_id=1, source_target_pairs={{0,64},{1,65},{2,66},{3,67},{4,68},{5,69},{6,70},{7,71},{8,72},{9,... | collective-permute-start | bytes 786440 | tf_op jit(solution)/shard_map/ppermute | solution.py:27
  (58 other events, 347.1 us)
Sparse Core Ops, SparseCore 0:
  10.3 76.8 all-gather.1
  117.9 42.5 reduce-scatter.1

commit v13 on v12

--- a/solution.py
+++ b/solution.py
@@ -92,7 +92,7 @@
         out_shape=outs,
         in_specs=[pl.BlockSpec(memory_space=pltpu.SMEM)]
         + [vmem] * len(vmem_args)
-        + [pl.BlockSpec(memory_space=pl.ANY)] * len(any_args),
+        + [pl.BlockSpec(memory_space=pltpu.HBM)] * len(any_args),
         out_specs=[pl.BlockSpec(memory_space=out_space)] * len(outs),
         scratch_shapes=[*scratch, pltpu.SemaphoreType.DMA((sems,))],
         compiler_params=pltpu.CompilerParams(vmem_limit_bytes=60 * 1024 * 1024),
@@ -331,12 +331,12 @@
     grad_x = out_gradient(place, cotangent, act, act_beside, in_blocks)
     grad_wout = wout.astype(F32) * scaling
     passed, back, grad_x, grad_wout = tie(passed, back, grad_x, grad_wout)
-    far = z_split(add([further[1], passed[1]]).astype(BF16), 1)
-    near = z_split(add([further[0], passed[0]]).astype(BF16), 1)
-    crossed, sums = tie(add([own[1], back[1], far]).astype(BF16), sums)
+    onward_sum = z_split(add([further, passed]).astype(BF16), 1)
+    total = add([own, back, onward_sum])
+    crossed, sums = tie(total[1].astype(BF16), sums)
     crossed = y_lo_swap(crossed)
     sums = sums + y_lo_swap(sums)
-    grad_win = add([own[0], back[0], near, crossed]) * scaling
+    grad_win = add([total[0], crossed]) * scaling
     grad_smid = keep_mid.astype(F32) * scaling * sums[0]
     grad_swide = keep_wide.astype(F32) * scaling * sums[1:].reshape(512)
     return (grad_x, grad_win, grad_wout, grad_smid, grad_swide)

time: 194 us -> 195 us (level)
    ppermute x51 -> x50, waiting for transfers between devices: 54.1 us -> 54.9 us  [permute(): return lax.ppermute(v, AXES, pairs)]
    ppermute x51 -> x50, starting transfers between devices: 54.7 us -> 54.9 us  [permute(): return lax.ppermute(v, AXES, pairs)]
  transfers between devices with their start and end apart: 53 -> 52, of which waited for: 24 -> 23; matrix products, arithmetic and copies ran while one was open for 15% -> 15% of each run, Pallas kernels for 16% -> 16%
where the time goes in v13:
time: 195 us; the launch traced here: 194 us
  waiting for transfers between devices  55 us (28%)
  starting transfers between devices  54.9 us (28%)
  Pallas kernels  31.2 us (16%)
  other arithmetic  23.4 us (12%)
  between operations  14.6 us (7%)
  matrix products  7.65 us (4%)
  local copies, waits for them, and re-layouts  7.32 us (4%)
    ppermute x50, waiting for transfers between devices, permute(): return lax.ppermute(v, AXES, pairs)  54.9 us
    ppermute x50, starting transfers between devices, permute(): return lax.ppermute(v, AXES, pairs)  54.9 us
    pallas_call x4, Pallas kernels, call(): pl.pallas_call(body, out_shape=outs, in_specs=[pl.BlockSpec(memory_space=...  31.2 us
    dot_general x1, matrix products, dot(): lax.dot_general(a, b, (((ca,), (cb,)), ((), ())), preferred_element_type=...  7.65 us
    unnamed x75, local copies, waits for them, and re-layouts  7.15 us
  transfers between devices with their start and end apart: 52, of which 23 were waited for; matrix products, arithmetic and copies ran while one was open for 15% of the time, Pallas kernels for 16%

profile of v13, /device:TPU:0, one launch (start us, length us, event | category | flops | bytes accessed | tf_op | source)
XLA Modules:
  0.0 194.1 jit_solution(15231768825639585875)
XLA Ops:
  9.8 2.1 %collective-permute-start.2 = (bf16[256,512]{1,0:T(8,128)(2,1)}, bf16[256,512]{1,0:T(8,128)(2,1)}, u32[]{:S(2)}, u32[]{:S(2)}) collective-permute-start(bf16[256,512]{1,0:T(8,128)(2,1)} %refs_0_.3), channel_id=1, source_target_pairs={{0,16},{1,17},{2,18},{3,19},{4,20},{5,21},{6,22},{7,23},{8,24},{9,... | collective-permute-start | bytes 786440 | tf_op jit(solution)/shard_map/ppermute | solution.py:27
  11.9 2.2 %collective-permute-start.1 = (bf16[256,512]{1,0:T(8,128)(2,1)}, bf16[256,512]{1,0:T(8,128)(2,1)}, u32[]{:S(2)}, u32[]{:S(2)}) collective-permute-start(bf16[256,512]{1,0:T(8,128)(2,1)} %refs_0_.3), channel_id=1, source_target_pairs={{0,48},{1,49},{2,50},{3,51},{4,52},{5,53},{6,54},{7,55},{8,56},{9,... | collective-permute-start | bytes 786440 | tf_op jit(solution)/shard_map/ppermute | solution.py:27
  16.4 2.6 %fusion.1 = (f32[512]{0:T(512)S(1)}, bf16[1536,512]{1,0:T(8,128)(2,1)S(1)}) fusion(bf16[1536,512]{1,0:T(8,128)(2,1)} %cot.1, bf16[1536,512]{1,0:T(8,128)(2,1)} %param.12, f32[512]{0:T(512)S(1)} %convert_multiply_fusion.4), kind=kLoop, calls=%fused_computation.3 | loop fusion | flops 4718080 | bytes 4722688 | tf_op jit(solution)/shard_map/reduce_sum | solution.py:250
  22.2 3.2 %collective-permute-start.3 = (bf16[256,512]{1,0:T(8,128)(2,1)}, bf16[256,512]{1,0:T(8,128)(2,1)S(1)}, u32[]{:S(2)}, u32[]{:S(2)}) collective-permute-start(bf16[256,512]{1,0:T(8,128)(2,1)} %collective-permute-done.refs_1_), channel_id=1, source_target_pairs={{0,48},{1,49},{2,50},{3,51},{4,52},{5,53},{6,54},{7,55},{8,56},{9,... | collective-permute-start | bytes 786440 | tf_op jit(solution)/shard_map/ppermute | solution.py:27
  28.8 2.5 %pad_maximum_fusion.conv = bf16[768,1024]{1,0:T(8,128)(2,1)} fusion(bf16[768,512]{1,0:T(8,128)(2,1)} %collective-permute-done.6, bf16[768,512]{1,0:T(8,128)(2,1)S(1)} %get-tuple-element.117), kind=kLoop, calls=%fused_computation.5 | loop fusion | flops 3145728 | bytes 3145728 | tf_op jit(solution)/shard_map/concatenate | solution.py:259
  31.3 3.9 %collective-permute-done.5.refs_6_ = bf16[256,512]{1,0:T(8,128)(2,1)S(1)} collective-permute-done((bf16[256,512]{1,0:T(8,128)(2,1)S(1)}, bf16[256,512]{1,0:T(8,128)(2,1)S(1)}, u32[]{:S(2)}, u32[]{:S(2)}) %collective-permute-start.5) | collective-permute-done | bytes 262176 | tf_op jit(solution)/shard_map/ppermute | solution.py:27
  37.9 2.6 %copy.15 = bf16[1536,512]{0,1:T(8,128)(2,1)} copy(bf16[1536,512]{1,0:T(8,128)(2,1)} %param.10) | data formatting | bytes 3145728 | tf_op args[0]
  47.1 6.5 %shard_map.137 = (bf16[2,768,256]{2,1,0:T(8,128)(2,1)}, bf16[2,768,256]{2,1,0:T(8,128)(2,1)}) custom-call(s32[2]{0:T(128)} %pad_add_fusion.here, bf16[768,1024]{1,0:T(8,128)(2,1)} %pad_maximum_fusion.conv, bf16[256,512]{1,0:T(8,128)(2,1)} %refs_0_.3, bf16[256,512]{1,0:T(8,128)(2,1)} %collective-permute-done.refs_1_, ...), custom_call_target="tpu_custom_call" | custom-call | flops 1610612736 | bytes 8388608 | tf_op jit(solution)/shard_map/pallas_call | solution.py:90
  53.7 2.8 %collective-permute-start.20 = (bf16[2,768,256]{2,1,0:T(8,128)(2,1)}, bf16[2,768,256]{2,1,0:T(8,128)(2,1)S(1)}, u32[]{:S(2)}, u32[]{:S(2)}) collective-permute-start(bf16[2,768,256]{2,1,0:T(8,128)(2,1)} %get-tuple-element.71), channel_id=1, source_target_pairs={{0,12},{1,5},{2,14},{3,7},{4,0},{5,9},{6,2},{7,11},{8,4},{9,13},{1... | collective-permute-start | bytes 2359304 | tf_op jit(solution)/shard_map/ppermute | solution.py:27
  58.7 2.8 %collective-permute-start.21 = (bf16[2,512,256]{2,1,0:T(8,128)(2,1)}, bf16[2,512,256]{2,1,0:T(8,128)(2,1)}, u32[]{:S(2)}, u32[]{:S(2)}) collective-permute-start(bf16[2,512,256]{2,1,0:T(8,128)(2,1)} %pad_maximum_fusion.1.refs_16_), channel_id=1, source_target_pairs={{0,48},{1,49},{2,50},{3,51},{4,52},{5,53},{6,54},{7,55},{8,56},{9,... | collective-permute-start | bytes 1572872 | tf_op jit(solution)/shard_map/ppermute | solution.py:27
  61.9 6.4 %shard_map.138 = (bf16[2,768,256]{2,1,0:T(8,128)(2,1)}, bf16[2,768,256]{2,1,0:T(8,128)(2,1)}) custom-call(s32[2]{0:T(128)} %pad_add_fusion.here, bf16[768,1024]{1,0:T(8,128)(2,1)} %pad_maximum_fusion.conv, bf16[256,512]{1,0:T(8,128)(2,1)} %refs_0_.3, bf16[256,512]{1,0:T(8,128)(2,1)} %collective-permute-done.refs_1_, ...), custom_call_target="tpu_custom_call" | custom-call | flops 1610612736 | bytes 8388608 | tf_op jit(solution)/shard_map/pallas_call | solution.py:90
  68.3 5.3 %collective-permute-done.22.refs_18_ = bf16[2,512,256]{2,1,0:T(8,128)(2,1)} collective-permute-done((bf16[2,512,256]{2,1,0:T(8,128)(2,1)}, bf16[2,512,256]{2,1,0:T(8,128)(2,1)}, u32[]{:S(2)}, u32[]{:S(2)}) %collective-permute-start.22) | collective-permute-done | bytes 524320 | tf_op jit(solution)/shard_map/ppermute | solution.py:27
  73.6 4.7 %collective-permute-done.20 = bf16[2,768,256]{2,1,0:T(8,128)(2,1)S(1)} collective-permute-done((bf16[2,768,256]{2,1,0:T(8,128)(2,1)}, bf16[2,768,256]{2,1,0:T(8,128)(2,1)S(1)}, u32[]{:S(2)}, u32[]{:S(2)}) %collective-permute-start.20) | collective-permute-done | bytes 786464 | tf_op jit(solution)/shard_map/ppermute | solution.py:27
  78.9 2.1 %fusion.10 = (bf16[768,256]{1,0:T(8,128)(2,1)}, bf16[768,256]{1,0:T(8,128)(2,1)S(1)}) fusion(bf16[2,768,256]{2,1,0:T(8,128)(2,1)S(1)} %collective-permute-done.19, bf16[2,768,256]{2,1,0:T(8,128)(2,1)} %get-tuple-element.79), kind=kLoop, calls=%fused_computation.29 | loop fusion | flops 1572864 | bytes 2359296 | tf_op jit(solution)/shard_map/convert_element_type | solution.py:294
  84.7 1.9 broadcast_select_fusion
  86.9 3.0 %collective-permute-done.23 = bf16[768,256]{1,0:T(8,128)(2,1)S(1)} collective-permute-done((bf16[768,256]{1,0:T(8,128)(2,1)S(1)}, bf16[768,256]{1,0:T(8,128)(2,1)S(1)}, u32[]{:S(2)}, u32[]{:S(2)}) %collective-permute-start.23) | collective-permute-done | bytes 393248 | tf_op jit(solution)/shard_map/ppermute | solution.py:27
  90.8 5.1 %collective-permute-start.24 = (bf16[768,256]{1,0:T(8,128)(2,1)}, bf16[768,256]{1,0:T(8,128)(2,1)}, u32[]{:S(2)}, u32[]{:S(2)}) collective-permute-start(bf16[768,256]{1,0:T(8,128)(2,1)} %fusion.3), channel_id=1, source_target_pairs={{0,2},{1,3},{2,0},{3,1},{4,6},{5,7},{6,4},{7,5},{8,10},{9,11},{10,... | collective-permute-start | bytes 1179656 | tf_op jit(solution)/shard_map/ppermute | solution.py:27
  95.9 7.7 %convolution_convert_fusion = bf16[2048,512]{1,0:T(8,128)(2,1)} fusion(bf16[1536,2048]{1,0:T(8,128)(2,1)} %all-gather.2.cloned.1.call-done, bf16[1536,512]{1,0:T(8,128)(2,1)S(1)} %get-tuple-element.116), kind=kOutput, calls=%fused_computation.4 | convolution fusion | flops 3222274048 | bytes 9961472 | tf_op jit(solution)/shard_map/dot_general | solution.py:63
  106.0 2.5 %collective-permute-start.28 = (bf16[768,256]{1,0:T(8,128)(2,1)S(1)}, bf16[768,256]{1,0:T(8,128)(2,1)S(1)}, u32[]{:S(2)}, u32[]{:S(2)}) collective-permute-start(bf16[768,256]{1,0:T(8,128)(2,1)S(1)} %get-tuple-element.112.refs_0_), channel_id=1, source_target_pairs={{0,12},{1,13},{2,14},{3,15},{4,0},{5,1},{6,2},{7,3},{8,4},{9,5},{1... | collective-permute-start | bytes 1179656 | tf_op jit(solution)/shard_map/ppermute | solution.py:27
  108.5 2.3 %collective-permute-start.27 = (bf16[768,256]{1,0:T(8,128)(2,1)S(1)}, bf16[768,256]{1,0:T(8,128)(2,1)S(1)}, u32[]{:S(2)}, u32[]{:S(2)}) collective-permute-start(bf16[768,256]{1,0:T(8,128)(2,1)S(1)} %get-tuple-element.112.refs_0_), channel_id=1, source_target_pairs={{0,2},{1,3},{2,0},{3,1},{4,6},{5,7},{6,4},{7,5},{8,10},{9,11},{10,... | collective-permute-start | bytes 1179656 | tf_op jit(solution)/shard_map/ppermute | solution.py:27
  110.8 3.7 %collective-permute-done.29.refs_4_ = bf16[768,256]{1,0:T(8,128)(2,1)S(1)} collective-permute-done((bf16[768,256]{1,0:T(8,128)(2,1)S(1)}, bf16[768,256]{1,0:T(8,128)(2,1)S(1)}, u32[]{:S(2)}, u32[]{:S(2)}) %collective-permute-start.29) | collective-permute-done | bytes 393248 | tf_op jit(solution)/shard_map/ppermute | solution.py:27
  115.1 2.7 %collective-permute-done.27.refs_1_ = bf16[768,256]{1,0:T(8,128)(2,1)S(1)} collective-permute-done((bf16[768,256]{1,0:T(8,128)(2,1)S(1)}, bf16[768,256]{1,0:T(8,128)(2,1)S(1)}, u32[]{:S(2)}, u32[]{:S(2)}) %collective-permute-start.27) | collective-permute-done | bytes 393248 | tf_op jit(solution)/shard_map/ppermute | solution.py:27
  118.4 2.7 %collective-permute-start.30 = (bf16[768,256]{1,0:T(8,128)(2,1)S(1)}, bf16[768,256]{1,0:T(8,128)(2,1)S(1)}, u32[]{:S(2)}, u32[]{:S(2)}) collective-permute-start(bf16[768,256]{1,0:T(8,128)(2,1)S(1)} %collective-permute-done.27.refs_1_), channel_id=1, source_target_pairs={{0,12},{1,13},{2,14},{3,15},{4,0},{5,1},{6,2},{7,3},{8,4},{9,5},{1... | collective-permute-start | bytes 1179656 | tf_op jit(solution)/shard_map/ppermute | solution.py:27
  124.0 2.0 %collective-permute-done.34 = f32[5,128]{1,0:T(8,128)S(1)} collective-permute-done((f32[5,128]{1,0:T(8,128)S(1)}, f32[5,128]{1,0:T(8,128)S(1)}, u32[]{:S(2)}, u32[]{:S(2)}) %collective-permute-start.34) | collective-permute-done | bytes 2592 | tf_op jit(solution)/shard_map/ppermute | solution.py:27
  126.0 5.1 %collective-permute-done.32.refs_6_ = bf16[768,256]{1,0:T(8,128)(2,1)S(1)} collective-permute-done((bf16[768,256]{1,0:T(8,128)(2,1)S(1)}, bf16[768,256]{1,0:T(8,128)(2,1)S(1)}, u32[]{:S(2)}, u32[]{:S(2)}) %collective-permute-start.32) | collective-permute-done | bytes 393248 | tf_op jit(solution)/shard_map/ppermute | solution.py:27
  132.0 4.5 %collective-permute-start.36 = (f32[5,128]{1,0:T(8,128)S(1)}, f32[5,128]{1,0:T(8,128)S(1)}, u32[]{:S(2)}, u32[]{:S(2)}) collective-permute-start(f32[5,128]{1,0:T(8,128)S(1)} %fusion.17), channel_id=1, source_target_pairs={{0,32},{1,33},{2,34},{3,35},{4,36},{5,37},{6,38},{7,39},{8,40},{9,... | collective-permute-start | bytes 7688 | tf_op jit(solution)/shard_map/ppermute | solution.py:27
  138.3 2.0 %collective-permute-done.35.refs_7_ = bf16[768,256]{1,0:T(8,128)(2,1)S(1)} collective-permute-done((bf16[768,256]{1,0:T(8,128)(2,1)S(1)}, bf16[768,256]{1,0:T(8,128)(2,1)S(1)}, u32[]{:S(2)}, u32[]{:S(2)}) %collective-permute-start.35) | collective-permute-done | bytes 393248 | tf_op jit(solution)/shard_map/ppermute | solution.py:27
  142.2 8.7 %shard_map.139 = (bf16[2,512,256]{2,1,0:T(8,128)(2,1)}, bf16[2,512,256]{2,1,0:T(8,128)(2,1)}, bf16[2,512,256]{2,1,0:T(8,128)(2,1)}, bf16[2,512,256]{2,1,0:T(8,128)(2,1)}) custom-call(s32[2]{0:T(128)} %pad_add_fusion.here, bf16[512,1536]{1,0:T(8,128)(2,1)} %bitcast.52, bf16[768,256]{1,0:T(8,128)(2,1)} %copy-done.8, bf16[768,256]{1,0:T(8,128)(2,1)} %copy-done.16, ...), custom_call_target="tpu_custom_call" | custom-call | flops 3221225472 | bytes 10485760 | tf_op jit(solution)/shard_map/pallas_call | solution.py:90
  151.0 3.3 %collective-permute-start.45 = (bf16[2,512,256]{2,1,0:T(8,128)(2,1)}, bf16[2,512,256]{2,1,0:T(8,128)(2,1)S(1)}, u32[]{:S(2)}, u32[]{:S(2)}) collective-permute-start(bf16[2,512,256]{2,1,0:T(8,128)(2,1)} %get-tuple-element.96), channel_id=1, source_target_pairs={{0,16},{1,49},{2,18},{3,51},{4,20},{5,53},{6,22},{7,55},{8,24},{9,... | collective-permute-start | bytes 1572872 | tf_op jit(solution)/shard_map/ppermute | solution.py:27
  154.8 9.6 %shard_map.140 = bf16[1536,512]{1,0:T(8,128)(2,1)} custom-call(s32[2]{0:T(128)} %pad_add_fusion.here, bf16[1536,512]{1,0:T(8,128)(2,1)} %cot.1, bf16[768,256]{1,0:T(8,128)(2,1)} %copy-done.8, bf16[768,256]{1,0:T(8,128)(2,1)} %copy-done.16, bf16[768,256]{1,0:T(8,128)(2,1)} %copy-done.5, bf16[768,256]{1,0:T(8,128)(2,1)} %copy-done.7, ...), custom_call_target="tpu_custom_call" | custom-call | flops 3221225472 | bytes 12582912 | tf_op jit(solution)/shard_map/pallas_call | solution.py:90
  169.5 8.8 %collective-permute-done.47 = bf16[2,512,256]{2,1,0:T(8,128)(2,1)S(1)} collective-permute-done((bf16[2,512,256]{2,1,0:T(8,128)(2,1)S(1)}, bf16[2,512,256]{2,1,0:T(8,128)(2,1)S(1)}, u32[]{:S(2)}, u32[]{:S(2)}) %collective-permute-start.47) | collective-permute-done | bytes 524320 | tf_op jit(solution)/shard_map/ppermute | solution.py:27
  183.4 3.0 %collective-permute-done.48 = bf16[512,256]{1,0:T(8,128)(2,1)S(1)} collective-permute-done((bf16[512,256]{1,0:T(8,128)(2,1)S(1)}, bf16[512,256]{1,0:T(8,128)(2,1)S(1)}, u32[]{:S(2)}, u32[]{:S(2)}) %collective-permute-start.48) | collective-permute-done | bytes 262176 | tf_op jit(solution)/shard_map/ppermute | solution.py:27
  (190 shorter events, 51.2 us)
Async XLA Ops:
  7.2 88.8 %all-gather.2.cloned.1.call-start = ((), (), s32[]{:S(2)}) async-start(), calls=%async_computation.1 | async-start | bytes 6684672 | tf_op jit(solution)/shard_map/all_gather | solution.py:243
  9.8 154.6 %reduce-scatter.2.cloned.1.call-start = ((), (), s32[]{:S(2)}) async-start(), calls=%async_computation.2 | async-start | bytes 2359296 | tf_op jit(solution)/shard_map/reduce_scatter | solution.py:310
  9.8 10.8 %collective-permute-start.2 = (bf16[256,512]{1,0:T(8,128)(2,1)}, bf16[256,512]{1,0:T(8,128)(2,1)}, u32[]{:S(2)}, u32[]{:S(2)}) collective-permute-start(bf16[256,512]{1,0:T(8,128)(2,1)} %refs_0_.3), channel_id=1, source_target_pairs={{0,16},{1,17},{2,18},{3,19},{4,20},{5,21},{6,22},{7,23},{8,24},{9,... | collective-permute-start | bytes 786440 | tf_op jit(solution)/shard_map/ppermute | solution.py:27
  11.9 8.7 %collective-permute-start.1 = (bf16[256,512]{1,0:T(8,128)(2,1)}, bf16[256,512]{1,0:T(8,128)(2,1)}, u32[]{:S(2)}, u32[]{:S(2)}) collective-permute-start(bf16[256,512]{1,0:T(8,128)(2,1)} %refs_0_.3), channel_id=1, source_target_pairs={{0,48},{1,49},{2,50},{3,51},{4,52},{5,53},{6,54},{7,55},{8,56},{9,... | collective-permute-start | bytes 786440 | tf_op jit(solution)/shard_map/ppermute | solution.py:27
  14.1 8.1 %collective-permute-start = (bf16[256,512]{1,0:T(8,128)(2,1)}, bf16[256,512]{1,0:T(8,128)(2,1)}, u32[]{:S(2)}, u32[]{:S(2)}) collective-permute-start(bf16[256,512]{1,0:T(8,128)(2,1)} %refs_0_.3), channel_id=1, source_target_pairs={{0,64},{1,65},{2,66},{3,67},{4,68},{5,69},{6,70},{7,71},{8,72},{9,... | collective-permute-start | bytes 786440 | tf_op jit(solution)/shard_map/ppermute | solution.py:27
  22.2 13.5 %collective-permute-start.4 = (bf16[256,512]{1,0:T(8,128)(2,1)}, bf16[256,512]{1,0:T(8,128)(2,1)S(1)}, u32[]{:S(2)}, u32[]{:S(2)}) collective-permute-start(bf16[256,512]{1,0:T(8,128)(2,1)} %collective-permute-done.refs_1_), channel_id=1, source_target_pairs={{0,16},{1,17},{2,18},{3,19},{4,20},{5,21},{6,22},{7,23},{8,24},{9,... | collective-permute-start | bytes 786440 | tf_op jit(solution)/shard_map/ppermute | solution.py:27
  22.2 13.5 %collective-permute-start.3 = (bf16[256,512]{1,0:T(8,128)(2,1)}, bf16[256,512]{1,0:T(8,128)(2,1)S(1)}, u32[]{:S(2)}, u32[]{:S(2)}) collective-permute-start(bf16[256,512]{1,0:T(8,128)(2,1)} %collective-permute-done.refs_1_), channel_id=1, source_target_pairs={{0,48},{1,49},{2,50},{3,51},{4,52},{5,53},{6,54},{7,55},{8,56},{9,... | collective-permute-start | bytes 786440 | tf_op jit(solution)/shard_map/ppermute | solution.py:27
  26.4 8.7 %collective-permute-start.5 = (bf16[256,512]{1,0:T(8,128)(2,1)S(1)}, bf16[256,512]{1,0:T(8,128)(2,1)S(1)}, u32[]{:S(2)}, u32[]{:S(2)}) collective-permute-start(bf16[256,512]{1,0:T(8,128)(2,1)S(1)} %broadcast_select_fusion.4), channel_id=1, source_target_pairs={{0,16},{1,49},{2,18},{3,51},{4,20},{5,53},{6,22},{7,55},{8,24},{9,... | collective-permute-start | bytes 786440 | tf_op jit(solution)/shard_map/ppermute | solution.py:27
  26.5 9.0 %collective-permute-start.7 = (bf16[512,256]{1,0:T(8,128)(2,1)S(1)}, bf16[512,256]{1,0:T(8,128)(2,1)}, u32[]{:S(2)}, u32[]{:S(2)}) collective-permute-start(bf16[512,256]{1,0:T(8,128)(2,1)S(1)} %copy-done.9), channel_id=1, source_target_pairs={{0,64},{1,65},{2,66},{3,67},{4,68},{5,69},{6,70},{7,71},{8,72},{9,... | collective-permute-start | bytes 786440 | tf_op jit(solution)/shard_map/ppermute | solution.py:27
  28.8 13.4 %collective-permute-start.11 = (bf16[256,512]{1,0:T(8,128)(2,1)}, bf16[256,512]{1,0:T(8,128)(2,1)S(1)}, u32[]{:S(2)}, u32[]{:S(2)}) collective-permute-start(bf16[256,512]{1,0:T(8,128)(2,1)} %refs_0_.3), channel_id=1, source_target_pairs={{0,1},{1,0},{2,3},{3,2},{4,5},{5,4},{6,7},{7,6},{8,9},{9,8},{10,11... | collective-permute-start | bytes 786440 | tf_op jit(solution)/shard_map/ppermute | solution.py:27
  44.3 12.2 %collective-permute-start.10 = (f32[2,128]{1,0:T(2,128)S(1)}, f32[2,128]{1,0:T(2,128)S(1)}, u32[]{:S(2)}, u32[]{:S(2)}) collective-permute-start(f32[2,128]{1,0:T(2,128)S(1)} %pad_maximum_fusion.4), channel_id=1, source_target_pairs={{0,1},{1,0},{2,3},{3,2},{4,5},{5,4},{6,7},{7,6},{8,9},{9,8},{10,11... | collective-permute-start | bytes 3080 | tf_op jit(solution)/shard_map/ppermute | solution.py:27
  53.7 24.6 %collective-permute-start.20 = (bf16[2,768,256]{2,1,0:T(8,128)(2,1)}, bf16[2,768,256]{2,1,0:T(8,128)(2,1)S(1)}, u32[]{:S(2)}, u32[]{:S(2)}) collective-permute-start(bf16[2,768,256]{2,1,0:T(8,128)(2,1)} %get-tuple-element.71), channel_id=1, source_target_pairs={{0,12},{1,5},{2,14},{3,7},{4,0},{5,9},{6,2},{7,11},{8,4},{9,13},{1... | collective-permute-start | bytes 2359304 | tf_op jit(solution)/shard_map/ppermute | solution.py:27
  56.5 22.4 %collective-permute-start.19 = (bf16[2,768,256]{2,1,0:T(8,128)(2,1)}, bf16[2,768,256]{2,1,0:T(8,128)(2,1)S(1)}, u32[]{:S(2)}, u32[]{:S(2)}) collective-permute-start(bf16[2,768,256]{2,1,0:T(8,128)(2,1)} %get-tuple-element.70), channel_id=1, source_target_pairs={{0,4},{1,13},{2,6},{3,15},{4,8},{5,1},{6,10},{7,3},{8,12},{9,5},{1... | collective-permute-start | bytes 2359304 | tf_op jit(solution)/shard_map/ppermute | solution.py:27
  58.3 15.3 %collective-permute-start.22 = (bf16[2,512,256]{2,1,0:T(8,128)(2,1)}, bf16[2,512,256]{2,1,0:T(8,128)(2,1)}, u32[]{:S(2)}, u32[]{:S(2)}) collective-permute-start(bf16[2,512,256]{2,1,0:T(8,128)(2,1)} %pad_maximum_fusion.1.refs_16_), channel_id=1, source_target_pairs={{0,16},{1,17},{2,18},{3,19},{4,20},{5,21},{6,22},{7,23},{8,24},{9,... | collective-permute-start | bytes 1572872 | tf_op jit(solution)/shard_map/ppermute | solution.py:27
  58.7 14.9 %collective-permute-start.21 = (bf16[2,512,256]{2,1,0:T(8,128)(2,1)}, bf16[2,512,256]{2,1,0:T(8,128)(2,1)}, u32[]{:S(2)}, u32[]{:S(2)}) collective-permute-start(bf16[2,512,256]{2,1,0:T(8,128)(2,1)} %pad_maximum_fusion.1.refs_16_), channel_id=1, source_target_pairs={{0,48},{1,49},{2,50},{3,51},{4,52},{5,53},{6,54},{7,55},{8,56},{9,... | collective-permute-start | bytes 1572872 | tf_op jit(solution)/shard_map/ppermute | solution.py:27
  61.6 20.5 %collective-permute-start.9 = (bf16[768,128]{1,0:T(8,128)(2,1)S(1)}, bf16[768,128]{1,0:T(8,128)(2,1)}, u32[]{:S(2)}, u32[]{:S(2)}) collective-permute-start(bf16[768,128]{1,0:T(8,128)(2,1)S(1)} %constant_dynamic-slice_fusion.2), channel_id=1, source_target_pairs={{0,1},{1,0},{2,3},{3,2},{4,5},{5,4},{6,7},{7,6},{8,9},{9,8},{10,11... | collective-permute-start | bytes 589832 | tf_op jit(solution)/shard_map/ppermute | solution.py:27
  80.9 9.0 %collective-permute-start.23 = (bf16[768,256]{1,0:T(8,128)(2,1)S(1)}, bf16[768,256]{1,0:T(8,128)(2,1)S(1)}, u32[]{:S(2)}, u32[]{:S(2)}) collective-permute-start(bf16[768,256]{1,0:T(8,128)(2,1)S(1)} %get-tuple-element.114), channel_id=1, source_target_pairs={{0,4},{1,13},{2,6},{3,15},{4,8},{5,1},{6,10},{7,3},{8,12},{9,5},{1... | collective-permute-start | bytes 1179656 | tf_op jit(solution)/shard_map/ppermute | solution.py:27
  83.1 20.5 %collective-permute-start.25 = (bf16[768,256]{1,0:T(8,128)(2,1)}, bf16[768,256]{1,0:T(8,128)(2,1)}, u32[]{:S(2)}, u32[]{:S(2)}) collective-permute-start(bf16[768,256]{1,0:T(8,128)(2,1)} %get-tuple-element.113), channel_id=1, source_target_pairs={{0,4},{1,13},{2,6},{3,15},{4,8},{5,1},{6,10},{7,3},{8,12},{9,5},{1... | collective-permute-start | bytes 1179656 | tf_op jit(solution)/shard_map/ppermute | solution.py:27
  86.6 17.0 %collective-permute-start.26 = (bf16[2,512,256]{2,1,0:T(8,128)(2,1)}, bf16[2,512,256]{2,1,0:T(8,128)(2,1)}, u32[]{:S(2)}, u32[]{:S(2)}) collective-permute-start(bf16[2,512,256]{2,1,0:T(8,128)(2,1)} %broadcast_select_fusion), channel_id=1, source_target_pairs={{0,16},{1,49},{2,18},{3,51},{4,20},{5,53},{6,22},{7,55},{8,24},{9,... | collective-permute-start | bytes 1572872 | tf_op jit(solution)/shard_map/ppermute | solution.py:27
  90.8 12.8 %collective-permute-start.24 = (bf16[768,256]{1,0:T(8,128)(2,1)}, bf16[768,256]{1,0:T(8,128)(2,1)}, u32[]{:S(2)}, u32[]{:S(2)}) collective-permute-start(bf16[768,256]{1,0:T(8,128)(2,1)} %fusion.3), channel_id=1, source_target_pairs={{0,2},{1,3},{2,0},{3,1},{4,6},{5,7},{6,4},{7,5},{8,10},{9,11},{10,... | collective-permute-start | bytes 1179656 | tf_op jit(solution)/shard_map/ppermute | solution.py:27
  105.2 9.3 %collective-permute-start.29 = (bf16[768,256]{1,0:T(8,128)(2,1)S(1)}, bf16[768,256]{1,0:T(8,128)(2,1)S(1)}, u32[]{:S(2)}, u32[]{:S(2)}) collective-permute-start(bf16[768,256]{1,0:T(8,128)(2,1)S(1)} %get-tuple-element.112.refs_0_), channel_id=1, source_target_pairs={{0,4},{1,5},{2,6},{3,7},{4,8},{5,9},{6,10},{7,11},{8,12},{9,13},{1... | collective-permute-start | bytes 1179656 | tf_op jit(solution)/shard_map/ppermute | solution.py:27
  106.0 9.1 %collective-permute-start.28 = (bf16[768,256]{1,0:T(8,128)(2,1)S(1)}, bf16[768,256]{1,0:T(8,128)(2,1)S(1)}, u32[]{:S(2)}, u32[]{:S(2)}) collective-permute-start(bf16[768,256]{1,0:T(8,128)(2,1)S(1)} %get-tuple-element.112.refs_0_), channel_id=1, source_target_pairs={{0,12},{1,13},{2,14},{3,15},{4,0},{5,1},{6,2},{7,3},{8,4},{9,5},{1... | collective-permute-start | bytes 1179656 | tf_op jit(solution)/shard_map/ppermute | solution.py:27
  108.5 9.3 %collective-permute-start.27 = (bf16[768,256]{1,0:T(8,128)(2,1)S(1)}, bf16[768,256]{1,0:T(8,128)(2,1)S(1)}, u32[]{:S(2)}, u32[]{:S(2)}) collective-permute-start(bf16[768,256]{1,0:T(8,128)(2,1)S(1)} %get-tuple-element.112.refs_0_), channel_id=1, source_target_pairs={{0,2},{1,3},{2,0},{3,1},{4,6},{5,7},{6,4},{7,5},{8,10},{9,11},{10,... | collective-permute-start | bytes 1179656 | tf_op jit(solution)/shard_map/ppermute | solution.py:27
  117.8 13.3 %collective-permute-start.31 = (bf16[768,256]{1,0:T(8,128)(2,1)S(1)}, bf16[768,256]{1,0:T(8,128)(2,1)S(1)}, u32[]{:S(2)}, u32[]{:S(2)}) collective-permute-start(bf16[768,256]{1,0:T(8,128)(2,1)S(1)} %collective-permute-done.27.refs_1_), channel_id=1, source_target_pairs={{0,4},{1,5},{2,6},{3,7},{4,8},{5,9},{6,10},{7,11},{8,12},{9,13},{1... | collective-permute-start | bytes 1179656 | tf_op jit(solution)/shard_map/ppermute | solution.py:27
  118.4 12.7 %collective-permute-start.30 = (bf16[768,256]{1,0:T(8,128)(2,1)S(1)}, bf16[768,256]{1,0:T(8,128)(2,1)S(1)}, u32[]{:S(2)}, u32[]{:S(2)}) collective-permute-start(bf16[768,256]{1,0:T(8,128)(2,1)S(1)} %collective-permute-done.27.refs_1_), channel_id=1, source_target_pairs={{0,12},{1,13},{2,14},{3,15},{4,0},{5,1},{6,2},{7,3},{8,4},{9,5},{1... | collective-permute-start | bytes 1179656 | tf_op jit(solution)/shard_map/ppermute | solution.py:27
  121.2 9.9 %collective-permute-start.32 = (bf16[768,256]{1,0:T(8,128)(2,1)S(1)}, bf16[768,256]{1,0:T(8,128)(2,1)S(1)}, u32[]{:S(2)}, u32[]{:S(2)}) collective-permute-start(bf16[768,256]{1,0:T(8,128)(2,1)S(1)} %broadcast_select_fusion.2), channel_id=1, source_target_pairs={{0,4},{1,13},{2,6},{3,15},{4,8},{5,1},{6,10},{7,3},{8,12},{9,5},{1... | collective-permute-start | bytes 1179656 | tf_op jit(solution)/shard_map/ppermute | solution.py:27
  124.0 12.6 %collective-permute-start.37 = (bf16[768,256]{1,0:T(8,128)(2,1)S(1)}, bf16[768,256]{1,0:T(8,128)(2,1)S(1)}, u32[]{:S(2)}, u32[]{:S(2)}) collective-permute-start(bf16[768,256]{1,0:T(8,128)(2,1)S(1)} %get-tuple-element.112.refs_0_), channel_id=1, source_target_pairs={{0,1},{1,0},{2,3},{3,2},{4,5},{5,4},{6,7},{7,6},{8,9},{9,8},{10,11... | collective-permute-start | bytes 1179656 | tf_op jit(solution)/shard_map/ppermute | solution.py:27
  125.9 11.2 %collective-permute-start.39 = (bf16[768,256]{1,0:T(8,128)(2,1)S(1)}, bf16[768,256]{1,0:T(8,128)(2,1)S(1)}, u32[]{:S(2)}, u32[]{:S(2)}) collective-permute-start(bf16[768,256]{1,0:T(8,128)(2,1)S(1)} %collective-permute-done.28.refs_2_), channel_id=1, source_target_pairs={{0,1},{1,0},{2,3},{3,2},{4,5},{5,4},{6,7},{7,6},{8,9},{9,8},{10,11... | collective-permute-start | bytes 1179656 | tf_op jit(solution)/shard_map/ppermute | solution.py:27
  131.2 9.2 %collective-permute-start.35 = (bf16[768,256]{1,0:T(8,128)(2,1)S(1)}, bf16[768,256]{1,0:T(8,128)(2,1)S(1)}, u32[]{:S(2)}, u32[]{:S(2)}) collective-permute-start(bf16[768,256]{1,0:T(8,128)(2,1)S(1)} %broadcast_select_fusion.1), channel_id=1, source_target_pairs={{0,4},{1,13},{2,6},{3,15},{4,8},{5,1},{6,10},{7,3},{8,12},{9,5},{1... | collective-permute-start | bytes 1179656 | tf_op jit(solution)/shard_map/ppermute | solution.py:27
  151.0 16.6 %collective-permute-start.45 = (bf16[2,512,256]{2,1,0:T(8,128)(2,1)}, bf16[2,512,256]{2,1,0:T(8,128)(2,1)S(1)}, u32[]{:S(2)}, u32[]{:S(2)}) collective-permute-start(bf16[2,512,256]{2,1,0:T(8,128)(2,1)} %get-tuple-element.96), channel_id=1, source_target_pairs={{0,16},{1,49},{2,18},{3,51},{4,20},{5,53},{6,22},{7,55},{8,24},{9,... | collective-permute-start | bytes 1572872 | tf_op jit(solution)/shard_map/ppermute | solution.py:27
  154.3 13.4 %collective-permute-start.46 = (bf16[2,512,256]{2,1,0:T(8,128)(2,1)}, bf16[2,512,256]{2,1,0:T(8,128)(2,1)S(1)}, u32[]{:S(2)}, u32[]{:S(2)}) collective-permute-start(bf16[2,512,256]{2,1,0:T(8,128)(2,1)} %get-tuple-element.97), channel_id=1, source_target_pairs={{0,48},{1,17},{2,50},{3,19},{4,52},{5,21},{6,54},{7,23},{8,56},{9,... | collective-permute-start | bytes 1572872 | tf_op jit(solution)/shard_map/ppermute | solution.py:27
  167.8 10.5 %collective-permute-start.47 = (bf16[2,512,256]{2,1,0:T(8,128)(2,1)S(1)}, bf16[2,512,256]{2,1,0:T(8,128)(2,1)S(1)}, u32[]{:S(2)}, u32[]{:S(2)}) collective-permute-start(bf16[2,512,256]{2,1,0:T(8,128)(2,1)S(1)} %add_convert_fusion), channel_id=1, source_target_pairs={{0,16},{1,49},{2,18},{3,51},{4,20},{5,53},{6,22},{7,55},{8,24},{9,... | collective-permute-start | bytes 1572872 | tf_op jit(solution)/shard_map/ppermute | solution.py:27
  (57 other events, 318.2 us)
Sparse Core Ops, SparseCore 0:
  10.3 76.8 all-gather.1
  117.9 42.7 reduce-scatter.1

commit v14 on v12

--- a/solution.py
+++ b/solution.py
@@ -95,7 +95,7 @@
         + [pl.BlockSpec(memory_space=pl.ANY)] * len(any_args),
         out_specs=[pl.BlockSpec(memory_space=out_space)] * len(outs),
         scratch_shapes=[*scratch, pltpu.SemaphoreType.DMA((sems,))],
-        compiler_params=pltpu.CompilerParams(vmem_limit_bytes=60 * 1024 * 1024),
+        compiler_params=pltpu.CompilerParams(vmem_limit_bytes=62 * 1024 * 1024),
         cost_estimate=pl.CostEstimate(flops=flops, bytes_accessed=loads, transcendentals=0),
     )(here, *vmem_args, *any_args)
 

time: 194 us -> 196 us (1.010)
  starting transfers between devices: 54.8 us -> 49.5 us
  waiting for transfers between devices: 54.2 us -> 59.1 us
    ppermute x51, starting transfers between devices: 54.7 us -> 49.5 us  [permute(): return lax.ppermute(v, AXES, pairs)]
    ppermute x51, waiting for transfers between devices: 54.1 us -> 59 us  [permute(): return lax.ppermute(v, AXES, pairs)]
where the time goes in v14:
time: 196 us; the launch traced here: 195 us
  waiting for transfers between devices  59.1 us (30%)
  starting transfers between devices  49.5 us (25%)
  Pallas kernels  31.7 us (16%)
  other arithmetic  23.4 us (12%)
  between operations  14.6 us (7%)
  local copies, waits for them, and re-layouts  8.9 us (5%)
  matrix products  7.68 us (4%)
    ppermute x51, waiting for transfers between devices, permute(): return lax.ppermute(v, AXES, pairs)  59 us
    ppermute x51, starting transfers between devices, permute(): return lax.ppermute(v, AXES, pairs)  49.5 us
    pallas_call x4, Pallas kernels, call(): pl.pallas_call(body, out_shape=outs, in_specs=[pl.BlockSpec(memory_space=...  31.7 us
    dot_general x1, matrix products, dot(): lax.dot_general(a, b, (((ca,), (cb,)), ((), ())), preferred_element_type=...  7.68 us
    unnamed x75, local copies, waits for them, and re-layouts  7.22 us
  transfers between devices with their start and end apart: 53, of which 24 were waited for; matrix products, arithmetic and copies ran while one was open for 15% of the time, Pallas kernels for 16%

profile of v14, /device:TPU:0, one launch (start us, length us, event | category | flops | bytes accessed | tf_op | source)
XLA Modules:
  0.0 194.9 jit_solution(2856332518532281910)
XLA Ops:
  9.8 2.1 %collective-permute-start.2 = (bf16[256,512]{1,0:T(8,128)(2,1)}, bf16[256,512]{1,0:T(8,128)(2,1)S(1)}, u32[]{:S(2)}, u32[]{:S(2)}) collective-permute-start(bf16[256,512]{1,0:T(8,128)(2,1)} %refs_0_.3), channel_id=1, source_target_pairs={{0,16},{1,17},{2,18},{3,19},{4,20},{5,21},{6,22},{7,23},{8,24},{9,... | collective-permute-start | bytes 786440 | tf_op jit(solution)/shard_map/ppermute | solution.py:27
  11.9 2.2 %collective-permute-start.1 = (bf16[256,512]{1,0:T(8,128)(2,1)}, bf16[256,512]{1,0:T(8,128)(2,1)S(1)}, u32[]{:S(2)}, u32[]{:S(2)}) collective-permute-start(bf16[256,512]{1,0:T(8,128)(2,1)} %refs_0_.3), channel_id=1, source_target_pairs={{0,48},{1,49},{2,50},{3,51},{4,52},{5,53},{6,54},{7,55},{8,56},{9,... | collective-permute-start | bytes 786440 | tf_op jit(solution)/shard_map/ppermute | solution.py:27
  16.4 2.6 %fusion.1 = (f32[512]{0:T(512)S(1)}, bf16[1536,512]{1,0:T(8,128)(2,1)S(1)}) fusion(bf16[1536,512]{1,0:T(8,128)(2,1)} %cot.1, bf16[1536,512]{1,0:T(8,128)(2,1)} %param.12, f32[512]{0:T(512)S(1)} %convert_multiply_fusion.4), kind=kLoop, calls=%fused_computation.3 | loop fusion | flops 4718080 | bytes 4722688 | tf_op jit(solution)/shard_map/reduce_sum | solution.py:250
  22.2 3.2 %collective-permute-start.3 = (bf16[256,512]{1,0:T(8,128)(2,1)}, bf16[256,512]{1,0:T(8,128)(2,1)S(1)}, u32[]{:S(2)}, u32[]{:S(2)}) collective-permute-start(bf16[256,512]{1,0:T(8,128)(2,1)} %collective-permute-done.refs_1_), channel_id=1, source_target_pairs={{0,48},{1,49},{2,50},{3,51},{4,52},{5,53},{6,54},{7,55},{8,56},{9,... | collective-permute-start | bytes 786440 | tf_op jit(solution)/shard_map/ppermute | solution.py:27
  27.8 2.5 %pad_maximum_fusion.conv = bf16[768,1024]{1,0:T(8,128)(2,1)} fusion(bf16[768,512]{1,0:T(8,128)(2,1)} %collective-permute-done.6, bf16[768,512]{1,0:T(8,128)(2,1)S(1)} %get-tuple-element.117), kind=kLoop, calls=%fused_computation.5 | loop fusion | flops 3145728 | bytes 3145728 | tf_op jit(solution)/shard_map/concatenate | solution.py:259
  30.3 4.9 %collective-permute-done.5.refs_6_ = bf16[256,512]{1,0:T(8,128)(2,1)S(1)} collective-permute-done((bf16[256,512]{1,0:T(8,128)(2,1)S(1)}, bf16[256,512]{1,0:T(8,128)(2,1)S(1)}, u32[]{:S(2)}, u32[]{:S(2)}) %collective-permute-start.5) | collective-permute-done | bytes 262176 | tf_op jit(solution)/shard_map/ppermute | solution.py:27
  37.8 2.7 %copy.15 = bf16[1536,512]{0,1:T(8,128)(2,1)} copy(bf16[1536,512]{1,0:T(8,128)(2,1)} %param.10) | data formatting | bytes 3145728 | tf_op args[0]
  46.4 7.0 %shard_map.137 = (bf16[2,768,256]{2,1,0:T(8,128)(2,1)}, bf16[2,768,256]{2,1,0:T(8,128)(2,1)}) custom-call(s32[2]{0:T(128)} %pad_add_fusion.here, bf16[768,1024]{1,0:T(8,128)(2,1)} %pad_maximum_fusion.conv, bf16[256,512]{1,0:T(8,128)(2,1)} %refs_0_.3, bf16[256,512]{1,0:T(8,128)(2,1)} %collective-permute-done.refs_1_, bf16[256,512]{1,0:T(8,128)(2,1)} %copy-done.11, ...), custom_call_target="tpu_custom_call" | custom-call | flops 1610612736 | bytes 8388608 | tf_op jit(solution)/shard_map/pallas_call | solution.py:90
  53.5 2.8 %collective-permute-start.20 = (bf16[2,768,256]{2,1,0:T(8,128)(2,1)}, bf16[2,768,256]{2,1,0:T(8,128)(2,1)}, u32[]{:S(2)}, u32[]{:S(2)}) collective-permute-start(bf16[2,768,256]{2,1,0:T(8,128)(2,1)} %get-tuple-element.71), channel_id=1, source_target_pairs={{0,12},{1,5},{2,14},{3,7},{4,0},{5,9},{6,2},{7,11},{8,4},{9,13},{1... | collective-permute-start | bytes 2359304 | tf_op jit(solution)/shard_map/ppermute | solution.py:27
  56.3 1.9 pad_maximum_fusion.1.refs_16_
  58.4 3.0 %collective-permute-start.21 = (bf16[2,512,256]{2,1,0:T(8,128)(2,1)}, bf16[2,512,256]{2,1,0:T(8,128)(2,1)}, u32[]{:S(2)}, u32[]{:S(2)}) collective-permute-start(bf16[2,512,256]{2,1,0:T(8,128)(2,1)} %pad_maximum_fusion.1.refs_16_), channel_id=1, source_target_pairs={{0,48},{1,49},{2,50},{3,51},{4,52},{5,53},{6,54},{7,55},{8,56},{9,... | collective-permute-start | bytes 1572872 | tf_op jit(solution)/shard_map/ppermute | solution.py:27
  62.2 6.5 %shard_map.138 = (bf16[2,768,256]{2,1,0:T(8,128)(2,1)}, bf16[2,768,256]{2,1,0:T(8,128)(2,1)}) custom-call(s32[2]{0:T(128)} %pad_add_fusion.here, bf16[768,1024]{1,0:T(8,128)(2,1)} %pad_maximum_fusion.conv, bf16[256,512]{1,0:T(8,128)(2,1)} %refs_0_.3, bf16[256,512]{1,0:T(8,128)(2,1)} %collective-permute-done.refs_1_, bf16[256,512]{1,0:T(8,128)(2,1)} %copy-done.11, ...), custom_call_target="tpu_custom_call" | custom-call | flops 1610612736 | bytes 8388608 | tf_op jit(solution)/shard_map/pallas_call | solution.py:90
  68.6 4.8 %collective-permute-done.22.refs_18_ = bf16[2,512,256]{2,1,0:T(8,128)(2,1)} collective-permute-done((bf16[2,512,256]{2,1,0:T(8,128)(2,1)}, bf16[2,512,256]{2,1,0:T(8,128)(2,1)}, u32[]{:S(2)}, u32[]{:S(2)}) %collective-permute-start.22) | collective-permute-done | bytes 524320 | tf_op jit(solution)/shard_map/ppermute | solution.py:27
  73.5 4.6 %collective-permute-done.20 = bf16[2,768,256]{2,1,0:T(8,128)(2,1)} collective-permute-done((bf16[2,768,256]{2,1,0:T(8,128)(2,1)}, bf16[2,768,256]{2,1,0:T(8,128)(2,1)}, u32[]{:S(2)}, u32[]{:S(2)}) %collective-permute-start.20) | collective-permute-done | bytes 786464 | tf_op jit(solution)/shard_map/ppermute | solution.py:27
  78.7 2.7 %fusion.11 = (bf16[768,256]{1,0:T(8,128)(2,1)}, bf16[768,256]{1,0:T(8,128)(2,1)S(1)}) fusion(bf16[2,768,256]{2,1,0:T(8,128)(2,1)} %collective-permute-done.19, bf16[2,768,256]{2,1,0:T(8,128)(2,1)} %get-tuple-element.79), kind=kLoop, calls=%fused_computation.30 | loop fusion | flops 1572864 | bytes 2359296 | tf_op jit(solution)/shard_map/convert_element_type | solution.py:294
  82.7 2.1 %collective-permute-start.25 = (bf16[768,256]{1,0:T(8,128)(2,1)}, bf16[768,256]{1,0:T(8,128)(2,1)}, u32[]{:S(2)}, u32[]{:S(2)}) collective-permute-start(bf16[768,256]{1,0:T(8,128)(2,1)} %get-tuple-element.113), channel_id=1, source_target_pairs={{0,4},{1,13},{2,6},{3,15},{4,8},{5,1},{6,10},{7,3},{8,12},{9,5},{1... | collective-permute-start | bytes 1179656 | tf_op jit(solution)/shard_map/ppermute | solution.py:27
  84.8 1.9 broadcast_select_fusion
  86.7 3.7 %collective-permute-done.23 = bf16[768,256]{1,0:T(8,128)(2,1)S(1)} collective-permute-done((bf16[768,256]{1,0:T(8,128)(2,1)S(1)}, bf16[768,256]{1,0:T(8,128)(2,1)S(1)}, u32[]{:S(2)}, u32[]{:S(2)}) %collective-permute-start.23) | collective-permute-done | bytes 393248 | tf_op jit(solution)/shard_map/ppermute | solution.py:27
  91.5 4.1 %collective-permute-start.24 = (bf16[768,256]{1,0:T(8,128)(2,1)S(1)}, bf16[768,256]{1,0:T(8,128)(2,1)}, u32[]{:S(2)}, u32[]{:S(2)}) collective-permute-start(bf16[768,256]{1,0:T(8,128)(2,1)S(1)} %fusion.3), channel_id=1, source_target_pairs={{0,2},{1,3},{2,0},{3,1},{4,6},{5,7},{6,4},{7,5},{8,10},{9,11},{10,... | collective-permute-start | bytes 1179656 | tf_op jit(solution)/shard_map/ppermute | solution.py:27
  95.7 7.7 %convolution_convert_fusion = bf16[2048,512]{1,0:T(8,128)(2,1)} fusion(bf16[1536,2048]{1,0:T(8,128)(2,1)} %all-gather.2.cloned.1.call-done, bf16[1536,512]{1,0:T(8,128)(2,1)S(1)} %get-tuple-element.116), kind=kOutput, calls=%fused_computation.4 | convolution fusion | flops 3222274048 | bytes 9961472 | tf_op jit(solution)/shard_map/dot_general | solution.py:63
  105.9 2.5 %collective-permute-start.28 = (bf16[768,256]{1,0:T(8,128)(2,1)S(1)}, bf16[768,256]{1,0:T(8,128)(2,1)S(1)}, u32[]{:S(2)}, u32[]{:S(2)}) collective-permute-start(bf16[768,256]{1,0:T(8,128)(2,1)S(1)} %get-tuple-element.112.refs_0_), channel_id=1, source_target_pairs={{0,12},{1,13},{2,14},{3,15},{4,0},{5,1},{6,2},{7,3},{8,4},{9,5},{1... | collective-permute-start | bytes 1179656 | tf_op jit(solution)/shard_map/ppermute | solution.py:27
  110.3 4.9 %collective-permute-done.29.refs_4_ = bf16[768,256]{1,0:T(8,128)(2,1)S(1)} collective-permute-done((bf16[768,256]{1,0:T(8,128)(2,1)S(1)}, bf16[768,256]{1,0:T(8,128)(2,1)S(1)}, u32[]{:S(2)}, u32[]{:S(2)}) %collective-permute-start.29) | collective-permute-done | bytes 393248 | tf_op jit(solution)/shard_map/ppermute | solution.py:27
  124.1 2.4 %collective-permute-done.34 = f32[5,128]{1,0:T(8,128)S(1)} collective-permute-done((f32[5,128]{1,0:T(8,128)S(1)}, f32[5,128]{1,0:T(8,128)S(1)}, u32[]{:S(2)}, u32[]{:S(2)}) %collective-permute-start.34) | collective-permute-done | bytes 2592 | tf_op jit(solution)/shard_map/ppermute | solution.py:27
  126.6 5.9 %collective-permute-done.32.refs_6_ = bf16[768,256]{1,0:T(8,128)(2,1)S(1)} collective-permute-done((bf16[768,256]{1,0:T(8,128)(2,1)S(1)}, bf16[768,256]{1,0:T(8,128)(2,1)S(1)}, u32[]{:S(2)}, u32[]{:S(2)}) %collective-permute-start.32) | collective-permute-done | bytes 393248 | tf_op jit(solution)/shard_map/ppermute | solution.py:27
  134.6 3.0 %collective-permute-start.36 = (f32[5,128]{1,0:T(8,128)S(1)}, f32[5,128]{1,0:T(8,128)S(1)}, u32[]{:S(2)}, u32[]{:S(2)}) collective-permute-start(f32[5,128]{1,0:T(8,128)S(1)} %fusion.19), channel_id=1, source_target_pairs={{0,32},{1,33},{2,34},{3,35},{4,36},{5,37},{6,38},{7,39},{8,40},{9,... | collective-permute-start | bytes 7688 | tf_op jit(solution)/shard_map/ppermute | solution.py:27
  139.9 3.3 %collective-permute-done.35.refs_7_ = bf16[768,256]{1,0:T(8,128)(2,1)S(1)} collective-permute-done((bf16[768,256]{1,0:T(8,128)(2,1)S(1)}, bf16[768,256]{1,0:T(8,128)(2,1)S(1)}, u32[]{:S(2)}, u32[]{:S(2)}) %collective-permute-start.35) | collective-permute-done | bytes 393248 | tf_op jit(solution)/shard_map/ppermute | solution.py:27
  145.7 8.6 %shard_map.139 = (bf16[2,512,256]{2,1,0:T(8,128)(2,1)}, bf16[2,512,256]{2,1,0:T(8,128)(2,1)}, bf16[2,512,256]{2,1,0:T(8,128)(2,1)}, bf16[2,512,256]{2,1,0:T(8,128)(2,1)}) custom-call(s32[2]{0:T(128)} %pad_add_fusion.here, bf16[512,1536]{1,0:T(8,128)(2,1)} %bitcast.58, bf16[768,256]{1,0:T(8,128)(2,1)} %copy-done.8, bf16[768,256]{1,0:T(8,128)(2,1)} %copy-done.19, ...), custom_call_target="tpu_custom_call" | custom-call | flops 3221225472 | bytes 10485760 | tf_op jit(solution)/shard_map/pallas_call | solution.py:90
  155.4 2.2 %collective-permute-start.46 = (bf16[2,512,256]{2,1,0:T(8,128)(2,1)}, bf16[2,512,256]{2,1,0:T(8,128)(2,1)S(1)}, u32[]{:S(2)}, u32[]{:S(2)}) collective-permute-start(bf16[2,512,256]{2,1,0:T(8,128)(2,1)} %get-tuple-element.97), channel_id=1, source_target_pairs={{0,48},{1,17},{2,50},{3,19},{4,52},{5,21},{6,54},{7,23},{8,56},{9,... | collective-permute-start | bytes 1572872 | tf_op jit(solution)/shard_map/ppermute | solution.py:27
  157.6 9.6 %shard_map.140 = bf16[1536,512]{1,0:T(8,128)(2,1)} custom-call(s32[2]{0:T(128)} %pad_add_fusion.here, bf16[1536,512]{1,0:T(8,128)(2,1)} %cot.1, bf16[768,256]{1,0:T(8,128)(2,1)} %copy-done.8, bf16[768,256]{1,0:T(8,128)(2,1)} %copy-done.19, bf16[768,256]{1,0:T(8,128)(2,1)} %copy-done.5, bf16[768,256]{1,0:T(8,128)(2,1)} %copy-done.7, ...), custom_call_target="tpu_custom_call" | custom-call | flops 3221225472 | bytes 12582912 | tf_op jit(solution)/shard_map/pallas_call | solution.py:90
  170.6 7.6 %collective-permute-done.48 = bf16[512,256]{1,0:T(8,128)(2,1)S(1)} collective-permute-done((bf16[512,256]{1,0:T(8,128)(2,1)S(1)}, bf16[512,256]{1,0:T(8,128)(2,1)S(1)}, u32[]{:S(2)}, u32[]{:S(2)}) %collective-permute-start.48) | collective-permute-done | bytes 262176 | tf_op jit(solution)/shard_map/ppermute | solution.py:27
  178.5 1.9 collective-permute-start.49
  183.1 3.0 %collective-permute-done.47 = bf16[512,256]{1,0:T(8,128)(2,1)S(1)} collective-permute-done((bf16[512,256]{1,0:T(8,128)(2,1)S(1)}, bf16[512,256]{1,0:T(8,128)(2,1)S(1)}, u32[]{:S(2)}, u32[]{:S(2)}) %collective-permute-start.47) | collective-permute-done | bytes 262176 | tf_op jit(solution)/shard_map/ppermute | solution.py:27
  (191 shorter events, 52.5 us)
Async XLA Ops:
  7.2 88.5 %all-gather.2.cloned.1.call-start = ((), (), s32[]{:S(2)}) async-start(), calls=%async_computation.1 | async-start | bytes 6684672 | tf_op jit(solution)/shard_map/all_gather | solution.py:243
  9.8 157.5 %reduce-scatter.2.cloned.1.call-start = ((), (), s32[]{:S(2)}) async-start(), calls=%async_computation.2 | async-start | bytes 2359296 | tf_op jit(solution)/shard_map/reduce_scatter | solution.py:310
  9.8 10.7 %collective-permute-start.2 = (bf16[256,512]{1,0:T(8,128)(2,1)}, bf16[256,512]{1,0:T(8,128)(2,1)S(1)}, u32[]{:S(2)}, u32[]{:S(2)}) collective-permute-start(bf16[256,512]{1,0:T(8,128)(2,1)} %refs_0_.3), channel_id=1, source_target_pairs={{0,16},{1,17},{2,18},{3,19},{4,20},{5,21},{6,22},{7,23},{8,24},{9,... | collective-permute-start | bytes 786440 | tf_op jit(solution)/shard_map/ppermute | solution.py:27
  11.9 8.6 %collective-permute-start.1 = (bf16[256,512]{1,0:T(8,128)(2,1)}, bf16[256,512]{1,0:T(8,128)(2,1)S(1)}, u32[]{:S(2)}, u32[]{:S(2)}) collective-permute-start(bf16[256,512]{1,0:T(8,128)(2,1)} %refs_0_.3), channel_id=1, source_target_pairs={{0,48},{1,49},{2,50},{3,51},{4,52},{5,53},{6,54},{7,55},{8,56},{9,... | collective-permute-start | bytes 786440 | tf_op jit(solution)/shard_map/ppermute | solution.py:27
  14.1 8.1 %collective-permute-start = (bf16[256,512]{1,0:T(8,128)(2,1)}, bf16[256,512]{1,0:T(8,128)(2,1)}, u32[]{:S(2)}, u32[]{:S(2)}) collective-permute-start(bf16[256,512]{1,0:T(8,128)(2,1)} %refs_0_.3), channel_id=1, source_target_pairs={{0,64},{1,65},{2,66},{3,67},{4,68},{5,69},{6,70},{7,71},{8,72},{9,... | collective-permute-start | bytes 786440 | tf_op jit(solution)/shard_map/ppermute | solution.py:27
  22.2 13.6 %collective-permute-start.4 = (bf16[256,512]{1,0:T(8,128)(2,1)}, bf16[256,512]{1,0:T(8,128)(2,1)S(1)}, u32[]{:S(2)}, u32[]{:S(2)}) collective-permute-start(bf16[256,512]{1,0:T(8,128)(2,1)} %collective-permute-done.refs_1_), channel_id=1, source_target_pairs={{0,16},{1,17},{2,18},{3,19},{4,20},{5,21},{6,22},{7,23},{8,24},{9,... | collective-permute-start | bytes 786440 | tf_op jit(solution)/shard_map/ppermute | solution.py:27
  22.2 13.6 %collective-permute-start.3 = (bf16[256,512]{1,0:T(8,128)(2,1)}, bf16[256,512]{1,0:T(8,128)(2,1)S(1)}, u32[]{:S(2)}, u32[]{:S(2)}) collective-permute-start(bf16[256,512]{1,0:T(8,128)(2,1)} %collective-permute-done.refs_1_), channel_id=1, source_target_pairs={{0,48},{1,49},{2,50},{3,51},{4,52},{5,53},{6,54},{7,55},{8,56},{9,... | collective-permute-start | bytes 786440 | tf_op jit(solution)/shard_map/ppermute | solution.py:27
  25.4 9.7 %collective-permute-start.5 = (bf16[256,512]{1,0:T(8,128)(2,1)S(1)}, bf16[256,512]{1,0:T(8,128)(2,1)S(1)}, u32[]{:S(2)}, u32[]{:S(2)}) collective-permute-start(bf16[256,512]{1,0:T(8,128)(2,1)S(1)} %broadcast_select_fusion.4), channel_id=1, source_target_pairs={{0,16},{1,49},{2,18},{3,51},{4,20},{5,53},{6,22},{7,55},{8,24},{9,... | collective-permute-start | bytes 786440 | tf_op jit(solution)/shard_map/ppermute | solution.py:27
  25.5 9.9 %collective-permute-start.7 = (bf16[512,256]{1,0:T(8,128)(2,1)S(1)}, bf16[512,256]{1,0:T(8,128)(2,1)S(1)}, u32[]{:S(2)}, u32[]{:S(2)}) collective-permute-start(bf16[512,256]{1,0:T(8,128)(2,1)S(1)} %copy-done.9), channel_id=1, source_target_pairs={{0,64},{1,65},{2,66},{3,67},{4,68},{5,69},{6,70},{7,71},{8,72},{9,... | collective-permute-start | bytes 786440 | tf_op jit(solution)/shard_map/ppermute | solution.py:27
  27.8 14.4 %collective-permute-start.11 = (bf16[256,512]{1,0:T(8,128)(2,1)}, bf16[256,512]{1,0:T(8,128)(2,1)}, u32[]{:S(2)}, u32[]{:S(2)}) collective-permute-start(bf16[256,512]{1,0:T(8,128)(2,1)} %refs_0_.3), channel_id=1, source_target_pairs={{0,1},{1,0},{2,3},{3,2},{4,5},{5,4},{6,7},{7,6},{8,9},{9,8},{10,11... | collective-permute-start | bytes 786440 | tf_op jit(solution)/shard_map/ppermute | solution.py:27
  44.3 11.9 %collective-permute-start.10 = (f32[2,128]{1,0:T(2,128)S(1)}, f32[2,128]{1,0:T(2,128)S(1)}, u32[]{:S(2)}, u32[]{:S(2)}) collective-permute-start(f32[2,128]{1,0:T(2,128)S(1)} %pad_maximum_fusion.4), channel_id=1, source_target_pairs={{0,1},{1,0},{2,3},{3,2},{4,5},{5,4},{6,7},{7,6},{8,9},{9,8},{10,11... | collective-permute-start | bytes 3080 | tf_op jit(solution)/shard_map/ppermute | solution.py:27
  53.5 24.6 %collective-permute-start.20 = (bf16[2,768,256]{2,1,0:T(8,128)(2,1)}, bf16[2,768,256]{2,1,0:T(8,128)(2,1)}, u32[]{:S(2)}, u32[]{:S(2)}) collective-permute-start(bf16[2,768,256]{2,1,0:T(8,128)(2,1)} %get-tuple-element.71), channel_id=1, source_target_pairs={{0,12},{1,5},{2,14},{3,7},{4,0},{5,9},{6,2},{7,11},{8,4},{9,13},{1... | collective-permute-start | bytes 2359304 | tf_op jit(solution)/shard_map/ppermute | solution.py:27
  56.3 22.5 %collective-permute-start.19 = (bf16[2,768,256]{2,1,0:T(8,128)(2,1)}, bf16[2,768,256]{2,1,0:T(8,128)(2,1)}, u32[]{:S(2)}, u32[]{:S(2)}) collective-permute-start(bf16[2,768,256]{2,1,0:T(8,128)(2,1)} %get-tuple-element.70), channel_id=1, source_target_pairs={{0,4},{1,13},{2,6},{3,15},{4,8},{5,1},{6,10},{7,3},{8,12},{9,5},{1... | collective-permute-start | bytes 2359304 | tf_op jit(solution)/shard_map/ppermute | solution.py:27
  58.2 15.3 %collective-permute-start.22 = (bf16[2,512,256]{2,1,0:T(8,128)(2,1)}, bf16[2,512,256]{2,1,0:T(8,128)(2,1)}, u32[]{:S(2)}, u32[]{:S(2)}) collective-permute-start(bf16[2,512,256]{2,1,0:T(8,128)(2,1)} %pad_maximum_fusion.1.refs_16_), channel_id=1, source_target_pairs={{0,16},{1,17},{2,18},{3,19},{4,20},{5,21},{6,22},{7,23},{8,24},{9,... | collective-permute-start | bytes 1572872 | tf_op jit(solution)/shard_map/ppermute | solution.py:27
  58.4 15.1 %collective-permute-start.21 = (bf16[2,512,256]{2,1,0:T(8,128)(2,1)}, bf16[2,512,256]{2,1,0:T(8,128)(2,1)}, u32[]{:S(2)}, u32[]{:S(2)}) collective-permute-start(bf16[2,512,256]{2,1,0:T(8,128)(2,1)} %pad_maximum_fusion.1.refs_16_), channel_id=1, source_target_pairs={{0,48},{1,49},{2,50},{3,51},{4,52},{5,53},{6,54},{7,55},{8,56},{9,... | collective-permute-start | bytes 1572872 | tf_op jit(solution)/shard_map/ppermute | solution.py:27
  62.1 19.5 %collective-permute-start.9 = (bf16[768,128]{1,0:T(8,128)(2,1)}, bf16[768,128]{1,0:T(8,128)(2,1)}, u32[]{:S(2)}, u32[]{:S(2)}) collective-permute-start(bf16[768,128]{1,0:T(8,128)(2,1)} %constant_dynamic-slice_fusion.2), channel_id=1, source_target_pairs={{0,1},{1,0},{2,3},{3,2},{4,5},{5,4},{6,7},{7,6},{8,9},{9,8},{10,11... | collective-permute-start | bytes 589832 | tf_op jit(solution)/shard_map/ppermute | solution.py:27
  81.4 9.0 %collective-permute-start.23 = (bf16[768,256]{1,0:T(8,128)(2,1)S(1)}, bf16[768,256]{1,0:T(8,128)(2,1)S(1)}, u32[]{:S(2)}, u32[]{:S(2)}) collective-permute-start(bf16[768,256]{1,0:T(8,128)(2,1)S(1)} %get-tuple-element.114), channel_id=1, source_target_pairs={{0,4},{1,13},{2,6},{3,15},{4,8},{5,1},{6,10},{7,3},{8,12},{9,5},{1... | collective-permute-start | bytes 1179656 | tf_op jit(solution)/shard_map/ppermute | solution.py:27
  82.7 20.7 %collective-permute-start.25 = (bf16[768,256]{1,0:T(8,128)(2,1)}, bf16[768,256]{1,0:T(8,128)(2,1)}, u32[]{:S(2)}, u32[]{:S(2)}) collective-permute-start(bf16[768,256]{1,0:T(8,128)(2,1)} %get-tuple-element.113), channel_id=1, source_target_pairs={{0,4},{1,13},{2,6},{3,15},{4,8},{5,1},{6,10},{7,3},{8,12},{9,5},{1... | collective-permute-start | bytes 1179656 | tf_op jit(solution)/shard_map/ppermute | solution.py:27
  86.7 16.7 %collective-permute-start.26 = (bf16[2,512,256]{2,1,0:T(8,128)(2,1)}, bf16[2,512,256]{2,1,0:T(8,128)(2,1)}, u32[]{:S(2)}, u32[]{:S(2)}) collective-permute-start(bf16[2,512,256]{2,1,0:T(8,128)(2,1)} %broadcast_select_fusion), channel_id=1, source_target_pairs={{0,16},{1,49},{2,18},{3,51},{4,20},{5,53},{6,22},{7,55},{8,24},{9,... | collective-permute-start | bytes 1572872 | tf_op jit(solution)/shard_map/ppermute | solution.py:27
  91.5 11.9 %collective-permute-start.24 = (bf16[768,256]{1,0:T(8,128)(2,1)S(1)}, bf16[768,256]{1,0:T(8,128)(2,1)}, u32[]{:S(2)}, u32[]{:S(2)}) collective-permute-start(bf16[768,256]{1,0:T(8,128)(2,1)S(1)} %fusion.3), channel_id=1, source_target_pairs={{0,2},{1,3},{2,0},{3,1},{4,6},{5,7},{6,4},{7,5},{8,10},{9,11},{10,... | collective-permute-start | bytes 1179656 | tf_op jit(solution)/shard_map/ppermute | solution.py:27
  105.2 10.1 %collective-permute-start.29 = (bf16[768,256]{1,0:T(8,128)(2,1)S(1)}, bf16[768,256]{1,0:T(8,128)(2,1)S(1)}, u32[]{:S(2)}, u32[]{:S(2)}) collective-permute-start(bf16[768,256]{1,0:T(8,128)(2,1)S(1)} %get-tuple-element.112.refs_0_), channel_id=1, source_target_pairs={{0,4},{1,5},{2,6},{3,7},{4,8},{5,9},{6,10},{7,11},{8,12},{9,13},{1... | collective-permute-start | bytes 1179656 | tf_op jit(solution)/shard_map/ppermute | solution.py:27
  105.9 10.9 %collective-permute-start.28 = (bf16[768,256]{1,0:T(8,128)(2,1)S(1)}, bf16[768,256]{1,0:T(8,128)(2,1)S(1)}, u32[]{:S(2)}, u32[]{:S(2)}) collective-permute-start(bf16[768,256]{1,0:T(8,128)(2,1)S(1)} %get-tuple-element.112.refs_0_), channel_id=1, source_target_pairs={{0,12},{1,13},{2,14},{3,15},{4,0},{5,1},{6,2},{7,3},{8,4},{9,5},{1... | collective-permute-start | bytes 1179656 | tf_op jit(solution)/shard_map/ppermute | solution.py:27
  108.5 9.9 %collective-permute-start.27 = (bf16[768,256]{1,0:T(8,128)(2,1)S(1)}, bf16[768,256]{1,0:T(8,128)(2,1)S(1)}, u32[]{:S(2)}, u32[]{:S(2)}) collective-permute-start(bf16[768,256]{1,0:T(8,128)(2,1)S(1)} %get-tuple-element.112.refs_0_), channel_id=1, source_target_pairs={{0,2},{1,3},{2,0},{3,1},{4,6},{5,7},{6,4},{7,5},{8,10},{9,11},{10,... | collective-permute-start | bytes 1179656 | tf_op jit(solution)/shard_map/ppermute | solution.py:27
  118.4 15.7 %collective-permute-start.31 = (bf16[768,256]{1,0:T(8,128)(2,1)S(1)}, bf16[768,256]{1,0:T(8,128)(2,1)S(1)}, u32[]{:S(2)}, u32[]{:S(2)}) collective-permute-start(bf16[768,256]{1,0:T(8,128)(2,1)S(1)} %collective-permute-done.27.refs_1_), channel_id=1, source_target_pairs={{0,4},{1,5},{2,6},{3,7},{4,8},{5,9},{6,10},{7,11},{8,12},{9,13},{1... | collective-permute-start | bytes 1179656 | tf_op jit(solution)/shard_map/ppermute | solution.py:27
  120.2 13.9 %collective-permute-start.30 = (bf16[768,256]{1,0:T(8,128)(2,1)S(1)}, bf16[768,256]{1,0:T(8,128)(2,1)S(1)}, u32[]{:S(2)}, u32[]{:S(2)}) collective-permute-start(bf16[768,256]{1,0:T(8,128)(2,1)S(1)} %collective-permute-done.27.refs_1_), channel_id=1, source_target_pairs={{0,12},{1,13},{2,14},{3,15},{4,0},{5,1},{6,2},{7,3},{8,4},{9,5},{1... | collective-permute-start | bytes 1179656 | tf_op jit(solution)/shard_map/ppermute | solution.py:27
  121.8 10.7 %collective-permute-start.32 = (bf16[768,256]{1,0:T(8,128)(2,1)S(1)}, bf16[768,256]{1,0:T(8,128)(2,1)S(1)}, u32[]{:S(2)}, u32[]{:S(2)}) collective-permute-start(bf16[768,256]{1,0:T(8,128)(2,1)S(1)} %broadcast_select_fusion.2), channel_id=1, source_target_pairs={{0,4},{1,13},{2,6},{3,15},{4,8},{5,1},{6,10},{7,3},{8,12},{9,5},{1... | collective-permute-start | bytes 1179656 | tf_op jit(solution)/shard_map/ppermute | solution.py:27
  124.1 13.5 %collective-permute-start.37 = (bf16[768,256]{1,0:T(8,128)(2,1)}, bf16[768,256]{1,0:T(8,128)(2,1)S(1)}, u32[]{:S(2)}, u32[]{:S(2)}) collective-permute-start(bf16[768,256]{1,0:T(8,128)(2,1)} %copy-done.8), channel_id=1, source_target_pairs={{0,1},{1,0},{2,3},{3,2},{4,5},{5,4},{6,7},{7,6},{8,9},{9,8},{10,11... | collective-permute-start | bytes 1179656 | tf_op jit(solution)/shard_map/ppermute | solution.py:27
  126.5 11.2 %collective-permute-start.39 = (bf16[768,256]{1,0:T(8,128)(2,1)S(1)}, bf16[768,256]{1,0:T(8,128)(2,1)S(1)}, u32[]{:S(2)}, u32[]{:S(2)}) collective-permute-start(bf16[768,256]{1,0:T(8,128)(2,1)S(1)} %collective-permute-done.28.refs_2_), channel_id=1, source_target_pairs={{0,1},{1,0},{2,3},{3,2},{4,5},{5,4},{6,7},{7,6},{8,9},{9,8},{10,11... | collective-permute-start | bytes 1179656 | tf_op jit(solution)/shard_map/ppermute | solution.py:27
  134.2 9.1 %collective-permute-start.35 = (bf16[768,256]{1,0:T(8,128)(2,1)S(1)}, bf16[768,256]{1,0:T(8,128)(2,1)S(1)}, u32[]{:S(2)}, u32[]{:S(2)}) collective-permute-start(bf16[768,256]{1,0:T(8,128)(2,1)S(1)} %broadcast_select_fusion.1), channel_id=1, source_target_pairs={{0,4},{1,13},{2,6},{3,15},{4,8},{5,1},{6,10},{7,3},{8,12},{9,5},{1... | collective-permute-start | bytes 1179656 | tf_op jit(solution)/shard_map/ppermute | solution.py:27
  154.3 16.1 %collective-permute-start.45 = (bf16[2,512,256]{2,1,0:T(8,128)(2,1)}, bf16[2,512,256]{2,1,0:T(8,128)(2,1)S(1)}, u32[]{:S(2)}, u32[]{:S(2)}) collective-permute-start(bf16[2,512,256]{2,1,0:T(8,128)(2,1)} %get-tuple-element.96), channel_id=1, source_target_pairs={{0,16},{1,49},{2,18},{3,51},{4,20},{5,53},{6,22},{7,55},{8,24},{9,... | collective-permute-start | bytes 1572872 | tf_op jit(solution)/shard_map/ppermute | solution.py:27
  155.4 15.0 %collective-permute-start.46 = (bf16[2,512,256]{2,1,0:T(8,128)(2,1)}, bf16[2,512,256]{2,1,0:T(8,128)(2,1)S(1)}, u32[]{:S(2)}, u32[]{:S(2)}) collective-permute-start(bf16[2,512,256]{2,1,0:T(8,128)(2,1)} %get-tuple-element.97), channel_id=1, source_target_pairs={{0,48},{1,17},{2,50},{3,19},{4,52},{5,21},{6,54},{7,23},{8,56},{9,... | collective-permute-start | bytes 1572872 | tf_op jit(solution)/shard_map/ppermute | solution.py:27
  178.5 8.6 %collective-permute-start.49 = (bf16[512,256]{1,0:T(8,128)(2,1)S(1)}, bf16[512,256]{1,0:T(8,128)(2,1)S(1)}, u32[]{:S(2)}, u32[]{:S(2)}) collective-permute-start(bf16[512,256]{1,0:T(8,128)(2,1)S(1)} %fusion.7), channel_id=1, source_target_pairs={{0,64},{1,65},{2,66},{3,67},{4,68},{5,69},{6,70},{7,71},{8,72},{9,... | collective-permute-start | bytes 786440 | tf_op jit(solution)/shard_map/ppermute | solution.py:27
  (58 other events, 353.3 us)
Sparse Core Ops, SparseCore 0:
  10.3 77.9 all-gather.1
  118.5 42.2 reduce-scatter.1

commit v15 on v12

--- a/solution.py
+++ b/solution.py
@@ -333,8 +333,7 @@
     passed, back, grad_x, grad_wout = tie(passed, back, grad_x, grad_wout)
     far = z_split(add([further[1], passed[1]]).astype(BF16), 1)
     near = z_split(add([further[0], passed[0]]).astype(BF16), 1)
-    crossed, sums = tie(add([own[1], back[1], far]).astype(BF16), sums)
-    crossed = y_lo_swap(crossed)
+    crossed = y_lo_swap(add([own[1], back[1], far]).astype(BF16))
     sums = sums + y_lo_swap(sums)
     grad_win = add([own[0], back[0], near, crossed]) * scaling
     grad_smid = keep_mid.astype(F32) * scaling * sums[0]

time: 194 us -> 191 us (0.985)
  waiting for transfers between devices: 54.2 us -> 50.3 us
    ppermute x51, waiting for transfers between devices: 54.1 us -> 50.3 us  [permute(): return lax.ppermute(v, AXES, pairs)]
where the time goes in v15:
time: 191 us
  starting transfers between devices  56.3 us (29%)
  waiting for transfers between devices  50.3 us (26%)
  Pallas kernels  31.2 us (16%)
  other arithmetic  23.4 us (12%)
  between operations  14.6 us (8%)
  matrix products  7.66 us (4%)
  local copies, waits for them, and re-layouts  7.29 us (4%)
    ppermute x51, starting transfers between devices, permute(): return lax.ppermute(v, AXES, pairs)  56.2 us
    ppermute x51, waiting for transfers between devices, permute(): return lax.ppermute(v, AXES, pairs)  50.3 us
    pallas_call x4, Pallas kernels, call(): pl.pallas_call(body, out_shape=outs, in_specs=[pl.BlockSpec(memory_space=...  31.2 us
    dot_general x1, matrix products, dot(): lax.dot_general(a, b, (((ca,), (cb,)), ((), ())), preferred_element_type=...  7.66 us
    unnamed x75, local copies, waits for them, and re-layouts  7.15 us
  transfers between devices with their start and end apart: 53, of which 24 were waited for; matrix products, arithmetic and copies ran while one was open for 15% of the time, Pallas kernels for 16%

profile of v15, /device:TPU:0, one launch (start us, length us, event | category | flops | bytes accessed | tf_op | source)
XLA Modules:
  0.0 190.8 jit_solution(6169473726418593661)
XLA Ops:
  9.8 2.1 %collective-permute-start.2 = (bf16[256,512]{1,0:T(8,128)(2,1)}, bf16[256,512]{1,0:T(8,128)(2,1)}, u32[]{:S(2)}, u32[]{:S(2)}) collective-permute-start(bf16[256,512]{1,0:T(8,128)(2,1)} %refs_0_.3), channel_id=1, source_target_pairs={{0,16},{1,17},{2,18},{3,19},{4,20},{5,21},{6,22},{7,23},{8,24},{9,... | collective-permute-start | bytes 786440 | tf_op jit(solution)/shard_map/ppermute | solution.py:27
  11.9 2.2 %collective-permute-start.1 = (bf16[256,512]{1,0:T(8,128)(2,1)}, bf16[256,512]{1,0:T(8,128)(2,1)}, u32[]{:S(2)}, u32[]{:S(2)}) collective-permute-start(bf16[256,512]{1,0:T(8,128)(2,1)} %refs_0_.3), channel_id=1, source_target_pairs={{0,48},{1,49},{2,50},{3,51},{4,52},{5,53},{6,54},{7,55},{8,56},{9,... | collective-permute-start | bytes 786440 | tf_op jit(solution)/shard_map/ppermute | solution.py:27
  16.4 2.6 %fusion.1 = (f32[512]{0:T(512)S(1)}, bf16[1536,512]{1,0:T(8,128)(2,1)S(1)}) fusion(bf16[1536,512]{1,0:T(8,128)(2,1)} %cot.1, bf16[1536,512]{1,0:T(8,128)(2,1)} %param.12, f32[512]{0:T(512)S(1)} %convert_multiply_fusion.4), kind=kLoop, calls=%fused_computation.3 | loop fusion | flops 4718080 | bytes 4722688 | tf_op jit(solution)/shard_map/reduce_sum | solution.py:250
  22.2 3.2 %collective-permute-start.3 = (bf16[256,512]{1,0:T(8,128)(2,1)}, bf16[256,512]{1,0:T(8,128)(2,1)S(1)}, u32[]{:S(2)}, u32[]{:S(2)}) collective-permute-start(bf16[256,512]{1,0:T(8,128)(2,1)} %collective-permute-done.refs_1_), channel_id=1, source_target_pairs={{0,48},{1,49},{2,50},{3,51},{4,52},{5,53},{6,54},{7,55},{8,56},{9,... | collective-permute-start | bytes 786440 | tf_op jit(solution)/shard_map/ppermute | solution.py:27
  28.8 2.5 %pad_maximum_fusion.conv = bf16[768,1024]{1,0:T(8,128)(2,1)} fusion(bf16[768,512]{1,0:T(8,128)(2,1)} %collective-permute-done.6, bf16[768,512]{1,0:T(8,128)(2,1)S(1)} %get-tuple-element.113), kind=kLoop, calls=%fused_computation.5 | loop fusion | flops 3145728 | bytes 3145728 | tf_op jit(solution)/shard_map/concatenate | solution.py:259
  31.2 3.9 %collective-permute-done.5.refs_6_ = bf16[256,512]{1,0:T(8,128)(2,1)S(1)} collective-permute-done((bf16[256,512]{1,0:T(8,128)(2,1)S(1)}, bf16[256,512]{1,0:T(8,128)(2,1)S(1)}, u32[]{:S(2)}, u32[]{:S(2)}) %collective-permute-start.5) | collective-permute-done | bytes 262176 | tf_op jit(solution)/shard_map/ppermute | solution.py:27
  38.0 2.7 %copy.15 = bf16[1536,512]{0,1:T(8,128)(2,1)} copy(bf16[1536,512]{1,0:T(8,128)(2,1)} %param.10) | data formatting | bytes 3145728 | tf_op args[0]
  47.1 6.5 %shard_map.137 = (bf16[2,768,256]{2,1,0:T(8,128)(2,1)}, bf16[2,768,256]{2,1,0:T(8,128)(2,1)}) custom-call(s32[2]{0:T(128)} %pad_add_fusion.here, bf16[768,1024]{1,0:T(8,128)(2,1)} %pad_maximum_fusion.conv, bf16[256,512]{1,0:T(8,128)(2,1)} %refs_0_.3, bf16[256,512]{1,0:T(8,128)(2,1)} %collective-permute-done.refs_1_, ...), custom_call_target="tpu_custom_call" | custom-call | flops 1610612736 | bytes 8388608 | tf_op jit(solution)/shard_map/pallas_call | solution.py:90
  53.7 2.8 %collective-permute-start.20 = (bf16[2,768,256]{2,1,0:T(8,128)(2,1)}, bf16[2,768,256]{2,1,0:T(8,128)(2,1)S(1)}, u32[]{:S(2)}, u32[]{:S(2)}) collective-permute-start(bf16[2,768,256]{2,1,0:T(8,128)(2,1)} %get-tuple-element.69), channel_id=1, source_target_pairs={{0,12},{1,5},{2,14},{3,7},{4,0},{5,9},{6,2},{7,11},{8,4},{9,13},{1... | collective-permute-start | bytes 2359304 | tf_op jit(solution)/shard_map/ppermute | solution.py:27
  58.7 2.8 %collective-permute-start.21 = (bf16[2,512,256]{2,1,0:T(8,128)(2,1)}, bf16[2,512,256]{2,1,0:T(8,128)(2,1)}, u32[]{:S(2)}, u32[]{:S(2)}) collective-permute-start(bf16[2,512,256]{2,1,0:T(8,128)(2,1)} %pad_maximum_fusion.1.refs_16_), channel_id=1, source_target_pairs={{0,48},{1,49},{2,50},{3,51},{4,52},{5,53},{6,54},{7,55},{8,56},{9,... | collective-permute-start | bytes 1572872 | tf_op jit(solution)/shard_map/ppermute | solution.py:27
  61.9 6.4 %shard_map.138 = (bf16[2,768,256]{2,1,0:T(8,128)(2,1)}, bf16[2,768,256]{2,1,0:T(8,128)(2,1)}) custom-call(s32[2]{0:T(128)} %pad_add_fusion.here, bf16[768,1024]{1,0:T(8,128)(2,1)} %pad_maximum_fusion.conv, bf16[256,512]{1,0:T(8,128)(2,1)} %refs_0_.3, bf16[256,512]{1,0:T(8,128)(2,1)} %collective-permute-done.refs_1_, ...), custom_call_target="tpu_custom_call" | custom-call | flops 1610612736 | bytes 8388608 | tf_op jit(solution)/shard_map/pallas_call | solution.py:90
  68.3 5.3 %collective-permute-done.22.refs_18_ = bf16[2,512,256]{2,1,0:T(8,128)(2,1)} collective-permute-done((bf16[2,512,256]{2,1,0:T(8,128)(2,1)}, bf16[2,512,256]{2,1,0:T(8,128)(2,1)}, u32[]{:S(2)}, u32[]{:S(2)}) %collective-permute-start.22) | collective-permute-done | bytes 524320 | tf_op jit(solution)/shard_map/ppermute | solution.py:27
  73.6 4.6 %collective-permute-done.20 = bf16[2,768,256]{2,1,0:T(8,128)(2,1)S(1)} collective-permute-done((bf16[2,768,256]{2,1,0:T(8,128)(2,1)}, bf16[2,768,256]{2,1,0:T(8,128)(2,1)S(1)}, u32[]{:S(2)}, u32[]{:S(2)}) %collective-permute-start.20) | collective-permute-done | bytes 786464 | tf_op jit(solution)/shard_map/ppermute | solution.py:27
  78.9 2.1 %fusion.11 = (bf16[768,256]{1,0:T(8,128)(2,1)}, bf16[768,256]{1,0:T(8,128)(2,1)S(1)}) fusion(bf16[2,768,256]{2,1,0:T(8,128)(2,1)S(1)} %collective-permute-done.19, bf16[2,768,256]{2,1,0:T(8,128)(2,1)} %get-tuple-element.77), kind=kLoop, calls=%fused_computation.30 | loop fusion | flops 1572864 | bytes 2359296 | tf_op jit(solution)/shard_map/convert_element_type | solution.py:294
  86.9 3.0 %collective-permute-done.23 = bf16[768,256]{1,0:T(8,128)(2,1)S(1)} collective-permute-done((bf16[768,256]{1,0:T(8,128)(2,1)S(1)}, bf16[768,256]{1,0:T(8,128)(2,1)S(1)}, u32[]{:S(2)}, u32[]{:S(2)}) %collective-permute-start.23) | collective-permute-done | bytes 393248 | tf_op jit(solution)/shard_map/ppermute | solution.py:27
  90.8 5.1 %collective-permute-start.24 = (bf16[768,256]{1,0:T(8,128)(2,1)}, bf16[768,256]{1,0:T(8,128)(2,1)}, u32[]{:S(2)}, u32[]{:S(2)}) collective-permute-start(bf16[768,256]{1,0:T(8,128)(2,1)} %fusion.3), channel_id=1, source_target_pairs={{0,2},{1,3},{2,0},{3,1},{4,6},{5,7},{6,4},{7,5},{8,10},{9,11},{10,... | collective-permute-start | bytes 1179656 | tf_op jit(solution)/shard_map/ppermute | solution.py:27
  96.0 7.7 %convolution_convert_fusion = bf16[2048,512]{1,0:T(8,128)(2,1)} fusion(bf16[1536,2048]{1,0:T(8,128)(2,1)} %all-gather.2.cloned.1.call-done, bf16[1536,512]{1,0:T(8,128)(2,1)S(1)} %get-tuple-element.112), kind=kOutput, calls=%fused_computation.4 | convolution fusion | flops 3222274048 | bytes 9961472 | tf_op jit(solution)/shard_map/dot_general | solution.py:63
  106.0 2.5 %collective-permute-start.28 = (bf16[768,256]{1,0:T(8,128)(2,1)S(1)}, bf16[768,256]{1,0:T(8,128)(2,1)S(1)}, u32[]{:S(2)}, u32[]{:S(2)}) collective-permute-start(bf16[768,256]{1,0:T(8,128)(2,1)S(1)} %get-tuple-element.108.refs_0_), channel_id=1, source_target_pairs={{0,12},{1,13},{2,14},{3,15},{4,0},{5,1},{6,2},{7,3},{8,4},{9,5},{1... | collective-permute-start | bytes 1179656 | tf_op jit(solution)/shard_map/ppermute | solution.py:27
  108.5 2.3 %collective-permute-start.27 = (bf16[768,256]{1,0:T(8,128)(2,1)S(1)}, bf16[768,256]{1,0:T(8,128)(2,1)S(1)}, u32[]{:S(2)}, u32[]{:S(2)}) collective-permute-start(bf16[768,256]{1,0:T(8,128)(2,1)S(1)} %get-tuple-element.108.refs_0_), channel_id=1, source_target_pairs={{0,2},{1,3},{2,0},{3,1},{4,6},{5,7},{6,4},{7,5},{8,10},{9,11},{10,... | collective-permute-start | bytes 1179656 | tf_op jit(solution)/shard_map/ppermute | solution.py:27
  110.8 3.7 %collective-permute-done.29.refs_4_ = bf16[768,256]{1,0:T(8,128)(2,1)S(1)} collective-permute-done((bf16[768,256]{1,0:T(8,128)(2,1)S(1)}, bf16[768,256]{1,0:T(8,128)(2,1)S(1)}, u32[]{:S(2)}, u32[]{:S(2)}) %collective-permute-start.29) | collective-permute-done | bytes 393248 | tf_op jit(solution)/shard_map/ppermute | solution.py:27
  115.1 2.7 %collective-permute-done.27.refs_1_ = bf16[768,256]{1,0:T(8,128)(2,1)S(1)} collective-permute-done((bf16[768,256]{1,0:T(8,128)(2,1)S(1)}, bf16[768,256]{1,0:T(8,128)(2,1)S(1)}, u32[]{:S(2)}, u32[]{:S(2)}) %collective-permute-start.27) | collective-permute-done | bytes 393248 | tf_op jit(solution)/shard_map/ppermute | solution.py:27
  118.4 2.7 %collective-permute-start.30 = (bf16[768,256]{1,0:T(8,128)(2,1)S(1)}, bf16[768,256]{1,0:T(8,128)(2,1)S(1)}, u32[]{:S(2)}, u32[]{:S(2)}) collective-permute-start(bf16[768,256]{1,0:T(8,128)(2,1)S(1)} %collective-permute-done.27.refs_1_), channel_id=1, source_target_pairs={{0,12},{1,13},{2,14},{3,15},{4,0},{5,1},{6,2},{7,3},{8,4},{9,5},{1... | collective-permute-start | bytes 1179656 | tf_op jit(solution)/shard_map/ppermute | solution.py:27
  124.0 2.0 %collective-permute-done.34 = f32[5,128]{1,0:T(8,128)S(1)} collective-permute-done((f32[5,128]{1,0:T(8,128)S(1)}, f32[5,128]{1,0:T(8,128)S(1)}, u32[]{:S(2)}, u32[]{:S(2)}) %collective-permute-start.34) | collective-permute-done | bytes 2592 | tf_op jit(solution)/shard_map/ppermute | solution.py:27
  126.0 5.1 %collective-permute-done.32.refs_6_ = bf16[768,256]{1,0:T(8,128)(2,1)S(1)} collective-permute-done((bf16[768,256]{1,0:T(8,128)(2,1)S(1)}, bf16[768,256]{1,0:T(8,128)(2,1)S(1)}, u32[]{:S(2)}, u32[]{:S(2)}) %collective-permute-start.32) | collective-permute-done | bytes 393248 | tf_op jit(solution)/shard_map/ppermute | solution.py:27
  132.0 4.3 %collective-permute-start.36 = (f32[5,128]{1,0:T(8,128)S(1)}, f32[5,128]{1,0:T(8,128)S(1)}, u32[]{:S(2)}, u32[]{:S(2)}) collective-permute-start(f32[5,128]{1,0:T(8,128)S(1)} %fusion.19), channel_id=1, source_target_pairs={{0,32},{1,33},{2,34},{3,35},{4,36},{5,37},{6,38},{7,39},{8,40},{9,... | collective-permute-start | bytes 7688 | tf_op jit(solution)/shard_map/ppermute | solution.py:27
  138.3 2.0 %collective-permute-done.35.refs_7_ = bf16[768,256]{1,0:T(8,128)(2,1)S(1)} collective-permute-done((bf16[768,256]{1,0:T(8,128)(2,1)S(1)}, bf16[768,256]{1,0:T(8,128)(2,1)S(1)}, u32[]{:S(2)}, u32[]{:S(2)}) %collective-permute-start.35) | collective-permute-done | bytes 393248 | tf_op jit(solution)/shard_map/ppermute | solution.py:27
  142.3 8.7 %shard_map.139 = (bf16[2,512,256]{2,1,0:T(8,128)(2,1)}, bf16[2,512,256]{2,1,0:T(8,128)(2,1)}, bf16[2,512,256]{2,1,0:T(8,128)(2,1)}, bf16[2,512,256]{2,1,0:T(8,128)(2,1)}) custom-call(s32[2]{0:T(128)} %pad_add_fusion.here, bf16[512,1536]{1,0:T(8,128)(2,1)} %bitcast.58, bf16[768,256]{1,0:T(8,128)(2,1)} %copy-done.8, bf16[768,256]{1,0:T(8,128)(2,1)} %copy-done.16, ...), custom_call_target="tpu_custom_call" | custom-call | flops 3221225472 | bytes 10485760 | tf_op jit(solution)/shard_map/pallas_call | solution.py:90
  151.0 3.2 %collective-permute-start.45 = (bf16[2,512,256]{2,1,0:T(8,128)(2,1)}, bf16[2,512,256]{2,1,0:T(8,128)(2,1)S(1)}, u32[]{:S(2)}, u32[]{:S(2)}) collective-permute-start(bf16[2,512,256]{2,1,0:T(8,128)(2,1)} %get-tuple-element.94), channel_id=1, source_target_pairs={{0,16},{1,49},{2,18},{3,51},{4,20},{5,53},{6,22},{7,55},{8,24},{9,... | collective-permute-start | bytes 1572872 | tf_op jit(solution)/shard_map/ppermute | solution.py:27
  154.8 9.6 %shard_map.140 = bf16[1536,512]{1,0:T(8,128)(2,1)} custom-call(s32[2]{0:T(128)} %pad_add_fusion.here, bf16[1536,512]{1,0:T(8,128)(2,1)} %cot.1, bf16[768,256]{1,0:T(8,128)(2,1)} %copy-done.8, bf16[768,256]{1,0:T(8,128)(2,1)} %copy-done.16, bf16[768,256]{1,0:T(8,128)(2,1)} %copy-done.5, bf16[768,256]{1,0:T(8,128)(2,1)} %copy-done.7, ...), custom_call_target="tpu_custom_call" | custom-call | flops 3221225472 | bytes 12582912 | tf_op jit(solution)/shard_map/pallas_call | solution.py:90
  169.9 3.1 %collective-permute-done.50 = f32[5,128]{1,0:T(8,128)S(1)} collective-permute-done((f32[5,128]{1,0:T(8,128)S(1)}, f32[5,128]{1,0:T(8,128)S(1)}, u32[]{:S(2)}, u32[]{:S(2)}) %collective-permute-start.50) | collective-permute-done | bytes 2592 | tf_op jit(solution)/shard_map/ppermute | solution.py:27
  178.6 2.0 %collective-permute-done.47 = bf16[512,256]{1,0:T(8,128)(2,1)S(1)} collective-permute-done((bf16[512,256]{1,0:T(8,128)(2,1)S(1)}, bf16[512,256]{1,0:T(8,128)(2,1)S(1)}, u32[]{:S(2)}, u32[]{:S(2)}) %collective-permute-start.47) | collective-permute-done | bytes 262176 | tf_op jit(solution)/shard_map/ppermute | solution.py:27
  180.6 2.4 %collective-permute-done.49 = bf16[512,256]{1,0:T(8,128)(2,1)S(1)} collective-permute-done((bf16[512,256]{1,0:T(8,128)(2,1)S(1)}, bf16[512,256]{1,0:T(8,128)(2,1)S(1)}, u32[]{:S(2)}, u32[]{:S(2)}) %collective-permute-start.49) | collective-permute-done | bytes 262176 | tf_op jit(solution)/shard_map/ppermute | solution.py:27
  (191 shorter events, 54.3 us)
Async XLA Ops:
  7.2 88.8 %all-gather.2.cloned.1.call-start = ((), (), s32[]{:S(2)}) async-start(), calls=%async_computation.1 | async-start | bytes 6684672 | tf_op jit(solution)/shard_map/all_gather | solution.py:243
  9.8 154.6 %reduce-scatter.2.cloned.1.call-start = ((), (), s32[]{:S(2)}) async-start(), calls=%async_computation.2 | async-start | bytes 2359296 | tf_op jit(solution)/shard_map/reduce_scatter | solution.py:310
  9.8 10.8 %collective-permute-start.2 = (bf16[256,512]{1,0:T(8,128)(2,1)}, bf16[256,512]{1,0:T(8,128)(2,1)}, u32[]{:S(2)}, u32[]{:S(2)}) collective-permute-start(bf16[256,512]{1,0:T(8,128)(2,1)} %refs_0_.3), channel_id=1, source_target_pairs={{0,16},{1,17},{2,18},{3,19},{4,20},{5,21},{6,22},{7,23},{8,24},{9,... | collective-permute-start | bytes 786440 | tf_op jit(solution)/shard_map/ppermute | solution.py:27
  11.9 8.7 %collective-permute-start.1 = (bf16[256,512]{1,0:T(8,128)(2,1)}, bf16[256,512]{1,0:T(8,128)(2,1)}, u32[]{:S(2)}, u32[]{:S(2)}) collective-permute-start(bf16[256,512]{1,0:T(8,128)(2,1)} %refs_0_.3), channel_id=1, source_target_pairs={{0,48},{1,49},{2,50},{3,51},{4,52},{5,53},{6,54},{7,55},{8,56},{9,... | collective-permute-start | bytes 786440 | tf_op jit(solution)/shard_map/ppermute | solution.py:27
  14.1 8.1 %collective-permute-start = (bf16[256,512]{1,0:T(8,128)(2,1)}, bf16[256,512]{1,0:T(8,128)(2,1)}, u32[]{:S(2)}, u32[]{:S(2)}) collective-permute-start(bf16[256,512]{1,0:T(8,128)(2,1)} %refs_0_.3), channel_id=1, source_target_pairs={{0,64},{1,65},{2,66},{3,67},{4,68},{5,69},{6,70},{7,71},{8,72},{9,... | collective-permute-start | bytes 786440 | tf_op jit(solution)/shard_map/ppermute | solution.py:27
  22.2 13.5 %collective-permute-start.4 = (bf16[256,512]{1,0:T(8,128)(2,1)}, bf16[256,512]{1,0:T(8,128)(2,1)S(1)}, u32[]{:S(2)}, u32[]{:S(2)}) collective-permute-start(bf16[256,512]{1,0:T(8,128)(2,1)} %collective-permute-done.refs_1_), channel_id=1, source_target_pairs={{0,16},{1,17},{2,18},{3,19},{4,20},{5,21},{6,22},{7,23},{8,24},{9,... | collective-permute-start | bytes 786440 | tf_op jit(solution)/shard_map/ppermute | solution.py:27
  22.2 13.5 %collective-permute-start.3 = (bf16[256,512]{1,0:T(8,128)(2,1)}, bf16[256,512]{1,0:T(8,128)(2,1)S(1)}, u32[]{:S(2)}, u32[]{:S(2)}) collective-permute-start(bf16[256,512]{1,0:T(8,128)(2,1)} %collective-permute-done.refs_1_), channel_id=1, source_target_pairs={{0,48},{1,49},{2,50},{3,51},{4,52},{5,53},{6,54},{7,55},{8,56},{9,... | collective-permute-start | bytes 786440 | tf_op jit(solution)/shard_map/ppermute | solution.py:27
  26.4 8.7 %collective-permute-start.5 = (bf16[256,512]{1,0:T(8,128)(2,1)S(1)}, bf16[256,512]{1,0:T(8,128)(2,1)S(1)}, u32[]{:S(2)}, u32[]{:S(2)}) collective-permute-start(bf16[256,512]{1,0:T(8,128)(2,1)S(1)} %broadcast_select_fusion.4), channel_id=1, source_target_pairs={{0,16},{1,49},{2,18},{3,51},{4,20},{5,53},{6,22},{7,55},{8,24},{9,... | collective-permute-start | bytes 786440 | tf_op jit(solution)/shard_map/ppermute | solution.py:27
  26.5 9.0 %collective-permute-start.7 = (bf16[512,256]{1,0:T(8,128)(2,1)S(1)}, bf16[512,256]{1,0:T(8,128)(2,1)}, u32[]{:S(2)}, u32[]{:S(2)}) collective-permute-start(bf16[512,256]{1,0:T(8,128)(2,1)S(1)} %copy-done.9), channel_id=1, source_target_pairs={{0,64},{1,65},{2,66},{3,67},{4,68},{5,69},{6,70},{7,71},{8,72},{9,... | collective-permute-start | bytes 786440 | tf_op jit(solution)/shard_map/ppermute | solution.py:27
  28.8 13.5 %collective-permute-start.11 = (bf16[256,512]{1,0:T(8,128)(2,1)}, bf16[256,512]{1,0:T(8,128)(2,1)S(1)}, u32[]{:S(2)}, u32[]{:S(2)}) collective-permute-start(bf16[256,512]{1,0:T(8,128)(2,1)} %refs_0_.3), channel_id=1, source_target_pairs={{0,1},{1,0},{2,3},{3,2},{4,5},{5,4},{6,7},{7,6},{8,9},{9,8},{10,11... | collective-permute-start | bytes 786440 | tf_op jit(solution)/shard_map/ppermute | solution.py:27
  36.5 7.8 %collective-permute-start.8 = (bf16[256,512]{1,0:T(8,128)(2,1)S(1)}, bf16[256,512]{1,0:T(8,128)(2,1)}, u32[]{:S(2)}, u32[]{:S(2)}) collective-permute-start(bf16[256,512]{1,0:T(8,128)(2,1)S(1)} %broadcast_select_fusion.3), channel_id=1, source_target_pairs={{0,16},{1,49},{2,18},{3,51},{4,20},{5,53},{6,22},{7,55},{8,24},{9,... | collective-permute-start | bytes 786440 | tf_op jit(solution)/shard_map/ppermute | solution.py:27
  44.3 12.2 %collective-permute-start.10 = (f32[2,128]{1,0:T(2,128)S(1)}, f32[2,128]{1,0:T(2,128)S(1)}, u32[]{:S(2)}, u32[]{:S(2)}) collective-permute-start(f32[2,128]{1,0:T(2,128)S(1)} %pad_maximum_fusion.4), channel_id=1, source_target_pairs={{0,1},{1,0},{2,3},{3,2},{4,5},{5,4},{6,7},{7,6},{8,9},{9,8},{10,11... | collective-permute-start | bytes 3080 | tf_op jit(solution)/shard_map/ppermute | solution.py:27
  53.7 24.6 %collective-permute-start.20 = (bf16[2,768,256]{2,1,0:T(8,128)(2,1)}, bf16[2,768,256]{2,1,0:T(8,128)(2,1)S(1)}, u32[]{:S(2)}, u32[]{:S(2)}) collective-permute-start(bf16[2,768,256]{2,1,0:T(8,128)(2,1)} %get-tuple-element.69), channel_id=1, source_target_pairs={{0,12},{1,5},{2,14},{3,7},{4,0},{5,9},{6,2},{7,11},{8,4},{9,13},{1... | collective-permute-start | bytes 2359304 | tf_op jit(solution)/shard_map/ppermute | solution.py:27
  56.5 22.4 %collective-permute-start.19 = (bf16[2,768,256]{2,1,0:T(8,128)(2,1)}, bf16[2,768,256]{2,1,0:T(8,128)(2,1)S(1)}, u32[]{:S(2)}, u32[]{:S(2)}) collective-permute-start(bf16[2,768,256]{2,1,0:T(8,128)(2,1)} %get-tuple-element.68), channel_id=1, source_target_pairs={{0,4},{1,13},{2,6},{3,15},{4,8},{5,1},{6,10},{7,3},{8,12},{9,5},{1... | collective-permute-start | bytes 2359304 | tf_op jit(solution)/shard_map/ppermute | solution.py:27
  58.3 15.3 %collective-permute-start.22 = (bf16[2,512,256]{2,1,0:T(8,128)(2,1)}, bf16[2,512,256]{2,1,0:T(8,128)(2,1)}, u32[]{:S(2)}, u32[]{:S(2)}) collective-permute-start(bf16[2,512,256]{2,1,0:T(8,128)(2,1)} %pad_maximum_fusion.1.refs_16_), channel_id=1, source_target_pairs={{0,16},{1,17},{2,18},{3,19},{4,20},{5,21},{6,22},{7,23},{8,24},{9,... | collective-permute-start | bytes 1572872 | tf_op jit(solution)/shard_map/ppermute | solution.py:27
  58.7 14.9 %collective-permute-start.21 = (bf16[2,512,256]{2,1,0:T(8,128)(2,1)}, bf16[2,512,256]{2,1,0:T(8,128)(2,1)}, u32[]{:S(2)}, u32[]{:S(2)}) collective-permute-start(bf16[2,512,256]{2,1,0:T(8,128)(2,1)} %pad_maximum_fusion.1.refs_16_), channel_id=1, source_target_pairs={{0,48},{1,49},{2,50},{3,51},{4,52},{5,53},{6,54},{7,55},{8,56},{9,... | collective-permute-start | bytes 1572872 | tf_op jit(solution)/shard_map/ppermute | solution.py:27
  61.6 20.5 %collective-permute-start.9 = (bf16[768,128]{1,0:T(8,128)(2,1)S(1)}, bf16[768,128]{1,0:T(8,128)(2,1)}, u32[]{:S(2)}, u32[]{:S(2)}) collective-permute-start(bf16[768,128]{1,0:T(8,128)(2,1)S(1)} %constant_dynamic-slice_fusion.2), channel_id=1, source_target_pairs={{0,1},{1,0},{2,3},{3,2},{4,5},{5,4},{6,7},{7,6},{8,9},{9,8},{10,11... | collective-permute-start | bytes 589832 | tf_op jit(solution)/shard_map/ppermute | solution.py:27
  80.9 9.0 %collective-permute-start.23 = (bf16[768,256]{1,0:T(8,128)(2,1)S(1)}, bf16[768,256]{1,0:T(8,128)(2,1)S(1)}, u32[]{:S(2)}, u32[]{:S(2)}) collective-permute-start(bf16[768,256]{1,0:T(8,128)(2,1)S(1)} %get-tuple-element.110), channel_id=1, source_target_pairs={{0,4},{1,13},{2,6},{3,15},{4,8},{5,1},{6,10},{7,3},{8,12},{9,5},{1... | collective-permute-start | bytes 1179656 | tf_op jit(solution)/shard_map/ppermute | solution.py:27
  83.1 20.5 %collective-permute-start.25 = (bf16[768,256]{1,0:T(8,128)(2,1)}, bf16[768,256]{1,0:T(8,128)(2,1)}, u32[]{:S(2)}, u32[]{:S(2)}) collective-permute-start(bf16[768,256]{1,0:T(8,128)(2,1)} %get-tuple-element.109), channel_id=1, source_target_pairs={{0,4},{1,13},{2,6},{3,15},{4,8},{5,1},{6,10},{7,3},{8,12},{9,5},{1... | collective-permute-start | bytes 1179656 | tf_op jit(solution)/shard_map/ppermute | solution.py:27
  86.6 17.0 %collective-permute-start.26 = (bf16[2,512,256]{2,1,0:T(8,128)(2,1)}, bf16[2,512,256]{2,1,0:T(8,128)(2,1)}, u32[]{:S(2)}, u32[]{:S(2)}) collective-permute-start(bf16[2,512,256]{2,1,0:T(8,128)(2,1)} %broadcast_select_fusion), channel_id=1, source_target_pairs={{0,16},{1,49},{2,18},{3,51},{4,20},{5,53},{6,22},{7,55},{8,24},{9,... | collective-permute-start | bytes 1572872 | tf_op jit(solution)/shard_map/ppermute | solution.py:27
  90.8 12.8 %collective-permute-start.24 = (bf16[768,256]{1,0:T(8,128)(2,1)}, bf16[768,256]{1,0:T(8,128)(2,1)}, u32[]{:S(2)}, u32[]{:S(2)}) collective-permute-start(bf16[768,256]{1,0:T(8,128)(2,1)} %fusion.3), channel_id=1, source_target_pairs={{0,2},{1,3},{2,0},{3,1},{4,6},{5,7},{6,4},{7,5},{8,10},{9,11},{10,... | collective-permute-start | bytes 1179656 | tf_op jit(solution)/shard_map/ppermute | solution.py:27
  105.2 9.3 %collective-permute-start.29 = (bf16[768,256]{1,0:T(8,128)(2,1)S(1)}, bf16[768,256]{1,0:T(8,128)(2,1)S(1)}, u32[]{:S(2)}, u32[]{:S(2)}) collective-permute-start(bf16[768,256]{1,0:T(8,128)(2,1)S(1)} %get-tuple-element.108.refs_0_), channel_id=1, source_target_pairs={{0,4},{1,5},{2,6},{3,7},{4,8},{5,9},{6,10},{7,11},{8,12},{9,13},{1... | collective-permute-start | bytes 1179656 | tf_op jit(solution)/shard_map/ppermute | solution.py:27
  106.0 9.1 %collective-permute-start.28 = (bf16[768,256]{1,0:T(8,128)(2,1)S(1)}, bf16[768,256]{1,0:T(8,128)(2,1)S(1)}, u32[]{:S(2)}, u32[]{:S(2)}) collective-permute-start(bf16[768,256]{1,0:T(8,128)(2,1)S(1)} %get-tuple-element.108.refs_0_), channel_id=1, source_target_pairs={{0,12},{1,13},{2,14},{3,15},{4,0},{5,1},{6,2},{7,3},{8,4},{9,5},{1... | collective-permute-start | bytes 1179656 | tf_op jit(solution)/shard_map/ppermute | solution.py:27
  108.5 9.3 %collective-permute-start.27 = (bf16[768,256]{1,0:T(8,128)(2,1)S(1)}, bf16[768,256]{1,0:T(8,128)(2,1)S(1)}, u32[]{:S(2)}, u32[]{:S(2)}) collective-permute-start(bf16[768,256]{1,0:T(8,128)(2,1)S(1)} %get-tuple-element.108.refs_0_), channel_id=1, source_target_pairs={{0,2},{1,3},{2,0},{3,1},{4,6},{5,7},{6,4},{7,5},{8,10},{9,11},{10,... | collective-permute-start | bytes 1179656 | tf_op jit(solution)/shard_map/ppermute | solution.py:27
  117.8 13.3 %collective-permute-start.31 = (bf16[768,256]{1,0:T(8,128)(2,1)S(1)}, bf16[768,256]{1,0:T(8,128)(2,1)S(1)}, u32[]{:S(2)}, u32[]{:S(2)}) collective-permute-start(bf16[768,256]{1,0:T(8,128)(2,1)S(1)} %collective-permute-done.27.refs_1_), channel_id=1, source_target_pairs={{0,4},{1,5},{2,6},{3,7},{4,8},{5,9},{6,10},{7,11},{8,12},{9,13},{1... | collective-permute-start | bytes 1179656 | tf_op jit(solution)/shard_map/ppermute | solution.py:27
  118.4 12.7 %collective-permute-start.30 = (bf16[768,256]{1,0:T(8,128)(2,1)S(1)}, bf16[768,256]{1,0:T(8,128)(2,1)S(1)}, u32[]{:S(2)}, u32[]{:S(2)}) collective-permute-start(bf16[768,256]{1,0:T(8,128)(2,1)S(1)} %collective-permute-done.27.refs_1_), channel_id=1, source_target_pairs={{0,12},{1,13},{2,14},{3,15},{4,0},{5,1},{6,2},{7,3},{8,4},{9,5},{1... | collective-permute-start | bytes 1179656 | tf_op jit(solution)/shard_map/ppermute | solution.py:27
  121.2 9.9 %collective-permute-start.32 = (bf16[768,256]{1,0:T(8,128)(2,1)S(1)}, bf16[768,256]{1,0:T(8,128)(2,1)S(1)}, u32[]{:S(2)}, u32[]{:S(2)}) collective-permute-start(bf16[768,256]{1,0:T(8,128)(2,1)S(1)} %broadcast_select_fusion.2), channel_id=1, source_target_pairs={{0,4},{1,13},{2,6},{3,15},{4,8},{5,1},{6,10},{7,3},{8,12},{9,5},{1... | collective-permute-start | bytes 1179656 | tf_op jit(solution)/shard_map/ppermute | solution.py:27
  124.0 12.3 %collective-permute-start.37 = (bf16[768,256]{1,0:T(8,128)(2,1)S(1)}, bf16[768,256]{1,0:T(8,128)(2,1)S(1)}, u32[]{:S(2)}, u32[]{:S(2)}) collective-permute-start(bf16[768,256]{1,0:T(8,128)(2,1)S(1)} %get-tuple-element.108.refs_0_), channel_id=1, source_target_pairs={{0,1},{1,0},{2,3},{3,2},{4,5},{5,4},{6,7},{7,6},{8,9},{9,8},{10,11... | collective-permute-start | bytes 1179656 | tf_op jit(solution)/shard_map/ppermute | solution.py:27
  126.0 11.1 %collective-permute-start.39 = (bf16[768,256]{1,0:T(8,128)(2,1)S(1)}, bf16[768,256]{1,0:T(8,128)(2,1)S(1)}, u32[]{:S(2)}, u32[]{:S(2)}) collective-permute-start(bf16[768,256]{1,0:T(8,128)(2,1)S(1)} %collective-permute-done.28.refs_2_), channel_id=1, source_target_pairs={{0,1},{1,0},{2,3},{3,2},{4,5},{5,4},{6,7},{7,6},{8,9},{9,8},{10,11... | collective-permute-start | bytes 1179656 | tf_op jit(solution)/shard_map/ppermute | solution.py:27
  131.2 9.2 %collective-permute-start.35 = (bf16[768,256]{1,0:T(8,128)(2,1)S(1)}, bf16[768,256]{1,0:T(8,128)(2,1)S(1)}, u32[]{:S(2)}, u32[]{:S(2)}) collective-permute-start(bf16[768,256]{1,0:T(8,128)(2,1)S(1)} %broadcast_select_fusion.1), channel_id=1, source_target_pairs={{0,4},{1,13},{2,6},{3,15},{4,8},{5,1},{6,10},{7,3},{8,12},{9,5},{1... | collective-permute-start | bytes 1179656 | tf_op jit(solution)/shard_map/ppermute | solution.py:27
  151.0 16.6 %collective-permute-start.45 = (bf16[2,512,256]{2,1,0:T(8,128)(2,1)}, bf16[2,512,256]{2,1,0:T(8,128)(2,1)S(1)}, u32[]{:S(2)}, u32[]{:S(2)}) collective-permute-start(bf16[2,512,256]{2,1,0:T(8,128)(2,1)} %get-tuple-element.94), channel_id=1, source_target_pairs={{0,16},{1,49},{2,18},{3,51},{4,20},{5,53},{6,22},{7,55},{8,24},{9,... | collective-permute-start | bytes 1572872 | tf_op jit(solution)/shard_map/ppermute | solution.py:27
  154.2 13.7 %collective-permute-start.46 = (bf16[2,512,256]{2,1,0:T(8,128)(2,1)}, bf16[2,512,256]{2,1,0:T(8,128)(2,1)S(1)}, u32[]{:S(2)}, u32[]{:S(2)}) collective-permute-start(bf16[2,512,256]{2,1,0:T(8,128)(2,1)} %get-tuple-element.95), channel_id=1, source_target_pairs={{0,48},{1,17},{2,50},{3,19},{4,52},{5,21},{6,54},{7,23},{8,56},{9,... | collective-permute-start | bytes 1572872 | tf_op jit(solution)/shard_map/ppermute | solution.py:27
  (58 other events, 342.4 us)
Sparse Core Ops, SparseCore 0:
  10.3 76.8 all-gather.1
  117.9 42.5 reduce-scatter.1
